TPU v7x, 32 devices: a whole 2x2x4 slice. The times are simulated.
32 devices in a mesh: band: 1, chan: 16 (over z, y, core), stn: 2 (over x).
Axes of the slice: x: 2, y: 2, z: 4, core: 2. Of those that a mesh axis runs over, the one named last changes fastest.
Arguments:
- observed: bfloat16 [8, 16, 2, 8, 256, 256], P('stn', ('band', 'chan')), may hold values from -18 to 18
- pair_table: int32 [8], P('stn'), may hold values from 0 to 3, as said below
- flag_rows: int32 [8], P('stn'), may hold values from 0 to 64
- gains: float32 [8, 8, 16, 512], P(None, None, ('band', 'chan'), 'stn'), may hold values from -3 to 3
- duals: float32 [8, 8, 16, 512], P(None, None, ('band', 'chan'), 'stn'), may hold values from -1.2 to 1.2
- prior_coeffs: float32 [8, 8, 4, 512], P('band', None, None, 'stn'), may hold values from -3 to 3
- delays: float32 [2, 8, 512], P(None, None, 'stn'), may hold values from -8 to 8
- brightness: float32 [8, 8], P('band'), may hold values from -2 to 2
Outputs:
- gains_out: float32 [8, 8, 16, 512], P(None, None, ('band', 'chan'), 'stn')
- coeffs_out: float32 [8, 8, 4, 512], P('band', None, None, 'stn')
- duals_out: float32 [8, 8, 16, 512], P(None, None, ('band', 'chan'), 'stn')
Inputs may be any that keep to these rules, and one draw needn't show every extreme that they name: `pair_table`: each pair id 0 .. 2 stands in exactly one slot; every other slot holds 3.
All inputs are finite; a program needn't handle non-finite values.
Results may differ from a plain program's by a relative error of at most 0.0003.
Values sent between devices are 32-bit elements; how exact they have to be, the bound alone decides.
No kernel may reach another device: no remote copies, remote signals or barrier semaphores. Data moves between devices by JAX's collectives and lax.ppermute only.
A program may use at most 128 MiB of HBM per device.

v0:
```python
import functools
import math

import jax
import jax.numpy as jnp
import numpy as np
from jax import lax
from jax.experimental import pallas as pl
from jax.experimental.pallas import tpu as pltpu
from jax.sharding import PartitionSpec as P

ITERS = 3
EPSILON = 1e-06
SPECTRAL_INDEX = 0.7
DIRS = 8
CHUNK = 128
VMEM_BYTES = 48 * 1024 * 1024
F32 = jnp.float32
BF16 = jnp.bfloat16

NT = (((1,), (1,)), ((), ()))
NN = (((1,), (0,)), ((), ()))
TN = (((0,), (0,)), ((), ()))


def dot(lhs, rhs, dims):
    return lax.dot_general(lhs, rhs, dims, preferred_element_type=F32)


def pair_lists(station_blocks):
    return [(p, q) for p in range(station_blocks) for q in range(p, station_blocks)]


def bernstein_np(total_channels):
    position = (np.arange(total_channels, dtype=np.float64) + 0.5) / total_channels
    others = 1.0 - position
    return np.stack(
        [others**3, 3.0 * position * others**2, 3.0 * position**2 * others, position**3], axis=1
    )


def split(x):
    high = x.astype(BF16)
    return high, (x - high.astype(F32)).astype(BF16)


def pack(x):
    high, low = split(x)
    return jnp.concatenate([high, low], axis=0)


def trig(delay, freq):
    turns = delay * freq
    turns = turns - jnp.floor(turns + 0.5)
    x = turns * math.pi
    x2 = x * x
    sin_half = x * (
        1.0
        + x2
        * (
            -1.0 / 6
            + x2
            * (
                1.0 / 120
                + x2
                * (
                    -1.0 / 5040
                    + x2 * (1.0 / 362880 + x2 * (-1.0 / 39916800 + x2 * (1.0 / 6227020800)))
                )
            )
        )
    )
    cos_half = 1.0 + x2 * (
        -0.5
        + x2
        * (
            1.0 / 24
            + x2
            * (
                -1.0 / 720
                + x2
                * (
                    1.0 / 40320
                    + x2 * (-1.0 / 3628800 + x2 * (1.0 / 479001600 + x2 * (-1.0 / 87178291200)))
                )
            )
        )
    )
    return 1.0 - 2.0 * sin_half * sin_half, 2.0 * sin_half * cos_half


def rotate(field, cosine, sine):
    re = [field[8 * m : 8 * m + 8] for m in range(4)]
    im = [field[32 + 8 * m : 40 + 8 * m] for m in range(4)]
    return (
        [cosine * re[m] - sine * im[m] for m in range(4)],
        [cosine * im[m] + sine * re[m] for m in range(4)],
    )


def coherency_rows(coh, width):
    reps = width // coh.shape[1]
    rows = [jnp.concatenate([coh[8 * e : 8 * e + 8]] * reps, axis=1) for e in range(8)]
    return rows[:4], rows[4:]


def left_rows(rot, bright):
    (a_re, a_im), (c_re, c_im) = rot, bright
    out = []
    for i in range(2):
        re_rows, im_rows = [], []
        for l in range(2):
            re = im = None
            for k in range(2):
                ar, ai, cr, ci = a_re[2 * i + k], a_im[2 * i + k], c_re[2 * k + l], c_im[2 * k + l]
                tr, ti = ar * cr - ai * ci, ar * ci + ai * cr
                re, im = (tr, ti) if re is None else (re + tr, im + ti)
            re_rows.append(re)
            im_rows.append(im)
        out.append(jnp.concatenate(re_rows + im_rows, axis=0))
    return out


def right_rows(rot):
    a_re, a_im = rot
    real = [
        jnp.concatenate([a_re[2 * j], a_re[2 * j + 1], a_im[2 * j], a_im[2 * j + 1]], axis=0)
        for j in range(2)
    ]
    imag = [
        jnp.concatenate([-a_im[2 * j], -a_im[2 * j + 1], a_re[2 * j], a_re[2 * j + 1]], axis=0)
        for j in range(2)
    ]
    return real + imag


def field_gradient(h_left, h_right, bright, cosine, sine):
    c_re, c_im = bright
    g_re, g_im = [], []
    for i in range(2):
        for k in range(2):
            j = i
            re = h_right[j][8 * k : 8 * k + 8] + h_right[2 + j][16 + 8 * k : 24 + 8 * k]
            im = h_right[j][16 + 8 * k : 24 + 8 * k] - h_right[2 + j][8 * k : 8 * k + 8]
            for l in range(2):
                lr = h_left[i][8 * l : 8 * l + 8]
                li = h_left[i][16 + 8 * l : 24 + 8 * l]
                cr, ci = c_re[2 * k + l], c_im[2 * k + l]
                re = re + lr * cr + li * ci
                im = im + li * cr - lr * ci
            g_re.append(cosine * re + sine * im)
            g_im.append(cosine * im - sine * re)
    return jnp.concatenate(g_re + g_im, axis=0)


def data_kernel(
    block,
    pairs,
    dumps,
    slots,
    penalty,
    with_target,
    table,
    flags,
    own,
    freq,
    field_ref,
    delay_ref,
    coh_ref,
    *refs,
):
    if with_target:
        target_ref, refs = refs[0], refs[1:]
    observed, out_ref, held, sems, xp, yp, hl, ha = refs
    stations = field_ref.shape[1]
    pair_count = len(pairs)

    def copy_of(slot, t):
        return pltpu.make_async_copy(observed.at[slot, t], held.at[slot, t], sems.at[slot, t])

    for slot in range(slots):

        @pl.when(table[slot] < pair_count)
        def _():
            for t in range(dumps):
                copy_of(slot, t).start()

    freq_value = freq[0]
    bright = coherency_rows(coh_ref[...], stations)
    for t in range(dumps):
        cosine, sine = trig(delay_ref[8 * t : 8 * t + 8, :], freq_value)
        rot = rotate(field_ref[...], cosine, sine)
        for i, rows in enumerate(left_rows(rot, bright)):
            xp[t, i] = pack(rows)
        for rj, rows in enumerate(right_rows(rot)):
            yp[t, rj] = pack(rows)
    hl[...] = jnp.zeros_like(hl)
    ha[...] = jnp.zeros_like(ha)

    def visit(slot, unused):
        pair = table[slot]

        @pl.when(pair < pair_count)
        def _():
            first, second = jnp.int32(0), jnp.int32(0)
            for k, (p, q) in enumerate(pairs):
                first = first + jnp.where(pair == k, p, 0)
                second = second + jnp.where(pair == k, q, 0)
            row = lax.broadcasted_iota(jnp.int32, (block, block), 0)
            col = lax.broadcasted_iota(jnp.int32, (block, block), 1)
            keep = (row < col) | (first < second)
            lane = lax.broadcasted_iota(jnp.int32, (1, block), 1)
            live = (lane >= flags[slot]).astype(F32)
            live16 = live.astype(BF16)
            at_p = pl.ds(pl.multiple_of(first * block, CHUNK), block)
            at_q = pl.ds(pl.multiple_of(second * block, CHUNK), block)
            for t in range(dumps):
                copy_of(slot, t).wait()
                acc_left = [None, None]
                acc_right = [None] * 4
                xs = [xp[t, i, :, at_p] * live16 for i in range(2)]
                ys = [yp[t, rj, :, at_q] for rj in range(4)]
                for r in range(2):
                    for i in range(2):
                        for j in range(2):
                            tile = held[slot, t, 4 * r + 2 * i + j]
                            tile = jnp.where(keep, tile, jnp.zeros_like(tile))
                            rj = 2 * r + j
                            left = dot(ys[rj], tile, NT)
                            right = dot(xs[i], tile, NN)
                            acc_left[i] = left if acc_left[i] is None else acc_left[i] + left
                            acc_right[rj] = right if acc_right[rj] is None else acc_right[rj] + right
                for i in range(2):
                    hl[t, i, :, at_p] += (acc_left[i][:32] + acc_left[i][32:]) * live
                for rj in range(4):
                    ha[t, rj, :, at_q] += acc_right[rj][:32] + acc_right[rj][32:]

        return unused

    lax.fori_loop(0, slots, visit, jnp.int32(0))

    total = None
    for t in range(dumps):
        cosine, sine = trig(delay_ref[8 * t : 8 * t + 8, :], freq_value)
        piece = field_gradient(
            [hl[t, i] for i in range(2)], [ha[t, rj] for rj in range(4)], bright, cosine, sine
        )
        total = piece if total is None else total + piece
    out_ref[...] = -total
    at_own = pl.ds(pl.multiple_of(own[0] * block, CHUNK), block)
    prior = field_ref[:, at_own]
    if with_target:
        prior = prior - target_ref[...]
    out_ref[:, at_own] += penalty * prior


def data_part(geometry, table, flags, own, freq, field, delays, coh, target, observed):
    block, pairs, penalty = geometry
    slots, dumps = observed.shape[:2]
    stations = field.shape[1]
    smem = pl.BlockSpec(memory_space=pltpu.SMEM)
    vmem = pl.BlockSpec(memory_space=pltpu.VMEM)
    hbm = pl.BlockSpec(memory_space=pl.ANY)
    with_target = target is not None
    body = functools.partial(data_kernel, block, pairs, dumps, slots, penalty, with_target)
    extra = (target,) if with_target else ()
    return pl.pallas_call(
        body,
        name="data_part",
        out_shape=jax.ShapeDtypeStruct(field.shape, F32),
        in_specs=[smem] * 4 + [vmem] * (3 + len(extra)) + [hbm],
        out_specs=vmem,
        scratch_shapes=[
            pltpu.VMEM(observed.shape, BF16),
            pltpu.SemaphoreType.DMA((slots, dumps)),
            pltpu.VMEM((dumps, 2, 64, stations), BF16),
            pltpu.VMEM((dumps, 4, 64, stations), BF16),
            pltpu.VMEM((dumps, 2, 32, stations), F32),
            pltpu.VMEM((dumps, 4, 32, stations), F32),
        ],
        compiler_params=pltpu.CompilerParams(vmem_limit_bytes=VMEM_BYTES),
        cost_estimate=pl.CostEstimate(
            flops=6000000000, bytes_accessed=8000000, transcendentals=0
        ),
    )(table, flags, own, freq, field, delays, coh, *extra, observed)


def fold_gram(high_low, other, rows):
    wide = dot(high_low, other[:rows], NT)
    return wide[:rows] + wide[rows:] + dot(high_low[:rows], other[rows:], NT)


def apply_gram(gram, packed, rows):
    size = gram.shape[0]
    both = pack(gram)
    wide = dot(both, packed[:rows], NN)
    return wide[:size] + wide[size:] + dot(both[:size], packed[rows:], NN)


def lanes(parts, start, size):
    return jnp.concatenate([part[:, start : start + size] for part in parts], axis=1)


def model_kernel(block, pairs, dumps, penalty, update, freq, *refs):
    if update:
        scal_ref, current_ref, previous_ref, linear_ref, mine_ref, theirs_ref, *refs = refs
    else:
        current_ref, mine_ref, theirs_ref, *refs = refs
    delay_ref, coh_ref, table_ref, current_out, linear_out, direction_out, sums_out, hl, ha = refs
    stations = current_ref.shape[1]
    chunk = min(CHUNK, block)
    per_block = block // chunk
    chunks = stations // chunk
    blocks = stations // block

    step_linear = mine_ref[...] + theirs_ref[...]
    if update:
        grad_sq = scal_ref[0:1, :]
        curvature = scal_ref[1:2, :]
        alpha = grad_sq / (curvature + penalty * grad_sq + EPSILON)
        alpha = jnp.concatenate([alpha] * (stations // 128), axis=1)
        current = current_ref[...] - alpha * previous_ref[...]
        linear = linear_ref[...] - alpha * step_linear
    else:
        current = current_ref[...]
        linear = step_linear
    current_out[...] = current
    linear_out[...] = linear

    ids, counts = table_ref[0:1, :], table_ref[1:2, :]
    lane = lax.broadcasted_iota(jnp.int32, (1, block), 1).astype(F32)
    masks = {}
    for k, pair in enumerate(pairs):
        flagged = jnp.sum(jnp.where(ids == float(k), counts, 0.0), axis=1, keepdims=True)
        masks[pair] = (lane >= flagged).astype(F32)

    def mask_of(pair, chunk_id):
        start = (chunk_id % per_block) * chunk
        return masks[pair][:, start : start + chunk]

    def twice(mask):
        return jnp.concatenate([mask, mask], axis=1)

    row = lax.broadcasted_iota(jnp.int32, (2 * chunk, 4 * chunk), 0) % chunk
    col = lax.broadcasted_iota(jnp.int32, (2 * chunk, 4 * chunk), 1) % chunk
    upper = row < col

    freq_value = freq[0]
    bright = coherency_rows(coh_ref[...], stations)

    def rect_terms(chunk_id):
        own = chunk_id // per_block
        terms = []
        inside = [c for c in range(chunk_id + 1, (own + 1) * per_block)]
        if inside:
            terms.append(((own, own), inside))
        for q in range(own + 1, blocks):
            terms.append(((own, q), list(range(q * per_block, (q + 1) * per_block))))
        return terms

    gradient = linear
    trigs = []
    for t in range(dumps):
        cosine, sine = trig(delay_ref[8 * t : 8 * t + 8, :], freq_value)
        trigs.append((cosine, sine))
        rot = rotate(current, cosine, sine)
        xs = [pack(v) for v in left_rows(rot, bright)]
        ys = [pack(v) for v in right_rows(rot)]
        gram_y = [
            fold_gram(lanes(ys, c * chunk, chunk), lanes(ys, c * chunk, chunk), 32)
            for c in range(chunks)
        ]
        sums_x = [None] * chunks
        for c in range(chunks):
            xc = lanes(xs, c * chunk, chunk)
            yc = lanes(ys, c * chunk, chunk)
            own = c // per_block
            xw = xc * twice(mask_of((own, own), c)).astype(BF16)
            yn = jnp.concatenate([yc[:32], yc[:32], yc[32:], yc[32:]], axis=0)
            model = dot(jnp.concatenate([xw, xw], axis=0), yn, TN)
            model = jnp.where(upper, model, 0.0)
            high, low = split(model)
            left = dot(yc, high, NT) + dot(yc, low, NT)
            right = dot(xw, high, NN) + dot(xw, low, NN)
            left = left[:32] + left[32:]
            right = right[:32] + right[32:]
            for pair, others in rect_terms(c):
                gram = gram_y[others[0]]
                for o in others[1:]:
                    gram = gram + gram_y[o]
                mask = twice(mask_of(pair, c))
                left = left + apply_gram(gram, xc, 32) * mask
                gram_x = fold_gram(xc * mask.astype(BF16), xc, 32)
                for o in others:
                    sums_x[o] = gram_x if sums_x[o] is None else sums_x[o] + gram_x
            if sums_x[c] is not None:
                right = right + apply_gram(sums_x[c], yc, 32)
            for i in range(2):
                hl[i, :, c * chunk : (c + 1) * chunk] = left[:, i * chunk : (i + 1) * chunk]
            for rj in range(4):
                ha[rj, :, c * chunk : (c + 1) * chunk] = right[:, rj * chunk : (rj + 1) * chunk]
        gradient = gradient + field_gradient(
            [hl[i] for i in range(2)], [ha[rj] for rj in range(4)], bright, cosine, sine
        )
    direction_out[...] = gradient
    direction = gradient

    squares = jnp.zeros((8, 4 * chunk), F32)
    grams = jnp.zeros((64, 64), F32)
    for t in range(dumps):
        cosine, sine = trigs[t]
        rot = rotate(current, cosine, sine)
        step = rotate(direction, cosine, sine)
        xs = [pack(v) for v in left_rows(rot, bright)]
        ys = [pack(v) for v in right_rows(rot)]
        dxs = [pack(v) for v in left_rows(step, bright)]
        dys = [pack(v) for v in right_rows(step)]

        def stacked(first, second, c):
            one = lanes(first, c * chunk, chunk)
            two = lanes(second, c * chunk, chunk)
            return jnp.concatenate([one[:32], two[:32], one[32:], two[32:]], axis=0)

        gram_y = [None] * chunks
        for c in range(chunks):
            xc = stacked(dxs, xs, c)
            yc = stacked(ys, dys, c)
            own = c // per_block
            xw = xc * twice(mask_of((own, own), c)).astype(BF16)
            tangent = dot(
                jnp.concatenate([xw, xw], axis=0),
                jnp.concatenate([yc[:64], yc[:64], yc[64:], yc[64:]], axis=0),
                TN,
            )
            tangent = jnp.where(upper, tangent, 0.0)
            square = tangent * tangent
            squares = squares + jnp.sum(square.reshape(2 * chunk // 8, 8, 4 * chunk), axis=0)
            if c > 0:
                gram_y[c] = fold_gram(yc, yc, 64)
        for c in range(chunks):
            for pair, others in rect_terms(c):
                gram = gram_y[others[0]]
                for o in others[1:]:
                    gram = gram + gram_y[o]
                xc = stacked(dxs, xs, c)
                gram_x = fold_gram(xc * twice(mask_of(pair, c)).astype(BF16), xc, 64)
                grams = grams + gram * gram_x
    curvature = jnp.sum(squares, keepdims=True) + jnp.sum(grams, keepdims=True)
    grad_sq = jnp.sum(direction * direction, keepdims=True)
    row8 = lax.broadcasted_iota(jnp.int32, (8, 128), 0)
    sums_out[...] = jnp.where(row8 == 0, grad_sq, jnp.where(row8 == 1, curvature, 0.0))


def model_part(geometry, dumps, freq, state, delays, coh, table):
    block, pairs, penalty = geometry
    smem = pl.BlockSpec(memory_space=pltpu.SMEM)
    vmem = pl.BlockSpec(memory_space=pltpu.VMEM)
    update = len(state) == 6
    field = state[1] if update else state[0]
    stations = field.shape[1]
    like = jax.ShapeDtypeStruct(field.shape, F32)
    return pl.pallas_call(
        functools.partial(model_kernel, block, pairs, dumps, penalty, update),
        name="model_part",
        out_shape=(like, like, like, jax.ShapeDtypeStruct((8, 128), F32)),
        in_specs=[smem] + [vmem] * (len(state) + 3),
        out_specs=(vmem,) * 4,
        scratch_shapes=[pltpu.VMEM((2, 32, stations), F32), pltpu.VMEM((4, 32, stations), F32)],
        compiler_params=pltpu.CompilerParams(vmem_limit_bytes=VMEM_BYTES),
        cost_estimate=pl.CostEstimate(
            flops=6000000000, bytes_accessed=2000000, transcendentals=0
        ),
    )(freq, *state, delays, coh, table)


def chan_sum(value, count):
    bit = 1
    while bit < count:
        offsets = [bit, 2 * bit, 3 * bit] if 4 * bit <= count else [bit]
        got = [lax.ppermute(value, "chan", [(i, i ^ o) for i in range(count)]) for o in offsets]
        if len(got) == 3:
            value = (value + got[0]) + (got[1] + got[2])
            bit *= 4
        else:
            value = value + got[0]
            bit *= 2
    return value


def other_stations(value, count):
    if count == 2:
        return lax.ppermute(value, "stn", [(0, 1), (1, 0)])
    return lax.psum(value, "stn") - value


def shards(observed, pair_table, flag_rows, gains, duals, prior_coeffs, delays, brightness):
    stn_count = lax.axis_size("stn")
    chan_count = lax.axis_size("chan")
    stn_index = lax.axis_index("stn")
    chan_index = lax.axis_index("chan")
    entries, dirs, chan_local, block = gains.shape
    slots, dumps = observed.shape[0], observed.shape[2]
    stations = block * stn_count
    pairs = pair_lists(stn_count)
    penalty = stations * dumps / 16.0
    geometry = (block, pairs, penalty)
    basis = bernstein_np(chan_count)
    solve = basis @ np.linalg.inv(basis.T @ basis)
    basis_row = lax.dynamic_slice_in_dim(jnp.asarray(basis, F32), chan_index, 1, 0)[0]
    solve_row = lax.dynamic_slice_in_dim(jnp.asarray(solve, F32), chan_index, 1, 0)[0]

    frequency = 1.0 + chan_index.astype(F32) / chan_count
    coh = brightness * frequency ** (-SPECTRAL_INDEX)
    coh = jnp.broadcast_to(coh.reshape(entries * dirs, 1), (entries * dirs, 128))
    freq = frequency.reshape(1)
    own = stn_index.reshape(1).astype(jnp.int32)

    gains_own = gains.reshape(entries * dirs, block)
    duals_own = duals.reshape(entries * dirs, block)
    ids = jnp.pad(pair_table.astype(F32), (0, block - slots), constant_values=-1.0)
    counts = jnp.pad(flag_rows.astype(F32), (0, block - slots))
    rows = jnp.concatenate(
        [gains_own, delays.reshape(dumps * dirs, block), ids[None], counts[None], jnp.zeros((6, block), F32)]
    )
    rows = lax.all_gather(rows, "stn", axis=1, tiled=True)
    field = rows[: entries * dirs]
    delay_all = rows[entries * dirs : entries * dirs + dumps * dirs]
    table = rows[entries * dirs + dumps * dirs :]

    prior = prior_coeffs.reshape(entries * dirs, 4, block)
    prior_fit = sum(basis_row[k] * prior[:, k] for k in range(4))
    target = prior_fit - duals_own

    observed = observed.reshape((slots,) + observed.shape[2:])
    data = functools.partial(data_part, geometry, pair_table, flag_rows, own, freq)
    mine = data(field, delay_all, coh, target, observed)
    theirs = other_stations(mine, stn_count)
    state = (field, mine, theirs)
    for iteration in range(ITERS):
        current, linear, direction, sums = model_part(
            geometry, dumps, freq, state, delay_all, coh, table
        )
        if iteration + 1 < ITERS:
            mine = data(direction, delay_all, coh, None, observed)
            theirs = other_stations(mine, stn_count)
        sums = chan_sum(sums, chan_count)
        state = (sums, current, direction, linear, mine, theirs)

    alpha = sums[0, 0] / (sums[1, 0] + penalty * sums[0, 0] + EPSILON)
    at_own = stn_index * block
    gains_new = lax.dynamic_slice_in_dim(
        current, at_own, block, 1
    ) - alpha * lax.dynamic_slice_in_dim(direction, at_own, block, 1)
    shifted = gains_new + duals_own
    parts = jnp.stack([solve_row[k] * shifted for k in range(4)])
    parts = parts.reshape(chan_count, -1, 128)
    parts = jnp.sum(lax.all_to_all(parts, "chan", 0, 0, tiled=True), axis=0)
    parts = jnp.broadcast_to(parts[None], (chan_count,) + parts.shape)
    coeffs = lax.all_to_all(parts, "chan", 0, 0, tiled=True).reshape(4, entries * dirs, block)
    fitted = sum(basis_row[k] * coeffs[k] for k in range(4))
    coeffs_out = jnp.transpose(coeffs.reshape(4, entries, dirs, block), (1, 2, 0, 3))
    return (
        gains_new.reshape(gains.shape),
        coeffs_out,
        (shifted - fitted).reshape(gains.shape),
    )


def solution(mesh):
    return jax.shard_map(
        shards,
        mesh=mesh,
        in_specs=(
            P("stn", ("band", "chan"), None, None, None, None),
            P("stn"),
            P("stn"),
            P(None, None, ("band", "chan"), "stn"),
            P(None, None, ("band", "chan"), "stn"),
            P("band", None, None, "stn"),
            P(None, None, "stn"),
            P("band", None),
        ),
        out_specs=(
            P(None, None, ("band", "chan"), "stn"),
            P("band", None, None, "stn"),
            P(None, None, ("band", "chan"), "stn"),
        ),
        check_vma=False,
    )
```

profile of v0, /device:TPU:0, one launch (start us, length us, event | category | flops | bytes accessed | tf_op | source)
XLA Modules:
  0.0 134.4 jit_solution(12651672675822333329)
XLA Ops:
  0.6 0.8 copy.28
  1.5 0.7 convert_element_type.12
  2.1 0.7 convert_element_type.13
  2.8 0.7 concatenate.3
  3.6 6.2 %all_gather.3 = f32[88,512]{1,0:T(8,128)S(1)} all-gather(f32[88,256]{1,0:T(8,128)S(1)} %concatenate.3), channel_id=1, replica_groups=mesh['band'=1,'chan'=16,'stn'=2] {'stn'}, dimensions={1}, use_global_device_ids=true | all-gather | bytes 270336 | tf_op jit(solution)/shard_map/all_gather | solution.py:525
  9.8 0.7 constant_dynamic-slice_fusion
  10.5 0.7 fusion.11
  11.2 1.0 copy.27
  12.2 0.7 broadcast_multiply_fusion
  13.0 3.4 %fusion.5.refs_0_ = f32[64,256]{1,0:T(8,128)S(1)} fusion(f32[64,4,256]{2,0,1:T(8,128)S(1)} %bitcast.43, f32[8,8,1,256]{3,2,1,0:T(1,128)} %param.14, f32[]{:T(128)} %bitcast.9, f32[]{:T(128)} %bitcast.8, f32[]{:T(128)} %bitcast.7, f32[]{:T(128)} %bitcast.5), kind=kLoop, calls=%fused_computation.12 | loop fusion | flops 131072 | bytes 393232 | tf_op jit(solution)/shard_map/sub | solution.py:532
  16.4 0.7 copy-done
  17.8 1.1 data_part.3.refs_1_
  18.9 6.7 %collective-permute-start = (f32[64,512]{1,0:T(8,128)S(1)}, f32[64,512]{1,0:T(8,128)S(1)}, u32[]{:S(2)}, u32[]{:S(2)}) collective-permute-start(f32[64,512]{1,0:T(8,128)S(1)} %data_part.3.refs_1_), channel_id=1, source_target_pairs={{0,1},{1,0},{2,3},{3,2},{4,5},{5,4},{6,7},{7,6},{8,9},{9,8},{10,11... | collective-permute-start | bytes 393224 | tf_op jit(solution)/shard_map/ppermute | solution.py:492
  25.6 2.9 %collective-permute-done.refs_2_ = f32[64,512]{1,0:T(8,128)S(1)} collective-permute-done((f32[64,512]{1,0:T(8,128)S(1)}, f32[64,512]{1,0:T(8,128)S(1)}, u32[]{:S(2)}, u32[]{:S(2)}) %collective-permute-start) | collective-permute-done | bytes 131104 | tf_op jit(solution)/shard_map/ppermute | solution.py:492
  28.5 5.3 %model_part.3 = (f32[64,512]{1,0:T(8,128)S(1)}, f32[64,512]{1,0:T(8,128)S(1)}, f32[64,512]{1,0:T(8,128)S(1)}, f32[8,128]{1,0:T(8,128)S(1)}) custom-call(f32[1]{0:T(128)} %bitcast.freq, f32[64,512]{1,0:T(8,128)S(1)} %slice.101.field_ref.refs_0_, f32[64,512]{1,0:T(8,128)S(1)} %data_part.3.refs_1_, f32[64,512]{1,0:T(8,128)S(1)} %collective-permute-done.refs_2_, ...), custom_call_target="tpu_custom_call" | custom-call | flops 6000000000 | bytes 2000000 | tf_op jit(solution)/shard_map/model_part/pallas_call | solution.py:462
  33.9 1.6 %collective-permute-start.2 = (f32[8,128]{1,0:T(8,128)S(1)}, f32[8,128]{1,0:T(8,128)S(1)}, u32[]{:S(2)}, u32[]{:S(2)}) collective-permute-start(f32[8,128]{1,0:T(8,128)S(1)} %get-tuple-element.14), channel_id=1, source_target_pairs={{0,4},{2,6},{4,0},{6,2},{8,12},{10,14},{12,8},{14,10},{16,20},{18,... | collective-permute-start | bytes 12296 | tf_op jit(solution)/shard_map/ppermute | solution.py:480
  35.8 1.8 %collective-permute-done.2 = f32[8,128]{1,0:T(8,128)S(1)} collective-permute-done((f32[8,128]{1,0:T(8,128)S(1)}, f32[8,128]{1,0:T(8,128)S(1)}, u32[]{:S(2)}, u32[]{:S(2)}) %collective-permute-start.2) | collective-permute-done | bytes 4128 | tf_op jit(solution)/shard_map/ppermute | solution.py:480
  37.6 0.9 collective-permute-done.3
  38.5 1.6 %collective-permute-start.4 = (f32[8,128]{1,0:T(8,128)S(1)}, f32[8,128]{1,0:T(8,128)S(1)}, u32[]{:S(2)}, u32[]{:S(2)}) collective-permute-start(f32[8,128]{1,0:T(8,128)S(1)} %add_add_fusion.5), channel_id=1, source_target_pairs={{0,8},{2,10},{4,12},{6,14},{8,0},{10,2},{12,4},{14,6},{16,24},{18,... | collective-permute-start | bytes 12296 | tf_op jit(solution)/shard_map/ppermute | solution.py:480
  40.1 2.6 %collective-permute-start.5 = (f32[8,128]{1,0:T(8,128)S(1)}, f32[8,128]{1,0:T(8,128)S(1)}, u32[]{:S(2)}, u32[]{:S(2)}) collective-permute-start(f32[8,128]{1,0:T(8,128)S(1)} %add_add_fusion.5), channel_id=1, source_target_pairs={{0,16},{2,18},{4,20},{6,22},{8,24},{10,26},{12,28},{14,30},{16,0},... | collective-permute-start | bytes 12296 | tf_op jit(solution)/shard_map/ppermute | solution.py:480
  42.9 1.1 data_part.4.refs_4_
  44.0 6.8 %collective-permute-start.7 = (f32[64,512]{1,0:T(8,128)S(1)}, f32[64,512]{1,0:T(8,128)S(1)}, u32[]{:S(2)}, u32[]{:S(2)}) collective-permute-start(f32[64,512]{1,0:T(8,128)S(1)} %data_part.4.refs_4_), channel_id=1, source_target_pairs={{0,1},{1,0},{2,3},{3,2},{4,5},{5,4},{6,7},{7,6},{8,9},{9,8},{10,11... | collective-permute-start | bytes 393224 | tf_op jit(solution)/shard_map/ppermute | solution.py:492
  50.8 3.0 %collective-permute-done.7.refs_5_ = f32[64,512]{1,0:T(8,128)S(1)} collective-permute-done((f32[64,512]{1,0:T(8,128)S(1)}, f32[64,512]{1,0:T(8,128)S(1)}, u32[]{:S(2)}, u32[]{:S(2)}) %collective-permute-start.7) | collective-permute-done | bytes 131104 | tf_op jit(solution)/shard_map/ppermute | solution.py:492
  53.8 5.3 %model_part.4 = (f32[64,512]{1,0:T(8,128)S(1)}, f32[64,512]{1,0:T(8,128)S(1)}, f32[64,512]{1,0:T(8,128)S(1)}, f32[8,128]{1,0:T(8,128)S(1)}) custom-call(f32[1]{0:T(128)} %bitcast.freq, f32[8,128]{1,0:T(8,128)S(1)} %add_add_fusion.4.refs_0_, f32[64,512]{1,0:T(8,128)S(1)} %get-tuple-element.15.refs_1_, f32[64,512]{1,0:T(8,128)S(1)} %get-tuple-element.16.field_ref.refs_2_, ...), custom_call_target="tpu_custom_call" | custom-call | flops 6000000000 | bytes 2000000 | tf_op jit(solution)/shard_map/model_part/pallas_call | solution.py:462
  59.9 1.5 %collective-permute-start.9 = (f32[8,128]{1,0:T(8,128)S(1)}, f32[8,128]{1,0:T(8,128)S(1)}, u32[]{:S(2)}, u32[]{:S(2)}) collective-permute-start(f32[8,128]{1,0:T(8,128)S(1)} %get-tuple-element.18), channel_id=1, source_target_pairs={{0,4},{2,6},{4,0},{6,2},{8,12},{10,14},{12,8},{14,10},{16,20},{18,... | collective-permute-start | bytes 12296 | tf_op jit(solution)/shard_map/ppermute | solution.py:480
  61.4 0.9 collective-permute-done.10
  62.3 1.2 collective-permute-done.9
  63.5 0.7 collective-permute-start.11
  64.2 3.5 %collective-permute-start.12 = (f32[8,128]{1,0:T(8,128)S(1)}, f32[8,128]{1,0:T(8,128)S(1)}, u32[]{:S(2)}, u32[]{:S(2)}) collective-permute-start(f32[8,128]{1,0:T(8,128)S(1)} %add_add_fusion.3), channel_id=1, source_target_pairs={{0,16},{2,18},{4,20},{6,22},{8,24},{10,26},{12,28},{14,30},{16,0},... | collective-permute-start | bytes 12296 | tf_op jit(solution)/shard_map/ppermute | solution.py:480
  67.9 1.3 data_part.5.refs_4_
  69.2 6.6 %collective-permute-start.14 = (f32[64,512]{1,0:T(8,128)S(1)}, f32[64,512]{1,0:T(8,128)S(1)}, u32[]{:S(2)}, u32[]{:S(2)}) collective-permute-start(f32[64,512]{1,0:T(8,128)S(1)} %data_part.5.refs_4_), channel_id=1, source_target_pairs={{0,1},{1,0},{2,3},{3,2},{4,5},{5,4},{6,7},{7,6},{8,9},{9,8},{10,11... | collective-permute-start | bytes 393224 | tf_op jit(solution)/shard_map/ppermute | solution.py:492
  75.8 2.9 %collective-permute-done.14.refs_5_ = f32[64,512]{1,0:T(8,128)S(1)} collective-permute-done((f32[64,512]{1,0:T(8,128)S(1)}, f32[64,512]{1,0:T(8,128)S(1)}, u32[]{:S(2)}, u32[]{:S(2)}) %collective-permute-start.14) | collective-permute-done | bytes 131104 | tf_op jit(solution)/shard_map/ppermute | solution.py:492
  78.7 5.3 %model_part.5 = (f32[64,512]{1,0:T(8,128)S(1)}, f32[64,512]{1,0:T(8,128)}, f32[64,512]{1,0:T(8,128)S(1)}, f32[8,128]{1,0:T(8,128)S(1)}) custom-call(f32[1]{0:T(128)} %bitcast.freq, f32[8,128]{1,0:T(8,128)S(1)} %add_add_fusion.2.refs_0_, f32[64,512]{1,0:T(8,128)S(1)} %get-tuple-element.19.refs_1_, f32[64,512]{1,0:T(8,128)S(1)} %get-tuple-element.20.field_ref.refs_2_, ...), custom_call_target="tpu_custom_call" | custom-call | flops 6000000000 | bytes 2000000 | tf_op jit(solution)/shard_map/model_part/pallas_call | solution.py:462
  84.1 1.4 %collective-permute-start.16 = (f32[8,128]{1,0:T(8,128)S(1)}, f32[8,128]{1,0:T(8,128)S(1)}, u32[]{:S(2)}, u32[]{:S(2)}) collective-permute-start(f32[8,128]{1,0:T(8,128)S(1)} %get-tuple-element.23), channel_id=1, source_target_pairs={{0,4},{2,6},{4,0},{6,2},{8,12},{10,14},{12,8},{14,10},{16,20},{18,... | collective-permute-start | bytes 12296 | tf_op jit(solution)/shard_map/ppermute | solution.py:480
  86.0 1.8 %collective-permute-done.16 = f32[8,128]{1,0:T(8,128)S(1)} collective-permute-done((f32[8,128]{1,0:T(8,128)S(1)}, f32[8,128]{1,0:T(8,128)S(1)}, u32[]{:S(2)}, u32[]{:S(2)}) %collective-permute-start.16) | collective-permute-done | bytes 4128 | tf_op jit(solution)/shard_map/ppermute | solution.py:480
  87.8 0.8 collective-permute-done.17
  88.9 3.8 %collective-permute-start.19 = (f32[8,128]{1,0:T(8,128)S(1)}, f32[8,128]{1,0:T(8,128)S(1)}, u32[]{:S(2)}, u32[]{:S(2)}) collective-permute-start(f32[8,128]{1,0:T(8,128)S(1)} %add_add_fusion.1), channel_id=1, source_target_pairs={{0,16},{2,18},{4,20},{6,22},{8,24},{10,26},{12,28},{14,30},{16,0},... | collective-permute-start | bytes 12296 | tf_op jit(solution)/shard_map/ppermute | solution.py:480
  93.6 0.8 collective-permute-done.19
  94.3 3.8 %collective-permute-done.20 = f32[8,128]{1,0:T(8,128)S(1)} collective-permute-done((f32[8,128]{1,0:T(8,128)S(1)}, f32[8,128]{1,0:T(8,128)S(1)}, u32[]{:S(2)}, u32[]{:S(2)}) %collective-permute-start.20) | collective-permute-done | bytes 4128 | tf_op jit(solution)/shard_map/ppermute | solution.py:480
  101.2 2.0 %multiply_bitcast_fusion.2 = (f32[1,64,256]{2,1,0:T(8,128)S(1)}, f32[1,64,256]{2,1,0:T(8,128)S(1)}, f32[1,64,256]{2,1,0:T(8,128)S(1)}) fusion(f32[64,256]{1,0:T(8,128)S(1)} %get-tuple-element.32, f32[]{:T(128)} %bitcast.17, f32[]{:T(128)} %bitcast.21, f32[]{:T(128)} %bitcast.19), kind=kLoop, calls=%fused_computation.23 | loop fusion | flops 49152 | bytes 262156 | tf_op jit(solution)/shard_map/stack | solution.py:555
  103.2 12.6 %all_to_all.10 = f32[16,32,128]{2,1,0:T(8,128)S(1)} all-to-all(f32[16,32,128]{2,1,0:T(8,128)S(1)} %reshape.94), channel_id=1, replica_groups=mesh['band'=1,'chan'=16,'stn'=2] {'chan'}, dimensions={0} | all-to-all | bytes 524288 | tf_op jit(solution)/shard_map/all_to_all | solution.py:557
  115.9 0.7 broadcast_in_dim.27
  116.6 3.5 %all-to-all-start.1 = ((f32[16,32,128]{2,1,0:T(8,128)}), f32[16,32,128]{2,1,0:T(8,128)S(1)}, u32[]{:S(2)}, u32[]{:S(2)}) async-start(f32[16,32,128]{2,1,0:T(8,128)} %broadcast_in_dim.27), calls=%async_computation.1 | async-start | bytes 524288 | tf_op jit(solution)/shard_map/all_to_all | solution.py:559
  120.2 0.7 copy.17
  120.9 9.3 %all-to-all-done.1 = f32[16,32,128]{2,1,0:T(8,128)S(1)} async-done(((f32[16,32,128]{2,1,0:T(8,128)}), f32[16,32,128]{2,1,0:T(8,128)S(1)}, u32[]{:S(2)}, u32[]{:S(2)}) %all-to-all-start.1) | async-done | bytes 262176 | tf_op jit(solution)/shard_map/all_to_all | solution.py:559
  130.2 2.5 %fusion = f32[4,32,128]{2,1,0:T(8,128)S(1)} fusion(f32[16,32,128]{2,1,0:T(8,128)S(1)} %all-to-all-done.1, f32[]{:T(128)} %bitcast.9, f32[]{:T(128)} %bitcast.8, f32[]{:T(128)} %bitcast.7, f32[]{:T(128)} %bitcast.5), kind=kLoop, calls=%fused_computation.3 | loop fusion | flops 114688 | bytes 327696 | tf_op jit(solution)/shard_map/add | solution.py:560
  132.8 0.7 copy.19
  133.5 0.9 copy.18
  (52 shorter events, 5.3 us)
Async XLA Ops:
  16.4 0.7 copy-start
  17.1 0.7 copy-start.2
  18.9 9.6 %collective-permute-start = (f32[64,512]{1,0:T(8,128)S(1)}, f32[64,512]{1,0:T(8,128)S(1)}, u32[]{:S(2)}, u32[]{:S(2)}) collective-permute-start(f32[64,512]{1,0:T(8,128)S(1)} %data_part.3.refs_1_), channel_id=1, source_target_pairs={{0,1},{1,0},{2,3},{3,2},{4,5},{5,4},{6,7},{7,6},{8,9},{9,8},{10,11... | collective-permute-start | bytes 393224 | tf_op jit(solution)/shard_map/ppermute | solution.py:492
  25.5 17.4 %copy-start.1 = (s32[4]{0:T(128)S(1)}, s32[4]{0:T(128)}, u32[]{:S(2)}) copy-start(s32[4]{0:T(128)} %table.5) | copy-start | bytes 52
  25.6 17.4 %copy-start.3 = (s32[4]{0:T(128)S(1)}, s32[4]{0:T(128)}, u32[]{:S(2)}) copy-start(s32[4]{0:T(128)} %flags.5) | copy-start | bytes 52
  33.8 1.9 %collective-permute-start.1 = (f32[8,128]{1,0:T(8,128)S(1)}, f32[8,128]{1,0:T(8,128)S(1)}, u32[]{:S(2)}, u32[]{:S(2)}) collective-permute-start(f32[8,128]{1,0:T(8,128)S(1)} %get-tuple-element.14), channel_id=1, source_target_pairs={{0,2},{2,0},{4,6},{6,4},{8,10},{10,8},{12,14},{14,12},{16,18},{18,... | collective-permute-start | bytes 12296 | tf_op jit(solution)/shard_map/ppermute | solution.py:480
  33.9 3.7 %collective-permute-start.2 = (f32[8,128]{1,0:T(8,128)S(1)}, f32[8,128]{1,0:T(8,128)S(1)}, u32[]{:S(2)}, u32[]{:S(2)}) collective-permute-start(f32[8,128]{1,0:T(8,128)S(1)} %get-tuple-element.14), channel_id=1, source_target_pairs={{0,4},{2,6},{4,0},{6,2},{8,12},{10,14},{12,8},{14,10},{16,20},{18,... | collective-permute-start | bytes 12296 | tf_op jit(solution)/shard_map/ppermute | solution.py:480
  35.5 3.0 %collective-permute-start.3 = (f32[8,128]{1,0:T(8,128)S(1)}, f32[8,128]{1,0:T(8,128)S(1)}, u32[]{:S(2)}, u32[]{:S(2)}) collective-permute-start(f32[8,128]{1,0:T(8,128)S(1)} %get-tuple-element.14), channel_id=1, source_target_pairs={{0,6},{2,4},{4,2},{6,0},{8,14},{10,12},{12,10},{14,8},{16,22},{18,... | collective-permute-start | bytes 12296 | tf_op jit(solution)/shard_map/ppermute | solution.py:480
  38.5 12.3 %collective-permute-start.4 = (f32[8,128]{1,0:T(8,128)S(1)}, f32[8,128]{1,0:T(8,128)S(1)}, u32[]{:S(2)}, u32[]{:S(2)}) collective-permute-start(f32[8,128]{1,0:T(8,128)S(1)} %add_add_fusion.5), channel_id=1, source_target_pairs={{0,8},{2,10},{4,12},{6,14},{8,0},{10,2},{12,4},{14,6},{16,24},{18,... | collective-permute-start | bytes 12296 | tf_op jit(solution)/shard_map/ppermute | solution.py:480
  40.1 10.7 %collective-permute-start.5 = (f32[8,128]{1,0:T(8,128)S(1)}, f32[8,128]{1,0:T(8,128)S(1)}, u32[]{:S(2)}, u32[]{:S(2)}) collective-permute-start(f32[8,128]{1,0:T(8,128)S(1)} %add_add_fusion.5), channel_id=1, source_target_pairs={{0,16},{2,18},{4,20},{6,22},{8,24},{10,26},{12,28},{14,30},{16,0},... | collective-permute-start | bytes 12296 | tf_op jit(solution)/shard_map/ppermute | solution.py:480
  42.7 8.1 %collective-permute-start.6 = (f32[8,128]{1,0:T(8,128)S(1)}, f32[8,128]{1,0:T(8,128)S(1)}, u32[]{:S(2)}, u32[]{:S(2)}) collective-permute-start(f32[8,128]{1,0:T(8,128)S(1)} %add_add_fusion.5), channel_id=1, source_target_pairs={{0,24},{2,26},{4,28},{6,30},{8,16},{10,18},{12,20},{14,22},{16,8},... | collective-permute-start | bytes 12296 | tf_op jit(solution)/shard_map/ppermute | solution.py:480
  44.0 9.8 %collective-permute-start.7 = (f32[64,512]{1,0:T(8,128)S(1)}, f32[64,512]{1,0:T(8,128)S(1)}, u32[]{:S(2)}, u32[]{:S(2)}) collective-permute-start(f32[64,512]{1,0:T(8,128)S(1)} %data_part.4.refs_4_), channel_id=1, source_target_pairs={{0,1},{1,0},{2,3},{3,2},{4,5},{5,4},{6,7},{7,6},{8,9},{9,8},{10,11... | collective-permute-start | bytes 393224 | tf_op jit(solution)/shard_map/ppermute | solution.py:492
  59.2 3.1 %collective-permute-start.10 = (f32[8,128]{1,0:T(8,128)S(1)}, f32[8,128]{1,0:T(8,128)S(1)}, u32[]{:S(2)}, u32[]{:S(2)}) collective-permute-start(f32[8,128]{1,0:T(8,128)S(1)} %get-tuple-element.18), channel_id=1, source_target_pairs={{0,6},{2,4},{4,2},{6,0},{8,14},{10,12},{12,10},{14,8},{16,22},{18,... | collective-permute-start | bytes 12296 | tf_op jit(solution)/shard_map/ppermute | solution.py:480
  59.2 3.0 %collective-permute-start.8 = (f32[8,128]{1,0:T(8,128)S(1)}, f32[8,128]{1,0:T(8,128)S(1)}, u32[]{:S(2)}, u32[]{:S(2)}) collective-permute-start(f32[8,128]{1,0:T(8,128)S(1)} %get-tuple-element.18), channel_id=1, source_target_pairs={{0,2},{2,0},{4,6},{6,4},{8,10},{10,8},{12,14},{14,12},{16,18},{18,... | collective-permute-start | bytes 12296 | tf_op jit(solution)/shard_map/ppermute | solution.py:480
  59.9 3.6 %collective-permute-start.9 = (f32[8,128]{1,0:T(8,128)S(1)}, f32[8,128]{1,0:T(8,128)S(1)}, u32[]{:S(2)}, u32[]{:S(2)}) collective-permute-start(f32[8,128]{1,0:T(8,128)S(1)} %get-tuple-element.18), channel_id=1, source_target_pairs={{0,4},{2,6},{4,0},{6,2},{8,12},{10,14},{12,8},{14,10},{16,20},{18,... | collective-permute-start | bytes 12296 | tf_op jit(solution)/shard_map/ppermute | solution.py:480
  63.5 12.3 %collective-permute-start.11 = (f32[8,128]{1,0:T(8,128)S(1)}, f32[8,128]{1,0:T(8,128)S(1)}, u32[]{:S(2)}, u32[]{:S(2)}) collective-permute-start(f32[8,128]{1,0:T(8,128)S(1)} %add_add_fusion.3), channel_id=1, source_target_pairs={{0,8},{2,10},{4,12},{6,14},{8,0},{10,2},{12,4},{14,6},{16,24},{18,... | collective-permute-start | bytes 12296 | tf_op jit(solution)/shard_map/ppermute | solution.py:480
  64.2 11.6 %collective-permute-start.12 = (f32[8,128]{1,0:T(8,128)S(1)}, f32[8,128]{1,0:T(8,128)S(1)}, u32[]{:S(2)}, u32[]{:S(2)}) collective-permute-start(f32[8,128]{1,0:T(8,128)S(1)} %add_add_fusion.3), channel_id=1, source_target_pairs={{0,16},{2,18},{4,20},{6,22},{8,24},{10,26},{12,28},{14,30},{16,0},... | collective-permute-start | bytes 12296 | tf_op jit(solution)/shard_map/ppermute | solution.py:480
  67.7 8.1 %collective-permute-start.13 = (f32[8,128]{1,0:T(8,128)S(1)}, f32[8,128]{1,0:T(8,128)S(1)}, u32[]{:S(2)}, u32[]{:S(2)}) collective-permute-start(f32[8,128]{1,0:T(8,128)S(1)} %add_add_fusion.3), channel_id=1, source_target_pairs={{0,24},{2,26},{4,28},{6,30},{8,16},{10,18},{12,20},{14,22},{16,8},... | collective-permute-start | bytes 12296 | tf_op jit(solution)/shard_map/ppermute | solution.py:480
  69.2 9.5 %collective-permute-start.14 = (f32[64,512]{1,0:T(8,128)S(1)}, f32[64,512]{1,0:T(8,128)S(1)}, u32[]{:S(2)}, u32[]{:S(2)}) collective-permute-start(f32[64,512]{1,0:T(8,128)S(1)} %data_part.5.refs_4_), channel_id=1, source_target_pairs={{0,1},{1,0},{2,3},{3,2},{4,5},{5,4},{6,7},{7,6},{8,9},{9,8},{10,11... | collective-permute-start | bytes 393224 | tf_op jit(solution)/shard_map/ppermute | solution.py:492
  78.7 21.9 %copy-start.4 = (f32[8,8,1,256]{3,2,1,0:T(1,128)S(1)}, f32[8,8,1,256]{3,2,1,0:T(1,128)}, u32[]{:S(2)}) copy-start(f32[8,8,1,256]{3,2,1,0:T(1,128)} %param.14) | copy-start | bytes 196612
  84.0 1.9 %collective-permute-start.15 = (f32[8,128]{1,0:T(8,128)S(1)}, f32[8,128]{1,0:T(8,128)S(1)}, u32[]{:S(2)}, u32[]{:S(2)}) collective-permute-start(f32[8,128]{1,0:T(8,128)S(1)} %get-tuple-element.23), channel_id=1, source_target_pairs={{0,2},{2,0},{4,6},{6,4},{8,10},{10,8},{12,14},{14,12},{16,18},{18,... | collective-permute-start | bytes 12296 | tf_op jit(solution)/shard_map/ppermute | solution.py:480
  84.1 3.7 %collective-permute-start.16 = (f32[8,128]{1,0:T(8,128)S(1)}, f32[8,128]{1,0:T(8,128)S(1)}, u32[]{:S(2)}, u32[]{:S(2)}) collective-permute-start(f32[8,128]{1,0:T(8,128)S(1)} %get-tuple-element.23), channel_id=1, source_target_pairs={{0,4},{2,6},{4,0},{6,2},{8,12},{10,14},{12,8},{14,10},{16,20},{18,... | collective-permute-start | bytes 12296 | tf_op jit(solution)/shard_map/ppermute | solution.py:480
  85.6 3.0 %collective-permute-start.17 = (f32[8,128]{1,0:T(8,128)S(1)}, f32[8,128]{1,0:T(8,128)S(1)}, u32[]{:S(2)}, u32[]{:S(2)}) collective-permute-start(f32[8,128]{1,0:T(8,128)S(1)} %get-tuple-element.23), channel_id=1, source_target_pairs={{0,6},{2,4},{4,2},{6,0},{8,14},{10,12},{12,10},{14,8},{16,22},{18,... | collective-permute-start | bytes 12296 | tf_op jit(solution)/shard_map/ppermute | solution.py:480
  88.6 5.0 %collective-permute-start.18 = (f32[8,128]{1,0:T(8,128)S(1)}, f32[8,128]{1,0:T(8,128)S(1)}, u32[]{:S(2)}, u32[]{:S(2)}) collective-permute-start(f32[8,128]{1,0:T(8,128)S(1)} %add_add_fusion.1), channel_id=1, source_target_pairs={{0,8},{2,10},{4,12},{6,14},{8,0},{10,2},{12,4},{14,6},{16,24},{18,... | collective-permute-start | bytes 12296 | tf_op jit(solution)/shard_map/ppermute | solution.py:480
  88.9 5.4 %collective-permute-start.19 = (f32[8,128]{1,0:T(8,128)S(1)}, f32[8,128]{1,0:T(8,128)S(1)}, u32[]{:S(2)}, u32[]{:S(2)}) collective-permute-start(f32[8,128]{1,0:T(8,128)S(1)} %add_add_fusion.1), channel_id=1, source_target_pairs={{0,16},{2,18},{4,20},{6,22},{8,24},{10,26},{12,28},{14,30},{16,0},... | collective-permute-start | bytes 12296 | tf_op jit(solution)/shard_map/ppermute | solution.py:480
  92.8 5.4 %collective-permute-start.20 = (f32[8,128]{1,0:T(8,128)S(1)}, f32[8,128]{1,0:T(8,128)S(1)}, u32[]{:S(2)}, u32[]{:S(2)}) collective-permute-start(f32[8,128]{1,0:T(8,128)S(1)} %add_add_fusion.1), channel_id=1, source_target_pairs={{0,24},{2,26},{4,28},{6,30},{8,16},{10,18},{12,20},{14,22},{16,8},... | collective-permute-start | bytes 12296 | tf_op jit(solution)/shard_map/ppermute | solution.py:480
  116.6 13.5 %all-to-all-start.1 = ((f32[16,32,128]{2,1,0:T(8,128)}), f32[16,32,128]{2,1,0:T(8,128)S(1)}, u32[]{:S(2)}, u32[]{:S(2)}) async-start(f32[16,32,128]{2,1,0:T(8,128)} %broadcast_in_dim.27), calls=%async_computation.1 | async-start | bytes 524288 | tf_op jit(solution)/shard_map/all_to_all | solution.py:559
where the time goes:
time: 133 us; the launch traced here: 134 us
  starting transfers between devices  42.8 us (32%)
  waiting for transfers between devices  30.3 us (23%)
  Pallas kernels  19.5 us (15%)
  blocking collectives  18.8 us (14%)
  other arithmetic  10.5 us (8%)
  local copies, waits for them, and re-layouts  9.74 us (7%)
  between operations  2.79 us (2%)
    ppermute x3, starting transfers between devices, other_stations(): return lax.ppermute(value, 'stn', [(0, 1), (1, 0)])  20 us
    ppermute x18, starting transfers between devices, chan_sum(): lax.ppermute(value, 'chan', [(i, i ^ o) for i in range(count)])  19.2 us
    pallas_call x3, Pallas kernels, model_part(): pl.pallas_call(functools.partial(model_kernel, block, pairs, dumps, penal...  16 us
    all_to_all x1, blocking collectives, shards(): parts = jnp.sum(lax.all_to_all(parts, 'chan', 0, 0, tiled=True), axis=0)  12.6 us
    ppermute x18, waiting for transfers between devices, chan_sum(): lax.ppermute(value, 'chan', [(i, i ^ o) for i in range(count)])  12.1 us
    all_to_all x1, waiting for transfers between devices, shards(): lax.all_to_all(parts, 'chan', 0, 0, tiled=True)  9.31 us
    ppermute x3, waiting for transfers between devices, other_stations(): return lax.ppermute(value, 'stn', [(0, 1), (1, 0)])  8.9 us
    all_gather x1, blocking collectives, shards(): rows = lax.all_gather(rows, 'stn', axis=1, tiled=True)  6.2 us
  transfers between devices with their start and end apart: 22, of which 12 were waited for; matrix products, arithmetic and copies ran while one was open for 1% of the time, Pallas kernels for 2%

commit v1 on v0

--- a/solution.py
+++ b/solution.py
@@ -153,27 +153,50 @@
     return jnp.concatenate(g_re + g_im, axis=0)
 
 
-def data_kernel(
-    block,
-    pairs,
-    dumps,
-    slots,
-    penalty,
-    with_target,
-    table,
-    flags,
-    own,
-    freq,
-    field_ref,
-    delay_ref,
-    coh_ref,
-    *refs,
-):
-    if with_target:
-        target_ref, refs = refs[0], refs[1:]
-    observed, out_ref, held, sems, xp, yp, hl, ha = refs
+def coherency_tile(brightness, freq):
+    spectral = jnp.exp(-SPECTRAL_INDEX * jnp.log(jnp.full((8, 128), freq, F32)))
+    tiles = []
+    for e in range(8):
+        column = jnp.transpose(jnp.broadcast_to(brightness[e : e + 1, :], (8, 8)))[:, :1]
+        tiles.append(column * spectral)
+    return jnp.concatenate(tiles, axis=0)
+
+
+def position_of(chan_count):
+    return lax.axis_index("chan").astype(F32) * (1.0 / chan_count)
+
+
+def frequency_of(chan_count):
+    return 1.0 + position_of(chan_count)
+
+
+def basis_of(chan_count):
+    x = position_of(chan_count) + 0.5 / chan_count
+    y = 1.0 - x
+    return [y * y * y, 3.0 * x * y * y, 3.0 * x * x * y, x * x * x]
+
+
+def solve_of(chan_count):
+    basis = bernstein_np(chan_count)
+    inverse = np.linalg.inv(basis.T @ basis)
+    row = basis_of(chan_count)
+    return [sum(row[m] * float(inverse[m, k]) for m in range(4)) for k in range(4)]
+
+
+def data_kernel(block, pairs, dumps, slots, penalty, chan_count, first_call, joined, *refs):
+    if first_call:
+        if joined:
+            table, flags, gains_all, delays_all, *refs = refs
+        else:
+            table, flags, gains_mine, gains_other, delays_mine, delays_other, *refs = refs
+        duals, prior, brightness, observed, field_ref, delay_ref, coh_ref, out_ref, *refs = refs
+    else:
+        table, flags, field_ref, delay_ref, coh_ref, observed, out_ref, *refs = refs
+    held, sems, xp, yp, hl, ha = refs
     stations = field_ref.shape[1]
     pair_count = len(pairs)
+    own = lax.axis_index("stn")
+    at_own = pl.ds(pl.multiple_of(own * block, CHUNK), block)
 
     def copy_of(slot, t):
         return pltpu.make_async_copy(observed.at[slot, t], held.at[slot, t], sems.at[slot, t])
@@ -185,7 +208,18 @@
             for t in range(dumps):
                 copy_of(slot, t).start()
 
-    freq_value = freq[0]
+    freq_value = frequency_of(chan_count)
+    if first_call:
+        if joined:
+            field_ref[...] = gains_all[:, 0, :]
+            delay_ref[...] = delays_all[...]
+        else:
+            at_other = pl.ds(pl.multiple_of((1 - own) * block, CHUNK), block)
+            field_ref[:, at_own] = gains_mine[:, 0, :]
+            field_ref[:, at_other] = gains_other[:, 0, :]
+            delay_ref[:, at_own] = delays_mine[...]
+            delay_ref[:, at_other] = delays_other[...]
+        coh_ref[...] = coherency_tile(brightness[...], freq_value)
     bright = coherency_rows(coh_ref[...], stations)
     for t in range(dumps):
         cosine, sine = trig(delay_ref[8 * t : 8 * t + 8, :], freq_value)
@@ -246,30 +280,42 @@
             [hl[t, i] for i in range(2)], [ha[t, rj] for rj in range(4)], bright, cosine, sine
         )
         total = piece if total is None else total + piece
-    out_ref[...] = -total
-    at_own = pl.ds(pl.multiple_of(own[0] * block, CHUNK), block)
-    prior = field_ref[:, at_own]
-    if with_target:
-        prior = prior - target_ref[...]
-    out_ref[:, at_own] += penalty * prior
-
-
-def data_part(geometry, table, flags, own, freq, field, delays, coh, target, observed):
-    block, pairs, penalty = geometry
+    out_ref[:64, :] = -total
+    out_ref[:64, at_own] += penalty * field_ref[:, at_own]
+    if first_call:
+        target = -duals[:, 0, :]
+        basis = basis_of(chan_count)
+        for k in range(4):
+            target = target + basis[k] * prior[:, k, :]
+        out_ref[:64, at_own] += -penalty * target
+        lane = lax.broadcasted_iota(jnp.int32, (8, stations), 1)
+        counts = jnp.zeros((8, stations), F32)
+        for slot in range(slots):
+            held_here = (lane == table[slot]) & (lane < pair_count)
+            counts = counts + jnp.where(held_here, flags[slot].astype(F32), 0.0)
+        out_ref[64:, :] = counts
+
+
+def data_part(geometry, table, flags, fields, observed):
+    block, pairs, penalty, chan_count, stations = geometry
     slots, dumps = observed.shape[:2]
-    stations = field.shape[1]
     smem = pl.BlockSpec(memory_space=pltpu.SMEM)
     vmem = pl.BlockSpec(memory_space=pltpu.VMEM)
     hbm = pl.BlockSpec(memory_space=pl.ANY)
-    with_target = target is not None
-    body = functools.partial(data_kernel, block, pairs, dumps, slots, penalty, with_target)
-    extra = (target,) if with_target else ()
+    first_call = len(fields) > 3
+    joined = len(fields) == 5
+    body = functools.partial(
+        data_kernel, block, pairs, dumps, slots, penalty, chan_count, first_call, joined
+    )
+    shapes = [(64, stations), (8 * dumps, stations), (64, 128), (72, stations)]
+    if not first_call:
+        shapes = [(64, stations)]
     return pl.pallas_call(
         body,
         name="data_part",
-        out_shape=jax.ShapeDtypeStruct(field.shape, F32),
-        in_specs=[smem] * 4 + [vmem] * (3 + len(extra)) + [hbm],
-        out_specs=vmem,
+        out_shape=tuple(jax.ShapeDtypeStruct(s, F32) for s in shapes),
+        in_specs=[smem] * 2 + [vmem] * len(fields) + [hbm],
+        out_specs=(vmem,) * len(shapes),
         scratch_shapes=[
             pltpu.VMEM(observed.shape, BF16),
             pltpu.SemaphoreType.DMA((slots, dumps)),
@@ -282,7 +328,7 @@
         cost_estimate=pl.CostEstimate(
             flops=6000000000, bytes_accessed=8000000, transcendentals=0
         ),
-    )(table, flags, own, freq, field, delays, coh, *extra, observed)
+    )(table, flags, *fields, observed)
 
 
 def fold_gram(high_low, other, rows):
@@ -301,38 +347,40 @@
     return jnp.concatenate([part[:, start : start + size] for part in parts], axis=1)
 
 
-def model_kernel(block, pairs, dumps, penalty, update, freq, *refs):
+def model_kernel(block, pairs, dumps, penalty, chan_count, update, *refs):
     if update:
-        scal_ref, current_ref, previous_ref, linear_ref, mine_ref, theirs_ref, *refs = refs
+        scal_ref, current_ref, previous_ref, linear_ref, counts_ref, mine_ref, theirs_ref, *refs = refs
+        delay_ref, coh_ref, current_out, *refs = refs
     else:
-        current_ref, mine_ref, theirs_ref, *refs = refs
-    delay_ref, coh_ref, table_ref, current_out, linear_out, direction_out, sums_out, hl, ha = refs
+        current_ref, mine_ref, theirs_ref, delay_ref, coh_ref, counts_out, *refs = refs
+    linear_out, direction_out, sums_out, hl, ha = refs
     stations = current_ref.shape[1]
     chunk = min(CHUNK, block)
     per_block = block // chunk
     chunks = stations // chunk
     blocks = stations // block
 
-    step_linear = mine_ref[...] + theirs_ref[...]
+    step_linear = mine_ref[:64, :] + theirs_ref[:64, :]
     if update:
+        counts = counts_ref[0:1, :]
         grad_sq = scal_ref[0:1, :]
         curvature = scal_ref[1:2, :]
         alpha = grad_sq / (curvature + penalty * grad_sq + EPSILON)
         alpha = jnp.concatenate([alpha] * (stations // 128), axis=1)
         current = current_ref[...] - alpha * previous_ref[...]
         linear = linear_ref[...] - alpha * step_linear
+        current_out[...] = current
     else:
+        counts_out[...] = mine_ref[64:, :128] + theirs_ref[64:, :128]
+        counts = mine_ref[64:65, :128] + theirs_ref[64:65, :128]
         current = current_ref[...]
         linear = step_linear
-    current_out[...] = current
     linear_out[...] = linear
 
-    ids, counts = table_ref[0:1, :], table_ref[1:2, :]
     lane = lax.broadcasted_iota(jnp.int32, (1, block), 1).astype(F32)
     masks = {}
     for k, pair in enumerate(pairs):
-        flagged = jnp.sum(jnp.where(ids == float(k), counts, 0.0), axis=1, keepdims=True)
-        masks[pair] = (lane >= flagged).astype(F32)
+        masks[pair] = (lane >= counts[:, k : k + 1]).astype(F32)
 
     def mask_of(pair, chunk_id):
         start = (chunk_id % per_block) * chunk
@@ -345,7 +393,7 @@
     col = lax.broadcasted_iota(jnp.int32, (2 * chunk, 4 * chunk), 1) % chunk
     upper = row < col
 
-    freq_value = freq[0]
+    freq_value = frequency_of(chan_count)
     bright = coherency_rows(coh_ref[...], stations)
 
     def rect_terms(chunk_id):
@@ -451,118 +499,162 @@
     sums_out[...] = jnp.where(row8 == 0, grad_sq, jnp.where(row8 == 1, curvature, 0.0))
 
 
-def model_part(geometry, dumps, freq, state, delays, coh, table):
-    block, pairs, penalty = geometry
-    smem = pl.BlockSpec(memory_space=pltpu.SMEM)
+def model_part(geometry, dumps, state, delays, coh):
+    block, pairs, penalty, chan_count, stations = geometry
     vmem = pl.BlockSpec(memory_space=pltpu.VMEM)
-    update = len(state) == 6
-    field = state[1] if update else state[0]
-    stations = field.shape[1]
-    like = jax.ShapeDtypeStruct(field.shape, F32)
+    update = len(state) > 3
+    like = jax.ShapeDtypeStruct((64, stations), F32)
+    tile = jax.ShapeDtypeStruct((8, 128), F32)
     return pl.pallas_call(
-        functools.partial(model_kernel, block, pairs, dumps, penalty, update),
+        functools.partial(model_kernel, block, pairs, dumps, penalty, chan_count, update),
         name="model_part",
-        out_shape=(like, like, like, jax.ShapeDtypeStruct((8, 128), F32)),
-        in_specs=[smem] + [vmem] * (len(state) + 3),
+        out_shape=(like if update else tile, like, like, tile),
+        in_specs=[vmem] * (len(state) + 2),
         out_specs=(vmem,) * 4,
         scratch_shapes=[pltpu.VMEM((2, 32, stations), F32), pltpu.VMEM((4, 32, stations), F32)],
         compiler_params=pltpu.CompilerParams(vmem_limit_bytes=VMEM_BYTES),
         cost_estimate=pl.CostEstimate(
             flops=6000000000, bytes_accessed=2000000, transcendentals=0
         ),
-    )(freq, *state, delays, coh, table)
-
-
-def chan_sum(value, count):
-    bit = 1
-    while bit < count:
-        offsets = [bit, 2 * bit, 3 * bit] if 4 * bit <= count else [bit]
-        got = [lax.ppermute(value, "chan", [(i, i ^ o) for i in range(count)]) for o in offsets]
-        if len(got) == 3:
-            value = (value + got[0]) + (got[1] + got[2])
-            bit *= 4
-        else:
-            value = value + got[0]
-            bit *= 2
-    return value
-
-
-def other_stations(value, count):
+    )(*state, delays, coh)
+
+
+def last_step_kernel(
+    block, penalty, chan_count, sums, current, direction, duals, gains_out, shifted_out, keep_out, send_out
+):
+    at_own = pl.ds(pl.multiple_of(lax.axis_index("stn") * block, CHUNK), block)
+    grad_sq = sums[0:1, :]
+    alpha = grad_sq / (sums[1:2, :] + penalty * grad_sq + EPSILON)
+    alpha = jnp.concatenate([alpha] * (block // 128), axis=1)
+    gains_new = current[:, at_own] - alpha * direction[:, at_own]
+    gains_out[:, 0, :] = gains_new
+    shifted = gains_new + duals[:, 0, :]
+    shifted_out[...] = shifted
+    half = block // 2
+    odd = lax.axis_index("chan") % 2 == 1
+    low, high = shifted[:, :half], shifted[:, half:]
+    keep, send = jnp.where(odd, high, low), jnp.where(odd, low, high)
+    for k, scale in enumerate(solve_of(chan_count)):
+        keep_out[64 * k : 64 * k + 64, :] = scale * keep
+        send_out[64 * k : 64 * k + 64, :] = scale * send
+
+
+def last_step(geometry, sums, current, direction, duals):
+    block, pairs, penalty, chan_count, stations = geometry
+    vmem = pl.BlockSpec(memory_space=pltpu.VMEM)
+    shapes = [(64, 1, block), (64, block), (256, block // 2), (256, block // 2)]
+    return pl.pallas_call(
+        functools.partial(last_step_kernel, block, penalty, chan_count),
+        name="last_step",
+        out_shape=tuple(jax.ShapeDtypeStruct(s, F32) for s in shapes),
+        in_specs=[vmem] * 4,
+        out_specs=(vmem,) * 4,
+    )(sums, current, direction, duals)
+
+
+def consensus_kernel(block, chan_count, mine, theirs, shifted, coeffs_out, duals_out):
+    odd = lax.axis_index("chan") % 2 == 1
+    fitted = None
+    for k, scale in enumerate(basis_of(chan_count)):
+        one, two = mine[64 * k : 64 * k + 64, :], theirs[64 * k : 64 * k + 64, :]
+        coeffs = jnp.concatenate([jnp.where(odd, two, one), jnp.where(odd, one, two)], axis=1)
+        coeffs_out[:, k, :] = coeffs
+        fitted = scale * coeffs if fitted is None else fitted + scale * coeffs
+    duals_out[:, 0, :] = shifted[...] - fitted
+
+
+def consensus(geometry, mine, theirs, shifted):
+    block, pairs, penalty, chan_count, stations = geometry
+    vmem = pl.BlockSpec(memory_space=pltpu.VMEM)
+    shapes = [(64, 4, block), (64, 1, block)]
+    return pl.pallas_call(
+        functools.partial(consensus_kernel, block, chan_count),
+        name="consensus",
+        out_shape=tuple(jax.ShapeDtypeStruct(s, F32) for s in shapes),
+        in_specs=[vmem] * 3,
+        out_specs=(vmem,) * 2,
+    )(mine, theirs, shifted)
+
+
+def swap(value, count, offset):
+    return lax.ppermute(value, "chan", [(i, i ^ offset) for i in range(count)])
+
+
+def sum_stage(value, count, bit):
+    if 4 * bit <= count:
+        got = [swap(value, count, o * bit) for o in (1, 2, 3)]
+        return 4 * bit, (value + got[0]) + (got[1] + got[2])
+    return 2 * bit, value + swap(value, count, bit)
+
+
+def other_stations(value):
+    return lax.ppermute(value, "stn", [(0, 1), (1, 0)])
+
+
+def both_stations(value, count):
     if count == 2:
-        return lax.ppermute(value, "stn", [(0, 1), (1, 0)])
-    return lax.psum(value, "stn") - value
+        return value, other_stations(value)
+    return jnp.zeros_like(value), lax.psum(value, "stn")
 
 
 def shards(observed, pair_table, flag_rows, gains, duals, prior_coeffs, delays, brightness):
     stn_count = lax.axis_size("stn")
     chan_count = lax.axis_size("chan")
-    stn_index = lax.axis_index("stn")
-    chan_index = lax.axis_index("chan")
     entries, dirs, chan_local, block = gains.shape
     slots, dumps = observed.shape[0], observed.shape[2]
     stations = block * stn_count
     pairs = pair_lists(stn_count)
     penalty = stations * dumps / 16.0
-    geometry = (block, pairs, penalty)
-    basis = bernstein_np(chan_count)
-    solve = basis @ np.linalg.inv(basis.T @ basis)
-    basis_row = lax.dynamic_slice_in_dim(jnp.asarray(basis, F32), chan_index, 1, 0)[0]
-    solve_row = lax.dynamic_slice_in_dim(jnp.asarray(solve, F32), chan_index, 1, 0)[0]
-
-    frequency = 1.0 + chan_index.astype(F32) / chan_count
-    coh = brightness * frequency ** (-SPECTRAL_INDEX)
-    coh = jnp.broadcast_to(coh.reshape(entries * dirs, 1), (entries * dirs, 128))
-    freq = frequency.reshape(1)
-    own = stn_index.reshape(1).astype(jnp.int32)
-
-    gains_own = gains.reshape(entries * dirs, block)
-    duals_own = duals.reshape(entries * dirs, block)
-    ids = jnp.pad(pair_table.astype(F32), (0, block - slots), constant_values=-1.0)
-    counts = jnp.pad(flag_rows.astype(F32), (0, block - slots))
-    rows = jnp.concatenate(
-        [gains_own, delays.reshape(dumps * dirs, block), ids[None], counts[None], jnp.zeros((6, block), F32)]
-    )
-    rows = lax.all_gather(rows, "stn", axis=1, tiled=True)
-    field = rows[: entries * dirs]
-    delay_all = rows[entries * dirs : entries * dirs + dumps * dirs]
-    table = rows[entries * dirs + dumps * dirs :]
-
+    geometry = (block, pairs, penalty, chan_count, stations)
+
+    observed = observed.reshape((slots,) + observed.shape[2:])
+    gains_own = gains.reshape(entries * dirs, 1, block)
+    duals_own = duals.reshape(entries * dirs, 1, block)
     prior = prior_coeffs.reshape(entries * dirs, 4, block)
-    prior_fit = sum(basis_row[k] * prior[:, k] for k in range(4))
-    target = prior_fit - duals_own
-
-    observed = observed.reshape((slots,) + observed.shape[2:])
-    data = functools.partial(data_part, geometry, pair_table, flag_rows, own, freq)
-    mine = data(field, delay_all, coh, target, observed)
-    theirs = other_stations(mine, stn_count)
-    state = (field, mine, theirs)
+    delays = delays.reshape(dumps * dirs, block)
+    if stn_count == 2:
+        parts = (gains_own, other_stations(gains_own), delays, other_stations(delays))
+    else:
+        parts = (
+            lax.all_gather(gains_own, "stn", axis=2, tiled=True),
+            lax.all_gather(delays, "stn", axis=1, tiled=True),
+        )
+
+    data = functools.partial(data_part, geometry, pair_table, flag_rows)
+    current, delay_all, coh, mine = data(parts + (duals_own, prior, brightness), observed)
+    mine, theirs = both_stations(mine, stn_count)
+    counts, linear, direction, sums = model_part(
+        geometry, dumps, (current, mine, theirs), delay_all, coh
+    )
     for iteration in range(ITERS):
-        current, linear, direction, sums = model_part(
-            geometry, dumps, freq, state, delay_all, coh, table
-        )
-        if iteration + 1 < ITERS:
-            mine = data(direction, delay_all, coh, None, observed)
-            theirs = other_stations(mine, stn_count)
-        sums = chan_sum(sums, chan_count)
-        state = (sums, current, direction, linear, mine, theirs)
-
-    alpha = sums[0, 0] / (sums[1, 0] + penalty * sums[0, 0] + EPSILON)
-    at_own = stn_index * block
-    gains_new = lax.dynamic_slice_in_dim(
-        current, at_own, block, 1
-    ) - alpha * lax.dynamic_slice_in_dim(direction, at_own, block, 1)
-    shifted = gains_new + duals_own
-    parts = jnp.stack([solve_row[k] * shifted for k in range(4)])
-    parts = parts.reshape(chan_count, -1, 128)
-    parts = jnp.sum(lax.all_to_all(parts, "chan", 0, 0, tiled=True), axis=0)
-    parts = jnp.broadcast_to(parts[None], (chan_count,) + parts.shape)
-    coeffs = lax.all_to_all(parts, "chan", 0, 0, tiled=True).reshape(4, entries * dirs, block)
-    fitted = sum(basis_row[k] * coeffs[k] for k in range(4))
-    coeffs_out = jnp.transpose(coeffs.reshape(4, entries, dirs, block), (1, 2, 0, 3))
+        last = iteration + 1 == ITERS
+        bit, sums = sum_stage(sums, chan_count, 1)
+        if not last:
+            (mine,) = data((direction, delay_all, coh), observed)
+            sums, mine = lax.optimization_barrier((sums, mine))
+            mine, theirs = both_stations(mine, stn_count)
+        while bit < chan_count:
+            bit, sums = sum_stage(sums, chan_count, bit)
+        if not last:
+            current, linear, direction, sums = model_part(
+                geometry,
+                dumps,
+                (sums, current, direction, linear, counts, mine, theirs),
+                delay_all,
+                coh,
+            )
+
+    gains_new, shifted, keep, send = last_step(geometry, sums, current, direction, duals_own)
+    total = keep + swap(send, chan_count, 1)
+    bit = 2
+    while bit < chan_count:
+        total = total + swap(total, chan_count, bit)
+        bit *= 2
+    coeffs, duals_new = consensus(geometry, total, swap(total, chan_count, 1), shifted)
     return (
         gains_new.reshape(gains.shape),
-        coeffs_out,
-        (shifted - fitted).reshape(gains.shape),
+        coeffs.reshape(entries, dirs, 4, block),
+        duals_new.reshape(gains.shape),
     )
 
 

time: 133 us -> 110 us (0.83); the launches traced: 134 us -> 109 us
  blocking collectives: 18.8 us -> 0 us
  Pallas kernels: 19.5 us -> 29.5 us
  other arithmetic: 10.5 us -> 1.6 us
  starting transfers between devices: 42.8 us -> 34 us
  waiting for transfers between devices: 30.3 us -> 35.8 us
  local copies, waits for them, and re-layouts: 9.74 us -> 7.3 us
  between operations: 2.79 us -> 0.83 us
    all_to_all x1 -> x0, blocking collectives: 12.6 us -> none  [shards(): parts = jnp.sum(lax.all_to_all(parts, 'chan', 0, 0, tiled=True), axis=0)]
    ppermute x18 -> x23, waiting for transfers between devices: 12.1 us -> 23.4 us  [swap(): return lax.ppermute(value, 'chan', [(i, i ^ offset) for i in range(count)])]
    pallas_call x3 -> x5, Pallas kernels: 3.5 us -> 13.6 us  [the longest x3 10.1 us: data_part(): pl.pallas_call(body, name='data_part', out_shape=tuple((jax.ShapeDtypeStr...]
    all_to_all x1 -> x0, waiting for transfers between devices: 9.31 us -> none  [shards(): lax.all_to_all(parts, 'chan', 0, 0, tiled=True)]
    ppermute x3 -> x5, starting transfers between devices: 20 us -> 11.3 us  [other_stations(): return lax.ppermute(value, 'stn', [(0, 1), (1, 0)])]
    all_gather x1 -> x0, blocking collectives: 6.2 us -> none  [shards(): rows = lax.all_gather(rows, 'stn', axis=1, tiled=True)]
    ppermute x18 -> x23, starting transfers between devices: 19.2 us -> 22.8 us  [swap(): return lax.ppermute(value, 'chan', [(i, i ^ offset) for i in range(count)])]
    all_to_all x1 -> x0, starting transfers between devices: 3.53 us -> none  [shards(): lax.all_to_all(parts, 'chan', 0, 0, tiled=True)]
  transfers between devices with their start and end apart: 22 -> 28, of which waited for: 12 -> 15; matrix products, arithmetic and copies ran while one was open for 1% -> 0% of each run, Pallas kernels for 2% -> 6%
where the time goes in v1:
time: 110 us; the launch traced here: 109 us
  waiting for transfers between devices  35.8 us (33%)
  starting transfers between devices  34 us (31%)
  Pallas kernels  29.5 us (27%)
  local copies, waits for them, and re-layouts  7.3 us (7%)
  other arithmetic  1.6 us (1%)
    ppermute x23, waiting for transfers between devices, swap(): return lax.ppermute(value, 'chan', [(i, i ^ offset) for i in range(count)])  23.4 us
    ppermute x23, starting transfers between devices, swap(): return lax.ppermute(value, 'chan', [(i, i ^ offset) for i in range(count)])  22.8 us
    pallas_call x3, Pallas kernels, model_part(): pl.pallas_call(functools.partial(model_kernel, block, pairs, dumps, penal...  15.8 us
    ppermute x5, waiting for transfers between devices, other_stations(): return lax.ppermute(value, 'stn', [(0, 1), (1, 0)])  12.4 us
    ppermute x5, starting transfers between devices, other_stations(): return lax.ppermute(value, 'stn', [(0, 1), (1, 0)])  11.3 us
    pallas_call x3, Pallas kernels, data_part(): pl.pallas_call(body, name='data_part', out_shape=tuple((jax.ShapeDtypeStr...  10.1 us
    unnamed x26, local copies, waits for them, and re-layouts  7.3 us
  transfers between devices with their start and end apart: 28, of which 15 were waited for; matrix products, arithmetic and copies ran while one was open for 0% of the time, Pallas kernels for 6%

profile of v1, /device:TPU:0, one launch (start us, length us, event | category | flops | bytes accessed | tf_op | source)
XLA Modules:
  0.0 109.1 jit_solution(1993259920992727539)
XLA Ops:
  0.6 3.0 %collective-permute-start = (f32[64,1,256]{2,1,0:T(1,128)}, f32[64,1,256]{2,1,0:T(1,128)S(1)}, u32[]{:S(2)}, u32[]{:S(2)}) collective-permute-start(f32[64,1,256]{2,1,0:T(1,128)} %bitcast.11), channel_id=1, source_target_pairs={{0,1},{1,0},{2,3},{3,2},{4,5},{5,4},{6,7},{7,6},{8,9},{9,8},{10,11... | collective-permute-start | bytes 196616 | tf_op jit(solution)/shard_map/ppermute | solution.py:591
  3.7 3.9 %collective-permute-done.1.refs_5_ = f32[16,256]{1,0:T(8,128)S(1)} collective-permute-done((f32[16,256]{1,0:T(8,128)}, f32[16,256]{1,0:T(8,128)S(1)}, u32[]{:S(2)}, u32[]{:S(2)}) %collective-permute-start.1) | collective-permute-done | bytes 16416 | tf_op jit(solution)/shard_map/ppermute | solution.py:591
  7.6 0.8 copy-done.2
  8.4 0.9 copy-done.3
  9.4 0.8 copy-done.4
  10.2 0.7 copy-done.5
  10.9 0.7 copy-done.6
  11.6 0.7 copy-done.7
  12.3 0.7 copy-done.9
  12.9 3.6 %data_part.3 = (f32[64,512]{1,0:T(8,128)S(1)}, f32[16,512]{1,0:T(8,128)S(1)}, f32[64,128]{1,0:T(8,128)S(1)}, f32[72,512]{1,0:T(8,128)S(1)}) custom-call(s32[4]{0:T(128)S(1)} %copy-done.7, s32[4]{0:T(128)S(1)} %copy-done.9, f32[64,1,256]{2,1,0:T(1,128)S(1)} %bitcast.12, f32[64,1,256]{2,1,0:T(1,128)S(1)} %collective-permute-done.refs_3_, ...), custom_call_target="tpu_custom_call" | custom-call | flops 6000000000 | bytes 8000000 | tf_op jit(solution)/shard_map/data_part/pallas_call | solution.py:313
  16.5 2.0 %collective-permute-start.2 = (f32[72,512]{1,0:T(8,128)S(1)}, f32[72,512]{1,0:T(8,128)S(1)}, u32[]{:S(2)}, u32[]{:S(2)}) collective-permute-start(f32[72,512]{1,0:T(8,128)S(1)} %get-tuple-element.29.refs_1_), channel_id=1, source_target_pairs={{0,1},{1,0},{2,3},{3,2},{4,5},{5,4},{6,7},{7,6},{8,9},{9,8},{10,11... | collective-permute-start | bytes 442376 | tf_op jit(solution)/shard_map/ppermute | solution.py:591
  18.5 3.2 %collective-permute-done.2.refs_2_ = f32[72,512]{1,0:T(8,128)S(1)} collective-permute-done((f32[72,512]{1,0:T(8,128)S(1)}, f32[72,512]{1,0:T(8,128)S(1)}, u32[]{:S(2)}, u32[]{:S(2)}) %collective-permute-start.2) | collective-permute-done | bytes 147488 | tf_op jit(solution)/shard_map/ppermute | solution.py:591
  21.7 5.3 %model_part.3 = (f32[8,128]{1,0:T(8,128)S(1)}, f32[64,512]{1,0:T(8,128)S(1)}, f32[64,512]{1,0:T(8,128)S(1)}, f32[8,128]{1,0:T(8,128)S(1)}) custom-call(f32[64,512]{1,0:T(8,128)S(1)} %get-tuple-element.28.refs_0_.refs_1_, f32[72,512]{1,0:T(8,128)S(1)} %get-tuple-element.29.refs_1_, f32[72,512]{1,0:T(8,128)S(1)} %collective-permute-done.2.refs_2_, ...), custom_call_target="tpu_custom_call" | custom-call | flops 6000000000 | bytes 2000000 | tf_op jit(solution)/shard_map/model_part/pallas_call | solution.py:508
  27.1 1.6 %collective-permute-start.4 = (f32[8,128]{1,0:T(8,128)S(1)}, f32[8,128]{1,0:T(8,128)S(1)}, u32[]{:S(2)}, u32[]{:S(2)}) collective-permute-start(f32[8,128]{1,0:T(8,128)S(1)} %get-tuple-element.32), channel_id=1, source_target_pairs={{0,4},{2,6},{4,0},{6,2},{8,12},{10,14},{12,8},{14,10},{16,20},{18,... | collective-permute-start | bytes 12296 | tf_op jit(solution)/shard_map/ppermute | solution.py:580
  28.9 3.3 %data_part.4.refs_5_ = f32[64,512]{1,0:T(8,128)S(1)} custom-call(s32[4]{0:T(128)S(1)} %copy-done.8, s32[4]{0:T(128)S(1)} %copy-done.10, f32[64,512]{1,0:T(8,128)S(1)} %get-tuple-element.33.refs_2_, f32[16,512]{1,0:T(8,128)S(1)} %get-tuple-element.30.refs_3_.refs_7_, f32[64,128]{1,0:T(8,128)S(1)} %get-tuple-element.31.refs_4_.refs_8_, ...), custom_call_target="tpu_custom_call" | custom-call | flops 6000000000 | bytes 8000000 | tf_op jit(solution)/shard_map/data_part/pallas_call | solution.py:313
  32.3 3.7 %collective-permute-start.8 = (f32[8,128]{1,0:T(8,128)S(1)}, f32[8,128]{1,0:T(8,128)S(1)}, u32[]{:S(2)}, u32[]{:S(2)}) collective-permute-start(f32[8,128]{1,0:T(8,128)S(1)} %add_add_fusion.5), channel_id=1, source_target_pairs={{0,24},{2,26},{4,28},{6,30},{8,16},{10,18},{12,20},{14,22},{16,8},... | collective-permute-start | bytes 12296 | tf_op jit(solution)/shard_map/ppermute | solution.py:580
  35.9 0.8 collective-permute-start.6
  36.7 3.2 %collective-permute-start.9 = (f32[64,512]{1,0:T(8,128)S(1)}, f32[64,512]{1,0:T(8,128)S(1)}, u32[]{:S(2)}, u32[]{:S(2)}) collective-permute-start(f32[64,512]{1,0:T(8,128)S(1)} %data_part.4.refs_5_), channel_id=1, source_target_pairs={{0,1},{1,0},{2,3},{3,2},{4,5},{5,4},{6,7},{7,6},{8,9},{9,8},{10,11... | collective-permute-start | bytes 393224 | tf_op jit(solution)/shard_map/ppermute | solution.py:591
  40.4 2.7 %collective-permute-done.9.refs_6_ = f32[64,512]{1,0:T(8,128)S(1)} collective-permute-done((f32[64,512]{1,0:T(8,128)S(1)}, f32[64,512]{1,0:T(8,128)S(1)}, u32[]{:S(2)}, u32[]{:S(2)}) %collective-permute-start.9) | collective-permute-done | bytes 131104 | tf_op jit(solution)/shard_map/ppermute | solution.py:591
  43.1 5.3 %model_part.4 = (f32[64,512]{1,0:T(8,128)S(1)}, f32[64,512]{1,0:T(8,128)S(1)}, f32[64,512]{1,0:T(8,128)S(1)}, f32[8,128]{1,0:T(8,128)S(1)}) custom-call(f32[8,128]{1,0:T(8,128)S(1)} %add_add_fusion.4.refs_0_, f32[64,512]{1,0:T(8,128)S(1)} %get-tuple-element.28.refs_0_.refs_1_, f32[64,512]{1,0:T(8,128)S(1)} %get-tuple-element.33.refs_2_, ...), custom_call_target="tpu_custom_call" | custom-call | flops 6000000000 | bytes 2000000 | tf_op jit(solution)/shard_map/model_part/pallas_call | solution.py:508
  48.5 1.3 %collective-permute-start.11 = (f32[8,128]{1,0:T(8,128)S(1)}, f32[8,128]{1,0:T(8,128)S(1)}, u32[]{:S(2)}, u32[]{:S(2)}) collective-permute-start(f32[8,128]{1,0:T(8,128)S(1)} %get-tuple-element.38), channel_id=1, source_target_pairs={{0,4},{2,6},{4,0},{6,2},{8,12},{10,14},{12,8},{14,10},{16,20},{18,... | collective-permute-start | bytes 12296 | tf_op jit(solution)/shard_map/ppermute | solution.py:580
  50.3 3.3 %data_part.5.refs_5_ = f32[64,512]{1,0:T(8,128)S(1)} custom-call(s32[4]{0:T(128)S(1)} %copy-done.8, s32[4]{0:T(128)S(1)} %copy-done.10, f32[64,512]{1,0:T(8,128)S(1)} %get-tuple-element.39.refs_2_, f32[16,512]{1,0:T(8,128)S(1)} %get-tuple-element.30.refs_3_.refs_7_, f32[64,128]{1,0:T(8,128)S(1)} %get-tuple-element.31.refs_4_.refs_8_, ...), custom_call_target="tpu_custom_call" | custom-call | flops 6000000000 | bytes 8000000 | tf_op jit(solution)/shard_map/data_part/pallas_call | solution.py:313
  53.7 3.5 %collective-permute-start.15 = (f32[8,128]{1,0:T(8,128)S(1)}, f32[8,128]{1,0:T(8,128)S(1)}, u32[]{:S(2)}, u32[]{:S(2)}) collective-permute-start(f32[8,128]{1,0:T(8,128)S(1)} %add_add_fusion.3), channel_id=1, source_target_pairs={{0,24},{2,26},{4,28},{6,30},{8,16},{10,18},{12,20},{14,22},{16,8},... | collective-permute-start | bytes 12296 | tf_op jit(solution)/shard_map/ppermute | solution.py:580
  57.2 0.9 collective-permute-start.13
  58.1 3.0 %collective-permute-start.16 = (f32[64,512]{1,0:T(8,128)S(1)}, f32[64,512]{1,0:T(8,128)S(1)}, u32[]{:S(2)}, u32[]{:S(2)}) collective-permute-start(f32[64,512]{1,0:T(8,128)S(1)} %data_part.5.refs_5_), channel_id=1, source_target_pairs={{0,1},{1,0},{2,3},{3,2},{4,5},{5,4},{6,7},{7,6},{8,9},{9,8},{10,11... | collective-permute-start | bytes 393224 | tf_op jit(solution)/shard_map/ppermute | solution.py:591
  61.7 2.6 %collective-permute-done.16.refs_6_ = f32[64,512]{1,0:T(8,128)S(1)} collective-permute-done((f32[64,512]{1,0:T(8,128)S(1)}, f32[64,512]{1,0:T(8,128)S(1)}, u32[]{:S(2)}, u32[]{:S(2)}) %collective-permute-start.16) | collective-permute-done | bytes 131104 | tf_op jit(solution)/shard_map/ppermute | solution.py:591
  64.3 5.3 %model_part.5 = (f32[64,512]{1,0:T(8,128)S(1)}, f32[64,512]{1,0:T(8,128)}, f32[64,512]{1,0:T(8,128)S(1)}, f32[8,128]{1,0:T(8,128)S(1)}) custom-call(f32[8,128]{1,0:T(8,128)S(1)} %add_add_fusion.2.refs_0_, f32[64,512]{1,0:T(8,128)S(1)} %get-tuple-element.41.refs_1_, f32[64,512]{1,0:T(8,128)S(1)} %get-tuple-element.39.refs_2_, ...), custom_call_target="tpu_custom_call" | custom-call | flops 6000000000 | bytes 2000000 | tf_op jit(solution)/shard_map/model_part/pallas_call | solution.py:508
  69.6 0.6 copy-done
  70.3 0.6 copy-done.1
  70.9 1.3 %collective-permute-start.18 = (f32[8,128]{1,0:T(8,128)S(1)}, f32[8,128]{1,0:T(8,128)S(1)}, u32[]{:S(2)}, u32[]{:S(2)}) collective-permute-start(f32[8,128]{1,0:T(8,128)S(1)} %get-tuple-element.44), channel_id=1, source_target_pairs={{0,4},{2,6},{4,0},{6,2},{8,12},{10,14},{12,8},{14,10},{16,20},{18,... | collective-permute-start | bytes 12296 | tf_op jit(solution)/shard_map/ppermute | solution.py:580
  72.8 1.2 %collective-permute-done.19 = f32[8,128]{1,0:T(8,128)S(1)} collective-permute-done((f32[8,128]{1,0:T(8,128)S(1)}, f32[8,128]{1,0:T(8,128)S(1)}, u32[]{:S(2)}, u32[]{:S(2)}) %collective-permute-start.19) | collective-permute-done | bytes 4128 | tf_op jit(solution)/shard_map/ppermute | solution.py:580
  74.0 0.6 collective-permute-done.18
  74.6 3.5 %collective-permute-start.22 = (f32[8,128]{1,0:T(8,128)S(1)}, f32[8,128]{1,0:T(8,128)S(1)}, u32[]{:S(2)}, u32[]{:S(2)}) collective-permute-start(f32[8,128]{1,0:T(8,128)S(1)} %add_add_fusion.1), channel_id=1, source_target_pairs={{0,24},{2,26},{4,28},{6,30},{8,16},{10,18},{12,20},{14,22},{16,8},... | collective-permute-start | bytes 12296 | tf_op jit(solution)/shard_map/ppermute | solution.py:580
  78.1 0.9 collective-permute-start.20
  79.0 1.0 collective-permute-done.22
  80.0 2.6 %collective-permute-done.21 = f32[8,128]{1,0:T(8,128)S(1)} collective-permute-done((f32[8,128]{1,0:T(8,128)S(1)}, f32[8,128]{1,0:T(8,128)S(1)}, u32[]{:S(2)}, u32[]{:S(2)}) %collective-permute-start.21) | collective-permute-done | bytes 4128 | tf_op jit(solution)/shard_map/ppermute | solution.py:580
  82.6 0.6 add_add_fusion.sums
  83.2 1.8 %last_step.1 = (f32[64,1,256]{2,1,0:T(1,128)}, f32[64,256]{1,0:T(8,128)}, f32[256,128]{1,0:T(8,128)}, f32[256,128]{1,0:T(8,128)}) custom-call(f32[8,128]{1,0:T(8,128)} %add_add_fusion.sums, f32[64,512]{1,0:T(8,128)} %copy-done, f32[64,512]{1,0:T(8,128)} %copy-done.1, f32[64,1,256]{2,1,0:T(1,128)} %bitcast.8), custom_call_target="tpu_custom_call" | custom-call | tf_op jit(solution)/shard_map/last_step/pallas_call | solution.py:546
  85.0 1.6 %collective-permute-done.23 = f32[256,128]{1,0:T(8,128)S(1)} collective-permute-done((f32[256,128]{1,0:T(8,128)}, f32[256,128]{1,0:T(8,128)S(1)}, u32[]{:S(2)}, u32[]{:S(2)}) %collective-permute-start.23) | collective-permute-done | bytes 131104 | tf_op jit(solution)/shard_map/ppermute | solution.py:580
  86.5 0.9 add.84
  87.5 1.5 %collective-permute-start.24 = (f32[256,128]{1,0:T(8,128)S(1)}, f32[256,128]{1,0:T(8,128)S(1)}, u32[]{:S(2)}, u32[]{:S(2)}) collective-permute-start(f32[256,128]{1,0:T(8,128)S(1)} %add.84), channel_id=1, source_target_pairs={{0,4},{2,6},{4,0},{6,2},{8,12},{10,14},{12,8},{14,10},{16,20},{18,... | collective-permute-start | bytes 393224 | tf_op jit(solution)/shard_map/ppermute | solution.py:580
  88.9 4.1 %collective-permute-done.24 = f32[256,128]{1,0:T(8,128)S(1)} collective-permute-done((f32[256,128]{1,0:T(8,128)S(1)}, f32[256,128]{1,0:T(8,128)S(1)}, u32[]{:S(2)}, u32[]{:S(2)}) %collective-permute-start.24) | collective-permute-done | bytes 131104 | tf_op jit(solution)/shard_map/ppermute | solution.py:580
  93.2 5.0 %collective-permute-done.25 = f32[256,128]{1,0:T(8,128)S(1)} collective-permute-done((f32[256,128]{1,0:T(8,128)S(1)}, f32[256,128]{1,0:T(8,128)S(1)}, u32[]{:S(2)}, u32[]{:S(2)}) %collective-permute-start.25) | collective-permute-done | bytes 131104 | tf_op jit(solution)/shard_map/ppermute | solution.py:580
  98.1 2.1 %collective-permute-start.26 = (f32[256,128]{1,0:T(8,128)S(1)}, f32[256,128]{1,0:T(8,128)S(1)}, u32[]{:S(2)}, u32[]{:S(2)}) collective-permute-start(f32[256,128]{1,0:T(8,128)S(1)} %add.86), channel_id=1, source_target_pairs={{0,16},{2,18},{4,20},{6,22},{8,24},{10,26},{12,28},{14,30},{16,0},... | collective-permute-start | bytes 393224 | tf_op jit(solution)/shard_map/ppermute | solution.py:580
  100.2 5.0 %collective-permute-done.26 = f32[256,128]{1,0:T(8,128)S(1)} collective-permute-done((f32[256,128]{1,0:T(8,128)S(1)}, f32[256,128]{1,0:T(8,128)S(1)}, u32[]{:S(2)}, u32[]{:S(2)}) %collective-permute-start.26) | collective-permute-done | bytes 131104 | tf_op jit(solution)/shard_map/ppermute | solution.py:580
  105.3 1.3 %collective-permute-done.27.theirs = f32[256,128]{1,0:T(8,128)S(1)} collective-permute-done((f32[256,128]{1,0:T(8,128)S(1)}, f32[256,128]{1,0:T(8,128)S(1)}, u32[]{:S(2)}, u32[]{:S(2)}) %collective-permute-start.27) | collective-permute-done | bytes 131104 | tf_op jit(solution)/shard_map/ppermute | solution.py:580
  106.7 0.7 copy-done.12
  107.3 1.8 %consensus.1 = (f32[64,4,256]{2,1,0:T(4,128)}, f32[64,1,256]{2,1,0:T(1,128)}) custom-call(f32[256,128]{1,0:T(8,128)} %copy-done.11, f32[256,128]{1,0:T(8,128)} %copy-done.12, f32[64,256]{1,0:T(8,128)} %get-tuple-element.50.shifted), custom_call_target="tpu_custom_call" | custom-call | tf_op jit(solution)/shard_map/consensus/pallas_call | solution.py:570
  (52 shorter events, 2.9 us)
Async XLA Ops:
  0.6 7.0 %collective-permute-start = (f32[64,1,256]{2,1,0:T(1,128)}, f32[64,1,256]{2,1,0:T(1,128)S(1)}, u32[]{:S(2)}, u32[]{:S(2)}) collective-permute-start(f32[64,1,256]{2,1,0:T(1,128)} %bitcast.11), channel_id=1, source_target_pairs={{0,1},{1,0},{2,3},{3,2},{4,5},{5,4},{6,7},{7,6},{8,9},{9,8},{10,11... | collective-permute-start | bytes 196616 | tf_op jit(solution)/shard_map/ppermute | solution.py:591
  3.6 3.9 %collective-permute-start.1 = (f32[16,256]{1,0:T(8,128)}, f32[16,256]{1,0:T(8,128)S(1)}, u32[]{:S(2)}, u32[]{:S(2)}) collective-permute-start(f32[16,256]{1,0:T(8,128)} %bitcast.13), channel_id=1, source_target_pairs={{0,1},{1,0},{2,3},{3,2},{4,5},{5,4},{6,7},{7,6},{8,9},{9,8},{10,11... | collective-permute-start | bytes 49160 | tf_op jit(solution)/shard_map/ppermute | solution.py:591
  7.6 0.8 copy-start.2
  8.4 0.9 copy-start.3
  9.4 0.8 copy-start.4
  10.2 0.7 copy-start.5
  10.9 0.7 copy-start.6
  11.6 0.7 copy-start.7
  12.3 0.7 copy-start.9
  16.5 5.2 %collective-permute-start.2 = (f32[72,512]{1,0:T(8,128)S(1)}, f32[72,512]{1,0:T(8,128)S(1)}, u32[]{:S(2)}, u32[]{:S(2)}) collective-permute-start(f32[72,512]{1,0:T(8,128)S(1)} %get-tuple-element.29.refs_1_), channel_id=1, source_target_pairs={{0,1},{1,0},{2,3},{3,2},{4,5},{5,4},{6,7},{7,6},{8,9},{9,8},{10,11... | collective-permute-start | bytes 442376 | tf_op jit(solution)/shard_map/ppermute | solution.py:591
  21.7 7.2 %copy-start.8 = (s32[4]{0:T(128)S(1)}, s32[4]{0:T(128)}, u32[]{:S(2)}) copy-start(s32[4]{0:T(128)} %refs_0_.5) | copy-start | bytes 52
  21.7 7.2 %copy-start.10 = (s32[4]{0:T(128)S(1)}, s32[4]{0:T(128)}, u32[]{:S(2)}) copy-start(s32[4]{0:T(128)} %refs_1_.5) | copy-start | bytes 52
  27.0 5.2 %collective-permute-start.5 = (f32[8,128]{1,0:T(8,128)S(1)}, f32[8,128]{1,0:T(8,128)S(1)}, u32[]{:S(2)}, u32[]{:S(2)}) collective-permute-start(f32[8,128]{1,0:T(8,128)S(1)} %get-tuple-element.32), channel_id=1, source_target_pairs={{0,6},{2,4},{4,2},{6,0},{8,14},{10,12},{12,10},{14,8},{16,22},{18,... | collective-permute-start | bytes 12296 | tf_op jit(solution)/shard_map/ppermute | solution.py:580
  27.1 5.1 %collective-permute-start.4 = (f32[8,128]{1,0:T(8,128)S(1)}, f32[8,128]{1,0:T(8,128)S(1)}, u32[]{:S(2)}, u32[]{:S(2)}) collective-permute-start(f32[8,128]{1,0:T(8,128)S(1)} %get-tuple-element.32), channel_id=1, source_target_pairs={{0,4},{2,6},{4,0},{6,2},{8,12},{10,14},{12,8},{14,10},{16,20},{18,... | collective-permute-start | bytes 12296 | tf_op jit(solution)/shard_map/ppermute | solution.py:580
  28.7 3.6 %collective-permute-start.3 = (f32[8,128]{1,0:T(8,128)S(1)}, f32[8,128]{1,0:T(8,128)S(1)}, u32[]{:S(2)}, u32[]{:S(2)}) collective-permute-start(f32[8,128]{1,0:T(8,128)S(1)} %get-tuple-element.32), channel_id=1, source_target_pairs={{0,2},{2,0},{4,6},{6,4},{8,10},{10,8},{12,14},{14,12},{16,18},{18,... | collective-permute-start | bytes 12296 | tf_op jit(solution)/shard_map/ppermute | solution.py:580
  32.3 7.6 %collective-permute-start.8 = (f32[8,128]{1,0:T(8,128)S(1)}, f32[8,128]{1,0:T(8,128)S(1)}, u32[]{:S(2)}, u32[]{:S(2)}) collective-permute-start(f32[8,128]{1,0:T(8,128)S(1)} %add_add_fusion.5), channel_id=1, source_target_pairs={{0,24},{2,26},{4,28},{6,30},{8,16},{10,18},{12,20},{14,22},{16,8},... | collective-permute-start | bytes 12296 | tf_op jit(solution)/shard_map/ppermute | solution.py:580
  35.9 4.5 %collective-permute-start.7 = (f32[8,128]{1,0:T(8,128)S(1)}, f32[8,128]{1,0:T(8,128)S(1)}, u32[]{:S(2)}, u32[]{:S(2)}) collective-permute-start(f32[8,128]{1,0:T(8,128)S(1)} %add_add_fusion.5), channel_id=1, source_target_pairs={{0,16},{2,18},{4,20},{6,22},{8,24},{10,26},{12,28},{14,30},{16,0},... | collective-permute-start | bytes 12296 | tf_op jit(solution)/shard_map/ppermute | solution.py:580
  35.9 4.5 %collective-permute-start.6 = (f32[8,128]{1,0:T(8,128)S(1)}, f32[8,128]{1,0:T(8,128)S(1)}, u32[]{:S(2)}, u32[]{:S(2)}) collective-permute-start(f32[8,128]{1,0:T(8,128)S(1)} %add_add_fusion.5), channel_id=1, source_target_pairs={{0,8},{2,10},{4,12},{6,14},{8,0},{10,2},{12,4},{14,6},{16,24},{18,... | collective-permute-start | bytes 12296 | tf_op jit(solution)/shard_map/ppermute | solution.py:580
  36.7 6.4 %collective-permute-start.9 = (f32[64,512]{1,0:T(8,128)S(1)}, f32[64,512]{1,0:T(8,128)S(1)}, u32[]{:S(2)}, u32[]{:S(2)}) collective-permute-start(f32[64,512]{1,0:T(8,128)S(1)} %data_part.4.refs_5_), channel_id=1, source_target_pairs={{0,1},{1,0},{2,3},{3,2},{4,5},{5,4},{6,7},{7,6},{8,9},{9,8},{10,11... | collective-permute-start | bytes 393224 | tf_op jit(solution)/shard_map/ppermute | solution.py:591
  48.4 5.2 %collective-permute-start.12 = (f32[8,128]{1,0:T(8,128)S(1)}, f32[8,128]{1,0:T(8,128)S(1)}, u32[]{:S(2)}, u32[]{:S(2)}) collective-permute-start(f32[8,128]{1,0:T(8,128)S(1)} %get-tuple-element.38), channel_id=1, source_target_pairs={{0,6},{2,4},{4,2},{6,0},{8,14},{10,12},{12,10},{14,8},{16,22},{18,... | collective-permute-start | bytes 12296 | tf_op jit(solution)/shard_map/ppermute | solution.py:580
  48.5 5.1 %collective-permute-start.11 = (f32[8,128]{1,0:T(8,128)S(1)}, f32[8,128]{1,0:T(8,128)S(1)}, u32[]{:S(2)}, u32[]{:S(2)}) collective-permute-start(f32[8,128]{1,0:T(8,128)S(1)} %get-tuple-element.38), channel_id=1, source_target_pairs={{0,4},{2,6},{4,0},{6,2},{8,12},{10,14},{12,8},{14,10},{16,20},{18,... | collective-permute-start | bytes 12296 | tf_op jit(solution)/shard_map/ppermute | solution.py:580
  49.8 3.8 %collective-permute-start.10 = (f32[8,128]{1,0:T(8,128)S(1)}, f32[8,128]{1,0:T(8,128)S(1)}, u32[]{:S(2)}, u32[]{:S(2)}) collective-permute-start(f32[8,128]{1,0:T(8,128)S(1)} %get-tuple-element.38), channel_id=1, source_target_pairs={{0,2},{2,0},{4,6},{6,4},{8,10},{10,8},{12,14},{14,12},{16,18},{18,... | collective-permute-start | bytes 12296 | tf_op jit(solution)/shard_map/ppermute | solution.py:580
  53.7 7.5 %collective-permute-start.15 = (f32[8,128]{1,0:T(8,128)S(1)}, f32[8,128]{1,0:T(8,128)S(1)}, u32[]{:S(2)}, u32[]{:S(2)}) collective-permute-start(f32[8,128]{1,0:T(8,128)S(1)} %add_add_fusion.3), channel_id=1, source_target_pairs={{0,24},{2,26},{4,28},{6,30},{8,16},{10,18},{12,20},{14,22},{16,8},... | collective-permute-start | bytes 12296 | tf_op jit(solution)/shard_map/ppermute | solution.py:580
  57.2 4.5 %collective-permute-start.14 = (f32[8,128]{1,0:T(8,128)S(1)}, f32[8,128]{1,0:T(8,128)S(1)}, u32[]{:S(2)}, u32[]{:S(2)}) collective-permute-start(f32[8,128]{1,0:T(8,128)S(1)} %add_add_fusion.3), channel_id=1, source_target_pairs={{0,16},{2,18},{4,20},{6,22},{8,24},{10,26},{12,28},{14,30},{16,0},... | collective-permute-start | bytes 12296 | tf_op jit(solution)/shard_map/ppermute | solution.py:580
  57.2 4.5 %collective-permute-start.13 = (f32[8,128]{1,0:T(8,128)S(1)}, f32[8,128]{1,0:T(8,128)S(1)}, u32[]{:S(2)}, u32[]{:S(2)}) collective-permute-start(f32[8,128]{1,0:T(8,128)S(1)} %add_add_fusion.3), channel_id=1, source_target_pairs={{0,8},{2,10},{4,12},{6,14},{8,0},{10,2},{12,4},{14,6},{16,24},{18,... | collective-permute-start | bytes 12296 | tf_op jit(solution)/shard_map/ppermute | solution.py:580
  58.1 6.2 %collective-permute-start.16 = (f32[64,512]{1,0:T(8,128)S(1)}, f32[64,512]{1,0:T(8,128)S(1)}, u32[]{:S(2)}, u32[]{:S(2)}) collective-permute-start(f32[64,512]{1,0:T(8,128)S(1)} %data_part.5.refs_5_), channel_id=1, source_target_pairs={{0,1},{1,0},{2,3},{3,2},{4,5},{5,4},{6,7},{7,6},{8,9},{9,8},{10,11... | collective-permute-start | bytes 393224 | tf_op jit(solution)/shard_map/ppermute | solution.py:591
  69.6 0.7 copy-start
  70.3 0.6 copy-start.1
  70.9 3.0 %collective-permute-start.19 = (f32[8,128]{1,0:T(8,128)S(1)}, f32[8,128]{1,0:T(8,128)S(1)}, u32[]{:S(2)}, u32[]{:S(2)}) collective-permute-start(f32[8,128]{1,0:T(8,128)S(1)} %get-tuple-element.44), channel_id=1, source_target_pairs={{0,6},{2,4},{4,2},{6,0},{8,14},{10,12},{12,10},{14,8},{16,22},{18,... | collective-permute-start | bytes 12296 | tf_op jit(solution)/shard_map/ppermute | solution.py:580
  70.9 3.6 %collective-permute-start.18 = (f32[8,128]{1,0:T(8,128)S(1)}, f32[8,128]{1,0:T(8,128)S(1)}, u32[]{:S(2)}, u32[]{:S(2)}) collective-permute-start(f32[8,128]{1,0:T(8,128)S(1)} %get-tuple-element.44), channel_id=1, source_target_pairs={{0,4},{2,6},{4,0},{6,2},{8,12},{10,14},{12,8},{14,10},{16,20},{18,... | collective-permute-start | bytes 12296 | tf_op jit(solution)/shard_map/ppermute | solution.py:580
  72.2 2.3 %collective-permute-start.17 = (f32[8,128]{1,0:T(8,128)S(1)}, f32[8,128]{1,0:T(8,128)S(1)}, u32[]{:S(2)}, u32[]{:S(2)}) collective-permute-start(f32[8,128]{1,0:T(8,128)S(1)} %get-tuple-element.44), channel_id=1, source_target_pairs={{0,2},{2,0},{4,6},{6,4},{8,10},{10,8},{12,14},{14,12},{16,18},{18,... | collective-permute-start | bytes 12296 | tf_op jit(solution)/shard_map/ppermute | solution.py:580
  74.6 5.5 %collective-permute-start.22 = (f32[8,128]{1,0:T(8,128)S(1)}, f32[8,128]{1,0:T(8,128)S(1)}, u32[]{:S(2)}, u32[]{:S(2)}) collective-permute-start(f32[8,128]{1,0:T(8,128)S(1)} %add_add_fusion.1), channel_id=1, source_target_pairs={{0,24},{2,26},{4,28},{6,30},{8,16},{10,18},{12,20},{14,22},{16,8},... | collective-permute-start | bytes 12296 | tf_op jit(solution)/shard_map/ppermute | solution.py:580
  78.1 4.5 %collective-permute-start.21 = (f32[8,128]{1,0:T(8,128)S(1)}, f32[8,128]{1,0:T(8,128)S(1)}, u32[]{:S(2)}, u32[]{:S(2)}) collective-permute-start(f32[8,128]{1,0:T(8,128)S(1)} %add_add_fusion.1), channel_id=1, source_target_pairs={{0,16},{2,18},{4,20},{6,22},{8,24},{10,26},{12,28},{14,30},{16,0},... | collective-permute-start | bytes 12296 | tf_op jit(solution)/shard_map/ppermute | solution.py:580
  78.1 4.5 %collective-permute-start.20 = (f32[8,128]{1,0:T(8,128)S(1)}, f32[8,128]{1,0:T(8,128)S(1)}, u32[]{:S(2)}, u32[]{:S(2)}) collective-permute-start(f32[8,128]{1,0:T(8,128)S(1)} %add_add_fusion.1), channel_id=1, source_target_pairs={{0,8},{2,10},{4,12},{6,14},{8,0},{10,2},{12,4},{14,6},{16,24},{18,... | collective-permute-start | bytes 12296 | tf_op jit(solution)/shard_map/ppermute | solution.py:580
  85.0 1.6 %collective-permute-start.23 = (f32[256,128]{1,0:T(8,128)}, f32[256,128]{1,0:T(8,128)S(1)}, u32[]{:S(2)}, u32[]{:S(2)}) collective-permute-start(f32[256,128]{1,0:T(8,128)} %get-tuple-element.49), channel_id=1, source_target_pairs={{0,2},{2,0},{4,6},{6,4},{8,10},{10,8},{12,14},{14,12},{16,18},{18,... | collective-permute-start | bytes 393224 | tf_op jit(solution)/shard_map/ppermute | solution.py:580
  87.5 5.6 %collective-permute-start.24 = (f32[256,128]{1,0:T(8,128)S(1)}, f32[256,128]{1,0:T(8,128)S(1)}, u32[]{:S(2)}, u32[]{:S(2)}) collective-permute-start(f32[256,128]{1,0:T(8,128)S(1)} %add.84), channel_id=1, source_target_pairs={{0,4},{2,6},{4,0},{6,2},{8,12},{10,14},{12,8},{14,10},{16,20},{18,... | collective-permute-start | bytes 393224 | tf_op jit(solution)/shard_map/ppermute | solution.py:580
  93.1 5.0 %collective-permute-start.25 = (f32[256,128]{1,0:T(8,128)S(1)}, f32[256,128]{1,0:T(8,128)S(1)}, u32[]{:S(2)}, u32[]{:S(2)}) collective-permute-start(f32[256,128]{1,0:T(8,128)S(1)} %add.85), channel_id=1, source_target_pairs={{0,8},{2,10},{4,12},{6,14},{8,0},{10,2},{12,4},{14,6},{16,24},{18,... | collective-permute-start | bytes 393224 | tf_op jit(solution)/shard_map/ppermute | solution.py:580
  98.1 7.1 %collective-permute-start.26 = (f32[256,128]{1,0:T(8,128)S(1)}, f32[256,128]{1,0:T(8,128)S(1)}, u32[]{:S(2)}, u32[]{:S(2)}) collective-permute-start(f32[256,128]{1,0:T(8,128)S(1)} %add.86), channel_id=1, source_target_pairs={{0,16},{2,18},{4,20},{6,22},{8,24},{10,26},{12,28},{14,30},{16,0},... | collective-permute-start | bytes 393224 | tf_op jit(solution)/shard_map/ppermute | solution.py:580
  105.2 1.4 %copy-start.11 = (f32[256,128]{1,0:T(8,128)}, f32[256,128]{1,0:T(8,128)S(1)}, u32[]{:S(2)}) copy-start(f32[256,128]{1,0:T(8,128)S(1)} %add.87.mine) | copy-start | bytes 393220
  105.2 1.4 %collective-permute-start.27 = (f32[256,128]{1,0:T(8,128)S(1)}, f32[256,128]{1,0:T(8,128)S(1)}, u32[]{:S(2)}, u32[]{:S(2)}) collective-permute-start(f32[256,128]{1,0:T(8,128)S(1)} %add.87.mine), channel_id=1, source_target_pairs={{0,2},{2,0},{4,6},{6,4},{8,10},{10,8},{12,14},{14,12},{16,18},{18,... | collective-permute-start | bytes 393224 | tf_op jit(solution)/shard_map/ppermute | solution.py:580
  106.7 0.7 copy-start.12

commit v2 on v1

v2 whole, which is shorter than its diff:
```python
import functools
import math

import jax
import jax.numpy as jnp
import numpy as np
from jax import lax
from jax.experimental import pallas as pl
from jax.experimental.pallas import tpu as pltpu
from jax.sharding import PartitionSpec as P

ITERS = 3
EPSILON = 1e-06
SPECTRAL_INDEX = 0.7
DIRS = 8
CHUNK = 128
VMEM_BYTES = 48 * 1024 * 1024
AHEAD = 2
F32 = jnp.float32
BF16 = jnp.bfloat16

NT = (((1,), (1,)), ((), ()))
NN = (((1,), (0,)), ((), ()))
TN = (((0,), (0,)), ((), ()))


def dot(lhs, rhs, dims):
    return lax.dot_general(lhs, rhs, dims, preferred_element_type=F32)


def pair_lists(station_blocks):
    return [(p, q) for p in range(station_blocks) for q in range(p, station_blocks)]


def bernstein_np(total_channels):
    position = (np.arange(total_channels, dtype=np.float64) + 0.5) / total_channels
    others = 1.0 - position
    return np.stack(
        [others**3, 3.0 * position * others**2, 3.0 * position**2 * others, position**3], axis=1
    )


def split(x):
    high = x.astype(BF16)
    return high, (x - high.astype(F32)).astype(BF16)


def pack(x):
    high, low = split(x)
    return jnp.concatenate([high, low], axis=0)


def trig(delay, freq):
    turns = delay * freq
    turns = turns - jnp.floor(turns + 0.5)
    x = turns * math.pi
    x2 = x * x
    sin_half = x * (
        1.0
        + x2
        * (
            -1.0 / 6
            + x2
            * (
                1.0 / 120
                + x2
                * (
                    -1.0 / 5040
                    + x2 * (1.0 / 362880 + x2 * (-1.0 / 39916800 + x2 * (1.0 / 6227020800)))
                )
            )
        )
    )
    cos_half = 1.0 + x2 * (
        -0.5
        + x2
        * (
            1.0 / 24
            + x2
            * (
                -1.0 / 720
                + x2
                * (
                    1.0 / 40320
                    + x2 * (-1.0 / 3628800 + x2 * (1.0 / 479001600 + x2 * (-1.0 / 87178291200)))
                )
            )
        )
    )
    return 1.0 - 2.0 * sin_half * sin_half, 2.0 * sin_half * cos_half


def rotate(field, cosine, sine):
    re = [field[8 * m : 8 * m + 8] for m in range(4)]
    im = [field[32 + 8 * m : 40 + 8 * m] for m in range(4)]
    return (
        [cosine * re[m] - sine * im[m] for m in range(4)],
        [cosine * im[m] + sine * re[m] for m in range(4)],
    )


def coherency_rows(coh, width):
    reps = width // coh.shape[1]
    rows = [jnp.concatenate([coh[8 * e : 8 * e + 8]] * reps, axis=1) for e in range(8)]
    return rows[:4], rows[4:]


def left_rows(rot, bright):
    (a_re, a_im), (c_re, c_im) = rot, bright
    out = []
    for i in range(2):
        re_rows, im_rows = [], []
        for l in range(2):
            re = im = None
            for k in range(2):
                ar, ai, cr, ci = a_re[2 * i + k], a_im[2 * i + k], c_re[2 * k + l], c_im[2 * k + l]
                tr, ti = ar * cr - ai * ci, ar * ci + ai * cr
                re, im = (tr, ti) if re is None else (re + tr, im + ti)
            re_rows.append(re)
            im_rows.append(im)
        out.append(jnp.concatenate(re_rows + im_rows, axis=0))
    return out


def right_rows(rot):
    a_re, a_im = rot
    real = [
        jnp.concatenate([a_re[2 * j], a_re[2 * j + 1], a_im[2 * j], a_im[2 * j + 1]], axis=0)
        for j in range(2)
    ]
    imag = [
        jnp.concatenate([-a_im[2 * j], -a_im[2 * j + 1], a_re[2 * j], a_re[2 * j + 1]], axis=0)
        for j in range(2)
    ]
    return real + imag


def field_gradient(h_left, h_right, bright, cosine, sine):
    c_re, c_im = bright
    g_re, g_im = [], []
    for i in range(2):
        for k in range(2):
            j = i
            re = h_right[j][8 * k : 8 * k + 8] + h_right[2 + j][16 + 8 * k : 24 + 8 * k]
            im = h_right[j][16 + 8 * k : 24 + 8 * k] - h_right[2 + j][8 * k : 8 * k + 8]
            for l in range(2):
                lr = h_left[i][8 * l : 8 * l + 8]
                li = h_left[i][16 + 8 * l : 24 + 8 * l]
                cr, ci = c_re[2 * k + l], c_im[2 * k + l]
                re = re + lr * cr + li * ci
                im = im + li * cr - lr * ci
            g_re.append(cosine * re + sine * im)
            g_im.append(cosine * im - sine * re)
    return jnp.concatenate(g_re + g_im, axis=0)


def coherency_tile(brightness, freq):
    spectral = jnp.exp(-SPECTRAL_INDEX * jnp.log(jnp.full((8, 128), freq, F32)))
    tiles = []
    for e in range(8):
        column = jnp.transpose(jnp.broadcast_to(brightness[e : e + 1, :], (8, 8)))[:, :1]
        tiles.append(column * spectral)
    return jnp.concatenate(tiles, axis=0)


def position_of(chan_count):
    return lax.axis_index("chan").astype(F32) * (1.0 / chan_count)


def frequency_of(chan_count):
    return 1.0 + position_of(chan_count)


def basis_of(chan_count):
    x = position_of(chan_count) + 0.5 / chan_count
    y = 1.0 - x
    return [y * y * y, 3.0 * x * y * y, 3.0 * x * x * y, x * x * x]


def solve_of(chan_count):
    basis = bernstein_np(chan_count)
    inverse = np.linalg.inv(basis.T @ basis)
    row = basis_of(chan_count)
    return [sum(row[m] * float(inverse[m, k]) for m in range(4)) for k in range(4)]


def vmem_specs(count):
    return [pl.BlockSpec(memory_space=pltpu.VMEM)] * count


def smem_specs(count):
    return [pl.BlockSpec(memory_space=pltpu.SMEM)] * count


def params():
    return pltpu.CompilerParams(vmem_limit_bytes=VMEM_BYTES)


def shape(*dims, dtype=F32):
    return jax.ShapeDtypeStruct(dims, dtype)


def own_lanes(block):
    return pl.ds(pl.multiple_of(lax.axis_index("stn") * block, CHUNK), block)


def pair_blocks(pairs, pair):
    first, second = jnp.int32(0), jnp.int32(0)
    for k, (p, q) in enumerate(pairs):
        first = first + jnp.where(pair == k, p, 0)
        second = second + jnp.where(pair == k, q, 0)
    return first, second


def prepare_kernel(block, pairs, slots, penalty, chan_count, *refs):
    table, flags, gains, duals, prior, bright, *refs = refs
    gains_out, duals_out, start_out, coh_out, counts_out = refs
    lane = lax.broadcasted_iota(jnp.int32, (8, 128), 1)
    counts = jnp.zeros((8, 128), F32)
    for slot in range(slots):
        held_here = (lane == table[slot]) & (lane < len(pairs))
        counts = counts + jnp.where(held_here, flags[slot].astype(F32), 0.0)
    counts_out[...] = counts
    coh_out[...] = coherency_tile(bright[...], frequency_of(chan_count))
    gains_out[...] = gains[:, 0, :]
    duals_own = duals[:, 0, :]
    duals_out[...] = duals_own
    target = -duals_own
    for k, scale in enumerate(basis_of(chan_count)):
        target = target + scale * prior[:, k, :]
    start_out[...] = -penalty * target


def prepare(geometry, table, flags, gains, duals, prior, brightness):
    block, pairs, dumps, penalty, chan_count, stations = geometry
    return pl.pallas_call(
        functools.partial(
            prepare_kernel, block, pairs, table.shape[0], penalty, chan_count
        ),
        name="prepare",
        out_shape=(
            shape(64, block),
            shape(64, block),
            shape(64, block),
            shape(64, 128),
            shape(8, 128),
        ),
        in_specs=smem_specs(2) + vmem_specs(4),
        out_specs=tuple(vmem_specs(5)),
        compiler_params=params(),
        cost_estimate=pl.CostEstimate(flops=1000000, bytes_accessed=2000000, transcendentals=0),
    )(table, flags, gains, duals, prior, brightness)


def data_kernel(block, pairs, dumps, slots, penalty, chan_count, first_call, joined, *refs):
    table, flags, observed, coh_ref, *refs = refs
    if first_call:
        if joined:
            gains_all, delays_all, *refs = refs
        else:
            gains_mine, gains_other, delays_mine, delays_other, *refs = refs
        start, counts_mine, ids_other, flags_other, out_ref, field_ref, delay_ref, counts_ref, *refs = refs
    else:
        field_ref, delay_ref, out_ref, *refs = refs
    held, sems, order, xp, yp, hl, ha = refs
    stations = field_ref.shape[1]
    pair_count = len(pairs)
    at_own = own_lanes(block)

    live_count = jnp.int32(0)
    for slot in range(slots):
        order[live_count] = jnp.int32(slot)
        live_count = live_count + jnp.where(table[slot] < pair_count, 1, 0)
    items = live_count * dumps

    def copy_of(item):
        slot, t = order[item // dumps], item % dumps
        return pltpu.make_async_copy(observed.at[slot, t], held.at[item], sems.at[item])

    for item in range(min(AHEAD, slots * dumps)):

        @pl.when(item < items)
        def _():
            copy_of(jnp.int32(item)).start()

    freq_value = frequency_of(chan_count)
    if first_call:
        if joined:
            field_ref[...] = gains_all[:, 0, :]
            delay_ref[...] = delays_all[...]
        else:
            at_other = pl.ds(pl.multiple_of((1 - lax.axis_index("stn")) * block, CHUNK), block)
            field_ref[:, at_own] = gains_mine[...]
            field_ref[:, at_other] = gains_other[:, 0, :]
            delay_ref[:, at_own] = delays_mine[...]
            delay_ref[:, at_other] = delays_other[...]
    bright = coherency_rows(coh_ref[...], stations)
    for t in range(dumps):
        cosine, sine = trig(delay_ref[8 * t : 8 * t + 8, :], freq_value)
        rot = rotate(field_ref[...], cosine, sine)
        for i, rows in enumerate(left_rows(rot, bright)):
            xp[t, i] = pack(rows)
        for rj, rows in enumerate(right_rows(rot)):
            yp[t, rj] = pack(rows)
    hl[...] = jnp.zeros_like(hl)
    ha[...] = jnp.zeros_like(ha)

    row = lax.broadcasted_iota(jnp.int32, (block, block), 0)
    col = lax.broadcasted_iota(jnp.int32, (block, block), 1)
    upper = row < col
    lane = lax.broadcasted_iota(jnp.int32, (1, block), 1)

    def visit(item, unused):
        slot, t = order[item // dumps], item % dumps
        first, second = pair_blocks(pairs, table[slot])
        keep = upper | (first < second)
        live = (lane >= flags[slot]).astype(F32)
        live16 = live.astype(BF16)
        at_p = pl.ds(pl.multiple_of(first * block, CHUNK), block)
        at_q = pl.ds(pl.multiple_of(second * block, CHUNK), block)
        copy_of(item).wait()

        @pl.when(item + AHEAD < items)
        def _():
            copy_of(item + AHEAD).start()

        acc_left = [None, None]
        acc_right = [None] * 4
        xs = [xp[t, i, :, at_p] * live16 for i in range(2)]
        ys = [yp[t, rj, :, at_q] for rj in range(4)]
        for r in range(2):
            for i in range(2):
                for j in range(2):
                    tile = held[item, 4 * r + 2 * i + j]
                    tile = jnp.where(keep, tile, jnp.zeros_like(tile))
                    rj = 2 * r + j
                    left = dot(ys[rj], tile, NT)
                    right = dot(xs[i], tile, NN)
                    acc_left[i] = left if acc_left[i] is None else acc_left[i] + left
                    acc_right[rj] = right if acc_right[rj] is None else acc_right[rj] + right
        for i in range(2):
            hl[t, i, :, at_p] += (acc_left[i][:32] + acc_left[i][32:]) * live
        for rj in range(4):
            ha[t, rj, :, at_q] += acc_right[rj][:32] + acc_right[rj][32:]
        return unused

    lax.fori_loop(0, items, visit, jnp.int32(0))

    total = None
    for t in range(dumps):
        cosine, sine = trig(delay_ref[8 * t : 8 * t + 8, :], freq_value)
        piece = field_gradient(
            [hl[t, i] for i in range(2)], [ha[t, rj] for rj in range(4)], bright, cosine, sine
        )
        total = piece if total is None else total + piece
    out_ref[...] = -total
    prior = penalty * field_ref[:, at_own]
    if first_call:
        prior = prior + start[...]
        counts = counts_mine[...]
        pair_lane = lax.broadcasted_iota(jnp.int32, (8, 128), 1)
        for k in range(pair_count):
            theirs = jnp.where(ids_other[...] == k, flags_other[...], 0).astype(F32)
            total_flags = jnp.sum(theirs, axis=1, keepdims=True)
            counts = counts + jnp.where(pair_lane == k, total_flags, 0.0)
        counts_ref[...] = counts
    out_ref[:, at_own] += prior


def data_part(geometry, table, flags, observed, coh, fields):
    block, pairs, dumps, penalty, chan_count, stations = geometry
    slots = observed.shape[0]
    first_call = len(fields) > 2
    joined = len(fields) == 6
    body = functools.partial(
        data_kernel, block, pairs, dumps, slots, penalty, chan_count, first_call, joined
    )
    shapes = [shape(64, stations)]
    if first_call:
        shapes += [shape(64, stations), shape(8 * dumps, stations), shape(8, 128)]
    return pl.pallas_call(
        body,
        name="data_part",
        out_shape=tuple(shapes),
        in_specs=smem_specs(2) + [pl.BlockSpec(memory_space=pl.ANY)] + vmem_specs(1 + len(fields)),
        out_specs=tuple(vmem_specs(len(shapes))),
        scratch_shapes=[
            pltpu.VMEM((slots * dumps,) + observed.shape[2:], BF16),
            pltpu.SemaphoreType.DMA((slots * dumps,)),
            pltpu.SMEM((slots,), jnp.int32),
            pltpu.VMEM((dumps, 2, 64, stations), BF16),
            pltpu.VMEM((dumps, 4, 64, stations), BF16),
            pltpu.VMEM((dumps, 2, 32, stations), F32),
            pltpu.VMEM((dumps, 4, 32, stations), F32),
        ],
        compiler_params=params(),
        cost_estimate=pl.CostEstimate(
            flops=6000000000, bytes_accessed=8000000, transcendentals=0
        ),
    )(table, flags, observed, coh, *fields)


def fold_gram(high_low, other, rows):
    wide = dot(high_low, other[:rows], NT)
    return wide[:rows] + wide[rows:] + dot(high_low[:rows], other[rows:], NT)


def apply_gram(gram, packed, rows):
    size = gram.shape[0]
    both = pack(gram)
    wide = dot(both, packed[:rows], NN)
    return wide[:size] + wide[size:] + dot(both[:size], packed[rows:], NN)


def lanes(parts, start, size):
    return jnp.concatenate([part[:, start : start + size] for part in parts], axis=1)


def twice(mask):
    return jnp.concatenate([mask, mask], axis=1)


class Chunks:
    def __init__(self, block, stations, pairs, counts):
        self.block = block
        self.size = min(CHUNK, block)
        self.per_block = block // self.size
        self.count = stations // self.size
        self.blocks = stations // block
        lane = lax.broadcasted_iota(jnp.int32, (1, block), 1).astype(F32)
        self.masks = {
            pair: (lane >= counts[:, k : k + 1]).astype(F32) for k, pair in enumerate(pairs)
        }
        row = lax.broadcasted_iota(jnp.int32, (2 * self.size, 4 * self.size), 0) % self.size
        col = lax.broadcasted_iota(jnp.int32, (2 * self.size, 4 * self.size), 1) % self.size
        self.upper = row < col

    def mask(self, pair, chunk):
        start = (chunk % self.per_block) * self.size
        return twice(self.masks[pair][:, start : start + self.size])

    def own_pair(self, chunk):
        return (chunk // self.per_block, chunk // self.per_block)

    def rect_terms(self, chunk):
        own = chunk // self.per_block
        terms = []
        inside = list(range(chunk + 1, (own + 1) * self.per_block))
        if inside:
            terms.append(((own, own), inside))
        for q in range(own + 1, self.blocks):
            terms.append(((own, q), list(range(q * self.per_block, (q + 1) * self.per_block))))
        return terms


def sum_of(parts):
    total = parts[0]
    for part in parts[1:]:
        total = total + part
    return total


def halves(rows, axis, bit):
    size = rows.shape[axis] // 2
    low = lax.slice_in_dim(rows, 0, size, axis=axis)
    high = lax.slice_in_dim(rows, size, 2 * size, axis=axis)
    odd = (lax.axis_index("chan") // bit) % 2 == 1
    return jnp.where(odd, high, low), jnp.where(odd, low, high)


def store_moments(fields, sums, chan_count, keep_out, send_out):
    for field_id, field in enumerate(fields):
        for out, part in zip((keep_out, send_out), halves(field, 1, 1)):
            for start, rows in zip((0, 264), halves(part, 0, 2)):
                for k, scale in enumerate(solve_of(chan_count)):
                    at = start + 128 * field_id + 32 * k
                    out[at : at + 32, :] = scale * rows
    for out in (keep_out, send_out):
        out[256:264, :] = sums
        out[520:528, :] = sums


def step_length(grad_sq, curvature, penalty):
    return grad_sq / (curvature + penalty * grad_sq + EPSILON)


def gradient_kernel(block, pairs, dumps, penalty, chan_count, update, *refs):
    counts_ref, delay_ref, coh_ref, current_ref, *refs = refs
    if update:
        sums_ref, direction_ref, *refs = refs
    gradient_out, *refs = refs
    if update:
        current_out, alpha_out, *refs = refs
    hl, ha = refs
    stations = current_ref.shape[1]
    chunks = Chunks(block, stations, pairs, counts_ref[0:1, :])
    size = chunks.size

    current = current_ref[...]
    if update:
        sums = jnp.sum(sums_ref[...], axis=0, keepdims=True)
        alpha = step_length(sums[:, 0:1], sums[:, 1:2], penalty)
        alpha_out[...] = jnp.broadcast_to(alpha, (8, 128))
        current = current - alpha * direction_ref[...]
        current_out[...] = current
    freq_value = frequency_of(chan_count)
    bright = coherency_rows(coh_ref[...], stations)
    gradient = None
    for t in range(dumps):
        cosine, sine = trig(delay_ref[8 * t : 8 * t + 8, :], freq_value)
        rot = rotate(current, cosine, sine)
        xs = [pack(v) for v in left_rows(rot, bright)]
        ys = [pack(v) for v in right_rows(rot)]
        gram_y = [
            fold_gram(lanes(ys, c * size, size), lanes(ys, c * size, size), 32)
            for c in range(chunks.count)
        ]
        sums_x = [None] * chunks.count
        for c in range(chunks.count):
            xc = lanes(xs, c * size, size)
            yc = lanes(ys, c * size, size)
            xw = xc * chunks.mask(chunks.own_pair(c), c).astype(BF16)
            yn = jnp.concatenate([yc[:32], yc[:32], yc[32:], yc[32:]], axis=0)
            model = dot(jnp.concatenate([xw, xw], axis=0), yn, TN)
            model = jnp.where(chunks.upper, model, 0.0)
            high, low = split(model)
            left = dot(yc, high, NT) + dot(yc, low, NT)
            right = dot(xw, high, NN) + dot(xw, low, NN)
            left = left[:32] + left[32:]
            right = right[:32] + right[32:]
            for pair, others in chunks.rect_terms(c):
                mask = chunks.mask(pair, c)
                left = left + apply_gram(sum_of([gram_y[o] for o in others]), xc, 32) * mask
                gram_x = fold_gram(xc * mask.astype(BF16), xc, 32)
                for o in others:
                    sums_x[o] = gram_x if sums_x[o] is None else sums_x[o] + gram_x
            if sums_x[c] is not None:
                right = right + apply_gram(sums_x[c], yc, 32)
            for i in range(2):
                hl[i, :, c * size : (c + 1) * size] = left[:, i * size : (i + 1) * size]
            for rj in range(4):
                ha[rj, :, c * size : (c + 1) * size] = right[:, rj * size : (rj + 1) * size]
        piece = field_gradient(
            [hl[i] for i in range(2)], [ha[rj] for rj in range(4)], bright, cosine, sine
        )
        gradient = piece if gradient is None else gradient + piece
    gradient_out[...] = gradient


def gradient_part(geometry, counts, delays, coh, current, step):
    block, pairs, dumps, penalty, chan_count, stations = geometry
    update = step is not None
    field = shape(64, stations)
    outs = [field]
    inputs = [counts, delays, coh, current]
    if update:
        inputs += step
        outs += [field, shape(8, 128)]
    return pl.pallas_call(
        functools.partial(gradient_kernel, block, pairs, dumps, penalty, chan_count, update),
        name="gradient_part",
        out_shape=tuple(outs),
        in_specs=vmem_specs(len(inputs)),
        out_specs=tuple(vmem_specs(len(outs))),
        scratch_shapes=[pltpu.VMEM((2, 32, stations), F32), pltpu.VMEM((4, 32, stations), F32)],
        compiler_params=params(),
        cost_estimate=pl.CostEstimate(
            flops=4000000000, bytes_accessed=2000000, transcendentals=0
        ),
    )(*inputs)


def curvature_kernel(block, pairs, dumps, penalty, chan_count, update, last, *refs):
    counts_ref, delay_ref, coh_ref, current_ref, gradient_ref, mine_ref, theirs_ref, *refs = refs
    if update:
        alpha_ref, linear_ref, *refs = refs
    if last:
        duals_ref, *refs = refs
    direction_out, *refs = refs
    if last:
        keep_out, send_out = refs
    else:
        linear_out, sums_out = refs
    stations = current_ref.shape[1]
    chunks = Chunks(block, stations, pairs, counts_ref[0:1, :])
    size = chunks.size

    current = current_ref[...]
    linear = mine_ref[...] + theirs_ref[...]
    if update:
        linear = linear_ref[...] - alpha_ref[0:1, 0:1] * linear
    direction = linear + gradient_ref[...]
    direction_out[...] = direction
    if not last:
        linear_out[...] = linear

    freq_value = frequency_of(chan_count)
    bright = coherency_rows(coh_ref[...], stations)
    squares = jnp.zeros((8, 4 * size), F32)
    grams = jnp.zeros((64, 64), F32)
    for t in range(dumps):
        cosine, sine = trig(delay_ref[8 * t : 8 * t + 8, :], freq_value)
        rot = rotate(current, cosine, sine)
        step = rotate(direction, cosine, sine)
        xs = [pack(v) for v in left_rows(rot, bright)]
        ys = [pack(v) for v in right_rows(rot)]
        dxs = [pack(v) for v in left_rows(step, bright)]
        dys = [pack(v) for v in right_rows(step)]

        def stacked(first, second, c):
            one = lanes(first, c * size, size)
            two = lanes(second, c * size, size)
            return jnp.concatenate([one[:32], two[:32], one[32:], two[32:]], axis=0)

        gram_y = [None] * chunks.count
        for c in range(chunks.count):
            xc = stacked(dxs, xs, c)
            yc = stacked(ys, dys, c)
            xw = xc * chunks.mask(chunks.own_pair(c), c).astype(BF16)
            tangent = dot(
                jnp.concatenate([xw, xw], axis=0),
                jnp.concatenate([yc[:64], yc[:64], yc[64:], yc[64:]], axis=0),
                TN,
            )
            tangent = jnp.where(chunks.upper, tangent, 0.0)
            square = tangent * tangent
            squares = squares + jnp.sum(square.reshape(2 * size // 8, 8, 4 * size), axis=0)
            if c > 0:
                gram_y[c] = fold_gram(yc, yc, 64)
        for c in range(chunks.count):
            for pair, others in chunks.rect_terms(c):
                xc = stacked(dxs, xs, c)
                gram_x = fold_gram(xc * chunks.mask(pair, c).astype(BF16), xc, 64)
                grams = grams + sum_of([gram_y[o] for o in others]) * gram_x
    curvature = jnp.sum(squares, keepdims=True) + jnp.sum(grams, keepdims=True)
    grad_sq = jnp.sum(direction * direction, keepdims=True)
    rows = 8 if last else chan_count
    lane = lax.broadcasted_iota(jnp.int32, (rows, block // 2 if last else 128), 1)
    sums = jnp.where(lane == 0, grad_sq, jnp.where(lane == 1, curvature, 0.0))
    if last:
        base = current_ref[:, own_lanes(block)] + duals_ref[...]
        store_moments(
            (base, direction_out[:, own_lanes(block)]), sums, chan_count, keep_out, send_out
        )
    else:
        sums_out[...] = sums


def curvature_part(geometry, counts, delays, coh, current, gradient, shares, before, duals):
    block, pairs, dumps, penalty, chan_count, stations = geometry
    update, last = before is not None, duals is not None
    field = shape(64, stations)
    if last:
        outs = [field] + [shape(528, block // 2)] * 2
    else:
        outs = [field, field, shape(chan_count, 128)]
    inputs = [counts, delays, coh, current, gradient, *shares]
    if update:
        inputs += before
    if last:
        inputs.append(duals)
    return pl.pallas_call(
        functools.partial(
            curvature_kernel, block, pairs, dumps, penalty, chan_count, update, last
        ),
        name="curvature_part",
        out_shape=tuple(outs),
        in_specs=vmem_specs(len(inputs)),
        out_specs=tuple(vmem_specs(len(outs))),
        compiler_params=params(),
        cost_estimate=pl.CostEstimate(
            flops=2000000000, bytes_accessed=2000000, transcendentals=0
        ),
    )(*inputs)


def combine_kernel(penalty, one, two, coeffs_out, alpha_out):
    total = one[...] + two[...]
    alpha = step_length(total[256:257, 0:1], total[256:257, 1:2], penalty)
    coeffs_out[...] = total[:128] - alpha * total[128:256]
    alpha_out[...] = jnp.broadcast_to(alpha, (8, 128))


def combine(geometry, one, two):
    penalty = geometry[3]
    return pl.pallas_call(
        functools.partial(combine_kernel, penalty),
        name="combine",
        out_shape=(shape(128, one.shape[1]), shape(8, 128)),
        in_specs=vmem_specs(2),
        out_specs=tuple(vmem_specs(2)),
        compiler_params=params(),
    )(one, two)


def last_step_kernel(block, alpha, current, direction, duals, gains_out, shifted_out):
    at_own = own_lanes(block)
    gains_new = current[:, at_own] - alpha[0:1, 0:1] * direction[:, at_own]
    gains_out[:, 0, :] = gains_new
    shifted_out[...] = gains_new + duals[...]


def last_step(geometry, *inputs):
    block = geometry[0]
    return pl.pallas_call(
        functools.partial(last_step_kernel, block),
        name="last_step",
        out_shape=(shape(64, 1, block), shape(64, block)),
        in_specs=vmem_specs(len(inputs)),
        out_specs=tuple(vmem_specs(2)),
        compiler_params=params(),
    )(*inputs)


def consensus_kernel(chan_count, own, core, row, both, shifted, coeffs_out, duals_out):
    place = lax.axis_index("chan")
    odd_core, odd_row = place % 2 == 1, (place // 2) % 2 == 1

    def joined(one, two, odd, axis):
        return jnp.concatenate([jnp.where(odd, two, one), jnp.where(odd, one, two)], axis=axis)

    fitted = None
    for k, scale in enumerate(basis_of(chan_count)):
        at = slice(32 * k, 32 * k + 32)
        coeffs = joined(
            joined(own[at, :], core[at, :], odd_core, 1),
            joined(row[at, :], both[at, :], odd_core, 1),
            odd_row,
            0,
        )
        coeffs_out[:, k, :] = coeffs
        fitted = scale * coeffs if fitted is None else fitted + scale * coeffs
    duals_out[:, 0, :] = shifted[...] - fitted


def consensus(geometry, *inputs):
    block, pairs, dumps, penalty, chan_count, stations = geometry
    return pl.pallas_call(
        functools.partial(consensus_kernel, chan_count),
        name="consensus",
        out_shape=(shape(64, 4, block), shape(64, 1, block)),
        in_specs=vmem_specs(len(inputs)),
        out_specs=tuple(vmem_specs(2)),
        compiler_params=params(),
    )(*inputs)


def swap(value, count, offset):
    return lax.ppermute(value, "chan", [(i, i ^ offset) for i in range(count)])


def other_stations(value):
    return lax.ppermute(value, "stn", [(0, 1), (1, 0)])


def both_stations(value, count):
    if count == 2:
        return value, other_stations(value)
    return jnp.zeros_like(value), lax.psum(value, "stn")


def shards(observed, pair_table, flag_rows, gains, duals, prior_coeffs, delays, brightness):
    stn_count = lax.axis_size("stn")
    chan_count = lax.axis_size("chan")
    entries, dirs, chan_local, block = gains.shape
    slots, dumps = observed.shape[0], observed.shape[2]
    stations = block * stn_count
    pairs = pair_lists(stn_count)
    penalty = stations * dumps / 16.0
    geometry = (block, pairs, dumps, penalty, chan_count, stations)

    observed = observed.reshape((slots,) + observed.shape[2:])
    gains_raw = gains.reshape(entries * dirs, 1, block)
    delays_raw = delays.reshape(dumps * dirs, block)
    duals_raw = duals.reshape(entries * dirs, 1, block)
    prior = prior_coeffs.reshape(entries * dirs, 4, block)
    ids_raw, flags_raw = pair_table.reshape(1, slots), flag_rows.reshape(1, slots)
    if stn_count == 2:
        gains_other, delays_other = other_stations(gains_raw), other_stations(delays_raw)
        ids_other, flags_other = other_stations(ids_raw), other_stations(flags_raw)
    else:
        gains_all = lax.all_gather(gains_raw, "stn", axis=2, tiled=True)
        delays_all = lax.all_gather(delays_raw, "stn", axis=1, tiled=True)
        ids_other = lax.all_gather(ids_raw, "stn", axis=1, tiled=True)
        flags_other = lax.all_gather(flags_raw, "stn", axis=1, tiled=True)
    gains_own, duals_own, start, coh, counts = prepare(
        geometry, pair_table, flag_rows, gains_raw, duals_raw, prior, brightness
    )
    if stn_count == 2:
        fields = (gains_own, gains_other, delays_raw, delays_other)
    else:
        fields = (gains_all, delays_all)
        counts = jnp.zeros_like(counts)
    data = functools.partial(data_part, geometry, pair_table, flag_rows, observed, coh)
    share, current, delay_all, counts = data(fields + (start, counts, ids_other, flags_other))
    shares = both_stations(share, stn_count)

    step = before = None
    for iteration in range(ITERS):
        last = iteration + 1 == ITERS
        gradient, *rest = gradient_part(geometry, counts, delay_all, coh, current, step)
        if step is not None:
            current, alpha = rest
            before = (alpha, linear)
        direction, *rest = curvature_part(
            geometry,
            counts,
            delay_all,
            coh,
            current,
            gradient,
            shares,
            before,
            duals_own if last else None,
        )
        if not last:
            linear, sums = rest
            sums = lax.all_to_all(sums, "chan", 0, 0, tiled=True)
            (share,) = data((direction, delay_all))
            shares = both_stations(share, stn_count)
            step = (sums, direction)

    keep, send = rest
    total = keep + swap(send, chan_count, 1)
    value, other = total[:264], swap(total[264:], chan_count, 2)
    bit = 4
    while bit < chan_count:
        value = value + other
        other = swap(value, chan_count, bit)
        bit *= 2
    quarter, alpha = combine(geometry, value, other)
    gains_new, shifted = last_step(geometry, alpha, current, direction, duals_own)
    quarters = [quarter] + [swap(quarter, chan_count, o) for o in (1, 2, 3)]
    coeffs, duals_new = consensus(geometry, *quarters, shifted)
    return (
        gains_new.reshape(gains.shape),
        coeffs.reshape(entries, dirs, 4, block),
        duals_new.reshape(gains.shape),
    )


def solution(mesh):
    return jax.shard_map(
        shards,
        mesh=mesh,
        in_specs=(
            P("stn", ("band", "chan"), None, None, None, None),
            P("stn"),
            P("stn"),
            P(None, None, ("band", "chan"), "stn"),
            P(None, None, ("band", "chan"), "stn"),
            P("band", None, None, "stn"),
            P(None, None, "stn"),
            P("band", None),
        ),
        out_specs=(
            P(None, None, ("band", "chan"), "stn"),
            P("band", None, None, "stn"),
            P(None, None, ("band", "chan"), "stn"),
        ),
        check_vma=False,
    )
```

time: 110 us -> 88.6 us (0.81)
  waiting for transfers between devices: 35.8 us -> 20.7 us
  starting transfers between devices: 34 us -> 26.1 us
  Pallas kernels: 29.5 us -> 34.9 us
  local copies, waits for them, and re-layouts: 7.3 us -> 5.35 us
  other arithmetic: 1.6 us -> 0.06 us
    ppermute x23 -> x7, starting transfers between devices: 22.8 us -> 8.05 us  [swap(): return lax.ppermute(value, 'chan', [(i, i ^ offset) for i in range(count)])]
    all_to_all x0 -> x2, starting transfers between devices: none -> 12.1 us  [shards(): sums = lax.all_to_all(sums, 'chan', 0, 0, tiled=True)]
    ppermute x5 -> x7, waiting for transfers between devices: 12.4 us -> 0.43 us  [other_stations(): return lax.ppermute(value, 'stn', [(0, 1), (1, 0)])]
    ppermute x23 -> x7, waiting for transfers between devices: 23.4 us -> 17 us  [swap(): return lax.ppermute(value, 'chan', [(i, i ^ offset) for i in range(count)])]
    pallas_call x8 -> x13, Pallas kernels: 29.5 us -> 34.9 us  [the longest x3 13.8 us: data_part(): pl.pallas_call(body, name='data_part', out_shape=tuple(shapes), in_specs=...]
    ppermute x5 -> x7, starting transfers between devices: 11.3 us -> 5.95 us  [other_stations(): return lax.ppermute(value, 'stn', [(0, 1), (1, 0)])]
    all_to_all x0 -> x2, waiting for transfers between devices: none -> 3.25 us  [shards(): sums = lax.all_to_all(sums, 'chan', 0, 0, tiled=True)]
    unnamed x26 -> x18, local copies, waits for them, and re-layouts: 7.3 us -> 5.34 us
  transfers between devices with their start and end apart: 28 -> 16, of which waited for: 15 -> 10; matrix products, arithmetic and copies ran while one was open for 0% -> 0% of each run, Pallas kernels for 6% -> 26%
where the time goes in v2:
time: 88.6 us; the launch traced here: 88 us
  Pallas kernels  34.9 us (39%)
  starting transfers between devices  26.1 us (29%)
  waiting for transfers between devices  20.7 us (23%)
  local copies, waits for them, and re-layouts  5.35 us (6%)
    ppermute x7, waiting for transfers between devices, swap(): return lax.ppermute(value, 'chan', [(i, i ^ offset) for i in range(count)])  17 us
    pallas_call x3, Pallas kernels, data_part(): pl.pallas_call(body, name='data_part', out_shape=tuple(shapes), in_specs=...  13.8 us
    pallas_call x3, Pallas kernels, gradient_part(): pl.pallas_call(functools.partial(gradient_kernel, block, pairs, dumps, pe...  12.3 us
    all_to_all x2, starting transfers between devices, shards(): sums = lax.all_to_all(sums, 'chan', 0, 0, tiled=True)  12.1 us
    ppermute x7, starting transfers between devices, swap(): return lax.ppermute(value, 'chan', [(i, i ^ offset) for i in range(count)])  8.05 us
    pallas_call x3, Pallas kernels, curvature_part(): pl.pallas_call(functools.partial(curvature_kernel, block, pairs, dumps, p...  6.35 us
    ppermute x7, starting transfers between devices, other_stations(): return lax.ppermute(value, 'stn', [(0, 1), (1, 0)])  5.95 us
    unnamed x18, local copies, waits for them, and re-layouts  5.34 us
  transfers between devices with their start and end apart: 16, of which 10 were waited for; matrix products, arithmetic and copies ran while one was open for 0% of the time, Pallas kernels for 26%

profile of v2, /device:TPU:0, one launch (start us, length us, event | category | flops | bytes accessed | tf_op | source)
XLA Modules:
  0.0 88.0 jit_solution(5264785559972269817)
XLA Ops:
  0.6 3.0 %collective-permute-start = (f32[64,1,256]{2,1,0:T(1,128)}, f32[64,1,256]{2,1,0:T(1,128)S(1)}, u32[]{:S(2)}, u32[]{:S(2)}) collective-permute-start(f32[64,1,256]{2,1,0:T(1,128)} %bitcast.20), channel_id=1, source_target_pairs={{0,1},{1,0},{2,3},{3,2},{4,5},{5,4},{6,7},{7,6},{8,9},{9,8},{10,11... | collective-permute-start | bytes 196616 | tf_op jit(solution)/shard_map/ppermute | solution.py:753
  3.6 0.1 collective-permute-start.1
  3.7 1.9 %collective-permute-start.3 = (s32[1,4]{1,0:T(1,128)}, s32[1,4]{1,0:T(1,128)S(1)}, u32[]{:S(2)}, u32[]{:S(2)}) collective-permute-start(s32[1,4]{1,0:T(1,128)} %bitcast.25), channel_id=1, source_target_pairs={{0,1},{1,0},{2,3},{3,2},{4,5},{5,4},{6,7},{7,6},{8,9},{9,8},{10,11... | collective-permute-start | bytes 56 | tf_op jit(solution)/shard_map/ppermute | solution.py:753
  5.7 0.1 collective-permute-start.2
  5.7 0.9 %copy-done = f32[8,8,4,256]{3,2,1,0:T(4,128)S(1)} copy-done((f32[8,8,4,256]{3,2,1,0:T(4,128)S(1)}, f32[8,8,4,256]{3,2,1,0:T(4,128)}, u32[]{:S(2)}) %copy-start) | copy-done | bytes 262168
  6.7 0.8 copy-done.1
  7.5 0.8 copy-done.2
  8.4 0.7 copy-done.3
  9.1 0.7 copy-done.4
  9.7 0.7 copy-done.6
  10.4 0.8 prepare.1
  11.2 0.0 copy-start.8
  11.2 0.7 copy-done.8
  11.9 4.6 %data_part.3 = (f32[64,512]{1,0:T(8,128)S(1)}, f32[64,512]{1,0:T(8,128)S(1)}, f32[16,512]{1,0:T(8,128)S(1)}, f32[8,128]{1,0:T(8,128)S(1)}) custom-call(s32[4]{0:T(128)S(1)} %copy-done.4, s32[4]{0:T(128)S(1)} %copy-done.6, bf16[4,2,8,256,256]{4,3,2,1,0:T(8,128)(2,1)} %bitcast.28, f32[64,128]{1,0:T(8,128)S(1)} %get-tuple-element.33.refs_3_.refs_2_, ...), custom_call_target="tpu_custom_call" | custom-call | flops 6000000000 | bytes 8000000 | tf_op jit(solution)/shard_map/data_part/pallas_call | solution.py:381
  16.5 0.7 collective-permute-start.4
  17.2 4.0 %gradient_part.3.refs_4_ = f32[64,512]{1,0:T(8,128)S(1)} custom-call(f32[8,128]{1,0:T(8,128)S(1)} %get-tuple-element.37.refs_0_, f32[16,512]{1,0:T(8,128)S(1)} %get-tuple-element.38.refs_1_.refs_5_, f32[64,128]{1,0:T(8,128)S(1)} %get-tuple-element.33.refs_3_.refs_2_, f32[64,512]{1,0:T(8,128)S(1)} %get-tuple-element.39.refs_3_), custom_call_target="tpu_custom_call" | custom-call | flops 4000000000 | bytes 2000000 | tf_op jit(solution)/shard_map/gradient_part/pallas_call | solution.py:559
  21.2 0.3 collective-permute-done.4.refs_6_
  21.6 2.3 %curvature_part.3 = (f32[64,512]{1,0:T(8,128)S(1)}, f32[64,512]{1,0:T(8,128)S(1)}, f32[16,128]{1,0:T(8,128)}) custom-call(f32[8,128]{1,0:T(8,128)S(1)} %get-tuple-element.37.refs_0_, f32[16,512]{1,0:T(8,128)S(1)} %get-tuple-element.38.refs_1_.refs_5_, f32[64,128]{1,0:T(8,128)S(1)} %get-tuple-element.33.refs_3_.refs_2_, ...), custom_call_target="tpu_custom_call" | custom-call | flops 2000000000 | bytes 2000000 | tf_op jit(solution)/shard_map/curvature_part/pallas_call | solution.py:662
  23.9 6.4 %all-to-all-start = ((f32[16,1,128]{2,1,0:T(1,128)}), f32[16,1,128]{2,1,0:T(1,128)S(1)}, u32[]{:S(2)}, u32[]{:S(2)}) async-start(f32[16,1,128]{2,1,0:T(1,128)} %bitcast.8), calls=%async_computation | async-start | bytes 16384 | tf_op jit(solution)/shard_map/all_to_all | solution.py:818
  30.3 4.6 %data_part.4.refs_5_ = f32[64,512]{1,0:T(8,128)S(1)} custom-call(s32[4]{0:T(128)S(1)} %copy-done.5, s32[4]{0:T(128)S(1)} %copy-done.7, bf16[4,2,8,256,256]{4,3,2,1,0:T(8,128)(2,1)} %bitcast.29, f32[64,128]{1,0:T(8,128)S(1)} %get-tuple-element.33.refs_3_.refs_2_, f32[64,512]{1,0:T(8,128)S(1)} %get-tuple-element.42.refs_5_.refs_4_, ...), custom_call_target="tpu_custom_call" | custom-call | flops 6000000000 | bytes 8000000 | tf_op jit(solution)/shard_map/data_part/pallas_call | solution.py:381
  34.9 0.1 collective-permute-start.5
  35.0 1.6 %all-to-all-done = f32[16,1,128]{2,1,0:T(1,128)S(1)} async-done(((f32[16,1,128]{2,1,0:T(1,128)}), f32[16,1,128]{2,1,0:T(1,128)S(1)}, u32[]{:S(2)}, u32[]{:S(2)}) %all-to-all-start) | async-done | bytes 8224 | tf_op jit(solution)/shard_map/all_to_all | solution.py:818
  36.6 4.1 %gradient_part.4 = (f32[64,512]{1,0:T(8,128)S(1)}, f32[64,512]{1,0:T(8,128)S(1)}, f32[8,128]{1,0:T(8,128)S(1)}) custom-call(f32[8,128]{1,0:T(8,128)S(1)} %get-tuple-element.37.refs_0_, f32[16,512]{1,0:T(8,128)S(1)} %get-tuple-element.38.refs_1_.refs_5_, f32[64,128]{1,0:T(8,128)S(1)} %get-tuple-element.33.refs_3_.refs_2_, ...), custom_call_target="tpu_custom_call" | custom-call | flops 4000000000 | bytes 2000000 | tf_op jit(solution)/shard_map/gradient_part/pallas_call | solution.py:559
  40.8 0.1 collective-permute-done.5.refs_6_
  40.8 2.3 %curvature_part.4 = (f32[64,512]{1,0:T(8,128)S(1)}, f32[64,512]{1,0:T(8,128)S(1)}, f32[16,128]{1,0:T(8,128)}) custom-call(f32[8,128]{1,0:T(8,128)S(1)} %get-tuple-element.37.refs_0_, f32[16,512]{1,0:T(8,128)S(1)} %get-tuple-element.38.refs_1_.refs_5_, f32[64,128]{1,0:T(8,128)S(1)} %get-tuple-element.33.refs_3_.refs_2_, ...), custom_call_target="tpu_custom_call" | custom-call | flops 2000000000 | bytes 2000000 | tf_op jit(solution)/shard_map/curvature_part/pallas_call | solution.py:662
  43.1 5.7 %all-to-all-start.1 = ((f32[16,1,128]{2,1,0:T(1,128)}), f32[16,1,128]{2,1,0:T(1,128)S(1)}, u32[]{:S(2)}, u32[]{:S(2)}) async-start(f32[16,1,128]{2,1,0:T(1,128)} %bitcast.11), calls=%async_computation.1 | async-start | bytes 16384 | tf_op jit(solution)/shard_map/all_to_all | solution.py:818
  48.9 4.6 %data_part.5.refs_5_ = f32[64,512]{1,0:T(8,128)S(1)} custom-call(s32[4]{0:T(128)S(1)} %copy-done.5, s32[4]{0:T(128)S(1)} %copy-done.7, bf16[4,2,8,256,256]{4,3,2,1,0:T(8,128)(2,1)} %bitcast.30, f32[64,128]{1,0:T(8,128)S(1)} %get-tuple-element.33.refs_3_.refs_2_, f32[64,512]{1,0:T(8,128)S(1)} %get-tuple-element.48.refs_5_.refs_4_, ...), custom_call_target="tpu_custom_call" | custom-call | flops 6000000000 | bytes 8000000 | tf_op jit(solution)/shard_map/data_part/pallas_call | solution.py:381
  53.5 0.1 collective-permute-start.6
  53.6 1.6 %all-to-all-done.1 = f32[16,1,128]{2,1,0:T(1,128)S(1)} async-done(((f32[16,1,128]{2,1,0:T(1,128)}), f32[16,1,128]{2,1,0:T(1,128)S(1)}, u32[]{:S(2)}, u32[]{:S(2)}) %all-to-all-start.1) | async-done | bytes 8224 | tf_op jit(solution)/shard_map/all_to_all | solution.py:818
  55.2 4.1 %gradient_part.5 = (f32[64,512]{1,0:T(8,128)S(1)}, f32[64,512]{1,0:T(8,128)S(1)}, f32[8,128]{1,0:T(8,128)S(1)}) custom-call(f32[8,128]{1,0:T(8,128)S(1)} %get-tuple-element.37.refs_0_, f32[16,512]{1,0:T(8,128)S(1)} %get-tuple-element.38.refs_1_.refs_5_, f32[64,128]{1,0:T(8,128)S(1)} %get-tuple-element.33.refs_3_.refs_2_, ...), custom_call_target="tpu_custom_call" | custom-call | flops 4000000000 | bytes 2000000 | tf_op jit(solution)/shard_map/gradient_part/pallas_call | solution.py:559
  59.3 0.0 collective-permute-done.6.refs_6_
  59.4 1.7 %curvature_part.5 = (f32[64,512]{1,0:T(8,128)S(1)}, f32[528,128]{1,0:T(8,128)S(1)}, f32[528,128]{1,0:T(8,128)S(1)}) custom-call(f32[8,128]{1,0:T(8,128)S(1)} %get-tuple-element.37.refs_0_, f32[16,512]{1,0:T(8,128)S(1)} %get-tuple-element.38.refs_1_.refs_5_, f32[64,128]{1,0:T(8,128)S(1)} %get-tuple-element.33.refs_3_.refs_2_, ...), custom_call_target="tpu_custom_call" | custom-call | flops 2000000000 | bytes 2000000 | tf_op jit(solution)/shard_map/curvature_part/pallas_call | solution.py:662
  61.1 0.1 collective-permute-start.7
  61.2 1.5 %collective-permute-done.7 = f32[528,128]{1,0:T(8,128)S(1)} collective-permute-done((f32[528,128]{1,0:T(8,128)S(1)}, f32[528,128]{1,0:T(8,128)S(1)}, u32[]{:S(2)}, u32[]{:S(2)}) %collective-permute-start.7) | collective-permute-done | bytes 270368 | tf_op jit(solution)/shard_map/ppermute | solution.py:749
  62.8 1.7 %collective-permute-start.8 = (f32[264,128]{1,0:T(8,128)S(1)}, f32[264,128]{1,0:T(8,128)S(1)}, u32[]{:S(2)}, u32[]{:S(2)}) collective-permute-start(f32[264,128]{1,0:T(8,128)S(1)} %slice.9), channel_id=1, source_target_pairs={{0,4},{2,6},{4,0},{6,2},{8,12},{10,14},{12,8},{14,10},{16,20},{18,... | collective-permute-start | bytes 405512 | tf_op jit(solution)/shard_map/ppermute | solution.py:749
  64.5 4.0 %collective-permute-done.8 = f32[264,128]{1,0:T(8,128)S(1)} collective-permute-done((f32[264,128]{1,0:T(8,128)S(1)}, f32[264,128]{1,0:T(8,128)S(1)}, u32[]{:S(2)}, u32[]{:S(2)}) %collective-permute-start.8) | collective-permute-done | bytes 135200 | tf_op jit(solution)/shard_map/ppermute | solution.py:749
  68.5 1.7 %collective-permute-start.9 = (f32[264,128]{1,0:T(8,128)S(1)}, f32[264,128]{1,0:T(8,128)S(1)}, u32[]{:S(2)}, u32[]{:S(2)}) collective-permute-start(f32[264,128]{1,0:T(8,128)S(1)} %slice_add_fusion), channel_id=1, source_target_pairs={{0,8},{2,10},{4,12},{6,14},{8,0},{10,2},{12,4},{14,6},{16,24},{18,... | collective-permute-start | bytes 405512 | tf_op jit(solution)/shard_map/ppermute | solution.py:749
  70.2 3.4 %collective-permute-done.9 = f32[264,128]{1,0:T(8,128)S(1)} collective-permute-done((f32[264,128]{1,0:T(8,128)S(1)}, f32[264,128]{1,0:T(8,128)S(1)}, u32[]{:S(2)}, u32[]{:S(2)}) %collective-permute-start.9) | collective-permute-done | bytes 135200 | tf_op jit(solution)/shard_map/ppermute | solution.py:749
  73.6 2.6 %collective-permute-start.10 = (f32[264,128]{1,0:T(8,128)S(1)}, f32[264,128]{1,0:T(8,128)S(1)}, u32[]{:S(2)}, u32[]{:S(2)}) collective-permute-start(f32[264,128]{1,0:T(8,128)S(1)} %add.11.one), channel_id=1, source_target_pairs={{0,16},{2,18},{4,20},{6,22},{8,24},{10,26},{12,28},{14,30},{16,0},... | collective-permute-start | bytes 405512 | tf_op jit(solution)/shard_map/ppermute | solution.py:749
  76.2 4.9 %collective-permute-done.10.two = f32[264,128]{1,0:T(8,128)S(1)} collective-permute-done((f32[264,128]{1,0:T(8,128)S(1)}, f32[264,128]{1,0:T(8,128)S(1)}, u32[]{:S(2)}, u32[]{:S(2)}) %collective-permute-start.10) | collective-permute-done | bytes 135200 | tf_op jit(solution)/shard_map/ppermute | solution.py:749
  81.1 0.2 combine.1
  81.3 0.1 collective-permute-start.13
  81.4 1.7 %collective-permute-start.12 = (f32[128,128]{1,0:T(8,128)S(1)}, f32[128,128]{1,0:T(8,128)S(1)}, u32[]{:S(2)}, u32[]{:S(2)}) collective-permute-start(f32[128,128]{1,0:T(8,128)S(1)} %get-tuple-element.59.own), channel_id=1, source_target_pairs={{0,4},{2,6},{4,0},{6,2},{8,12},{10,14},{12,8},{14,10},{16,20},{18,... | collective-permute-start | bytes 196616 | tf_op jit(solution)/shard_map/ppermute | solution.py:749
  83.1 0.1 collective-permute-start.11
  83.2 0.7 last_step.1
  83.9 1.6 %collective-permute-done.13.both = f32[128,128]{1,0:T(8,128)S(1)} collective-permute-done((f32[128,128]{1,0:T(8,128)S(1)}, f32[128,128]{1,0:T(8,128)S(1)}, u32[]{:S(2)}, u32[]{:S(2)}) %collective-permute-start.13) | collective-permute-done | bytes 65568 | tf_op jit(solution)/shard_map/ppermute | solution.py:749
  85.5 1.6 %collective-permute-done.12.row = f32[128,128]{1,0:T(8,128)S(1)} collective-permute-done((f32[128,128]{1,0:T(8,128)S(1)}, f32[128,128]{1,0:T(8,128)S(1)}, u32[]{:S(2)}, u32[]{:S(2)}) %collective-permute-start.12) | collective-permute-done | bytes 65568 | tf_op jit(solution)/shard_map/ppermute | solution.py:749
  87.2 0.8 consensus.1
  (19 shorter events, 0.1 us)
Async XLA Ops:
  0.6 10.5 %collective-permute-start = (f32[64,1,256]{2,1,0:T(1,128)}, f32[64,1,256]{2,1,0:T(1,128)S(1)}, u32[]{:S(2)}, u32[]{:S(2)}) collective-permute-start(f32[64,1,256]{2,1,0:T(1,128)} %bitcast.20), channel_id=1, source_target_pairs={{0,1},{1,0},{2,3},{3,2},{4,5},{5,4},{6,7},{7,6},{8,9},{9,8},{10,11... | collective-permute-start | bytes 196616 | tf_op jit(solution)/shard_map/ppermute | solution.py:753
  3.6 7.5 %collective-permute-start.1 = (f32[16,256]{1,0:T(8,128)}, f32[16,256]{1,0:T(8,128)S(1)}, u32[]{:S(2)}, u32[]{:S(2)}) collective-permute-start(f32[16,256]{1,0:T(8,128)} %bitcast.26), channel_id=1, source_target_pairs={{0,1},{1,0},{2,3},{3,2},{4,5},{5,4},{6,7},{7,6},{8,9},{9,8},{10,11... | collective-permute-start | bytes 49160 | tf_op jit(solution)/shard_map/ppermute | solution.py:753
  3.7 7.4 %collective-permute-start.3 = (s32[1,4]{1,0:T(1,128)}, s32[1,4]{1,0:T(1,128)S(1)}, u32[]{:S(2)}, u32[]{:S(2)}) collective-permute-start(s32[1,4]{1,0:T(1,128)} %bitcast.25), channel_id=1, source_target_pairs={{0,1},{1,0},{2,3},{3,2},{4,5},{5,4},{6,7},{7,6},{8,9},{9,8},{10,11... | collective-permute-start | bytes 56 | tf_op jit(solution)/shard_map/ppermute | solution.py:753
  5.7 5.5 %collective-permute-start.2 = (s32[1,4]{1,0:T(1,128)}, s32[1,4]{1,0:T(1,128)S(1)}, u32[]{:S(2)}, u32[]{:S(2)}) collective-permute-start(s32[1,4]{1,0:T(1,128)} %bitcast.24), channel_id=1, source_target_pairs={{0,1},{1,0},{2,3},{3,2},{4,5},{5,4},{6,7},{7,6},{8,9},{9,8},{10,11... | collective-permute-start | bytes 56 | tf_op jit(solution)/shard_map/ppermute | solution.py:753
  5.7 0.9 %copy-start = (f32[8,8,4,256]{3,2,1,0:T(4,128)S(1)}, f32[8,8,4,256]{3,2,1,0:T(4,128)}, u32[]{:S(2)}) copy-start(f32[8,8,4,256]{3,2,1,0:T(4,128)} %param.13) | copy-start | bytes 786436
  6.7 0.8 copy-start.1
  7.5 0.8 copy-start.2
  8.4 0.7 copy-start.3
  9.1 0.7 copy-start.4
  9.7 0.7 copy-start.6
  11.2 0.7 copy-start.8
  16.5 5.0 %collective-permute-start.4 = (f32[64,512]{1,0:T(8,128)S(1)}, f32[64,512]{1,0:T(8,128)S(1)}, u32[]{:S(2)}, u32[]{:S(2)}) collective-permute-start(f32[64,512]{1,0:T(8,128)S(1)} %get-tuple-element.40.refs_5_), channel_id=1, source_target_pairs={{0,1},{1,0},{2,3},{3,2},{4,5},{5,4},{6,7},{7,6},{8,9},{9,8},{10,11... | collective-permute-start | bytes 393224 | tf_op jit(solution)/shard_map/ppermute | solution.py:753
  17.2 13.1 %copy-start.5 = (s32[4]{0:T(128)S(1)}, s32[4]{0:T(128)}, u32[]{:S(2)}) copy-start(s32[4]{0:T(128)} %refs_0_.7) | copy-start | bytes 52
  17.2 13.1 %copy-start.7 = (s32[4]{0:T(128)S(1)}, s32[4]{0:T(128)}, u32[]{:S(2)}) copy-start(s32[4]{0:T(128)} %refs_1_.7) | copy-start | bytes 52
  23.9 12.7 %all-to-all-start = ((f32[16,1,128]{2,1,0:T(1,128)}), f32[16,1,128]{2,1,0:T(1,128)S(1)}, u32[]{:S(2)}, u32[]{:S(2)}) async-start(f32[16,1,128]{2,1,0:T(1,128)} %bitcast.8), calls=%async_computation | async-start | bytes 16384 | tf_op jit(solution)/shard_map/all_to_all | solution.py:818
  34.9 5.9 %collective-permute-start.5 = (f32[64,512]{1,0:T(8,128)S(1)}, f32[64,512]{1,0:T(8,128)S(1)}, u32[]{:S(2)}, u32[]{:S(2)}) collective-permute-start(f32[64,512]{1,0:T(8,128)S(1)} %data_part.4.refs_5_), channel_id=1, source_target_pairs={{0,1},{1,0},{2,3},{3,2},{4,5},{5,4},{6,7},{7,6},{8,9},{9,8},{10,11... | collective-permute-start | bytes 393224 | tf_op jit(solution)/shard_map/ppermute | solution.py:753
  43.1 12.1 %all-to-all-start.1 = ((f32[16,1,128]{2,1,0:T(1,128)}), f32[16,1,128]{2,1,0:T(1,128)S(1)}, u32[]{:S(2)}, u32[]{:S(2)}) async-start(f32[16,1,128]{2,1,0:T(1,128)} %bitcast.11), calls=%async_computation.1 | async-start | bytes 16384 | tf_op jit(solution)/shard_map/all_to_all | solution.py:818
  53.5 5.9 %collective-permute-start.6 = (f32[64,512]{1,0:T(8,128)S(1)}, f32[64,512]{1,0:T(8,128)S(1)}, u32[]{:S(2)}, u32[]{:S(2)}) collective-permute-start(f32[64,512]{1,0:T(8,128)S(1)} %data_part.5.refs_5_), channel_id=1, source_target_pairs={{0,1},{1,0},{2,3},{3,2},{4,5},{5,4},{6,7},{7,6},{8,9},{9,8},{10,11... | collective-permute-start | bytes 393224 | tf_op jit(solution)/shard_map/ppermute | solution.py:753
  61.1 1.6 %collective-permute-start.7 = (f32[528,128]{1,0:T(8,128)S(1)}, f32[528,128]{1,0:T(8,128)S(1)}, u32[]{:S(2)}, u32[]{:S(2)}) collective-permute-start(f32[528,128]{1,0:T(8,128)S(1)} %get-tuple-element.55), channel_id=1, source_target_pairs={{0,2},{2,0},{4,6},{6,4},{8,10},{10,8},{12,14},{14,12},{16,18},{18,... | collective-permute-start | bytes 811016 | tf_op jit(solution)/shard_map/ppermute | solution.py:749
  62.8 5.7 %collective-permute-start.8 = (f32[264,128]{1,0:T(8,128)S(1)}, f32[264,128]{1,0:T(8,128)S(1)}, u32[]{:S(2)}, u32[]{:S(2)}) collective-permute-start(f32[264,128]{1,0:T(8,128)S(1)} %slice.9), channel_id=1, source_target_pairs={{0,4},{2,6},{4,0},{6,2},{8,12},{10,14},{12,8},{14,10},{16,20},{18,... | collective-permute-start | bytes 405512 | tf_op jit(solution)/shard_map/ppermute | solution.py:749
  68.5 5.1 %collective-permute-start.9 = (f32[264,128]{1,0:T(8,128)S(1)}, f32[264,128]{1,0:T(8,128)S(1)}, u32[]{:S(2)}, u32[]{:S(2)}) collective-permute-start(f32[264,128]{1,0:T(8,128)S(1)} %slice_add_fusion), channel_id=1, source_target_pairs={{0,8},{2,10},{4,12},{6,14},{8,0},{10,2},{12,4},{14,6},{16,24},{18,... | collective-permute-start | bytes 405512 | tf_op jit(solution)/shard_map/ppermute | solution.py:749
  73.6 7.5 %collective-permute-start.10 = (f32[264,128]{1,0:T(8,128)S(1)}, f32[264,128]{1,0:T(8,128)S(1)}, u32[]{:S(2)}, u32[]{:S(2)}) collective-permute-start(f32[264,128]{1,0:T(8,128)S(1)} %add.11.one), channel_id=1, source_target_pairs={{0,16},{2,18},{4,20},{6,22},{8,24},{10,26},{12,28},{14,30},{16,0},... | collective-permute-start | bytes 405512 | tf_op jit(solution)/shard_map/ppermute | solution.py:749
  81.3 4.2 %collective-permute-start.13 = (f32[128,128]{1,0:T(8,128)S(1)}, f32[128,128]{1,0:T(8,128)S(1)}, u32[]{:S(2)}, u32[]{:S(2)}) collective-permute-start(f32[128,128]{1,0:T(8,128)S(1)} %get-tuple-element.59.own), channel_id=1, source_target_pairs={{0,6},{2,4},{4,2},{6,0},{8,14},{10,12},{12,10},{14,8},{16,22},{18,... | collective-permute-start | bytes 196616 | tf_op jit(solution)/shard_map/ppermute | solution.py:749
  81.4 5.8 %collective-permute-start.12 = (f32[128,128]{1,0:T(8,128)S(1)}, f32[128,128]{1,0:T(8,128)S(1)}, u32[]{:S(2)}, u32[]{:S(2)}) collective-permute-start(f32[128,128]{1,0:T(8,128)S(1)} %get-tuple-element.59.own), channel_id=1, source_target_pairs={{0,4},{2,6},{4,0},{6,2},{8,12},{10,14},{12,8},{14,10},{16,20},{18,... | collective-permute-start | bytes 196616 | tf_op jit(solution)/shard_map/ppermute | solution.py:749
  83.1 4.1 %collective-permute-start.11 = (f32[128,128]{1,0:T(8,128)S(1)}, f32[128,128]{1,0:T(8,128)S(1)}, u32[]{:S(2)}, u32[]{:S(2)}) collective-permute-start(f32[128,128]{1,0:T(8,128)S(1)} %get-tuple-element.59.own), channel_id=1, source_target_pairs={{0,2},{2,0},{4,6},{6,4},{8,10},{10,8},{12,14},{14,12},{16,18},{18,... | collective-permute-start | bytes 196616 | tf_op jit(solution)/shard_map/ppermute | solution.py:749

commit v3 on v2

--- a/solution.py
+++ b/solution.py
@@ -163,24 +163,27 @@
     return jnp.concatenate(tiles, axis=0)
 
 
-def position_of(chan_count):
-    return lax.axis_index("chan").astype(F32) * (1.0 / chan_count)
+def position_of(chan_count, offset=0):
+    place = lax.axis_index("chan")
+    if offset:
+        place = place ^ offset
+    return place.astype(F32) * (1.0 / chan_count)
 
 
 def frequency_of(chan_count):
     return 1.0 + position_of(chan_count)
 
 
-def basis_of(chan_count):
-    x = position_of(chan_count) + 0.5 / chan_count
+def basis_of(chan_count, offset=0):
+    x = position_of(chan_count, offset) + 0.5 / chan_count
     y = 1.0 - x
     return [y * y * y, 3.0 * x * y * y, 3.0 * x * x * y, x * x * x]
 
 
-def solve_of(chan_count):
+def solve_of(chan_count, offset):
     basis = bernstein_np(chan_count)
     inverse = np.linalg.inv(basis.T @ basis)
-    row = basis_of(chan_count)
+    row = basis_of(chan_count, offset)
     return [sum(row[m] * float(inverse[m, k]) for m in range(4)) for k in range(4)]
 
 
@@ -213,8 +216,8 @@
 
 
 def prepare_kernel(block, pairs, slots, penalty, chan_count, *refs):
-    table, flags, gains, duals, prior, bright, *refs = refs
-    gains_out, duals_out, start_out, coh_out, counts_out = refs
+    table, flags, duals, prior, bright, *refs = refs
+    duals_out, start_out, coh_out, counts_out = refs
     lane = lax.broadcasted_iota(jnp.int32, (8, 128), 1)
     counts = jnp.zeros((8, 128), F32)
     for slot in range(slots):
@@ -222,7 +225,6 @@
         counts = counts + jnp.where(held_here, flags[slot].astype(F32), 0.0)
     counts_out[...] = counts
     coh_out[...] = coherency_tile(bright[...], frequency_of(chan_count))
-    gains_out[...] = gains[:, 0, :]
     duals_own = duals[:, 0, :]
     duals_out[...] = duals_own
     target = -duals_own
@@ -231,7 +233,7 @@
     start_out[...] = -penalty * target
 
 
-def prepare(geometry, table, flags, gains, duals, prior, brightness):
+def prepare(geometry, table, flags, duals, prior, brightness):
     block, pairs, dumps, penalty, chan_count, stations = geometry
     return pl.pallas_call(
         functools.partial(
@@ -241,28 +243,27 @@
         out_shape=(
             shape(64, block),
             shape(64, block),
-            shape(64, block),
             shape(64, 128),
             shape(8, 128),
         ),
-        in_specs=smem_specs(2) + vmem_specs(4),
-        out_specs=tuple(vmem_specs(5)),
+        in_specs=smem_specs(2) + vmem_specs(3),
+        out_specs=tuple(vmem_specs(4)),
         compiler_params=params(),
         cost_estimate=pl.CostEstimate(flops=1000000, bytes_accessed=2000000, transcendentals=0),
-    )(table, flags, gains, duals, prior, brightness)
+    )(table, flags, duals, prior, brightness)
 
 
 def data_kernel(block, pairs, dumps, slots, penalty, chan_count, first_call, joined, *refs):
     table, flags, observed, coh_ref, *refs = refs
     if first_call:
         if joined:
-            gains_all, delays_all, *refs = refs
+            rows_all, *refs = refs
         else:
-            gains_mine, gains_other, delays_mine, delays_other, *refs = refs
-        start, counts_mine, ids_other, flags_other, out_ref, field_ref, delay_ref, counts_ref, *refs = refs
+            rows_mine, rows_other, *refs = refs
+        start, counts_mine, ints_other, out_ref, field_ref, delay_ref, counts_ref, *refs = refs
     else:
         field_ref, delay_ref, out_ref, *refs = refs
-    held, sems, order, xp, yp, hl, ha = refs
+    held, sems, order, keep, xp, yp, hl, ha = refs
     stations = field_ref.shape[1]
     pair_count = len(pairs)
     at_own = own_lanes(block)
@@ -286,14 +287,13 @@
     freq_value = frequency_of(chan_count)
     if first_call:
         if joined:
-            field_ref[...] = gains_all[:, 0, :]
-            delay_ref[...] = delays_all[...]
+            field_ref[...] = rows_all[:64, 0, :]
+            delay_ref[...] = rows_all[64:, 0, :]
         else:
             at_other = pl.ds(pl.multiple_of((1 - lax.axis_index("stn")) * block, CHUNK), block)
-            field_ref[:, at_own] = gains_mine[...]
-            field_ref[:, at_other] = gains_other[:, 0, :]
-            delay_ref[:, at_own] = delays_mine[...]
-            delay_ref[:, at_other] = delays_other[...]
+            for at, rows in ((at_own, rows_mine), (at_other, rows_other)):
+                field_ref[:, at] = rows[:64, 0, :]
+                delay_ref[:, at] = rows[64:, 0, :]
     bright = coherency_rows(coh_ref[...], stations)
     for t in range(dumps):
         cosine, sine = trig(delay_ref[8 * t : 8 * t + 8, :], freq_value)
@@ -307,13 +307,14 @@
 
     row = lax.broadcasted_iota(jnp.int32, (block, block), 0)
     col = lax.broadcasted_iota(jnp.int32, (block, block), 1)
-    upper = row < col
+    keep[0] = (row < col).astype(F32).astype(BF16)
+    keep[1] = jnp.ones((block, block), BF16)
     lane = lax.broadcasted_iota(jnp.int32, (1, block), 1)
 
     def visit(item, unused):
         slot, t = order[item // dumps], item % dumps
         first, second = pair_blocks(pairs, table[slot])
-        keep = upper | (first < second)
+        kept = keep[jnp.where(first < second, 1, 0)]
         live = (lane >= flags[slot]).astype(F32)
         live16 = live.astype(BF16)
         at_p = pl.ds(pl.multiple_of(first * block, CHUNK), block)
@@ -332,7 +333,7 @@
             for i in range(2):
                 for j in range(2):
                     tile = held[item, 4 * r + 2 * i + j]
-                    tile = jnp.where(keep, tile, jnp.zeros_like(tile))
+                    tile = tile * kept
                     rj = 2 * r + j
                     left = dot(ys[rj], tile, NT)
                     right = dot(xs[i], tile, NN)
@@ -360,7 +361,7 @@
         counts = counts_mine[...]
         pair_lane = lax.broadcasted_iota(jnp.int32, (8, 128), 1)
         for k in range(pair_count):
-            theirs = jnp.where(ids_other[...] == k, flags_other[...], 0).astype(F32)
+            theirs = jnp.where(ints_other[0:1, :] == k, ints_other[1:2, :], 0).astype(F32)
             total_flags = jnp.sum(theirs, axis=1, keepdims=True)
             counts = counts + jnp.where(pair_lane == k, total_flags, 0.0)
         counts_ref[...] = counts
@@ -371,7 +372,7 @@
     block, pairs, dumps, penalty, chan_count, stations = geometry
     slots = observed.shape[0]
     first_call = len(fields) > 2
-    joined = len(fields) == 6
+    joined = len(fields) == 4
     body = functools.partial(
         data_kernel, block, pairs, dumps, slots, penalty, chan_count, first_call, joined
     )
@@ -388,6 +389,7 @@
             pltpu.VMEM((slots * dumps,) + observed.shape[2:], BF16),
             pltpu.SemaphoreType.DMA((slots * dumps,)),
             pltpu.SMEM((slots,), jnp.int32),
+            pltpu.VMEM((2, block, block), BF16),
             pltpu.VMEM((dumps, 2, 64, stations), BF16),
             pltpu.VMEM((dumps, 4, 64, stations), BF16),
             pltpu.VMEM((dumps, 2, 32, stations), F32),
@@ -460,24 +462,22 @@
     return total
 
 
-def halves(rows, axis, bit):
+def halves(rows, axis, odd):
     size = rows.shape[axis] // 2
     low = lax.slice_in_dim(rows, 0, size, axis=axis)
     high = lax.slice_in_dim(rows, size, 2 * size, axis=axis)
-    odd = (lax.axis_index("chan") // bit) % 2 == 1
     return jnp.where(odd, high, low), jnp.where(odd, low, high)
 
 
-def store_moments(fields, sums, chan_count, keep_out, send_out):
-    for field_id, field in enumerate(fields):
-        for out, part in zip((keep_out, send_out), halves(field, 1, 1)):
-            for start, rows in zip((0, 264), halves(part, 0, 2)):
-                for k, scale in enumerate(solve_of(chan_count)):
-                    at = start + 128 * field_id + 32 * k
-                    out[at : at + 32, :] = scale * rows
-    for out in (keep_out, send_out):
-        out[256:264, :] = sums
-        out[520:528, :] = sums
+def store_quarters(fields, sums, outs):
+    place = lax.axis_index("chan")
+    odd_lanes, odd_rows = place % 2 == 1, (place // 2) % 2 == 1
+    for n, field in enumerate(fields):
+        for o, part in enumerate(halves(field, 1, odd_lanes)):
+            for p, quarter in enumerate(halves(part, 0, odd_rows)):
+                outs[o + 2 * p][32 * n : 32 * n + 32, :] = quarter
+    for out in outs:
+        out[32 * len(fields) :, :] = sums
 
 
 def step_length(grad_sq, curvature, penalty):
@@ -491,7 +491,7 @@
     gradient_out, *refs = refs
     if update:
         current_out, alpha_out, *refs = refs
-    hl, ha = refs
+    xp, yp, hl, ha = refs
     stations = current_ref.shape[1]
     chunks = Chunks(block, stations, pairs, counts_ref[0:1, :])
     size = chunks.size
@@ -511,6 +511,10 @@
         rot = rotate(current, cosine, sine)
         xs = [pack(v) for v in left_rows(rot, bright)]
         ys = [pack(v) for v in right_rows(rot)]
+        for i in range(2):
+            xp[t, i] = xs[i]
+        for rj in range(4):
+            yp[t, rj] = ys[rj]
         gram_y = [
             fold_gram(lanes(ys, c * size, size), lanes(ys, c * size, size), 32)
             for c in range(chunks.count)
@@ -556,6 +560,7 @@
     if update:
         inputs += step
         outs += [field, shape(8, 128)]
+    outs += [shape(dumps, rows, 64, stations, dtype=BF16) for rows in (2, 4)]
     return pl.pallas_call(
         functools.partial(gradient_kernel, block, pairs, dumps, penalty, chan_count, update),
         name="gradient_part",
@@ -571,21 +576,18 @@
 
 
 def curvature_kernel(block, pairs, dumps, penalty, chan_count, update, last, *refs):
-    counts_ref, delay_ref, coh_ref, current_ref, gradient_ref, mine_ref, theirs_ref, *refs = refs
+    counts_ref, delay_ref, coh_ref, xp, yp, gradient_ref, mine_ref, theirs_ref, *refs = refs
     if update:
         alpha_ref, linear_ref, *refs = refs
     if last:
-        duals_ref, *refs = refs
+        duals_ref, current_ref, *refs = refs
     direction_out, *refs = refs
-    if last:
-        keep_out, send_out = refs
-    else:
+    if not last:
         linear_out, sums_out = refs
-    stations = current_ref.shape[1]
+    stations = mine_ref.shape[1]
     chunks = Chunks(block, stations, pairs, counts_ref[0:1, :])
     size = chunks.size
 
-    current = current_ref[...]
     linear = mine_ref[...] + theirs_ref[...]
     if update:
         linear = linear_ref[...] - alpha_ref[0:1, 0:1] * linear
@@ -598,12 +600,19 @@
     bright = coherency_rows(coh_ref[...], stations)
     squares = jnp.zeros((8, 4 * size), F32)
     grams = jnp.zeros((64, 64), F32)
-    for t in range(dumps):
-        cosine, sine = trig(delay_ref[8 * t : 8 * t + 8, :], freq_value)
-        rot = rotate(current, cosine, sine)
+    if last:
+        visited, repeats, copies = range(dumps), 1, 1
+    else:
+        stn_count = stations // block
+        shared = stn_count % dumps == 0
+        visited = [lax.axis_index("stn") % dumps] if shared else range(dumps)
+        repeats, copies = (stn_count // dumps if shared else stn_count), stn_count
+    for t in visited:
+        delay = delay_ref[pl.ds(pl.multiple_of(8 * t, 8), 8), :]
+        cosine, sine = trig(delay, freq_value)
         step = rotate(direction, cosine, sine)
-        xs = [pack(v) for v in left_rows(rot, bright)]
-        ys = [pack(v) for v in right_rows(rot)]
+        xs = [xp[t, i] for i in range(2)]
+        ys = [yp[t, rj] for rj in range(4)]
         dxs = [pack(v) for v in left_rows(step, bright)]
         dys = [pack(v) for v in right_rows(step)]
 
@@ -634,34 +643,34 @@
                 grams = grams + sum_of([gram_y[o] for o in others]) * gram_x
     curvature = jnp.sum(squares, keepdims=True) + jnp.sum(grams, keepdims=True)
     grad_sq = jnp.sum(direction * direction, keepdims=True)
-    rows = 8 if last else chan_count
+    grad_sq = grad_sq * (1.0 / copies)
+    curvature = curvature * (1.0 / repeats)
+    rows = 8 if last else chan_count * copies
     lane = lax.broadcasted_iota(jnp.int32, (rows, block // 2 if last else 128), 1)
     sums = jnp.where(lane == 0, grad_sq, jnp.where(lane == 1, curvature, 0.0))
     if last:
         base = current_ref[:, own_lanes(block)] + duals_ref[...]
-        store_moments(
-            (base, direction_out[:, own_lanes(block)]), sums, chan_count, keep_out, send_out
-        )
+        store_quarters((base, direction_out[:, own_lanes(block)]), sums, refs)
     else:
         sums_out[...] = sums
 
 
-def curvature_part(geometry, counts, delays, coh, current, gradient, shares, before, duals):
+def curvature_part(geometry, counts, delays, coh, factors, gradient, shares, before, last):
     block, pairs, dumps, penalty, chan_count, stations = geometry
-    update, last = before is not None, duals is not None
+    update = before is not None
     field = shape(64, stations)
-    if last:
-        outs = [field] + [shape(528, block // 2)] * 2
+    if last is not None:
+        outs = [field] + [shape(72, block // 2)] * 4
     else:
-        outs = [field, field, shape(chan_count, 128)]
-    inputs = [counts, delays, coh, current, gradient, *shares]
+        outs = [field, field, shape(chan_count * (stations // block), 128)]
+    inputs = [counts, delays, coh, *factors, gradient, *shares]
     if update:
         inputs += before
-    if last:
-        inputs.append(duals)
+    if last is not None:
+        inputs += last
     return pl.pallas_call(
         functools.partial(
-            curvature_kernel, block, pairs, dumps, penalty, chan_count, update, last
+            curvature_kernel, block, pairs, dumps, penalty, chan_count, update, last is not None
         ),
         name="curvature_part",
         out_shape=tuple(outs),
@@ -672,6 +681,33 @@
             flops=2000000000, bytes_accessed=2000000, transcendentals=0
         ),
     )(*inputs)
+
+
+def weigh_kernel(chan_count, *refs):
+    *parts, out = refs
+    scales = [solve_of(chan_count, offset) for offset in range(4)]
+    for n in range(2):
+        for k in range(4):
+            at = 128 * n + 32 * k
+            terms = [scales[o][k] * parts[o][32 * n : 32 * n + 32, :] for o in range(4)]
+            out[at : at + 32, :] = sum_in_pairs(terms)
+    out[256:, :] = sum_in_pairs([part[64:, :] for part in parts])
+
+
+def sum_in_pairs(terms):
+    return (terms[0] + terms[1]) + (terms[2] + terms[3])
+
+
+def weigh(geometry, *parts):
+    chan_count = geometry[4]
+    return pl.pallas_call(
+        functools.partial(weigh_kernel, chan_count),
+        name="weigh",
+        out_shape=shape(264, parts[0].shape[1]),
+        in_specs=vmem_specs(4),
+        out_specs=vmem_specs(1)[0],
+        compiler_params=params(),
+    )(*parts)
 
 
 def combine_kernel(penalty, one, two, coeffs_out, alpha_out):
@@ -770,29 +806,25 @@
     geometry = (block, pairs, dumps, penalty, chan_count, stations)
 
     observed = observed.reshape((slots,) + observed.shape[2:])
-    gains_raw = gains.reshape(entries * dirs, 1, block)
-    delays_raw = delays.reshape(dumps * dirs, block)
     duals_raw = duals.reshape(entries * dirs, 1, block)
     prior = prior_coeffs.reshape(entries * dirs, 4, block)
-    ids_raw, flags_raw = pair_table.reshape(1, slots), flag_rows.reshape(1, slots)
+    rows = jnp.concatenate(
+        [gains.reshape(entries * dirs, 1, block), delays.reshape(dumps * dirs, 1, block)]
+    )
+    ints = jnp.stack([pair_table, flag_rows])
     if stn_count == 2:
-        gains_other, delays_other = other_stations(gains_raw), other_stations(delays_raw)
-        ids_other, flags_other = other_stations(ids_raw), other_stations(flags_raw)
+        fields = (rows, other_stations(rows))
+        ints_other = other_stations(ints)
     else:
-        gains_all = lax.all_gather(gains_raw, "stn", axis=2, tiled=True)
-        delays_all = lax.all_gather(delays_raw, "stn", axis=1, tiled=True)
-        ids_other = lax.all_gather(ids_raw, "stn", axis=1, tiled=True)
-        flags_other = lax.all_gather(flags_raw, "stn", axis=1, tiled=True)
-    gains_own, duals_own, start, coh, counts = prepare(
-        geometry, pair_table, flag_rows, gains_raw, duals_raw, prior, brightness
+        fields = (lax.all_gather(rows, "stn", axis=2, tiled=True),)
+        ints_other = lax.all_gather(ints, "stn", axis=1, tiled=True)
+    duals_own, start, coh, counts = prepare(
+        geometry, pair_table, flag_rows, duals_raw, prior, brightness
     )
-    if stn_count == 2:
-        fields = (gains_own, gains_other, delays_raw, delays_other)
-    else:
-        fields = (gains_all, delays_all)
+    if stn_count != 2:
         counts = jnp.zeros_like(counts)
     data = functools.partial(data_part, geometry, pair_table, flag_rows, observed, coh)
-    share, current, delay_all, counts = data(fields + (start, counts, ids_other, flags_other))
+    share, current, delay_all, counts = data(fields + (start, counts, ints_other))
     shares = both_stations(share, stn_count)
 
     step = before = None
@@ -800,34 +832,32 @@
         last = iteration + 1 == ITERS
         gradient, *rest = gradient_part(geometry, counts, delay_all, coh, current, step)
         if step is not None:
-            current, alpha = rest
+            current, alpha, *rest = rest
             before = (alpha, linear)
         direction, *rest = curvature_part(
             geometry,
             counts,
             delay_all,
             coh,
-            current,
+            rest,
             gradient,
             shares,
             before,
-            duals_own if last else None,
+            (duals_own, current) if last else None,
         )
         if not last:
             linear, sums = rest
-            sums = lax.all_to_all(sums, "chan", 0, 0, tiled=True)
+            sums = lax.all_to_all(sums, ("chan", "stn"), 0, 0, tiled=True)
             (share,) = data((direction, delay_all))
             shares = both_stations(share, stn_count)
             step = (sums, direction)
 
-    keep, send = rest
-    total = keep + swap(send, chan_count, 1)
-    value, other = total[:264], swap(total[264:], chan_count, 2)
-    bit = 4
-    while bit < chan_count:
-        value = value + other
+    quarters = rest[:1] + [swap(rest[o], chan_count, o) for o in (1, 2, 3)]
+    value, bit = weigh(geometry, *quarters), 4
+    other = swap(value, chan_count, bit)
+    while 2 * bit < chan_count:
+        value, bit = value + other, 2 * bit
         other = swap(value, chan_count, bit)
-        bit *= 2
     quarter, alpha = combine(geometry, value, other)
     gains_new, shifted = last_step(geometry, alpha, current, direction, duals_own)
     quarters = [quarter] + [swap(quarter, chan_count, o) for o in (1, 2, 3)]

time: 88.6 us -> 85.2 us (0.962); the launches traced: 88 us -> 86.4 us
  starting transfers between devices: 26.1 us -> 21.9 us
  Pallas kernels: 34.9 us -> 37.4 us
  other arithmetic: 0.06 us -> 1.61 us
    pallas_call x3, Pallas kernels: 13.8 us -> 17.9 us  [data_part(): pl.pallas_call(body, name='data_part', out_shape=tuple(shapes), in_specs=...]
    ppermute x7 -> x5, starting transfers between devices: 5.95 us -> 3.23 us  [other_stations(): return lax.ppermute(value, 'stn', [(0, 1), (1, 0)])]
    pallas_call x3, Pallas kernels: 6.35 us -> 4.72 us  [curvature_part(): pl.pallas_call(functools.partial(curvature_kernel, block, pairs, dumps, p...]
    unnamed x18 -> x14, local copies, waits for them, and re-layouts: 5.34 us -> 3.8 us
    ppermute x7 -> x5, waiting for transfers between devices: 0.43 us -> 1.83 us  [other_stations(): return lax.ppermute(value, 'stn', [(0, 1), (1, 0)])]
    all_to_all x2, starting transfers between devices: 12.1 us -> 10.8 us  [shards(): sums = lax.all_to_all(sums, ('chan', 'stn'), 0, 0, tiled=True)]
    all_to_all x2, waiting for transfers between devices: 3.25 us -> 2.06 us  [shards(): sums = lax.all_to_all(sums, ('chan', 'stn'), 0, 0, tiled=True)]
    concatenate x0 -> x1, other arithmetic: none -> 0.91 us  [shards(): jnp.concatenate([gains.reshape(entries * dirs, 1, block), delays.reshape(...]
  transfers between devices with their start and end apart: 16 -> 15, of which waited for: 10 -> 11; matrix products, arithmetic and copies ran while one was open for 0% -> 1% of each run, Pallas kernels for 26% -> 30%
where the time goes in v3:
time: 85.2 us; the launch traced here: 86.4 us
  Pallas kernels  37.4 us (44%)
  starting transfers between devices  21.9 us (26%)
  waiting for transfers between devices  20.1 us (24%)
  local copies, waits for them, and re-layouts  4.53 us (5%)
  other arithmetic  1.61 us (2%)
    pallas_call x3, Pallas kernels, data_part(): pl.pallas_call(body, name='data_part', out_shape=tuple(shapes), in_specs=...  17.9 us
    ppermute x8, waiting for transfers between devices, swap(): return lax.ppermute(value, 'chan', [(i, i ^ offset) for i in range(count)])  16.2 us
    pallas_call x3, Pallas kernels, gradient_part(): pl.pallas_call(functools.partial(gradient_kernel, block, pairs, dumps, pe...  12.3 us
    all_to_all x2, starting transfers between devices, shards(): sums = lax.all_to_all(sums, ('chan', 'stn'), 0, 0, tiled=True)  10.8 us
    ppermute x8, starting transfers between devices, swap(): return lax.ppermute(value, 'chan', [(i, i ^ offset) for i in range(count)])  7.83 us
    pallas_call x3, Pallas kernels, curvature_part(): pl.pallas_call(functools.partial(curvature_kernel, block, pairs, dumps, p...  4.72 us
    unnamed x14, local copies, waits for them, and re-layouts  3.8 us
    ppermute x5, starting transfers between devices, other_stations(): return lax.ppermute(value, 'stn', [(0, 1), (1, 0)])  3.23 us
  transfers between devices with their start and end apart: 15, of which 11 were waited for; matrix products, arithmetic and copies ran while one was open for 1% of the time, Pallas kernels for 30%

profile of v3, /device:TPU:0, one launch (start us, length us, event | category | flops | bytes accessed | tf_op | source)
XLA Modules:
  0.0 86.4 jit_solution(2954018667348131674)
XLA Ops:
  0.6 0.7 reshape.38
  1.4 0.9 %pad_maximum_fusion.refs_4_ = f32[80,1,256]{2,1,0:T(1,128)S(1)} fusion(f32[16,1,256]{2,1,0:T(1,128)S(1)} %reshape.38, f32[64,1,256]{2,1,0:T(1,128)} %bitcast.23), kind=kLoop, calls=%fused_computation | loop fusion | flops 20480 | bytes 163840 | tf_op jit(solution)/shard_map/concatenate | solution.py:811
  2.3 3.0 %collective-permute-start = (f32[80,1,256]{2,1,0:T(1,128)S(1)}, f32[80,1,256]{2,1,0:T(1,128)S(1)}, u32[]{:S(2)}, u32[]{:S(2)}) collective-permute-start(f32[80,1,256]{2,1,0:T(1,128)S(1)} %pad_maximum_fusion.refs_4_), channel_id=1, source_target_pairs={{0,1},{1,0},{2,3},{3,2},{4,5},{5,4},{6,7},{7,6},{8,9},{9,8},{10,11... | collective-permute-start | bytes 245768 | tf_op jit(solution)/shard_map/ppermute | solution.py:789
  5.3 0.7 pad_add_fusion
  6.0 0.0 collective-permute-start.1
  6.0 0.9 %copy-done = f32[8,8,4,256]{3,2,1,0:T(4,128)S(1)} copy-done((f32[8,8,4,256]{3,2,1,0:T(4,128)S(1)}, f32[8,8,4,256]{3,2,1,0:T(4,128)}, u32[]{:S(2)}) %copy-start) | copy-done | bytes 262168
  6.9 0.8 copy-done.1
  7.8 0.7 copy-done.2
  8.5 0.7 copy-done.3
  9.1 0.7 copy-done.5
  9.8 0.7 prepare.1
  10.5 5.9 %data_part.3 = (f32[64,512]{1,0:T(8,128)S(1)}, f32[64,512]{1,0:T(8,128)S(1)}, f32[16,512]{1,0:T(8,128)S(1)}, f32[8,128]{1,0:T(8,128)S(1)}) custom-call(s32[4]{0:T(128)S(1)} %copy-done.3, s32[4]{0:T(128)S(1)} %copy-done.5, bf16[4,2,8,256,256]{4,3,2,1,0:T(8,128)(2,1)} %bitcast.24, f32[64,128]{1,0:T(8,128)S(1)} %get-tuple-element.41.refs_3_.refs_2_, ...), custom_call_target="tpu_custom_call" | custom-call | flops 6000000000 | bytes 8000000 | tf_op jit(solution)/shard_map/data_part/pallas_call | solution.py:382
  16.5 0.1 collective-permute-start.2
  16.6 4.0 %gradient_part.3 = (f32[64,512]{1,0:T(8,128)S(1)}, bf16[2,2,64,512]{3,2,1,0:T(8,128)(2,1)S(1)}, bf16[2,4,64,512]{3,2,1,0:T(8,128)(2,1)S(1)}) custom-call(f32[8,128]{1,0:T(8,128)S(1)} %get-tuple-element.44.refs_0_, f32[16,512]{1,0:T(8,128)S(1)} %get-tuple-element.45.refs_1_.refs_5_, f32[64,128]{1,0:T(8,128)S(1)} %get-tuple-element.41.refs_3_.refs_2_, ...), custom_call_target="tpu_custom_call" | custom-call | flops 4000000000 | bytes 2000000 | tf_op jit(solution)/shard_map/gradient_part/pallas_call | solution.py:564
  20.6 0.9 %collective-permute-done.2.refs_7_ = f32[64,512]{1,0:T(8,128)S(1)} collective-permute-done((f32[64,512]{1,0:T(8,128)S(1)}, f32[64,512]{1,0:T(8,128)S(1)}, u32[]{:S(2)}, u32[]{:S(2)}) %collective-permute-start.2) | collective-permute-done | bytes 131104 | tf_op jit(solution)/shard_map/ppermute | solution.py:789
  21.5 1.6 %curvature_part.3 = (f32[64,512]{1,0:T(8,128)S(1)}, f32[64,512]{1,0:T(8,128)S(1)}, f32[32,128]{1,0:T(8,128)}) custom-call(f32[8,128]{1,0:T(8,128)S(1)} %get-tuple-element.44.refs_0_, f32[16,512]{1,0:T(8,128)S(1)} %get-tuple-element.45.refs_1_.refs_5_, f32[64,128]{1,0:T(8,128)S(1)} %get-tuple-element.41.refs_3_.refs_2_, ...), custom_call_target="tpu_custom_call" | custom-call | flops 2000000000 | bytes 2000000 | tf_op jit(solution)/shard_map/curvature_part/pallas_call | solution.py:671
  23.1 5.9 %all-to-all-start = ((f32[32,1,128]{2,1,0:T(1,128)}), f32[32,1,128]{2,1,0:T(1,128)S(1)}, u32[]{:S(2)}, u32[]{:S(2)}) async-start(f32[32,1,128]{2,1,0:T(1,128)} %bitcast.7), calls=%async_computation | async-start | bytes 32768 | tf_op jit(solution)/shard_map/all_to_all | solution.py:850
  29.0 5.9 %data_part.4.refs_6_ = f32[64,512]{1,0:T(8,128)S(1)} custom-call(s32[4]{0:T(128)S(1)} %copy-done.4, s32[4]{0:T(128)S(1)} %copy-done.6, bf16[4,2,8,256,256]{4,3,2,1,0:T(8,128)(2,1)} %bitcast.25, f32[64,128]{1,0:T(8,128)S(1)} %get-tuple-element.41.refs_3_.refs_2_, f32[64,512]{1,0:T(8,128)S(1)} %get-tuple-element.52.refs_5_.refs_4_, ...), custom_call_target="tpu_custom_call" | custom-call | flops 6000000000 | bytes 8000000 | tf_op jit(solution)/shard_map/data_part/pallas_call | solution.py:382
  34.9 0.1 collective-permute-start.3
  35.0 1.1 %all-to-all-done = f32[32,1,128]{2,1,0:T(1,128)S(1)} async-done(((f32[32,1,128]{2,1,0:T(1,128)}), f32[32,1,128]{2,1,0:T(1,128)S(1)}, u32[]{:S(2)}, u32[]{:S(2)}) %all-to-all-start) | async-done | bytes 16416 | tf_op jit(solution)/shard_map/all_to_all | solution.py:850
  36.1 4.2 %gradient_part.4 = (f32[64,512]{1,0:T(8,128)S(1)}, f32[64,512]{1,0:T(8,128)S(1)}, f32[8,128]{1,0:T(8,128)S(1)}, bf16[2,2,64,512]{3,2,1,0:T(8,128)(2,1)S(1)}, bf16[2,4,64,512]{3,2,1,0:T(8,128)(2,1)S(1)}) custom-call(f32[8,128]{1,0:T(8,128)S(1)} %get-tuple-element.44.refs_0_, f32[16,512]{1,0:T(8,128)S(1)} %get-tuple-element.45.refs_1_.refs_5_, ...), custom_call_target="tpu_custom_call" | custom-call | flops 4000000000 | bytes 2000000 | tf_op jit(solution)/shard_map/gradient_part/pallas_call | solution.py:564
  40.3 0.4 collective-permute-done.3.refs_7_
  40.7 1.6 %curvature_part.4 = (f32[64,512]{1,0:T(8,128)S(1)}, f32[64,512]{1,0:T(8,128)S(1)}, f32[32,128]{1,0:T(8,128)}) custom-call(f32[8,128]{1,0:T(8,128)S(1)} %get-tuple-element.44.refs_0_, f32[16,512]{1,0:T(8,128)S(1)} %get-tuple-element.45.refs_1_.refs_5_, f32[64,128]{1,0:T(8,128)S(1)} %get-tuple-element.41.refs_3_.refs_2_, ...), custom_call_target="tpu_custom_call" | custom-call | flops 2000000000 | bytes 2000000 | tf_op jit(solution)/shard_map/curvature_part/pallas_call | solution.py:671
  42.2 4.9 %all-to-all-start.1 = ((f32[32,1,128]{2,1,0:T(1,128)}), f32[32,1,128]{2,1,0:T(1,128)S(1)}, u32[]{:S(2)}, u32[]{:S(2)}) async-start(f32[32,1,128]{2,1,0:T(1,128)} %bitcast.10), calls=%async_computation.1 | async-start | bytes 32768 | tf_op jit(solution)/shard_map/all_to_all | solution.py:850
  47.1 6.1 %data_part.5.refs_6_ = f32[64,512]{1,0:T(8,128)S(1)} custom-call(s32[4]{0:T(128)S(1)} %copy-done.4, s32[4]{0:T(128)S(1)} %copy-done.6, bf16[4,2,8,256,256]{4,3,2,1,0:T(8,128)(2,1)} %bitcast.26, f32[64,128]{1,0:T(8,128)S(1)} %get-tuple-element.41.refs_3_.refs_2_, f32[64,512]{1,0:T(8,128)S(1)} %get-tuple-element.60.refs_5_.refs_4_, ...), custom_call_target="tpu_custom_call" | custom-call | flops 6000000000 | bytes 8000000 | tf_op jit(solution)/shard_map/data_part/pallas_call | solution.py:382
  53.2 0.1 collective-permute-start.4
  53.3 1.0 %all-to-all-done.1 = f32[32,1,128]{2,1,0:T(1,128)S(1)} async-done(((f32[32,1,128]{2,1,0:T(1,128)}), f32[32,1,128]{2,1,0:T(1,128)S(1)}, u32[]{:S(2)}, u32[]{:S(2)}) %all-to-all-start.1) | async-done | bytes 16416 | tf_op jit(solution)/shard_map/all_to_all | solution.py:850
  54.3 4.2 %gradient_part.5 = (f32[64,512]{1,0:T(8,128)S(1)}, f32[64,512]{1,0:T(8,128)S(1)}, f32[8,128]{1,0:T(8,128)S(1)}, bf16[2,2,64,512]{3,2,1,0:T(8,128)(2,1)S(1)}, bf16[2,4,64,512]{3,2,1,0:T(8,128)(2,1)S(1)}) custom-call(f32[8,128]{1,0:T(8,128)S(1)} %get-tuple-element.44.refs_0_, f32[16,512]{1,0:T(8,128)S(1)} %get-tuple-element.45.refs_1_.refs_5_, ...), custom_call_target="tpu_custom_call" | custom-call | flops 4000000000 | bytes 2000000 | tf_op jit(solution)/shard_map/gradient_part/pallas_call | solution.py:564
  58.4 0.5 collective-permute-done.4.refs_7_
  58.9 1.6 %curvature_part.5 = (f32[64,512]{1,0:T(8,128)S(1)}, f32[72,128]{1,0:T(8,128)S(1)}, f32[72,128]{1,0:T(8,128)S(1)}, f32[72,128]{1,0:T(8,128)S(1)}, f32[72,128]{1,0:T(8,128)S(1)}) custom-call(f32[8,128]{1,0:T(8,128)S(1)} %get-tuple-element.44.refs_0_, f32[16,512]{1,0:T(8,128)S(1)} %get-tuple-element.45.refs_1_.refs_5_, ...), custom_call_target="tpu_custom_call" | custom-call | flops 2000000000 | bytes 2000000 | tf_op jit(solution)/shard_map/curvature_part/pallas_call | solution.py:671
  60.5 0.1 collective-permute-start.5
  60.6 1.7 %collective-permute-start.6 = (f32[72,128]{1,0:T(8,128)S(1)}, f32[72,128]{1,0:T(8,128)S(1)}, u32[]{:S(2)}, u32[]{:S(2)}) collective-permute-start(f32[72,128]{1,0:T(8,128)S(1)} %get-tuple-element.70), channel_id=1, source_target_pairs={{0,4},{2,6},{4,0},{6,2},{8,12},{10,14},{12,8},{14,10},{16,20},{18,... | collective-permute-start | bytes 110600 | tf_op jit(solution)/shard_map/ppermute | solution.py:785
  62.3 0.1 collective-permute-start.7
  62.5 2.2 %collective-permute-done.6.refs_2_ = f32[72,128]{1,0:T(8,128)S(1)} collective-permute-done((f32[72,128]{1,0:T(8,128)S(1)}, f32[72,128]{1,0:T(8,128)S(1)}, u32[]{:S(2)}, u32[]{:S(2)}) %collective-permute-start.6) | collective-permute-done | bytes 36896 | tf_op jit(solution)/shard_map/ppermute | solution.py:785
  64.6 1.1 %collective-permute-done.7.refs_3_ = f32[72,128]{1,0:T(8,128)S(1)} collective-permute-done((f32[72,128]{1,0:T(8,128)S(1)}, f32[72,128]{1,0:T(8,128)S(1)}, u32[]{:S(2)}, u32[]{:S(2)}) %collective-permute-start.7) | collective-permute-done | bytes 36896 | tf_op jit(solution)/shard_map/ppermute | solution.py:785
  65.8 0.1 weigh.1
  65.8 1.5 %collective-permute-start.8 = (f32[264,128]{1,0:T(8,128)S(1)}, f32[264,128]{1,0:T(8,128)S(1)}, u32[]{:S(2)}, u32[]{:S(2)}) collective-permute-start(f32[264,128]{1,0:T(8,128)S(1)} %weigh.1), channel_id=1, source_target_pairs={{0,8},{2,10},{4,12},{6,14},{8,0},{10,2},{12,4},{14,6},{16,24},{18,... | collective-permute-start | bytes 405512 | tf_op jit(solution)/shard_map/ppermute | solution.py:785
  67.4 4.2 %collective-permute-done.8 = f32[264,128]{1,0:T(8,128)S(1)} collective-permute-done((f32[264,128]{1,0:T(8,128)S(1)}, f32[264,128]{1,0:T(8,128)S(1)}, u32[]{:S(2)}, u32[]{:S(2)}) %collective-permute-start.8) | collective-permute-done | bytes 135200 | tf_op jit(solution)/shard_map/ppermute | solution.py:785
  71.6 2.4 %collective-permute-start.9 = (f32[264,128]{1,0:T(8,128)S(1)}, f32[264,128]{1,0:T(8,128)S(1)}, u32[]{:S(2)}, u32[]{:S(2)}) collective-permute-start(f32[264,128]{1,0:T(8,128)S(1)} %add.3.one), channel_id=1, source_target_pairs={{0,16},{2,18},{4,20},{6,22},{8,24},{10,26},{12,28},{14,30},{16,0},... | collective-permute-start | bytes 405512 | tf_op jit(solution)/shard_map/ppermute | solution.py:785
  74.0 6.2 %collective-permute-done.9.two = f32[264,128]{1,0:T(8,128)S(1)} collective-permute-done((f32[264,128]{1,0:T(8,128)S(1)}, f32[264,128]{1,0:T(8,128)S(1)}, u32[]{:S(2)}, u32[]{:S(2)}) %collective-permute-start.9) | collective-permute-done | bytes 135200 | tf_op jit(solution)/shard_map/ppermute | solution.py:785
  80.3 0.2 combine.1
  80.5 0.1 collective-permute-start.12
  80.6 0.9 %collective-permute-start.11 = (f32[128,128]{1,0:T(8,128)S(1)}, f32[128,128]{1,0:T(8,128)S(1)}, u32[]{:S(2)}, u32[]{:S(2)}) collective-permute-start(f32[128,128]{1,0:T(8,128)S(1)} %get-tuple-element.75.own), channel_id=1, source_target_pairs={{0,4},{2,6},{4,0},{6,2},{8,12},{10,14},{12,8},{14,10},{16,20},{18,... | collective-permute-start | bytes 196616 | tf_op jit(solution)/shard_map/ppermute | solution.py:785
  81.5 0.9 %collective-permute-start.10 = (f32[128,128]{1,0:T(8,128)S(1)}, f32[128,128]{1,0:T(8,128)S(1)}, u32[]{:S(2)}, u32[]{:S(2)}) collective-permute-start(f32[128,128]{1,0:T(8,128)S(1)} %get-tuple-element.75.own), channel_id=1, source_target_pairs={{0,2},{2,0},{4,6},{6,4},{8,10},{10,8},{12,14},{14,12},{16,18},{18,... | collective-permute-start | bytes 196616 | tf_op jit(solution)/shard_map/ppermute | solution.py:785
  82.4 0.7 last_step.1
  83.1 1.5 %collective-permute-done.12.both = f32[128,128]{1,0:T(8,128)S(1)} collective-permute-done((f32[128,128]{1,0:T(8,128)S(1)}, f32[128,128]{1,0:T(8,128)S(1)}, u32[]{:S(2)}, u32[]{:S(2)}) %collective-permute-start.12) | collective-permute-done | bytes 65568 | tf_op jit(solution)/shard_map/ppermute | solution.py:785
  84.6 0.9 %collective-permute-done.11.row = f32[128,128]{1,0:T(8,128)S(1)} collective-permute-done((f32[128,128]{1,0:T(8,128)S(1)}, f32[128,128]{1,0:T(8,128)S(1)}, u32[]{:S(2)}, u32[]{:S(2)}) %collective-permute-start.11) | collective-permute-done | bytes 65568 | tf_op jit(solution)/shard_map/ppermute | solution.py:785
  85.5 0.8 consensus.1
  (14 shorter events, 0.1 us)
Async XLA Ops:
  2.3 8.2 %collective-permute-start = (f32[80,1,256]{2,1,0:T(1,128)S(1)}, f32[80,1,256]{2,1,0:T(1,128)S(1)}, u32[]{:S(2)}, u32[]{:S(2)}) collective-permute-start(f32[80,1,256]{2,1,0:T(1,128)S(1)} %pad_maximum_fusion.refs_4_), channel_id=1, source_target_pairs={{0,1},{1,0},{2,3},{3,2},{4,5},{5,4},{6,7},{7,6},{8,9},{9,8},{10,11... | collective-permute-start | bytes 245768 | tf_op jit(solution)/shard_map/ppermute | solution.py:789
  6.0 4.5 %collective-permute-start.1 = (s32[2,4]{1,0:T(2,128)S(1)}, s32[2,4]{1,0:T(2,128)S(1)}, u32[]{:S(2)}, u32[]{:S(2)}) collective-permute-start(s32[2,4]{1,0:T(2,128)S(1)} %pad_add_fusion), channel_id=1, source_target_pairs={{0,1},{1,0},{2,3},{3,2},{4,5},{5,4},{6,7},{7,6},{8,9},{9,8},{10,11... | collective-permute-start | bytes 104 | tf_op jit(solution)/shard_map/ppermute | solution.py:789
  6.0 0.9 %copy-start = (f32[8,8,4,256]{3,2,1,0:T(4,128)S(1)}, f32[8,8,4,256]{3,2,1,0:T(4,128)}, u32[]{:S(2)}) copy-start(f32[8,8,4,256]{3,2,1,0:T(4,128)} %param.13) | copy-start | bytes 786436
  6.9 0.8 copy-start.1
  7.8 0.7 copy-start.2
  8.5 0.7 copy-start.3
  9.1 0.7 copy-start.5
  16.5 5.0 %collective-permute-start.2 = (f32[64,512]{1,0:T(8,128)S(1)}, f32[64,512]{1,0:T(8,128)S(1)}, u32[]{:S(2)}, u32[]{:S(2)}) collective-permute-start(f32[64,512]{1,0:T(8,128)S(1)} %get-tuple-element.50.refs_6_), channel_id=1, source_target_pairs={{0,1},{1,0},{2,3},{3,2},{4,5},{5,4},{6,7},{7,6},{8,9},{9,8},{10,11... | collective-permute-start | bytes 393224 | tf_op jit(solution)/shard_map/ppermute | solution.py:789
  16.5 12.5 %copy-start.4 = (s32[4]{0:T(128)S(1)}, s32[4]{0:T(128)}, u32[]{:S(2)}) copy-start(s32[4]{0:T(128)} %refs_0_.7) | copy-start | bytes 52
  16.5 12.5 %copy-start.6 = (s32[4]{0:T(128)S(1)}, s32[4]{0:T(128)}, u32[]{:S(2)}) copy-start(s32[4]{0:T(128)} %refs_1_.7) | copy-start | bytes 52
  23.1 13.1 %all-to-all-start = ((f32[32,1,128]{2,1,0:T(1,128)}), f32[32,1,128]{2,1,0:T(1,128)S(1)}, u32[]{:S(2)}, u32[]{:S(2)}) async-start(f32[32,1,128]{2,1,0:T(1,128)} %bitcast.7), calls=%async_computation | async-start | bytes 32768 | tf_op jit(solution)/shard_map/all_to_all | solution.py:850
  34.9 5.7 %collective-permute-start.3 = (f32[64,512]{1,0:T(8,128)S(1)}, f32[64,512]{1,0:T(8,128)S(1)}, u32[]{:S(2)}, u32[]{:S(2)}) collective-permute-start(f32[64,512]{1,0:T(8,128)S(1)} %data_part.4.refs_6_), channel_id=1, source_target_pairs={{0,1},{1,0},{2,3},{3,2},{4,5},{5,4},{6,7},{7,6},{8,9},{9,8},{10,11... | collective-permute-start | bytes 393224 | tf_op jit(solution)/shard_map/ppermute | solution.py:789
  42.2 12.0 %all-to-all-start.1 = ((f32[32,1,128]{2,1,0:T(1,128)}), f32[32,1,128]{2,1,0:T(1,128)S(1)}, u32[]{:S(2)}, u32[]{:S(2)}) async-start(f32[32,1,128]{2,1,0:T(1,128)} %bitcast.10), calls=%async_computation.1 | async-start | bytes 32768 | tf_op jit(solution)/shard_map/all_to_all | solution.py:850
  53.2 5.7 %collective-permute-start.4 = (f32[64,512]{1,0:T(8,128)S(1)}, f32[64,512]{1,0:T(8,128)S(1)}, u32[]{:S(2)}, u32[]{:S(2)}) collective-permute-start(f32[64,512]{1,0:T(8,128)S(1)} %data_part.5.refs_6_), channel_id=1, source_target_pairs={{0,1},{1,0},{2,3},{3,2},{4,5},{5,4},{6,7},{7,6},{8,9},{9,8},{10,11... | collective-permute-start | bytes 393224 | tf_op jit(solution)/shard_map/ppermute | solution.py:789
  60.5 1.9 %collective-permute-start.5 = (f32[72,128]{1,0:T(8,128)S(1)}, f32[72,128]{1,0:T(8,128)S(1)}, u32[]{:S(2)}, u32[]{:S(2)}) collective-permute-start(f32[72,128]{1,0:T(8,128)S(1)} %get-tuple-element.69), channel_id=1, source_target_pairs={{0,2},{2,0},{4,6},{6,4},{8,10},{10,8},{12,14},{14,12},{16,18},{18,... | collective-permute-start | bytes 110600 | tf_op jit(solution)/shard_map/ppermute | solution.py:785
  60.6 4.0 %collective-permute-start.6 = (f32[72,128]{1,0:T(8,128)S(1)}, f32[72,128]{1,0:T(8,128)S(1)}, u32[]{:S(2)}, u32[]{:S(2)}) collective-permute-start(f32[72,128]{1,0:T(8,128)S(1)} %get-tuple-element.70), channel_id=1, source_target_pairs={{0,4},{2,6},{4,0},{6,2},{8,12},{10,14},{12,8},{14,10},{16,20},{18,... | collective-permute-start | bytes 110600 | tf_op jit(solution)/shard_map/ppermute | solution.py:785
  62.3 3.4 %collective-permute-start.7 = (f32[72,128]{1,0:T(8,128)S(1)}, f32[72,128]{1,0:T(8,128)S(1)}, u32[]{:S(2)}, u32[]{:S(2)}) collective-permute-start(f32[72,128]{1,0:T(8,128)S(1)} %get-tuple-element.71), channel_id=1, source_target_pairs={{0,6},{2,4},{4,2},{6,0},{8,14},{10,12},{12,10},{14,8},{16,22},{18,... | collective-permute-start | bytes 110600 | tf_op jit(solution)/shard_map/ppermute | solution.py:785
  65.8 5.7 %collective-permute-start.8 = (f32[264,128]{1,0:T(8,128)S(1)}, f32[264,128]{1,0:T(8,128)S(1)}, u32[]{:S(2)}, u32[]{:S(2)}) collective-permute-start(f32[264,128]{1,0:T(8,128)S(1)} %weigh.1), channel_id=1, source_target_pairs={{0,8},{2,10},{4,12},{6,14},{8,0},{10,2},{12,4},{14,6},{16,24},{18,... | collective-permute-start | bytes 405512 | tf_op jit(solution)/shard_map/ppermute | solution.py:785
  71.6 8.7 %collective-permute-start.9 = (f32[264,128]{1,0:T(8,128)S(1)}, f32[264,128]{1,0:T(8,128)S(1)}, u32[]{:S(2)}, u32[]{:S(2)}) collective-permute-start(f32[264,128]{1,0:T(8,128)S(1)} %add.3.one), channel_id=1, source_target_pairs={{0,16},{2,18},{4,20},{6,22},{8,24},{10,26},{12,28},{14,30},{16,0},... | collective-permute-start | bytes 405512 | tf_op jit(solution)/shard_map/ppermute | solution.py:785
  80.5 4.1 %collective-permute-start.12 = (f32[128,128]{1,0:T(8,128)S(1)}, f32[128,128]{1,0:T(8,128)S(1)}, u32[]{:S(2)}, u32[]{:S(2)}) collective-permute-start(f32[128,128]{1,0:T(8,128)S(1)} %get-tuple-element.75.own), channel_id=1, source_target_pairs={{0,6},{2,4},{4,2},{6,0},{8,14},{10,12},{12,10},{14,8},{16,22},{18,... | collective-permute-start | bytes 196616 | tf_op jit(solution)/shard_map/ppermute | solution.py:785
  80.6 5.0 %collective-permute-start.11 = (f32[128,128]{1,0:T(8,128)S(1)}, f32[128,128]{1,0:T(8,128)S(1)}, u32[]{:S(2)}, u32[]{:S(2)}) collective-permute-start(f32[128,128]{1,0:T(8,128)S(1)} %get-tuple-element.75.own), channel_id=1, source_target_pairs={{0,4},{2,6},{4,0},{6,2},{8,12},{10,14},{12,8},{14,10},{16,20},{18,... | collective-permute-start | bytes 196616 | tf_op jit(solution)/shard_map/ppermute | solution.py:785
  81.5 4.0 %collective-permute-start.10 = (f32[128,128]{1,0:T(8,128)S(1)}, f32[128,128]{1,0:T(8,128)S(1)}, u32[]{:S(2)}, u32[]{:S(2)}) collective-permute-start(f32[128,128]{1,0:T(8,128)S(1)} %get-tuple-element.75.own), channel_id=1, source_target_pairs={{0,2},{2,0},{4,6},{6,4},{8,10},{10,8},{12,14},{14,12},{16,18},{18,... | collective-permute-start | bytes 196616 | tf_op jit(solution)/shard_map/ppermute | solution.py:785

commit v4 on v3

--- a/solution.py
+++ b/solution.py
@@ -14,10 +14,13 @@
 SPECTRAL_INDEX = 0.7
 DIRS = 8
 CHUNK = 128
-VMEM_BYTES = 48 * 1024 * 1024
+VMEM_BYTES = 24 * 1024 * 1024
+COPY_BYTES = 48 * 1024 * 1024
 AHEAD = 2
 F32 = jnp.float32
 BF16 = jnp.bfloat16
+
+COSTLY = pl.CostEstimate(flops=20000000000, bytes_accessed=20000000, transcendentals=0)
 
 NT = (((1,), (1,)), ((), ()))
 NN = (((1,), (0,)), ((), ()))
@@ -195,8 +198,8 @@
     return [pl.BlockSpec(memory_space=pltpu.SMEM)] * count
 
 
-def params():
-    return pltpu.CompilerParams(vmem_limit_bytes=VMEM_BYTES)
+def params(limit=None):
+    return pltpu.CompilerParams(vmem_limit_bytes=limit or VMEM_BYTES)
 
 
 def shape(*dims, dtype=F32):
@@ -213,6 +216,47 @@
         first = first + jnp.where(pair == k, p, 0)
         second = second + jnp.where(pair == k, q, 0)
     return first, second
+
+
+def masks_kernel(masks):
+    block = masks.shape[1]
+    row = lax.broadcasted_iota(jnp.int32, (block, block), 0)
+    col = lax.broadcasted_iota(jnp.int32, (block, block), 1)
+    masks[0] = (row < col).astype(F32).astype(BF16)
+    masks[1] = jnp.ones((block, block), BF16)
+
+
+def baseline_masks(block):
+    return pl.pallas_call(
+        masks_kernel,
+        name="baseline_masks",
+        out_shape=shape(2, block, block, dtype=BF16),
+        out_specs=vmem_specs(1)[0],
+        compiler_params=params(),
+        cost_estimate=COSTLY,
+    )()
+
+
+def rows_kernel(masks, gains, delays, ids, flags, rows):
+    fields, stations = gains.shape[0] + delays.shape[0], gains.shape[2]
+    rows[: gains.shape[0]] = gains[...]
+    rows[gains.shape[0] : fields] = delays[...].reshape(delays.shape[0], 1, stations)
+    rows[fields:] = jnp.full((2, 1, stations), -1.0, F32)
+    slots = ids.shape[1]
+    rows[fields, :, :slots] = ids[...].astype(F32)
+    rows[fields + 1, :, :slots] = flags[...].astype(F32)
+
+
+def field_rows(masks, gains, delays, ids, flags):
+    return pl.pallas_call(
+        rows_kernel,
+        name="field_rows",
+        out_shape=shape(gains.shape[0] + delays.shape[0] + 2, 1, gains.shape[2]),
+        in_specs=vmem_specs(5),
+        out_specs=vmem_specs(1)[0],
+        compiler_params=params(),
+        cost_estimate=COSTLY,
+    )(masks, gains, delays, ids, flags)
 
 
 def prepare_kernel(block, pairs, slots, penalty, chan_count, *refs):
@@ -254,16 +298,19 @@
 
 
 def data_kernel(block, pairs, dumps, slots, penalty, chan_count, first_call, joined, *refs):
-    table, flags, observed, coh_ref, *refs = refs
+    table, flags, observed, coh_ref, keep, *refs = refs
     if first_call:
         if joined:
             rows_all, *refs = refs
         else:
             rows_mine, rows_other, *refs = refs
-        start, counts_mine, ints_other, out_ref, field_ref, delay_ref, counts_ref, *refs = refs
+        start, counts_mine, out_ref, field_ref, delay_ref, counts_ref, *refs = refs
     else:
         field_ref, delay_ref, out_ref, *refs = refs
-    held, sems, order, keep, xp, yp, hl, ha = refs
+    if first_call:
+        order, xp, yp, hl, ha = refs
+    else:
+        held, sems, order, xp, yp, hl, ha = refs
     stations = field_ref.shape[1]
     pair_count = len(pairs)
     at_own = own_lanes(block)
@@ -278,22 +325,24 @@
         slot, t = order[item // dumps], item % dumps
         return pltpu.make_async_copy(observed.at[slot, t], held.at[item], sems.at[item])
 
-    for item in range(min(AHEAD, slots * dumps)):
-
-        @pl.when(item < items)
-        def _():
-            copy_of(jnp.int32(item)).start()
+    if not first_call:
+        for item in range(min(AHEAD, slots * dumps)):
+
+            @pl.when(item < items)
+            def _():
+                copy_of(jnp.int32(item)).start()
 
     freq_value = frequency_of(chan_count)
     if first_call:
         if joined:
+            rows_other = rows_all
             field_ref[...] = rows_all[:64, 0, :]
-            delay_ref[...] = rows_all[64:, 0, :]
+            delay_ref[...] = rows_all[64 : 64 + 8 * dumps, 0, :]
         else:
             at_other = pl.ds(pl.multiple_of((1 - lax.axis_index("stn")) * block, CHUNK), block)
             for at, rows in ((at_own, rows_mine), (at_other, rows_other)):
                 field_ref[:, at] = rows[:64, 0, :]
-                delay_ref[:, at] = rows[64:, 0, :]
+                delay_ref[:, at] = rows[64 : 64 + 8 * dumps, 0, :]
     bright = coherency_rows(coh_ref[...], stations)
     for t in range(dumps):
         cosine, sine = trig(delay_ref[8 * t : 8 * t + 8, :], freq_value)
@@ -305,10 +354,6 @@
     hl[...] = jnp.zeros_like(hl)
     ha[...] = jnp.zeros_like(ha)
 
-    row = lax.broadcasted_iota(jnp.int32, (block, block), 0)
-    col = lax.broadcasted_iota(jnp.int32, (block, block), 1)
-    keep[0] = (row < col).astype(F32).astype(BF16)
-    keep[1] = jnp.ones((block, block), BF16)
     lane = lax.broadcasted_iota(jnp.int32, (1, block), 1)
 
     def visit(item, unused):
@@ -319,11 +364,12 @@
         live16 = live.astype(BF16)
         at_p = pl.ds(pl.multiple_of(first * block, CHUNK), block)
         at_q = pl.ds(pl.multiple_of(second * block, CHUNK), block)
-        copy_of(item).wait()
-
-        @pl.when(item + AHEAD < items)
-        def _():
-            copy_of(item + AHEAD).start()
+        if not first_call:
+            copy_of(item).wait()
+
+            @pl.when(item + AHEAD < items)
+            def _():
+                copy_of(item + AHEAD).start()
 
         acc_left = [None, None]
         acc_right = [None] * 4
@@ -332,7 +378,8 @@
         for r in range(2):
             for i in range(2):
                 for j in range(2):
-                    tile = held[item, 4 * r + 2 * i + j]
+                    m = 4 * r + 2 * i + j
+                    tile = observed[slot, t, m] if first_call else held[item, m]
                     tile = tile * kept
                     rj = 2 * r + j
                     left = dot(ys[rj], tile, NT)
@@ -359,47 +406,53 @@
     if first_call:
         prior = prior + start[...]
         counts = counts_mine[...]
+        ids_other, flags_other = rows_other[64 + 8 * dumps], rows_other[65 + 8 * dumps]
         pair_lane = lax.broadcasted_iota(jnp.int32, (8, 128), 1)
         for k in range(pair_count):
-            theirs = jnp.where(ints_other[0:1, :] == k, ints_other[1:2, :], 0).astype(F32)
+            theirs = jnp.where(ids_other == float(k), flags_other, 0.0)
             total_flags = jnp.sum(theirs, axis=1, keepdims=True)
             counts = counts + jnp.where(pair_lane == k, total_flags, 0.0)
         counts_ref[...] = counts
     out_ref[:, at_own] += prior
 
 
-def data_part(geometry, table, flags, observed, coh, fields):
+def data_part(geometry, table, flags, observed, coh, masks, fields):
     block, pairs, dumps, penalty, chan_count, stations = geometry
     slots = observed.shape[0]
     first_call = len(fields) > 2
-    joined = len(fields) == 4
+    joined = len(fields) == 3
     body = functools.partial(
         data_kernel, block, pairs, dumps, slots, penalty, chan_count, first_call, joined
     )
     shapes = [shape(64, stations)]
     if first_call:
         shapes += [shape(64, stations), shape(8 * dumps, stations), shape(8, 128)]
+        place, copies = vmem_specs(1), []
+    else:
+        place = [pl.BlockSpec(memory_space=pl.ANY)]
+        copies = [
+            pltpu.VMEM((slots * dumps,) + observed.shape[2:], BF16),
+            pltpu.SemaphoreType.DMA((slots * dumps,)),
+        ]
     return pl.pallas_call(
         body,
         name="data_part",
         out_shape=tuple(shapes),
-        in_specs=smem_specs(2) + [pl.BlockSpec(memory_space=pl.ANY)] + vmem_specs(1 + len(fields)),
+        in_specs=smem_specs(2) + place + vmem_specs(2 + len(fields)),
         out_specs=tuple(vmem_specs(len(shapes))),
-        scratch_shapes=[
-            pltpu.VMEM((slots * dumps,) + observed.shape[2:], BF16),
-            pltpu.SemaphoreType.DMA((slots * dumps,)),
+        scratch_shapes=copies
+        + [
             pltpu.SMEM((slots,), jnp.int32),
-            pltpu.VMEM((2, block, block), BF16),
             pltpu.VMEM((dumps, 2, 64, stations), BF16),
             pltpu.VMEM((dumps, 4, 64, stations), BF16),
             pltpu.VMEM((dumps, 2, 32, stations), F32),
             pltpu.VMEM((dumps, 4, 32, stations), F32),
         ],
-        compiler_params=params(),
+        compiler_params=params() if first_call else params(COPY_BYTES),
         cost_estimate=pl.CostEstimate(
             flops=6000000000, bytes_accessed=8000000, transcendentals=0
         ),
-    )(table, flags, observed, coh, *fields)
+    )(table, flags, observed, coh, masks, *fields)
 
 
 def fold_gram(high_low, other, rows):
@@ -808,23 +861,25 @@
     observed = observed.reshape((slots,) + observed.shape[2:])
     duals_raw = duals.reshape(entries * dirs, 1, block)
     prior = prior_coeffs.reshape(entries * dirs, 4, block)
-    rows = jnp.concatenate(
-        [gains.reshape(entries * dirs, 1, block), delays.reshape(dumps * dirs, 1, block)]
+    masks = baseline_masks(block)
+    rows = field_rows(
+        masks,
+        gains.reshape(entries * dirs, 1, block),
+        delays.reshape(dumps * dirs, block),
+        pair_table.reshape(1, slots),
+        flag_rows.reshape(1, slots),
     )
-    ints = jnp.stack([pair_table, flag_rows])
     if stn_count == 2:
         fields = (rows, other_stations(rows))
-        ints_other = other_stations(ints)
     else:
         fields = (lax.all_gather(rows, "stn", axis=2, tiled=True),)
-        ints_other = lax.all_gather(ints, "stn", axis=1, tiled=True)
     duals_own, start, coh, counts = prepare(
         geometry, pair_table, flag_rows, duals_raw, prior, brightness
     )
     if stn_count != 2:
         counts = jnp.zeros_like(counts)
-    data = functools.partial(data_part, geometry, pair_table, flag_rows, observed, coh)
-    share, current, delay_all, counts = data(fields + (start, counts, ints_other))
+    data = functools.partial(data_part, geometry, pair_table, flag_rows, observed, coh, masks)
+    share, current, delay_all, counts = data(fields + (start, counts))
     shares = both_stations(share, stn_count)
 
     step = before = None

time: 85.2 us -> 79.1 us (0.928)
  Pallas kernels: 37.4 us -> 28.7 us
  starting transfers between devices: 21.9 us -> 30.5 us
  local copies, waits for them, and re-layouts: 4.53 us -> 0.83 us
  other arithmetic: 1.61 us -> 0.02 us
  waiting for transfers between devices: 20.1 us -> 18.6 us
    ppermute x5 -> x4, starting transfers between devices: 3.23 us -> 12.6 us  [other_stations(): return lax.ppermute(value, 'stn', [(0, 1), (1, 0)])]
    pallas_call x3, Pallas kernels: 17.9 us -> 9.1 us  [data_part(): pl.pallas_call(body, name='data_part', out_shape=tuple(shapes), in_specs=...]
    unnamed x14 -> x18, local copies, waits for them, and re-layouts: 3.8 us -> 0.83 us
    concatenate x1 -> x0, other arithmetic: 0.91 us -> none  [shards(): jnp.concatenate([gains.reshape(entries * dirs, 1, block), delays.reshape(...]
    all_to_all x2, waiting for transfers between devices: 2.06 us -> 1.18 us  [shards(): sums = lax.all_to_all(sums, ('chan', 'stn'), 0, 0, tiled=True)]
    ppermute x5 -> x4, waiting for transfers between devices: 1.83 us -> 1.76 us  [other_stations(): return lax.ppermute(value, 'stn', [(0, 1), (1, 0)])]
  transfers between devices with their start and end apart: 15 -> 14, of which waited for: 11 -> 9; matrix products, arithmetic and copies ran while one was open for 1% -> 0% of each run, Pallas kernels for 30% -> 26%
where the time goes in v4:
time: 79.1 us; the launch traced here: 79.4 us
  starting transfers between devices  30.5 us (39%)
  Pallas kernels  28.7 us (36%)
  waiting for transfers between devices  18.6 us (24%)
  between operations  0.84 us (1%)
  local copies, waits for them, and re-layouts  0.83 us (1%)
    ppermute x8, waiting for transfers between devices, swap(): return lax.ppermute(value, 'chan', [(i, i ^ offset) for i in range(count)])  15.6 us
    ppermute x4, starting transfers between devices, other_stations(): return lax.ppermute(value, 'stn', [(0, 1), (1, 0)])  12.6 us
    pallas_call x3, Pallas kernels, gradient_part(): pl.pallas_call(functools.partial(gradient_kernel, block, pairs, dumps, pe...  12.3 us
    all_to_all x2, starting transfers between devices, shards(): sums = lax.all_to_all(sums, ('chan', 'stn'), 0, 0, tiled=True)  10.1 us
    pallas_call x3, Pallas kernels, data_part(): pl.pallas_call(body, name='data_part', out_shape=tuple(shapes), in_specs=...  9.1 us
    ppermute x8, starting transfers between devices, swap(): return lax.ppermute(value, 'chan', [(i, i ^ offset) for i in range(count)])  7.81 us
    pallas_call x3, Pallas kernels, curvature_part(): pl.pallas_call(functools.partial(curvature_kernel, block, pairs, dumps, p...  4.71 us
    ppermute x4, waiting for transfers between devices, other_stations(): return lax.ppermute(value, 'stn', [(0, 1), (1, 0)])  1.76 us
  transfers between devices with their start and end apart: 14, of which 9 were waited for; matrix products, arithmetic and copies ran while one was open for 0% of the time, Pallas kernels for 26%

profile of v4, /device:TPU:0, one launch (start us, length us, event | category | flops | bytes accessed | tf_op | source)
XLA Modules:
  0.0 79.4 jit_solution(17484282093667338905)
XLA Ops:
  0.7 0.0 slice-start
  0.7 0.6 copy-done.3
  1.3 0.0 copy-done.4
  1.3 0.1 copy-done.6
  1.4 0.1 copy-done.5
  1.6 3.0 %collective-permute-start = (f32[82,1,256]{2,1,0:T(1,128)S(1)}, f32[82,1,256]{2,1,0:T(1,128)S(1)}, u32[]{:S(2)}, u32[]{:S(2)}) collective-permute-start(f32[82,1,256]{2,1,0:T(1,128)S(1)} %field_rows.1.refs_5_), channel_id=1, source_target_pairs={{0,1},{1,0},{2,3},{3,2},{4,5},{5,4},{6,7},{7,6},{8,9},{9,8},{10,11... | collective-permute-start | bytes 251912 | tf_op jit(solution)/shard_map/ppermute | solution.py:842
  4.6 0.0 copy-done
  4.6 0.7 prepare.1
  5.3 1.7 %collective-permute-done.refs_6_ = f32[82,1,256]{2,1,0:T(1,128)S(1)} collective-permute-done((f32[82,1,256]{2,1,0:T(1,128)S(1)}, f32[82,1,256]{2,1,0:T(1,128)S(1)}, u32[]{:S(2)}, u32[]{:S(2)}) %collective-permute-start) | collective-permute-done | bytes 84000 | tf_op jit(solution)/shard_map/ppermute | solution.py:842
  7.1 2.3 %data_part.3 = (f32[64,512]{1,0:T(8,128)S(1)}, f32[64,512]{1,0:T(8,128)S(1)}, f32[16,512]{1,0:T(8,128)S(1)}, f32[8,128]{1,0:T(8,128)S(1)}) custom-call(s32[4]{0:T(128)S(1)} %copy-done.3, s32[4]{0:T(128)S(1)} %copy-done.4, bf16[4,2,8,256,256]{4,3,2,1,0:T(8,128)(2,1)S(1)} %bitcast.28, f32[64,128]{1,0:T(8,128)S(1)} %get-tuple-element.41.refs_3_.refs_2_, ...), custom_call_target="tpu_custom_call" | custom-call | flops 6000000000 | bytes 8000000 | tf_op jit(solution)/shard_map/data_part/pallas_call | solution.py:437
  9.4 3.3 %collective-permute-start.1 = (f32[64,512]{1,0:T(8,128)S(1)}, f32[64,512]{1,0:T(8,128)S(1)}, u32[]{:S(2)}, u32[]{:S(2)}) collective-permute-start(f32[64,512]{1,0:T(8,128)S(1)} %get-tuple-element.50.refs_6_), channel_id=1, source_target_pairs={{0,1},{1,0},{2,3},{3,2},{4,5},{5,4},{6,7},{7,6},{8,9},{9,8},{10,11... | collective-permute-start | bytes 393224 | tf_op jit(solution)/shard_map/ppermute | solution.py:842
  12.7 4.0 %gradient_part.3 = (f32[64,512]{1,0:T(8,128)S(1)}, bf16[2,2,64,512]{3,2,1,0:T(8,128)(2,1)S(1)}, bf16[2,4,64,512]{3,2,1,0:T(8,128)(2,1)S(1)}) custom-call(f32[8,128]{1,0:T(8,128)S(1)} %get-tuple-element.44.refs_0_, f32[16,512]{1,0:T(8,128)S(1)} %get-tuple-element.45.refs_1_.refs_6_, f32[64,128]{1,0:T(8,128)S(1)} %get-tuple-element.41.refs_3_.refs_2_, ...), custom_call_target="tpu_custom_call" | custom-call | flops 4000000000 | bytes 2000000 | tf_op jit(solution)/shard_map/gradient_part/pallas_call | solution.py:617
  16.7 0.0 collective-permute-done.1.refs_7_
  16.7 1.6 %curvature_part.3 = (f32[64,512]{1,0:T(8,128)S(1)}, f32[64,512]{1,0:T(8,128)S(1)}, f32[32,128]{1,0:T(8,128)}) custom-call(f32[8,128]{1,0:T(8,128)S(1)} %get-tuple-element.44.refs_0_, f32[16,512]{1,0:T(8,128)S(1)} %get-tuple-element.45.refs_1_.refs_6_, f32[64,128]{1,0:T(8,128)S(1)} %get-tuple-element.41.refs_3_.refs_2_, ...), custom_call_target="tpu_custom_call" | custom-call | flops 2000000000 | bytes 2000000 | tf_op jit(solution)/shard_map/curvature_part/pallas_call | solution.py:724
  18.3 5.3 %all-to-all-start = ((f32[32,1,128]{2,1,0:T(1,128)}), f32[32,1,128]{2,1,0:T(1,128)S(1)}, u32[]{:S(2)}, u32[]{:S(2)}) async-start(f32[32,1,128]{2,1,0:T(1,128)} %bitcast.8), calls=%async_computation | async-start | bytes 32768 | tf_op jit(solution)/shard_map/all_to_all | solution.py:905
  23.7 3.3 %data_part.4.refs_6_ = f32[64,512]{1,0:T(8,128)S(1)} custom-call(s32[4]{0:T(128)S(1)} %copy-done.3, s32[4]{0:T(128)S(1)} %copy-done.4, bf16[4,2,8,256,256]{4,3,2,1,0:T(8,128)(2,1)} %bitcast.24, f32[64,128]{1,0:T(8,128)S(1)} %get-tuple-element.41.refs_3_.refs_2_, bf16[2,256,256]{2,1,0:T(8,128)(2,1)S(1)} %baseline_masks.1.masks.refs_4_, ...), custom_call_target="tpu_custom_call" | custom-call | flops 6000000000 | bytes 8000000 | tf_op jit(solution)/shard_map/data_part/pallas_call | solution.py:437
  27.0 3.1 %collective-permute-start.2 = (f32[64,512]{1,0:T(8,128)S(1)}, f32[64,512]{1,0:T(8,128)S(1)}, u32[]{:S(2)}, u32[]{:S(2)}) collective-permute-start(f32[64,512]{1,0:T(8,128)S(1)} %data_part.4.refs_6_), channel_id=1, source_target_pairs={{0,1},{1,0},{2,3},{3,2},{4,5},{5,4},{6,7},{7,6},{8,9},{9,8},{10,11... | collective-permute-start | bytes 393224 | tf_op jit(solution)/shard_map/ppermute | solution.py:842
  30.1 0.7 all-to-all-done
  30.8 4.2 %gradient_part.4 = (f32[64,512]{1,0:T(8,128)S(1)}, f32[64,512]{1,0:T(8,128)S(1)}, f32[8,128]{1,0:T(8,128)S(1)}, bf16[2,2,64,512]{3,2,1,0:T(8,128)(2,1)S(1)}, bf16[2,4,64,512]{3,2,1,0:T(8,128)(2,1)S(1)}) custom-call(f32[8,128]{1,0:T(8,128)S(1)} %get-tuple-element.44.refs_0_, f32[16,512]{1,0:T(8,128)S(1)} %get-tuple-element.45.refs_1_.refs_6_, ...), custom_call_target="tpu_custom_call" | custom-call | flops 4000000000 | bytes 2000000 | tf_op jit(solution)/shard_map/gradient_part/pallas_call | solution.py:617
  34.9 0.0 collective-permute-done.2.refs_7_
  35.0 1.6 %curvature_part.4 = (f32[64,512]{1,0:T(8,128)S(1)}, f32[64,512]{1,0:T(8,128)S(1)}, f32[32,128]{1,0:T(8,128)}) custom-call(f32[8,128]{1,0:T(8,128)S(1)} %get-tuple-element.44.refs_0_, f32[16,512]{1,0:T(8,128)S(1)} %get-tuple-element.45.refs_1_.refs_6_, f32[64,128]{1,0:T(8,128)S(1)} %get-tuple-element.41.refs_3_.refs_2_, ...), custom_call_target="tpu_custom_call" | custom-call | flops 2000000000 | bytes 2000000 | tf_op jit(solution)/shard_map/curvature_part/pallas_call | solution.py:724
  36.5 4.8 %all-to-all-start.1 = ((f32[32,1,128]{2,1,0:T(1,128)}), f32[32,1,128]{2,1,0:T(1,128)S(1)}, u32[]{:S(2)}, u32[]{:S(2)}) async-start(f32[32,1,128]{2,1,0:T(1,128)} %bitcast.11), calls=%async_computation.1 | async-start | bytes 32768 | tf_op jit(solution)/shard_map/all_to_all | solution.py:905
  41.3 3.5 %data_part.5.refs_6_ = f32[64,512]{1,0:T(8,128)S(1)} custom-call(s32[4]{0:T(128)S(1)} %copy-done.3, s32[4]{0:T(128)S(1)} %copy-done.4, bf16[4,2,8,256,256]{4,3,2,1,0:T(8,128)(2,1)} %bitcast.25, f32[64,128]{1,0:T(8,128)S(1)} %get-tuple-element.41.refs_3_.refs_2_, bf16[2,256,256]{2,1,0:T(8,128)(2,1)S(1)} %baseline_masks.1.masks.refs_4_, ...), custom_call_target="tpu_custom_call" | custom-call | flops 6000000000 | bytes 8000000 | tf_op jit(solution)/shard_map/data_part/pallas_call | solution.py:437
  44.8 3.1 %collective-permute-start.3 = (f32[64,512]{1,0:T(8,128)S(1)}, f32[64,512]{1,0:T(8,128)S(1)}, u32[]{:S(2)}, u32[]{:S(2)}) collective-permute-start(f32[64,512]{1,0:T(8,128)S(1)} %data_part.5.refs_6_), channel_id=1, source_target_pairs={{0,1},{1,0},{2,3},{3,2},{4,5},{5,4},{6,7},{7,6},{8,9},{9,8},{10,11... | collective-permute-start | bytes 393224 | tf_op jit(solution)/shard_map/ppermute | solution.py:842
  47.9 0.5 all-to-all-done.1
  48.4 4.2 %gradient_part.5 = (f32[64,512]{1,0:T(8,128)S(1)}, f32[64,512]{1,0:T(8,128)S(1)}, f32[8,128]{1,0:T(8,128)S(1)}, bf16[2,2,64,512]{3,2,1,0:T(8,128)(2,1)S(1)}, bf16[2,4,64,512]{3,2,1,0:T(8,128)(2,1)S(1)}) custom-call(f32[8,128]{1,0:T(8,128)S(1)} %get-tuple-element.44.refs_0_, f32[16,512]{1,0:T(8,128)S(1)} %get-tuple-element.45.refs_1_.refs_6_, ...), custom_call_target="tpu_custom_call" | custom-call | flops 4000000000 | bytes 2000000 | tf_op jit(solution)/shard_map/gradient_part/pallas_call | solution.py:617
  52.6 0.0 collective-permute-done.3.refs_7_
  52.6 1.6 %curvature_part.5 = (f32[64,512]{1,0:T(8,128)S(1)}, f32[72,128]{1,0:T(8,128)S(1)}, f32[72,128]{1,0:T(8,128)S(1)}, f32[72,128]{1,0:T(8,128)S(1)}, f32[72,128]{1,0:T(8,128)S(1)}) custom-call(f32[8,128]{1,0:T(8,128)S(1)} %get-tuple-element.44.refs_0_, f32[16,512]{1,0:T(8,128)S(1)} %get-tuple-element.45.refs_1_.refs_6_, ...), custom_call_target="tpu_custom_call" | custom-call | flops 2000000000 | bytes 2000000 | tf_op jit(solution)/shard_map/curvature_part/pallas_call | solution.py:724
  54.2 0.1 collective-permute-start.4
  54.3 1.0 %collective-permute-start.5 = (f32[72,128]{1,0:T(8,128)S(1)}, f32[72,128]{1,0:T(8,128)S(1)}, u32[]{:S(2)}, u32[]{:S(2)}) collective-permute-start(f32[72,128]{1,0:T(8,128)S(1)} %get-tuple-element.70), channel_id=1, source_target_pairs={{0,4},{2,6},{4,0},{6,2},{8,12},{10,14},{12,8},{14,10},{16,20},{18,... | collective-permute-start | bytes 110600 | tf_op jit(solution)/shard_map/ppermute | solution.py:838
  55.3 0.8 %collective-permute-start.6 = (f32[72,128]{1,0:T(8,128)S(1)}, f32[72,128]{1,0:T(8,128)S(1)}, u32[]{:S(2)}, u32[]{:S(2)}) collective-permute-start(f32[72,128]{1,0:T(8,128)S(1)} %get-tuple-element.71), channel_id=1, source_target_pairs={{0,6},{2,4},{4,2},{6,0},{8,14},{10,12},{12,10},{14,8},{16,22},{18,... | collective-permute-start | bytes 110600 | tf_op jit(solution)/shard_map/ppermute | solution.py:838
  56.1 0.0 collective-permute-done.4.refs_1_
  56.1 2.3 %collective-permute-done.5.refs_2_ = f32[72,128]{1,0:T(8,128)S(1)} collective-permute-done((f32[72,128]{1,0:T(8,128)S(1)}, f32[72,128]{1,0:T(8,128)S(1)}, u32[]{:S(2)}, u32[]{:S(2)}) %collective-permute-start.5) | collective-permute-done | bytes 36896 | tf_op jit(solution)/shard_map/ppermute | solution.py:838
  58.4 0.4 collective-permute-done.6.refs_3_
  58.7 0.1 weigh.1
  58.8 1.5 %collective-permute-start.7 = (f32[264,128]{1,0:T(8,128)S(1)}, f32[264,128]{1,0:T(8,128)S(1)}, u32[]{:S(2)}, u32[]{:S(2)}) collective-permute-start(f32[264,128]{1,0:T(8,128)S(1)} %weigh.1), channel_id=1, source_target_pairs={{0,8},{2,10},{4,12},{6,14},{8,0},{10,2},{12,4},{14,6},{16,24},{18,... | collective-permute-start | bytes 405512 | tf_op jit(solution)/shard_map/ppermute | solution.py:838
  60.3 4.2 %collective-permute-done.7 = f32[264,128]{1,0:T(8,128)S(1)} collective-permute-done((f32[264,128]{1,0:T(8,128)S(1)}, f32[264,128]{1,0:T(8,128)S(1)}, u32[]{:S(2)}, u32[]{:S(2)}) %collective-permute-start.7) | collective-permute-done | bytes 135200 | tf_op jit(solution)/shard_map/ppermute | solution.py:838
  64.5 2.4 %collective-permute-start.8 = (f32[264,128]{1,0:T(8,128)S(1)}, f32[264,128]{1,0:T(8,128)S(1)}, u32[]{:S(2)}, u32[]{:S(2)}) collective-permute-start(f32[264,128]{1,0:T(8,128)S(1)} %add.3.one), channel_id=1, source_target_pairs={{0,16},{2,18},{4,20},{6,22},{8,24},{10,26},{12,28},{14,30},{16,0},... | collective-permute-start | bytes 405512 | tf_op jit(solution)/shard_map/ppermute | solution.py:838
  67.0 6.2 %collective-permute-done.8.two = f32[264,128]{1,0:T(8,128)S(1)} collective-permute-done((f32[264,128]{1,0:T(8,128)S(1)}, f32[264,128]{1,0:T(8,128)S(1)}, u32[]{:S(2)}, u32[]{:S(2)}) %collective-permute-start.8) | collective-permute-done | bytes 135200 | tf_op jit(solution)/shard_map/ppermute | solution.py:838
  73.2 0.2 combine.1
  73.4 0.1 collective-permute-start.11
  73.5 1.1 %collective-permute-start.10 = (f32[128,128]{1,0:T(8,128)S(1)}, f32[128,128]{1,0:T(8,128)S(1)}, u32[]{:S(2)}, u32[]{:S(2)}) collective-permute-start(f32[128,128]{1,0:T(8,128)S(1)} %get-tuple-element.75.own), channel_id=1, source_target_pairs={{0,4},{2,6},{4,0},{6,2},{8,12},{10,14},{12,8},{14,10},{16,20},{18,... | collective-permute-start | bytes 196616 | tf_op jit(solution)/shard_map/ppermute | solution.py:838
  74.6 0.7 collective-permute-start.9
  75.3 0.7 last_step.1
  76.0 1.7 %collective-permute-done.11.both = f32[128,128]{1,0:T(8,128)S(1)} collective-permute-done((f32[128,128]{1,0:T(8,128)S(1)}, f32[128,128]{1,0:T(8,128)S(1)}, u32[]{:S(2)}, u32[]{:S(2)}) %collective-permute-start.11) | collective-permute-done | bytes 65568 | tf_op jit(solution)/shard_map/ppermute | solution.py:838
  77.8 0.8 %collective-permute-done.10.row = f32[128,128]{1,0:T(8,128)S(1)} collective-permute-done((f32[128,128]{1,0:T(8,128)S(1)}, f32[128,128]{1,0:T(8,128)S(1)}, u32[]{:S(2)}, u32[]{:S(2)}) %collective-permute-start.10) | collective-permute-done | bytes 65568 | tf_op jit(solution)/shard_map/ppermute | solution.py:838
  78.6 0.0 collective-permute-done.9.core
  78.6 0.8 %consensus.1 = (f32[64,4,256]{2,1,0:T(4,128)}, f32[64,1,256]{2,1,0:T(1,128)}) custom-call(f32[128,128]{1,0:T(8,128)S(1)} %get-tuple-element.75.own, f32[128,128]{1,0:T(8,128)S(1)} %collective-permute-done.9.core, f32[128,128]{1,0:T(8,128)S(1)} %collective-permute-done.10.row, f32[128,128]{1,0:T(8,128)S(1)} %collective-permute-done.11.both, ...), custom_call_target="tpu_custom_call" | custom-call | tf_op jit(solution)/shard_map/consensus/pallas_call | solution.py:827
  (16 shorter events, 0.1 us)
Async XLA Ops:
  0.6 0.7 copy-start.3
  0.6 0.7 copy-start.4
  0.7 0.7 copy-start.6
  0.7 0.9 %copy-start.5 = (f32[8,8,1,256]{3,2,1,0:T(1,128)S(1)}, f32[8,8,1,256]{3,2,1,0:T(1,128)}, u32[]{:S(2)}) copy-start(f32[8,8,1,256]{3,2,1,0:T(1,128)} %param.11) | copy-start | bytes 196612
  0.7 6.4 %slice-start = ((s8[8388608]{0:T(1024)(128)(4,1)}), s8[4194304]{0:T(1024)(128)(4,1)S(1)}, s32[]{:S(2)}) async-start(s8[8388608]{0:T(1024)(128)(4,1)} %bitcast.26), calls=%async_computation.2 | async-start | bytes 8388608
  1.5 3.1 %copy-start = (f32[8,8,4,256]{3,2,1,0:T(4,128)S(1)}, f32[8,8,4,256]{3,2,1,0:T(4,128)}, u32[]{:S(2)}) copy-start(f32[8,8,4,256]{3,2,1,0:T(4,128)} %param.13) | copy-start | bytes 786436
  1.5 3.1 %copy-start.1 = (f32[8,8,1,256]{3,2,1,0:T(1,128)S(1)}, f32[8,8,1,256]{3,2,1,0:T(1,128)}, u32[]{:S(2)}) copy-start(f32[8,8,1,256]{3,2,1,0:T(1,128)} %param.12) | copy-start | bytes 196612
  1.5 3.1 %copy-start.2 = (f32[8,8]{1,0:T(8,128)S(1)}, f32[8,8]{1,0:T(8,128)}, u32[]{:S(2)}) copy-start(f32[8,8]{1,0:T(8,128)} %refs_4_.1) | copy-start | bytes 772
  1.5 5.5 %slice-start.1 = ((s8[8388608]{0:T(1024)(128)(4,1)}), s8[4194304]{0:T(1024)(128)(4,1)S(1)}, s32[]{:S(2)}) async-start(s8[8388608]{0:T(1024)(128)(4,1)} %bitcast.26), calls=%async_computation.3 | async-start | bytes 8388608
  1.6 5.5 %collective-permute-start = (f32[82,1,256]{2,1,0:T(1,128)S(1)}, f32[82,1,256]{2,1,0:T(1,128)S(1)}, u32[]{:S(2)}, u32[]{:S(2)}) collective-permute-start(f32[82,1,256]{2,1,0:T(1,128)S(1)} %field_rows.1.refs_5_), channel_id=1, source_target_pairs={{0,1},{1,0},{2,3},{3,2},{4,5},{5,4},{6,7},{7,6},{8,9},{9,8},{10,11... | collective-permute-start | bytes 251912 | tf_op jit(solution)/shard_map/ppermute | solution.py:842
  9.4 7.3 %collective-permute-start.1 = (f32[64,512]{1,0:T(8,128)S(1)}, f32[64,512]{1,0:T(8,128)S(1)}, u32[]{:S(2)}, u32[]{:S(2)}) collective-permute-start(f32[64,512]{1,0:T(8,128)S(1)} %get-tuple-element.50.refs_6_), channel_id=1, source_target_pairs={{0,1},{1,0},{2,3},{3,2},{4,5},{5,4},{6,7},{7,6},{8,9},{9,8},{10,11... | collective-permute-start | bytes 393224 | tf_op jit(solution)/shard_map/ppermute | solution.py:842
  18.3 12.5 %all-to-all-start = ((f32[32,1,128]{2,1,0:T(1,128)}), f32[32,1,128]{2,1,0:T(1,128)S(1)}, u32[]{:S(2)}, u32[]{:S(2)}) async-start(f32[32,1,128]{2,1,0:T(1,128)} %bitcast.8), calls=%async_computation | async-start | bytes 32768 | tf_op jit(solution)/shard_map/all_to_all | solution.py:905
  27.0 8.0 %collective-permute-start.2 = (f32[64,512]{1,0:T(8,128)S(1)}, f32[64,512]{1,0:T(8,128)S(1)}, u32[]{:S(2)}, u32[]{:S(2)}) collective-permute-start(f32[64,512]{1,0:T(8,128)S(1)} %data_part.4.refs_6_), channel_id=1, source_target_pairs={{0,1},{1,0},{2,3},{3,2},{4,5},{5,4},{6,7},{7,6},{8,9},{9,8},{10,11... | collective-permute-start | bytes 393224 | tf_op jit(solution)/shard_map/ppermute | solution.py:842
  36.5 11.9 %all-to-all-start.1 = ((f32[32,1,128]{2,1,0:T(1,128)}), f32[32,1,128]{2,1,0:T(1,128)S(1)}, u32[]{:S(2)}, u32[]{:S(2)}) async-start(f32[32,1,128]{2,1,0:T(1,128)} %bitcast.11), calls=%async_computation.1 | async-start | bytes 32768 | tf_op jit(solution)/shard_map/all_to_all | solution.py:905
  44.8 7.8 %collective-permute-start.3 = (f32[64,512]{1,0:T(8,128)S(1)}, f32[64,512]{1,0:T(8,128)S(1)}, u32[]{:S(2)}, u32[]{:S(2)}) collective-permute-start(f32[64,512]{1,0:T(8,128)S(1)} %data_part.5.refs_6_), channel_id=1, source_target_pairs={{0,1},{1,0},{2,3},{3,2},{4,5},{5,4},{6,7},{7,6},{8,9},{9,8},{10,11... | collective-permute-start | bytes 393224 | tf_op jit(solution)/shard_map/ppermute | solution.py:842
  54.2 1.9 %collective-permute-start.4 = (f32[72,128]{1,0:T(8,128)S(1)}, f32[72,128]{1,0:T(8,128)S(1)}, u32[]{:S(2)}, u32[]{:S(2)}) collective-permute-start(f32[72,128]{1,0:T(8,128)S(1)} %get-tuple-element.69), channel_id=1, source_target_pairs={{0,2},{2,0},{4,6},{6,4},{8,10},{10,8},{12,14},{14,12},{16,18},{18,... | collective-permute-start | bytes 110600 | tf_op jit(solution)/shard_map/ppermute | solution.py:838
  54.3 4.1 %collective-permute-start.5 = (f32[72,128]{1,0:T(8,128)S(1)}, f32[72,128]{1,0:T(8,128)S(1)}, u32[]{:S(2)}, u32[]{:S(2)}) collective-permute-start(f32[72,128]{1,0:T(8,128)S(1)} %get-tuple-element.70), channel_id=1, source_target_pairs={{0,4},{2,6},{4,0},{6,2},{8,12},{10,14},{12,8},{14,10},{16,20},{18,... | collective-permute-start | bytes 110600 | tf_op jit(solution)/shard_map/ppermute | solution.py:838
  55.3 3.5 %collective-permute-start.6 = (f32[72,128]{1,0:T(8,128)S(1)}, f32[72,128]{1,0:T(8,128)S(1)}, u32[]{:S(2)}, u32[]{:S(2)}) collective-permute-start(f32[72,128]{1,0:T(8,128)S(1)} %get-tuple-element.71), channel_id=1, source_target_pairs={{0,6},{2,4},{4,2},{6,0},{8,14},{10,12},{12,10},{14,8},{16,22},{18,... | collective-permute-start | bytes 110600 | tf_op jit(solution)/shard_map/ppermute | solution.py:838
  58.8 5.7 %collective-permute-start.7 = (f32[264,128]{1,0:T(8,128)S(1)}, f32[264,128]{1,0:T(8,128)S(1)}, u32[]{:S(2)}, u32[]{:S(2)}) collective-permute-start(f32[264,128]{1,0:T(8,128)S(1)} %weigh.1), channel_id=1, source_target_pairs={{0,8},{2,10},{4,12},{6,14},{8,0},{10,2},{12,4},{14,6},{16,24},{18,... | collective-permute-start | bytes 405512 | tf_op jit(solution)/shard_map/ppermute | solution.py:838
  64.5 8.7 %collective-permute-start.8 = (f32[264,128]{1,0:T(8,128)S(1)}, f32[264,128]{1,0:T(8,128)S(1)}, u32[]{:S(2)}, u32[]{:S(2)}) collective-permute-start(f32[264,128]{1,0:T(8,128)S(1)} %add.3.one), channel_id=1, source_target_pairs={{0,16},{2,18},{4,20},{6,22},{8,24},{10,26},{12,28},{14,30},{16,0},... | collective-permute-start | bytes 405512 | tf_op jit(solution)/shard_map/ppermute | solution.py:838
  73.4 4.4 %collective-permute-start.11 = (f32[128,128]{1,0:T(8,128)S(1)}, f32[128,128]{1,0:T(8,128)S(1)}, u32[]{:S(2)}, u32[]{:S(2)}) collective-permute-start(f32[128,128]{1,0:T(8,128)S(1)} %get-tuple-element.75.own), channel_id=1, source_target_pairs={{0,6},{2,4},{4,2},{6,0},{8,14},{10,12},{12,10},{14,8},{16,22},{18,... | collective-permute-start | bytes 196616 | tf_op jit(solution)/shard_map/ppermute | solution.py:838
  73.5 5.1 %collective-permute-start.10 = (f32[128,128]{1,0:T(8,128)S(1)}, f32[128,128]{1,0:T(8,128)S(1)}, u32[]{:S(2)}, u32[]{:S(2)}) collective-permute-start(f32[128,128]{1,0:T(8,128)S(1)} %get-tuple-element.75.own), channel_id=1, source_target_pairs={{0,4},{2,6},{4,0},{6,2},{8,12},{10,14},{12,8},{14,10},{16,20},{18,... | collective-permute-start | bytes 196616 | tf_op jit(solution)/shard_map/ppermute | solution.py:838
  74.6 4.0 %collective-permute-start.9 = (f32[128,128]{1,0:T(8,128)S(1)}, f32[128,128]{1,0:T(8,128)S(1)}, u32[]{:S(2)}, u32[]{:S(2)}) collective-permute-start(f32[128,128]{1,0:T(8,128)S(1)} %get-tuple-element.75.own), channel_id=1, source_target_pairs={{0,2},{2,0},{4,6},{6,4},{8,10},{10,8},{12,14},{14,12},{16,18},{18,... | collective-permute-start | bytes 196616 | tf_op jit(solution)/shard_map/ppermute | solution.py:838

commit v5 on v4

--- a/solution.py
+++ b/solution.py
@@ -304,9 +304,9 @@
             rows_all, *refs = refs
         else:
             rows_mine, rows_other, *refs = refs
-        start, counts_mine, out_ref, field_ref, delay_ref, counts_ref, *refs = refs
+        start, counts_mine, out_ref, field_ref, delay_ref, counts_ref, lead, *refs = refs
     else:
-        field_ref, delay_ref, out_ref, *refs = refs
+        lead, field_ref, delay_ref, out_ref, *refs = refs
     if first_call:
         order, xp, yp, hl, ha = refs
     else:
@@ -326,7 +326,7 @@
         return pltpu.make_async_copy(observed.at[slot, t], held.at[item], sems.at[item])
 
     if not first_call:
-        for item in range(min(AHEAD, slots * dumps)):
+        for item in range(1, min(1 + AHEAD, slots * dumps)):
 
             @pl.when(item < items)
             def _():
@@ -356,7 +356,7 @@
 
     lane = lax.broadcasted_iota(jnp.int32, (1, block), 1)
 
-    def visit(item, unused):
+    def visit(item, tiles):
         slot, t = order[item // dumps], item % dumps
         first, second = pair_blocks(pairs, table[slot])
         kept = keep[jnp.where(first < second, 1, 0)]
@@ -364,13 +364,6 @@
         live16 = live.astype(BF16)
         at_p = pl.ds(pl.multiple_of(first * block, CHUNK), block)
         at_q = pl.ds(pl.multiple_of(second * block, CHUNK), block)
-        if not first_call:
-            copy_of(item).wait()
-
-            @pl.when(item + AHEAD < items)
-            def _():
-                copy_of(item + AHEAD).start()
-
         acc_left = [None, None]
         acc_right = [None] * 4
         xs = [xp[t, i, :, at_p] * live16 for i in range(2)]
@@ -378,9 +371,7 @@
         for r in range(2):
             for i in range(2):
                 for j in range(2):
-                    m = 4 * r + 2 * i + j
-                    tile = observed[slot, t, m] if first_call else held[item, m]
-                    tile = tile * kept
+                    tile = tiles[4 * r + 2 * i + j] * kept
                     rj = 2 * r + j
                     left = dot(ys[rj], tile, NT)
                     right = dot(xs[i], tile, NN)
@@ -390,9 +381,34 @@
             hl[t, i, :, at_p] += (acc_left[i][:32] + acc_left[i][32:]) * live
         for rj in range(4):
             ha[t, rj, :, at_q] += acc_right[rj][:32] + acc_right[rj][32:]
+
+    def visit_held(item, unused):
+        copy_of(item).wait()
+
+        @pl.when(item + AHEAD < items)
+        def _():
+            copy_of(item + AHEAD).start()
+
+        visit(item, held.at[item])
         return unused
 
-    lax.fori_loop(0, items, visit, jnp.int32(0))
+    def visit_there(item, unused):
+        visit(item, observed.at[order[item // dumps], item % dumps])
+        return unused
+
+    if first_call:
+        lax.fori_loop(0, items, visit_there, jnp.int32(0))
+
+        @pl.when(items > 0)
+        def _():
+            lead[...] = observed[order[0], 0]
+    else:
+
+        @pl.when(items > 0)
+        def _():
+            visit(jnp.int32(0), lead)
+
+        lax.fori_loop(1, items, visit_held, jnp.int32(0))
 
     total = None
     for t in range(dumps):
@@ -419,7 +435,7 @@
 def data_part(geometry, table, flags, observed, coh, masks, fields):
     block, pairs, dumps, penalty, chan_count, stations = geometry
     slots = observed.shape[0]
-    first_call = len(fields) > 2
+    first_call = len(fields[0].shape) == 3 and fields[0].dtype == F32
     joined = len(fields) == 3
     body = functools.partial(
         data_kernel, block, pairs, dumps, slots, penalty, chan_count, first_call, joined
@@ -427,6 +443,7 @@
     shapes = [shape(64, stations)]
     if first_call:
         shapes += [shape(64, stations), shape(8 * dumps, stations), shape(8, 128)]
+        shapes.append(shape(*observed.shape[2:], dtype=BF16))
         place, copies = vmem_specs(1), []
     else:
         place = [pl.BlockSpec(memory_space=pl.ANY)]
@@ -879,7 +896,7 @@
     if stn_count != 2:
         counts = jnp.zeros_like(counts)
     data = functools.partial(data_part, geometry, pair_table, flag_rows, observed, coh, masks)
-    share, current, delay_all, counts = data(fields + (start, counts))
+    share, current, delay_all, counts, lead = data(fields + (start, counts))
     shares = both_stations(share, stn_count)
 
     step = before = None
@@ -903,7 +920,7 @@
         if not last:
             linear, sums = rest
             sums = lax.all_to_all(sums, ("chan", "stn"), 0, 0, tiled=True)
-            (share,) = data((direction, delay_all))
+            (share,) = data((lead, direction, delay_all))
             shares = both_stations(share, stn_count)
             step = (sums, direction)
 

time: 79.1 us -> 79 us (level)
  waiting for transfers between devices: 18.6 us -> 21.4 us
  starting transfers between devices: 30.5 us -> 28.8 us
  Pallas kernels: 28.7 us -> 27.5 us
    ppermute x8, waiting for transfers between devices: 15.6 us -> 17.1 us  [swap(): return lax.ppermute(value, 'chan', [(i, i ^ offset) for i in range(count)])]
    all_to_all x2, waiting for transfers between devices: 1.18 us -> 2.47 us  [shards(): sums = lax.all_to_all(sums, ('chan', 'stn'), 0, 0, tiled=True)]
    pallas_call x3, Pallas kernels: 9.1 us -> 7.91 us  [data_part(): pl.pallas_call(body, name='data_part', out_shape=tuple(shapes), in_specs=...]
    ppermute x8, starting transfers between devices: 7.81 us -> 6.74 us  [swap(): return lax.ppermute(value, 'chan', [(i, i ^ offset) for i in range(count)])]
  transfers between devices with their start and end apart: 14 -> 14, of which waited for: 9 -> 8; matrix products, arithmetic and copies ran while one was open for 0% -> 0% of each run, Pallas kernels for 26% -> 24%
where the time goes in v5:
time: 79 us; the launch traced here: 79.3 us
  starting transfers between devices  28.8 us (36%)
  Pallas kernels  27.5 us (35%)
  waiting for transfers between devices  21.4 us (27%)
  local copies, waits for them, and re-layouts  0.83 us (1%)
  between operations  0.83 us (1%)
    ppermute x8, waiting for transfers between devices, swap(): return lax.ppermute(value, 'chan', [(i, i ^ offset) for i in range(count)])  17.1 us
    ppermute x4, starting transfers between devices, other_stations(): return lax.ppermute(value, 'stn', [(0, 1), (1, 0)])  12.6 us
    pallas_call x3, Pallas kernels, gradient_part(): pl.pallas_call(functools.partial(gradient_kernel, block, pairs, dumps, pe...  12.3 us
    all_to_all x2, starting transfers between devices, shards(): sums = lax.all_to_all(sums, ('chan', 'stn'), 0, 0, tiled=True)  9.46 us
    pallas_call x3, Pallas kernels, data_part(): pl.pallas_call(body, name='data_part', out_shape=tuple(shapes), in_specs=...  7.91 us
    ppermute x8, starting transfers between devices, swap(): return lax.ppermute(value, 'chan', [(i, i ^ offset) for i in range(count)])  6.74 us
    pallas_call x3, Pallas kernels, curvature_part(): pl.pallas_call(functools.partial(curvature_kernel, block, pairs, dumps, p...  4.71 us
    all_to_all x2, waiting for transfers between devices, shards(): sums = lax.all_to_all(sums, ('chan', 'stn'), 0, 0, tiled=True)  2.47 us
  transfers between devices with their start and end apart: 14, of which 8 were waited for; matrix products, arithmetic and copies ran while one was open for 0% of the time, Pallas kernels for 24%

profile of v5, /device:TPU:0, one launch (start us, length us, event | category | flops | bytes accessed | tf_op | source)
XLA Modules:
  0.0 79.3 jit_solution(7857994996823526575)
XLA Ops:
  0.6 0.0 copy-start.3
  0.7 0.0 slice-start
  0.7 0.6 copy-done.3
  1.3 0.0 copy-done.4
  1.3 0.1 copy-done.6
  1.4 0.1 copy-done.5
  1.6 3.0 %collective-permute-start = (f32[82,1,256]{2,1,0:T(1,128)S(1)}, f32[82,1,256]{2,1,0:T(1,128)S(1)}, u32[]{:S(2)}, u32[]{:S(2)}) collective-permute-start(f32[82,1,256]{2,1,0:T(1,128)S(1)} %field_rows.1.refs_5_), channel_id=1, source_target_pairs={{0,1},{1,0},{2,3},{3,2},{4,5},{5,4},{6,7},{7,6},{8,9},{9,8},{10,11... | collective-permute-start | bytes 251912 | tf_op jit(solution)/shard_map/ppermute | solution.py:859
  4.6 0.7 prepare.1
  5.3 1.7 %collective-permute-done.refs_6_ = f32[82,1,256]{2,1,0:T(1,128)S(1)} collective-permute-done((f32[82,1,256]{2,1,0:T(1,128)S(1)}, f32[82,1,256]{2,1,0:T(1,128)S(1)}, u32[]{:S(2)}, u32[]{:S(2)}) %collective-permute-start) | collective-permute-done | bytes 84000 | tf_op jit(solution)/shard_map/ppermute | solution.py:859
  7.1 2.4 %data_part.3 = (f32[64,512]{1,0:T(8,128)S(1)}, f32[64,512]{1,0:T(8,128)S(1)}, f32[16,512]{1,0:T(8,128)S(1)}, f32[8,128]{1,0:T(8,128)S(1)}, bf16[8,256,256]{2,1,0:T(8,128)(2,1)S(1)}) custom-call(s32[4]{0:T(128)S(1)} %copy-done.3, s32[4]{0:T(128)S(1)} %copy-done.4, bf16[4,2,8,256,256]{4,3,2,1,0:T(8,128)(2,1)S(1)} %bitcast.28, ...), custom_call_target="tpu_custom_call" | custom-call | flops 6000000000 | bytes 8000000 | tf_op jit(solution)/shard_map/data_part/pallas_call | solution.py:454
  9.5 3.3 %collective-permute-start.1 = (f32[64,512]{1,0:T(8,128)S(1)}, f32[64,512]{1,0:T(8,128)S(1)}, u32[]{:S(2)}, u32[]{:S(2)}) collective-permute-start(f32[64,512]{1,0:T(8,128)S(1)} %get-tuple-element.51.refs_6_), channel_id=1, source_target_pairs={{0,1},{1,0},{2,3},{3,2},{4,5},{5,4},{6,7},{7,6},{8,9},{9,8},{10,11... | collective-permute-start | bytes 393224 | tf_op jit(solution)/shard_map/ppermute | solution.py:859
  12.8 4.0 %gradient_part.3 = (f32[64,512]{1,0:T(8,128)S(1)}, bf16[2,2,64,512]{3,2,1,0:T(8,128)(2,1)S(1)}, bf16[2,4,64,512]{3,2,1,0:T(8,128)(2,1)S(1)}) custom-call(f32[8,128]{1,0:T(8,128)S(1)} %get-tuple-element.45.refs_0_, f32[16,512]{1,0:T(8,128)S(1)} %get-tuple-element.46.refs_1_.refs_7_, f32[64,128]{1,0:T(8,128)S(1)} %get-tuple-element.42.refs_3_.refs_2_, ...), custom_call_target="tpu_custom_call" | custom-call | flops 4000000000 | bytes 2000000 | tf_op jit(solution)/shard_map/gradient_part/pallas_call | solution.py:634
  16.8 0.0 collective-permute-done.1.refs_7_
  16.8 1.6 %curvature_part.3 = (f32[64,512]{1,0:T(8,128)S(1)}, f32[64,512]{1,0:T(8,128)S(1)}, f32[32,128]{1,0:T(8,128)}) custom-call(f32[8,128]{1,0:T(8,128)S(1)} %get-tuple-element.45.refs_0_, f32[16,512]{1,0:T(8,128)S(1)} %get-tuple-element.46.refs_1_.refs_7_, f32[64,128]{1,0:T(8,128)S(1)} %get-tuple-element.42.refs_3_.refs_2_, ...), custom_call_target="tpu_custom_call" | custom-call | flops 2000000000 | bytes 2000000 | tf_op jit(solution)/shard_map/curvature_part/pallas_call | solution.py:741
  18.4 5.3 %all-to-all-start = ((f32[32,1,128]{2,1,0:T(1,128)}), f32[32,1,128]{2,1,0:T(1,128)S(1)}, u32[]{:S(2)}, u32[]{:S(2)}) async-start(f32[32,1,128]{2,1,0:T(1,128)} %bitcast.8), calls=%async_computation | async-start | bytes 32768 | tf_op jit(solution)/shard_map/all_to_all | solution.py:922
  23.7 2.7 %data_part.4.refs_6_ = f32[64,512]{1,0:T(8,128)S(1)} custom-call(s32[4]{0:T(128)S(1)} %copy-done.3, s32[4]{0:T(128)S(1)} %copy-done.4, bf16[4,2,8,256,256]{4,3,2,1,0:T(8,128)(2,1)} %bitcast.24, f32[64,128]{1,0:T(8,128)S(1)} %get-tuple-element.42.refs_3_.refs_2_, bf16[2,256,256]{2,1,0:T(8,128)(2,1)S(1)} %baseline_masks.1.masks.refs_4_, ...), custom_call_target="tpu_custom_call" | custom-call | flops 6000000000 | bytes 8000000 | tf_op jit(solution)/shard_map/data_part/pallas_call | solution.py:454
  26.4 3.1 %collective-permute-start.2 = (f32[64,512]{1,0:T(8,128)S(1)}, f32[64,512]{1,0:T(8,128)S(1)}, u32[]{:S(2)}, u32[]{:S(2)}) collective-permute-start(f32[64,512]{1,0:T(8,128)S(1)} %data_part.4.refs_6_), channel_id=1, source_target_pairs={{0,1},{1,0},{2,3},{3,2},{4,5},{5,4},{6,7},{7,6},{8,9},{9,8},{10,11... | collective-permute-start | bytes 393224 | tf_op jit(solution)/shard_map/ppermute | solution.py:859
  29.5 1.3 %all-to-all-done = f32[32,1,128]{2,1,0:T(1,128)S(1)} async-done(((f32[32,1,128]{2,1,0:T(1,128)}), f32[32,1,128]{2,1,0:T(1,128)S(1)}, u32[]{:S(2)}, u32[]{:S(2)}) %all-to-all-start) | async-done | bytes 16416 | tf_op jit(solution)/shard_map/all_to_all | solution.py:922
  30.8 4.2 %gradient_part.4 = (f32[64,512]{1,0:T(8,128)S(1)}, f32[64,512]{1,0:T(8,128)S(1)}, f32[8,128]{1,0:T(8,128)S(1)}, bf16[2,2,64,512]{3,2,1,0:T(8,128)(2,1)S(1)}, bf16[2,4,64,512]{3,2,1,0:T(8,128)(2,1)S(1)}) custom-call(f32[8,128]{1,0:T(8,128)S(1)} %get-tuple-element.45.refs_0_, f32[16,512]{1,0:T(8,128)S(1)} %get-tuple-element.46.refs_1_.refs_7_, ...), custom_call_target="tpu_custom_call" | custom-call | flops 4000000000 | bytes 2000000 | tf_op jit(solution)/shard_map/gradient_part/pallas_call | solution.py:634
  35.0 0.0 collective-permute-done.2.refs_7_
  35.0 1.6 %curvature_part.4 = (f32[64,512]{1,0:T(8,128)S(1)}, f32[64,512]{1,0:T(8,128)S(1)}, f32[32,128]{1,0:T(8,128)}) custom-call(f32[8,128]{1,0:T(8,128)S(1)} %get-tuple-element.45.refs_0_, f32[16,512]{1,0:T(8,128)S(1)} %get-tuple-element.46.refs_1_.refs_7_, f32[64,128]{1,0:T(8,128)S(1)} %get-tuple-element.42.refs_3_.refs_2_, ...), custom_call_target="tpu_custom_call" | custom-call | flops 2000000000 | bytes 2000000 | tf_op jit(solution)/shard_map/curvature_part/pallas_call | solution.py:741
  36.6 4.1 %all-to-all-start.1 = ((f32[32,1,128]{2,1,0:T(1,128)}), f32[32,1,128]{2,1,0:T(1,128)S(1)}, u32[]{:S(2)}, u32[]{:S(2)}) async-start(f32[32,1,128]{2,1,0:T(1,128)} %bitcast.11), calls=%async_computation.1 | async-start | bytes 32768 | tf_op jit(solution)/shard_map/all_to_all | solution.py:922
  40.7 2.8 %data_part.5.refs_6_ = f32[64,512]{1,0:T(8,128)S(1)} custom-call(s32[4]{0:T(128)S(1)} %copy-done.3, s32[4]{0:T(128)S(1)} %copy-done.4, bf16[4,2,8,256,256]{4,3,2,1,0:T(8,128)(2,1)} %bitcast.25, f32[64,128]{1,0:T(8,128)S(1)} %get-tuple-element.42.refs_3_.refs_2_, bf16[2,256,256]{2,1,0:T(8,128)(2,1)S(1)} %baseline_masks.1.masks.refs_4_, ...), custom_call_target="tpu_custom_call" | custom-call | flops 6000000000 | bytes 8000000 | tf_op jit(solution)/shard_map/data_part/pallas_call | solution.py:454
  43.5 3.1 %collective-permute-start.3 = (f32[64,512]{1,0:T(8,128)S(1)}, f32[64,512]{1,0:T(8,128)S(1)}, u32[]{:S(2)}, u32[]{:S(2)}) collective-permute-start(f32[64,512]{1,0:T(8,128)S(1)} %data_part.5.refs_6_), channel_id=1, source_target_pairs={{0,1},{1,0},{2,3},{3,2},{4,5},{5,4},{6,7},{7,6},{8,9},{9,8},{10,11... | collective-permute-start | bytes 393224 | tf_op jit(solution)/shard_map/ppermute | solution.py:859
  46.7 1.2 %all-to-all-done.1 = f32[32,1,128]{2,1,0:T(1,128)S(1)} async-done(((f32[32,1,128]{2,1,0:T(1,128)}), f32[32,1,128]{2,1,0:T(1,128)S(1)}, u32[]{:S(2)}, u32[]{:S(2)}) %all-to-all-start.1) | async-done | bytes 16416 | tf_op jit(solution)/shard_map/all_to_all | solution.py:922
  47.8 4.2 %gradient_part.5 = (f32[64,512]{1,0:T(8,128)S(1)}, f32[64,512]{1,0:T(8,128)S(1)}, f32[8,128]{1,0:T(8,128)S(1)}, bf16[2,2,64,512]{3,2,1,0:T(8,128)(2,1)S(1)}, bf16[2,4,64,512]{3,2,1,0:T(8,128)(2,1)S(1)}) custom-call(f32[8,128]{1,0:T(8,128)S(1)} %get-tuple-element.45.refs_0_, f32[16,512]{1,0:T(8,128)S(1)} %get-tuple-element.46.refs_1_.refs_7_, ...), custom_call_target="tpu_custom_call" | custom-call | flops 4000000000 | bytes 2000000 | tf_op jit(solution)/shard_map/gradient_part/pallas_call | solution.py:634
  52.0 0.0 collective-permute-done.3.refs_7_
  52.0 1.6 %curvature_part.5 = (f32[64,512]{1,0:T(8,128)S(1)}, f32[72,128]{1,0:T(8,128)S(1)}, f32[72,128]{1,0:T(8,128)S(1)}, f32[72,128]{1,0:T(8,128)S(1)}, f32[72,128]{1,0:T(8,128)S(1)}) custom-call(f32[8,128]{1,0:T(8,128)S(1)} %get-tuple-element.45.refs_0_, f32[16,512]{1,0:T(8,128)S(1)} %get-tuple-element.46.refs_1_.refs_7_, ...), custom_call_target="tpu_custom_call" | custom-call | flops 2000000000 | bytes 2000000 | tf_op jit(solution)/shard_map/curvature_part/pallas_call | solution.py:741
  53.6 0.1 collective-permute-start.4
  53.7 0.6 collective-permute-start.5
  54.2 1.3 %collective-permute-start.6 = (f32[72,128]{1,0:T(8,128)S(1)}, f32[72,128]{1,0:T(8,128)S(1)}, u32[]{:S(2)}, u32[]{:S(2)}) collective-permute-start(f32[72,128]{1,0:T(8,128)S(1)} %get-tuple-element.73), channel_id=1, source_target_pairs={{0,6},{2,4},{4,2},{6,0},{8,14},{10,12},{12,10},{14,8},{16,22},{18,... | collective-permute-start | bytes 110600 | tf_op jit(solution)/shard_map/ppermute | solution.py:855
  55.5 0.0 collective-permute-done.4.refs_1_
  55.5 2.5 %collective-permute-done.5.refs_2_ = f32[72,128]{1,0:T(8,128)S(1)} collective-permute-done((f32[72,128]{1,0:T(8,128)S(1)}, f32[72,128]{1,0:T(8,128)S(1)}, u32[]{:S(2)}, u32[]{:S(2)}) %collective-permute-start.5) | collective-permute-done | bytes 36896 | tf_op jit(solution)/shard_map/ppermute | solution.py:855
  58.0 0.0 collective-permute-done.6.refs_3_
  58.0 0.1 weigh.1
  58.1 1.0 %collective-permute-start.7 = (f32[264,128]{1,0:T(8,128)S(1)}, f32[264,128]{1,0:T(8,128)S(1)}, u32[]{:S(2)}, u32[]{:S(2)}) collective-permute-start(f32[264,128]{1,0:T(8,128)S(1)} %weigh.1), channel_id=1, source_target_pairs={{0,8},{2,10},{4,12},{6,14},{8,0},{10,2},{12,4},{14,6},{16,24},{18,... | collective-permute-start | bytes 405512 | tf_op jit(solution)/shard_map/ppermute | solution.py:855
  59.1 4.8 %collective-permute-done.7 = f32[264,128]{1,0:T(8,128)S(1)} collective-permute-done((f32[264,128]{1,0:T(8,128)S(1)}, f32[264,128]{1,0:T(8,128)S(1)}, u32[]{:S(2)}, u32[]{:S(2)}) %collective-permute-start.7) | collective-permute-done | bytes 135200 | tf_op jit(solution)/shard_map/ppermute | solution.py:855
  63.9 1.9 %collective-permute-start.8 = (f32[264,128]{1,0:T(8,128)S(1)}, f32[264,128]{1,0:T(8,128)S(1)}, u32[]{:S(2)}, u32[]{:S(2)}) collective-permute-start(f32[264,128]{1,0:T(8,128)S(1)} %add.3.one), channel_id=1, source_target_pairs={{0,16},{2,18},{4,20},{6,22},{8,24},{10,26},{12,28},{14,30},{16,0},... | collective-permute-start | bytes 405512 | tf_op jit(solution)/shard_map/ppermute | solution.py:855
  65.8 6.8 %collective-permute-done.8.two = f32[264,128]{1,0:T(8,128)S(1)} collective-permute-done((f32[264,128]{1,0:T(8,128)S(1)}, f32[264,128]{1,0:T(8,128)S(1)}, u32[]{:S(2)}, u32[]{:S(2)}) %collective-permute-start.8) | collective-permute-done | bytes 135200 | tf_op jit(solution)/shard_map/ppermute | solution.py:855
  72.6 0.2 combine.1
  72.8 0.7 collective-permute-start.11
  73.5 0.7 collective-permute-start.10
  74.1 0.6 collective-permute-start.9
  74.7 0.7 last_step.1
  75.4 1.7 %collective-permute-done.11.both = f32[128,128]{1,0:T(8,128)S(1)} collective-permute-done((f32[128,128]{1,0:T(8,128)S(1)}, f32[128,128]{1,0:T(8,128)S(1)}, u32[]{:S(2)}, u32[]{:S(2)}) %collective-permute-start.11) | collective-permute-done | bytes 65568 | tf_op jit(solution)/shard_map/ppermute | solution.py:855
  77.1 1.4 %collective-permute-done.10.row = f32[128,128]{1,0:T(8,128)S(1)} collective-permute-done((f32[128,128]{1,0:T(8,128)S(1)}, f32[128,128]{1,0:T(8,128)S(1)}, u32[]{:S(2)}, u32[]{:S(2)}) %collective-permute-start.10) | collective-permute-done | bytes 65568 | tf_op jit(solution)/shard_map/ppermute | solution.py:855
  78.5 0.0 collective-permute-done.9.core
  78.5 0.8 %consensus.1 = (f32[64,4,256]{2,1,0:T(4,128)}, f32[64,1,256]{2,1,0:T(1,128)}) custom-call(f32[128,128]{1,0:T(8,128)S(1)} %get-tuple-element.77.own, f32[128,128]{1,0:T(8,128)S(1)} %collective-permute-done.9.core, f32[128,128]{1,0:T(8,128)S(1)} %collective-permute-done.10.row, f32[128,128]{1,0:T(8,128)S(1)} %collective-permute-done.11.both, ...), custom_call_target="tpu_custom_call" | custom-call | tf_op jit(solution)/shard_map/consensus/pallas_call | solution.py:844
  (16 shorter events, 0.1 us)
Async XLA Ops:
  0.6 0.7 copy-start.3
  0.6 0.7 copy-start.4
  0.7 0.7 copy-start.6
  0.7 0.9 %copy-start.5 = (f32[8,8,1,256]{3,2,1,0:T(1,128)S(1)}, f32[8,8,1,256]{3,2,1,0:T(1,128)}, u32[]{:S(2)}) copy-start(f32[8,8,1,256]{3,2,1,0:T(1,128)} %param.11) | copy-start | bytes 196612
  0.7 6.4 %slice-start = ((s8[8388608]{0:T(1024)(128)(4,1)}), s8[4194304]{0:T(1024)(128)(4,1)S(1)}, s32[]{:S(2)}) async-start(s8[8388608]{0:T(1024)(128)(4,1)} %bitcast.26), calls=%async_computation.2 | async-start | bytes 8388608
  1.5 3.1 %copy-start = (f32[8,8,4,256]{3,2,1,0:T(4,128)S(1)}, f32[8,8,4,256]{3,2,1,0:T(4,128)}, u32[]{:S(2)}) copy-start(f32[8,8,4,256]{3,2,1,0:T(4,128)} %param.13) | copy-start | bytes 786436
  1.5 3.1 %copy-start.1 = (f32[8,8,1,256]{3,2,1,0:T(1,128)S(1)}, f32[8,8,1,256]{3,2,1,0:T(1,128)}, u32[]{:S(2)}) copy-start(f32[8,8,1,256]{3,2,1,0:T(1,128)} %param.12) | copy-start | bytes 196612
  1.5 3.1 %copy-start.2 = (f32[8,8]{1,0:T(8,128)S(1)}, f32[8,8]{1,0:T(8,128)}, u32[]{:S(2)}) copy-start(f32[8,8]{1,0:T(8,128)} %refs_4_.1) | copy-start | bytes 772
  1.5 5.5 %slice-start.1 = ((s8[8388608]{0:T(1024)(128)(4,1)}), s8[4194304]{0:T(1024)(128)(4,1)S(1)}, s32[]{:S(2)}) async-start(s8[8388608]{0:T(1024)(128)(4,1)} %bitcast.26), calls=%async_computation.3 | async-start | bytes 8388608
  1.6 5.5 %collective-permute-start = (f32[82,1,256]{2,1,0:T(1,128)S(1)}, f32[82,1,256]{2,1,0:T(1,128)S(1)}, u32[]{:S(2)}, u32[]{:S(2)}) collective-permute-start(f32[82,1,256]{2,1,0:T(1,128)S(1)} %field_rows.1.refs_5_), channel_id=1, source_target_pairs={{0,1},{1,0},{2,3},{3,2},{4,5},{5,4},{6,7},{7,6},{8,9},{9,8},{10,11... | collective-permute-start | bytes 251912 | tf_op jit(solution)/shard_map/ppermute | solution.py:859
  9.5 7.3 %collective-permute-start.1 = (f32[64,512]{1,0:T(8,128)S(1)}, f32[64,512]{1,0:T(8,128)S(1)}, u32[]{:S(2)}, u32[]{:S(2)}) collective-permute-start(f32[64,512]{1,0:T(8,128)S(1)} %get-tuple-element.51.refs_6_), channel_id=1, source_target_pairs={{0,1},{1,0},{2,3},{3,2},{4,5},{5,4},{6,7},{7,6},{8,9},{9,8},{10,11... | collective-permute-start | bytes 393224 | tf_op jit(solution)/shard_map/ppermute | solution.py:859
  18.4 12.5 %all-to-all-start = ((f32[32,1,128]{2,1,0:T(1,128)}), f32[32,1,128]{2,1,0:T(1,128)S(1)}, u32[]{:S(2)}, u32[]{:S(2)}) async-start(f32[32,1,128]{2,1,0:T(1,128)} %bitcast.8), calls=%async_computation | async-start | bytes 32768 | tf_op jit(solution)/shard_map/all_to_all | solution.py:922
  26.4 8.6 %collective-permute-start.2 = (f32[64,512]{1,0:T(8,128)S(1)}, f32[64,512]{1,0:T(8,128)S(1)}, u32[]{:S(2)}, u32[]{:S(2)}) collective-permute-start(f32[64,512]{1,0:T(8,128)S(1)} %data_part.4.refs_6_), channel_id=1, source_target_pairs={{0,1},{1,0},{2,3},{3,2},{4,5},{5,4},{6,7},{7,6},{8,9},{9,8},{10,11... | collective-permute-start | bytes 393224 | tf_op jit(solution)/shard_map/ppermute | solution.py:859
  36.6 11.2 %all-to-all-start.1 = ((f32[32,1,128]{2,1,0:T(1,128)}), f32[32,1,128]{2,1,0:T(1,128)S(1)}, u32[]{:S(2)}, u32[]{:S(2)}) async-start(f32[32,1,128]{2,1,0:T(1,128)} %bitcast.11), calls=%async_computation.1 | async-start | bytes 32768 | tf_op jit(solution)/shard_map/all_to_all | solution.py:922
  43.5 8.5 %collective-permute-start.3 = (f32[64,512]{1,0:T(8,128)S(1)}, f32[64,512]{1,0:T(8,128)S(1)}, u32[]{:S(2)}, u32[]{:S(2)}) collective-permute-start(f32[64,512]{1,0:T(8,128)S(1)} %data_part.5.refs_6_), channel_id=1, source_target_pairs={{0,1},{1,0},{2,3},{3,2},{4,5},{5,4},{6,7},{7,6},{8,9},{9,8},{10,11... | collective-permute-start | bytes 393224 | tf_op jit(solution)/shard_map/ppermute | solution.py:859
  53.6 1.9 %collective-permute-start.4 = (f32[72,128]{1,0:T(8,128)S(1)}, f32[72,128]{1,0:T(8,128)S(1)}, u32[]{:S(2)}, u32[]{:S(2)}) collective-permute-start(f32[72,128]{1,0:T(8,128)S(1)} %get-tuple-element.71), channel_id=1, source_target_pairs={{0,2},{2,0},{4,6},{6,4},{8,10},{10,8},{12,14},{14,12},{16,18},{18,... | collective-permute-start | bytes 110600 | tf_op jit(solution)/shard_map/ppermute | solution.py:855
  53.7 4.3 %collective-permute-start.5 = (f32[72,128]{1,0:T(8,128)S(1)}, f32[72,128]{1,0:T(8,128)S(1)}, u32[]{:S(2)}, u32[]{:S(2)}) collective-permute-start(f32[72,128]{1,0:T(8,128)S(1)} %get-tuple-element.72), channel_id=1, source_target_pairs={{0,4},{2,6},{4,0},{6,2},{8,12},{10,14},{12,8},{14,10},{16,20},{18,... | collective-permute-start | bytes 110600 | tf_op jit(solution)/shard_map/ppermute | solution.py:855
  54.2 3.8 %collective-permute-start.6 = (f32[72,128]{1,0:T(8,128)S(1)}, f32[72,128]{1,0:T(8,128)S(1)}, u32[]{:S(2)}, u32[]{:S(2)}) collective-permute-start(f32[72,128]{1,0:T(8,128)S(1)} %get-tuple-element.73), channel_id=1, source_target_pairs={{0,6},{2,4},{4,2},{6,0},{8,14},{10,12},{12,10},{14,8},{16,22},{18,... | collective-permute-start | bytes 110600 | tf_op jit(solution)/shard_map/ppermute | solution.py:855
  58.1 5.8 %collective-permute-start.7 = (f32[264,128]{1,0:T(8,128)S(1)}, f32[264,128]{1,0:T(8,128)S(1)}, u32[]{:S(2)}, u32[]{:S(2)}) collective-permute-start(f32[264,128]{1,0:T(8,128)S(1)} %weigh.1), channel_id=1, source_target_pairs={{0,8},{2,10},{4,12},{6,14},{8,0},{10,2},{12,4},{14,6},{16,24},{18,... | collective-permute-start | bytes 405512 | tf_op jit(solution)/shard_map/ppermute | solution.py:855
  63.9 8.7 %collective-permute-start.8 = (f32[264,128]{1,0:T(8,128)S(1)}, f32[264,128]{1,0:T(8,128)S(1)}, u32[]{:S(2)}, u32[]{:S(2)}) collective-permute-start(f32[264,128]{1,0:T(8,128)S(1)} %add.3.one), channel_id=1, source_target_pairs={{0,16},{2,18},{4,20},{6,22},{8,24},{10,26},{12,28},{14,30},{16,0},... | collective-permute-start | bytes 405512 | tf_op jit(solution)/shard_map/ppermute | solution.py:855
  72.8 4.3 %collective-permute-start.11 = (f32[128,128]{1,0:T(8,128)S(1)}, f32[128,128]{1,0:T(8,128)S(1)}, u32[]{:S(2)}, u32[]{:S(2)}) collective-permute-start(f32[128,128]{1,0:T(8,128)S(1)} %get-tuple-element.77.own), channel_id=1, source_target_pairs={{0,6},{2,4},{4,2},{6,0},{8,14},{10,12},{12,10},{14,8},{16,22},{18,... | collective-permute-start | bytes 196616 | tf_op jit(solution)/shard_map/ppermute | solution.py:855
  73.5 5.0 %collective-permute-start.10 = (f32[128,128]{1,0:T(8,128)S(1)}, f32[128,128]{1,0:T(8,128)S(1)}, u32[]{:S(2)}, u32[]{:S(2)}) collective-permute-start(f32[128,128]{1,0:T(8,128)S(1)} %get-tuple-element.77.own), channel_id=1, source_target_pairs={{0,4},{2,6},{4,0},{6,2},{8,12},{10,14},{12,8},{14,10},{16,20},{18,... | collective-permute-start | bytes 196616 | tf_op jit(solution)/shard_map/ppermute | solution.py:855
  74.1 4.3 %collective-permute-start.9 = (f32[128,128]{1,0:T(8,128)S(1)}, f32[128,128]{1,0:T(8,128)S(1)}, u32[]{:S(2)}, u32[]{:S(2)}) collective-permute-start(f32[128,128]{1,0:T(8,128)S(1)} %get-tuple-element.77.own), channel_id=1, source_target_pairs={{0,2},{2,0},{4,6},{6,4},{8,10},{10,8},{12,14},{14,12},{16,18},{18,... | collective-permute-start | bytes 196616 | tf_op jit(solution)/shard_map/ppermute | solution.py:855

commit v6 on v5

--- a/solution.py
+++ b/solution.py
@@ -539,15 +539,17 @@
     return jnp.where(odd, high, low), jnp.where(odd, low, high)
 
 
-def store_quarters(fields, sums, outs):
+def store_eighths(fields, sums, outs):
     place = lax.axis_index("chan")
-    odd_lanes, odd_rows = place % 2 == 1, (place // 2) % 2 == 1
+    odd_lanes, odd_low, odd_high = place % 2 == 1, (place // 2) % 2 == 1, (place // 4) % 2 == 1
     for n, field in enumerate(fields):
-        for o, part in enumerate(halves(field, 1, odd_lanes)):
-            for p, quarter in enumerate(halves(part, 0, odd_rows)):
-                outs[o + 2 * p][32 * n : 32 * n + 32, :] = quarter
+        for out, part in zip(outs, halves(field, 1, odd_lanes)):
+            for high, half in enumerate(halves(part, 0, odd_high)):
+                for low, rows in enumerate(halves(half, 0, odd_low)):
+                    at = 32 * (2 * high + low) + 16 * n
+                    out[at : at + 16, :] = rows
     for out in outs:
-        out[32 * len(fields) :, :] = sums
+        out[128:, :] = sums
 
 
 def step_length(grad_sq, curvature, penalty):
@@ -720,7 +722,7 @@
     sums = jnp.where(lane == 0, grad_sq, jnp.where(lane == 1, curvature, 0.0))
     if last:
         base = current_ref[:, own_lanes(block)] + duals_ref[...]
-        store_quarters((base, direction_out[:, own_lanes(block)]), sums, refs)
+        store_eighths((base, direction_out[:, own_lanes(block)]), sums, refs)
     else:
         sums_out[...] = sums
 
@@ -730,7 +732,7 @@
     update = before is not None
     field = shape(64, stations)
     if last is not None:
-        outs = [field] + [shape(72, block // 2)] * 4
+        outs = [field] + [shape(136, block // 2)] * 2
     else:
         outs = [field, field, shape(chan_count * (stations // block), 128)]
     inputs = [counts, delays, coh, *factors, gradient, *shares]
@@ -753,27 +755,49 @@
     )(*inputs)
 
 
+def regroup_kernel(mine, theirs, *outs):
+    for o, out in enumerate(outs):
+        out[:32, :] = mine[32 * o : 32 * o + 32, :]
+        out[32:64, :] = theirs[32 * o : 32 * o + 32, :]
+        out[64:, :] = mine[128:, :] + theirs[128:, :]
+
+
+def regroup(mine, theirs):
+    return pl.pallas_call(
+        regroup_kernel,
+        name="regroup",
+        out_shape=(shape(72, mine.shape[1]),) * 4,
+        in_specs=vmem_specs(2),
+        out_specs=tuple(vmem_specs(4)),
+        compiler_params=params(),
+    )(mine, theirs)
+
+
+def sum_in_pairs(terms):
+    return (terms[0] + terms[1]) + (terms[2] + terms[3])
+
+
 def weigh_kernel(chan_count, *refs):
     *parts, out = refs
-    scales = [solve_of(chan_count, offset) for offset in range(4)]
+    scales = [solve_of(chan_count, offset) for offset in range(8)]
     for n in range(2):
         for k in range(4):
-            at = 128 * n + 32 * k
-            terms = [scales[o][k] * parts[o][32 * n : 32 * n + 32, :] for o in range(4)]
-            out[at : at + 32, :] = sum_in_pairs(terms)
-    out[256:, :] = sum_in_pairs([part[64:, :] for part in parts])
-
-
-def sum_in_pairs(terms):
-    return (terms[0] + terms[1]) + (terms[2] + terms[3])
-
-
-def weigh(geometry, *parts):
+            terms = []
+            for o, part in enumerate(parts):
+                one = part[16 * n : 16 * n + 16, :]
+                two = part[32 + 16 * n : 48 + 16 * n, :]
+                terms.append(scales[2 * o][k] * one + scales[2 * o + 1][k] * two)
+            at = 64 * n + 16 * k
+            out[at : at + 16, :] = sum_in_pairs(terms)
+    out[128:, :] = sum_in_pairs([part[64:, :] for part in parts])
+
+
+def weigh(geometry, parts):
     chan_count = geometry[4]
     return pl.pallas_call(
         functools.partial(weigh_kernel, chan_count),
         name="weigh",
-        out_shape=shape(264, parts[0].shape[1]),
+        out_shape=shape(136, parts[0].shape[1]),
         in_specs=vmem_specs(4),
         out_specs=vmem_specs(1)[0],
         compiler_params=params(),
@@ -782,8 +806,8 @@
 
 def combine_kernel(penalty, one, two, coeffs_out, alpha_out):
     total = one[...] + two[...]
-    alpha = step_length(total[256:257, 0:1], total[256:257, 1:2], penalty)
-    coeffs_out[...] = total[:128] - alpha * total[128:256]
+    alpha = step_length(total[128:129, 0:1], total[128:129, 1:2], penalty)
+    coeffs_out[...] = total[:64] - alpha * total[64:128]
     alpha_out[...] = jnp.broadcast_to(alpha, (8, 128))
 
 
@@ -792,7 +816,7 @@
     return pl.pallas_call(
         functools.partial(combine_kernel, penalty),
         name="combine",
-        out_shape=(shape(128, one.shape[1]), shape(8, 128)),
+        out_shape=(shape(64, one.shape[1]), shape(8, 128)),
         in_specs=vmem_specs(2),
         out_specs=tuple(vmem_specs(2)),
         compiler_params=params(),
@@ -803,7 +827,7 @@
     at_own = own_lanes(block)
     gains_new = current[:, at_own] - alpha[0:1, 0:1] * direction[:, at_own]
     gains_out[:, 0, :] = gains_new
-    shifted_out[...] = gains_new + duals[...]
+    shifted_out[:, 0, :] = gains_new + duals[...]
 
 
 def last_step(geometry, *inputs):
@@ -811,32 +835,26 @@
     return pl.pallas_call(
         functools.partial(last_step_kernel, block),
         name="last_step",
-        out_shape=(shape(64, 1, block), shape(64, block)),
+        out_shape=(shape(64, 1, block), shape(64, 1, block)),
         in_specs=vmem_specs(len(inputs)),
         out_specs=tuple(vmem_specs(2)),
         compiler_params=params(),
     )(*inputs)
 
 
-def consensus_kernel(chan_count, own, core, row, both, shifted, coeffs_out, duals_out):
+def consensus_kernel(chan_count, mine, theirs, shifted, coeffs_out, duals_out):
     place = lax.axis_index("chan")
-    odd_core, odd_row = place % 2 == 1, (place // 2) % 2 == 1
-
-    def joined(one, two, odd, axis):
-        return jnp.concatenate([jnp.where(odd, two, one), jnp.where(odd, one, two)], axis=axis)
-
-    fitted = None
-    for k, scale in enumerate(basis_of(chan_count)):
-        at = slice(32 * k, 32 * k + 32)
-        coeffs = joined(
-            joined(own[at, :], core[at, :], odd_core, 1),
-            joined(row[at, :], both[at, :], odd_core, 1),
-            odd_row,
-            0,
-        )
-        coeffs_out[:, k, :] = coeffs
-        fitted = scale * coeffs if fitted is None else fitted + scale * coeffs
-    duals_out[:, 0, :] = shifted[...] - fitted
+    odd = place % 2 == 1
+    for o in range(4):
+        rows = pl.ds((((place // 2) % 4) ^ o) * 16, 16)
+        fitted = None
+        for k, scale in enumerate(basis_of(chan_count)):
+            at = slice(64 * o + 16 * k, 64 * o + 16 * k + 16)
+            one, two = mine[at, :], theirs[at, :]
+            coeffs = jnp.concatenate([jnp.where(odd, two, one), jnp.where(odd, one, two)], axis=1)
+            coeffs_out[rows, k, :] = coeffs
+            fitted = scale * coeffs if fitted is None else fitted + scale * coeffs
+        duals_out[rows, 0, :] = shifted[rows, 0, :] - fitted
 
 
 def consensus(geometry, *inputs):
@@ -924,16 +942,18 @@
             shares = both_stations(share, stn_count)
             step = (sums, direction)
 
-    quarters = rest[:1] + [swap(rest[o], chan_count, o) for o in (1, 2, 3)]
-    value, bit = weigh(geometry, *quarters), 4
+    keep, send = rest
+    own, *others = regroup(keep, swap(send, chan_count, 1))
+    parts = [own] + [swap(part, chan_count, 2 + 2 * o) for o, part in enumerate(others)]
+    value, bit = weigh(geometry, parts), 8
     other = swap(value, chan_count, bit)
     while 2 * bit < chan_count:
         value, bit = value + other, 2 * bit
         other = swap(value, chan_count, bit)
-    quarter, alpha = combine(geometry, value, other)
+    rows, alpha = combine(geometry, value, other)
     gains_new, shifted = last_step(geometry, alpha, current, direction, duals_own)
-    quarters = [quarter] + [swap(quarter, chan_count, o) for o in (1, 2, 3)]
-    coeffs, duals_new = consensus(geometry, *quarters, shifted)
+    mine = jnp.concatenate([rows] + [swap(rows, chan_count, o) for o in (2, 4, 6)])
+    coeffs, duals_new = consensus(geometry, mine, swap(mine, chan_count, 1), shifted)
     return (
         gains_new.reshape(gains.shape),
         coeffs.reshape(entries, dirs, 4, block),

time: 79 us -> 75.3 us (0.953); the launches traced: 79.3 us -> 74.4 us
  starting transfers between devices: 28.8 us -> 23.8 us
  Pallas kernels: 27.5 us -> 31.4 us
  waiting for transfers between devices: 21.4 us -> 17.5 us
    ppermute x4, starting transfers between devices: 12.6 us -> 4.81 us  [other_stations(): return lax.ppermute(value, 'stn', [(0, 1), (1, 0)])]
    ppermute x8 -> x9, waiting for transfers between devices: 17.1 us -> 10.4 us  [swap(): return lax.ppermute(value, 'chan', [(i, i ^ offset) for i in range(count)])]
    pallas_call x3, Pallas kernels: 7.91 us -> 11.8 us  [data_part(): pl.pallas_call(body, name='data_part', out_shape=tuple(shapes), in_specs=...]
    ppermute x8 -> x9, starting transfers between devices: 6.74 us -> 9.76 us  [swap(): return lax.ppermute(value, 'chan', [(i, i ^ offset) for i in range(count)])]
    all_to_all x2, waiting for transfers between devices: 2.47 us -> 5.08 us  [shards(): sums = lax.all_to_all(sums, ('chan', 'stn'), 0, 0, tiled=True)]
  transfers between devices with their start and end apart: 14 -> 15, of which waited for: 8 -> 11; matrix products, arithmetic and copies ran while one was open for 0% -> 0% of each run, Pallas kernels for 24% -> 29%
where the time goes in v6:
time: 75.3 us; the launch traced here: 74.4 us
  Pallas kernels  31.4 us (42%)
  starting transfers between devices  23.8 us (32%)
  waiting for transfers between devices  17.5 us (23%)
  local copies, waits for them, and re-layouts  0.85 us (1%)
  between operations  0.85 us (1%)
    pallas_call x3, Pallas kernels, gradient_part(): pl.pallas_call(functools.partial(gradient_kernel, block, pairs, dumps, pe...  12.3 us
    pallas_call x3, Pallas kernels, data_part(): pl.pallas_call(body, name='data_part', out_shape=tuple(shapes), in_specs=...  11.8 us
    ppermute x9, waiting for transfers between devices, swap(): return lax.ppermute(value, 'chan', [(i, i ^ offset) for i in range(count)])  10.4 us
    ppermute x9, starting transfers between devices, swap(): return lax.ppermute(value, 'chan', [(i, i ^ offset) for i in range(count)])  9.76 us
    all_to_all x2, starting transfers between devices, shards(): sums = lax.all_to_all(sums, ('chan', 'stn'), 0, 0, tiled=True)  9.21 us
    all_to_all x2, waiting for transfers between devices, shards(): sums = lax.all_to_all(sums, ('chan', 'stn'), 0, 0, tiled=True)  5.08 us
    ppermute x4, starting transfers between devices, other_stations(): return lax.ppermute(value, 'stn', [(0, 1), (1, 0)])  4.81 us
    pallas_call x3, Pallas kernels, curvature_part(): pl.pallas_call(functools.partial(curvature_kernel, block, pairs, dumps, p...  4.72 us
  transfers between devices with their start and end apart: 15, of which 11 were waited for; matrix products, arithmetic and copies ran while one was open for 0% of the time, Pallas kernels for 29%

profile of v6, /device:TPU:0, one launch (start us, length us, event | category | flops | bytes accessed | tf_op | source)
XLA Modules:
  0.0 74.4 jit_solution(6528316256860113250)
XLA Ops:
  0.7 0.0 slice-start
  0.7 0.6 copy-done.3
  1.3 0.0 copy-done.4
  1.3 0.1 copy-done.6
  1.4 0.1 copy-done.5
  1.6 3.0 %collective-permute-start = (f32[82,1,256]{2,1,0:T(1,128)S(1)}, f32[82,1,256]{2,1,0:T(1,128)S(1)}, u32[]{:S(2)}, u32[]{:S(2)}) collective-permute-start(f32[82,1,256]{2,1,0:T(1,128)S(1)} %field_rows.1.refs_5_), channel_id=1, source_target_pairs={{0,1},{1,0},{2,3},{3,2},{4,5},{5,4},{6,7},{7,6},{8,9},{9,8},{10,11... | collective-permute-start | bytes 251912 | tf_op jit(solution)/shard_map/ppermute | solution.py:877
  4.6 0.7 prepare.1
  5.3 1.7 %collective-permute-done.refs_6_ = f32[82,1,256]{2,1,0:T(1,128)S(1)} collective-permute-done((f32[82,1,256]{2,1,0:T(1,128)S(1)}, f32[82,1,256]{2,1,0:T(1,128)S(1)}, u32[]{:S(2)}, u32[]{:S(2)}) %collective-permute-start) | collective-permute-done | bytes 84000 | tf_op jit(solution)/shard_map/ppermute | solution.py:877
  7.1 3.7 %data_part.3 = (f32[64,512]{1,0:T(8,128)S(1)}, f32[64,512]{1,0:T(8,128)S(1)}, f32[16,512]{1,0:T(8,128)S(1)}, f32[8,128]{1,0:T(8,128)S(1)}, bf16[8,256,256]{2,1,0:T(8,128)(2,1)S(1)}) custom-call(s32[4]{0:T(128)S(1)} %copy-done.3, s32[4]{0:T(128)S(1)} %copy-done.4, bf16[4,2,8,256,256]{4,3,2,1,0:T(8,128)(2,1)S(1)} %bitcast.28, ...), custom_call_target="tpu_custom_call" | custom-call | flops 6000000000 | bytes 8000000 | tf_op jit(solution)/shard_map/data_part/pallas_call | solution.py:454
  10.8 0.8 %collective-permute-start.1 = (f32[64,512]{1,0:T(8,128)S(1)}, f32[64,512]{1,0:T(8,128)S(1)}, u32[]{:S(2)}, u32[]{:S(2)}) collective-permute-start(f32[64,512]{1,0:T(8,128)S(1)} %get-tuple-element.53.refs_6_), channel_id=1, source_target_pairs={{0,1},{1,0},{2,3},{3,2},{4,5},{5,4},{6,7},{7,6},{8,9},{9,8},{10,11... | collective-permute-start | bytes 393224 | tf_op jit(solution)/shard_map/ppermute | solution.py:877
  11.5 4.0 %gradient_part.3 = (f32[64,512]{1,0:T(8,128)S(1)}, bf16[2,2,64,512]{3,2,1,0:T(8,128)(2,1)S(1)}, bf16[2,4,64,512]{3,2,1,0:T(8,128)(2,1)S(1)}) custom-call(f32[8,128]{1,0:T(8,128)S(1)} %get-tuple-element.47.refs_0_, f32[16,512]{1,0:T(8,128)S(1)} %get-tuple-element.48.refs_1_.refs_7_, f32[64,128]{1,0:T(8,128)S(1)} %get-tuple-element.44.refs_3_.refs_2_, ...), custom_call_target="tpu_custom_call" | custom-call | flops 4000000000 | bytes 2000000 | tf_op jit(solution)/shard_map/gradient_part/pallas_call | solution.py:636
  15.5 0.3 collective-permute-done.1.refs_7_
  15.8 1.6 %curvature_part.3 = (f32[64,512]{1,0:T(8,128)S(1)}, f32[64,512]{1,0:T(8,128)S(1)}, f32[32,128]{1,0:T(8,128)}) custom-call(f32[8,128]{1,0:T(8,128)S(1)} %get-tuple-element.47.refs_0_, f32[16,512]{1,0:T(8,128)S(1)} %get-tuple-element.48.refs_1_.refs_7_, f32[64,128]{1,0:T(8,128)S(1)} %get-tuple-element.44.refs_3_.refs_2_, ...), custom_call_target="tpu_custom_call" | custom-call | flops 2000000000 | bytes 2000000 | tf_op jit(solution)/shard_map/curvature_part/pallas_call | solution.py:743
  17.4 5.9 %all-to-all-start = ((f32[32,1,128]{2,1,0:T(1,128)}), f32[32,1,128]{2,1,0:T(1,128)S(1)}, u32[]{:S(2)}, u32[]{:S(2)}) async-start(f32[32,1,128]{2,1,0:T(1,128)} %bitcast.8), calls=%async_computation | async-start | bytes 32768 | tf_op jit(solution)/shard_map/all_to_all | solution.py:940
  23.3 4.0 %data_part.4.refs_6_ = f32[64,512]{1,0:T(8,128)S(1)} custom-call(s32[4]{0:T(128)S(1)} %copy-done.3, s32[4]{0:T(128)S(1)} %copy-done.4, bf16[4,2,8,256,256]{4,3,2,1,0:T(8,128)(2,1)} %bitcast.24, f32[64,128]{1,0:T(8,128)S(1)} %get-tuple-element.44.refs_3_.refs_2_, bf16[2,256,256]{2,1,0:T(8,128)(2,1)S(1)} %baseline_masks.1.masks.refs_4_, ...), custom_call_target="tpu_custom_call" | custom-call | flops 6000000000 | bytes 8000000 | tf_op jit(solution)/shard_map/data_part/pallas_call | solution.py:454
  27.2 0.5 collective-permute-start.2
  27.8 2.6 %all-to-all-done = f32[32,1,128]{2,1,0:T(1,128)S(1)} async-done(((f32[32,1,128]{2,1,0:T(1,128)}), f32[32,1,128]{2,1,0:T(1,128)S(1)}, u32[]{:S(2)}, u32[]{:S(2)}) %all-to-all-start) | async-done | bytes 16416 | tf_op jit(solution)/shard_map/all_to_all | solution.py:940
  30.4 4.2 %gradient_part.4 = (f32[64,512]{1,0:T(8,128)S(1)}, f32[64,512]{1,0:T(8,128)S(1)}, f32[8,128]{1,0:T(8,128)S(1)}, bf16[2,2,64,512]{3,2,1,0:T(8,128)(2,1)S(1)}, bf16[2,4,64,512]{3,2,1,0:T(8,128)(2,1)S(1)}) custom-call(f32[8,128]{1,0:T(8,128)S(1)} %get-tuple-element.47.refs_0_, f32[16,512]{1,0:T(8,128)S(1)} %get-tuple-element.48.refs_1_.refs_7_, ...), custom_call_target="tpu_custom_call" | custom-call | flops 4000000000 | bytes 2000000 | tf_op jit(solution)/shard_map/gradient_part/pallas_call | solution.py:636
  34.6 0.0 collective-permute-done.2.refs_7_
  34.6 1.6 %curvature_part.4 = (f32[64,512]{1,0:T(8,128)S(1)}, f32[64,512]{1,0:T(8,128)S(1)}, f32[32,128]{1,0:T(8,128)}) custom-call(f32[8,128]{1,0:T(8,128)S(1)} %get-tuple-element.47.refs_0_, f32[16,512]{1,0:T(8,128)S(1)} %get-tuple-element.48.refs_1_.refs_7_, f32[64,128]{1,0:T(8,128)S(1)} %get-tuple-element.44.refs_3_.refs_2_, ...), custom_call_target="tpu_custom_call" | custom-call | flops 2000000000 | bytes 2000000 | tf_op jit(solution)/shard_map/curvature_part/pallas_call | solution.py:743
  36.1 3.3 %all-to-all-start.1 = ((f32[32,1,128]{2,1,0:T(1,128)}), f32[32,1,128]{2,1,0:T(1,128)S(1)}, u32[]{:S(2)}, u32[]{:S(2)}) async-start(f32[32,1,128]{2,1,0:T(1,128)} %bitcast.11), calls=%async_computation.1 | async-start | bytes 32768 | tf_op jit(solution)/shard_map/all_to_all | solution.py:940
  39.4 4.1 %data_part.5.refs_6_ = f32[64,512]{1,0:T(8,128)S(1)} custom-call(s32[4]{0:T(128)S(1)} %copy-done.3, s32[4]{0:T(128)S(1)} %copy-done.4, bf16[4,2,8,256,256]{4,3,2,1,0:T(8,128)(2,1)} %bitcast.25, f32[64,128]{1,0:T(8,128)S(1)} %get-tuple-element.44.refs_3_.refs_2_, bf16[2,256,256]{2,1,0:T(8,128)(2,1)S(1)} %baseline_masks.1.masks.refs_4_, ...), custom_call_target="tpu_custom_call" | custom-call | flops 6000000000 | bytes 8000000 | tf_op jit(solution)/shard_map/data_part/pallas_call | solution.py:454
  43.6 0.5 collective-permute-start.3
  44.1 2.5 %all-to-all-done.1 = f32[32,1,128]{2,1,0:T(1,128)S(1)} async-done(((f32[32,1,128]{2,1,0:T(1,128)}), f32[32,1,128]{2,1,0:T(1,128)S(1)}, u32[]{:S(2)}, u32[]{:S(2)}) %all-to-all-start.1) | async-done | bytes 16416 | tf_op jit(solution)/shard_map/all_to_all | solution.py:940
  46.6 4.2 %gradient_part.5 = (f32[64,512]{1,0:T(8,128)S(1)}, f32[64,512]{1,0:T(8,128)S(1)}, f32[8,128]{1,0:T(8,128)S(1)}, bf16[2,2,64,512]{3,2,1,0:T(8,128)(2,1)S(1)}, bf16[2,4,64,512]{3,2,1,0:T(8,128)(2,1)S(1)}) custom-call(f32[8,128]{1,0:T(8,128)S(1)} %get-tuple-element.47.refs_0_, f32[16,512]{1,0:T(8,128)S(1)} %get-tuple-element.48.refs_1_.refs_7_, ...), custom_call_target="tpu_custom_call" | custom-call | flops 4000000000 | bytes 2000000 | tf_op jit(solution)/shard_map/gradient_part/pallas_call | solution.py:636
  50.7 0.0 collective-permute-done.3.refs_7_
  50.7 1.6 %curvature_part.5 = (f32[64,512]{1,0:T(8,128)S(1)}, f32[136,128]{1,0:T(8,128)S(1)}, f32[136,128]{1,0:T(8,128)S(1)}) custom-call(f32[8,128]{1,0:T(8,128)S(1)} %get-tuple-element.47.refs_0_, f32[16,512]{1,0:T(8,128)S(1)} %get-tuple-element.48.refs_1_.refs_7_, f32[64,128]{1,0:T(8,128)S(1)} %get-tuple-element.44.refs_3_.refs_2_, ...), custom_call_target="tpu_custom_call" | custom-call | flops 2000000000 | bytes 2000000 | tf_op jit(solution)/shard_map/curvature_part/pallas_call | solution.py:743
  52.3 0.1 collective-permute-start.4
  52.4 1.2 %collective-permute-done.4.theirs = f32[136,128]{1,0:T(8,128)S(1)} collective-permute-done((f32[136,128]{1,0:T(8,128)S(1)}, f32[136,128]{1,0:T(8,128)S(1)}, u32[]{:S(2)}, u32[]{:S(2)}) %collective-permute-start.4) | collective-permute-done | bytes 69664 | tf_op jit(solution)/shard_map/ppermute | solution.py:873
  53.7 0.6 collective-permute-start.5
  54.3 1.2 %collective-permute-start.6 = (f32[72,128]{1,0:T(8,128)S(1)}, f32[72,128]{1,0:T(8,128)S(1)}, u32[]{:S(2)}, u32[]{:S(2)}) collective-permute-start(f32[72,128]{1,0:T(8,128)S(1)} %get-tuple-element.76), channel_id=1, source_target_pairs={{0,8},{2,10},{4,12},{6,14},{8,0},{10,2},{12,4},{14,6},{16,24},{18,... | collective-permute-start | bytes 110600 | tf_op jit(solution)/shard_map/ppermute | solution.py:873
  55.4 1.8 %collective-permute-start.7 = (f32[72,128]{1,0:T(8,128)S(1)}, f32[72,128]{1,0:T(8,128)S(1)}, u32[]{:S(2)}, u32[]{:S(2)}) collective-permute-start(f32[72,128]{1,0:T(8,128)S(1)} %get-tuple-element.77), channel_id=1, source_target_pairs={{0,12},{2,14},{4,8},{6,10},{8,4},{10,6},{12,0},{14,2},{16,28},{18,... | collective-permute-start | bytes 110600 | tf_op jit(solution)/shard_map/ppermute | solution.py:873
  57.2 0.5 collective-permute-done.5.refs_1_
  57.7 0.9 %collective-permute-done.6.refs_2_ = f32[72,128]{1,0:T(8,128)S(1)} collective-permute-done((f32[72,128]{1,0:T(8,128)S(1)}, f32[72,128]{1,0:T(8,128)S(1)}, u32[]{:S(2)}, u32[]{:S(2)}) %collective-permute-start.6) | collective-permute-done | bytes 36896 | tf_op jit(solution)/shard_map/ppermute | solution.py:873
  58.6 1.7 %collective-permute-done.7.refs_3_ = f32[72,128]{1,0:T(8,128)S(1)} collective-permute-done((f32[72,128]{1,0:T(8,128)S(1)}, f32[72,128]{1,0:T(8,128)S(1)}, u32[]{:S(2)}, u32[]{:S(2)}) %collective-permute-start.7) | collective-permute-done | bytes 36896 | tf_op jit(solution)/shard_map/ppermute | solution.py:873
  60.3 0.1 weigh.1.one
  60.4 2.5 %collective-permute-start.8 = (f32[136,128]{1,0:T(8,128)S(1)}, f32[136,128]{1,0:T(8,128)S(1)}, u32[]{:S(2)}, u32[]{:S(2)}) collective-permute-start(f32[136,128]{1,0:T(8,128)S(1)} %weigh.1.one), channel_id=1, source_target_pairs={{0,16},{2,18},{4,20},{6,22},{8,24},{10,26},{12,28},{14,30},{16,0},... | collective-permute-start | bytes 208904 | tf_op jit(solution)/shard_map/ppermute | solution.py:873
  62.9 3.5 %collective-permute-done.8.two = f32[136,128]{1,0:T(8,128)S(1)} collective-permute-done((f32[136,128]{1,0:T(8,128)S(1)}, f32[136,128]{1,0:T(8,128)S(1)}, u32[]{:S(2)}, u32[]{:S(2)}) %collective-permute-start.8) | collective-permute-done | bytes 69664 | tf_op jit(solution)/shard_map/ppermute | solution.py:873
  66.4 0.2 combine.1
  66.6 1.1 %collective-permute-start.11 = (f32[64,128]{1,0:T(8,128)S(1)}, f32[64,128]{1,0:T(8,128)S(1)}, u32[]{:S(2)}, u32[]{:S(2)}) collective-permute-start(f32[64,128]{1,0:T(8,128)S(1)} %get-tuple-element.81), channel_id=1, source_target_pairs={{0,12},{2,14},{4,8},{6,10},{8,4},{10,6},{12,0},{14,2},{16,28},{18,... | collective-permute-start | bytes 98312 | tf_op jit(solution)/shard_map/ppermute | solution.py:873
  67.7 0.4 collective-permute-start.10
  68.2 2.0 %collective-permute-start.9 = (f32[64,128]{1,0:T(8,128)S(1)}, f32[64,128]{1,0:T(8,128)S(1)}, u32[]{:S(2)}, u32[]{:S(2)}) collective-permute-start(f32[64,128]{1,0:T(8,128)S(1)} %get-tuple-element.81), channel_id=1, source_target_pairs={{0,4},{2,6},{4,0},{6,2},{8,12},{10,14},{12,8},{14,10},{16,20},{18,... | collective-permute-start | bytes 98312 | tf_op jit(solution)/shard_map/ppermute | solution.py:873
  70.2 1.9 %collective-permute-done.9 = f32[64,128]{1,0:T(8,128)S(1)} collective-permute-done((f32[64,128]{1,0:T(8,128)S(1)}, f32[64,128]{1,0:T(8,128)S(1)}, u32[]{:S(2)}, u32[]{:S(2)}) %collective-permute-start.9) | collective-permute-done | bytes 32800 | tf_op jit(solution)/shard_map/ppermute | solution.py:873
  72.1 0.0 collective-permute-done.10
  72.1 0.1 collective-permute-start.12
  72.2 0.7 last_step.1
  72.9 0.6 collective-permute-done.12.theirs
  73.5 0.9 %consensus.1 = (f32[64,4,256]{2,1,0:T(4,128)}, f32[64,1,256]{2,1,0:T(1,128)}) custom-call(f32[256,128]{1,0:T(8,128)S(1)} %constant_dynamic-update-slice_fusion.mine, f32[256,128]{1,0:T(8,128)S(1)} %collective-permute-done.12.theirs, f32[64,1,256]{2,1,0:T(1,128)S(1)} %get-tuple-element.82.shifted), custom_call_target="tpu_custom_call" | custom-call | tf_op jit(solution)/shard_map/consensus/pallas_call | solution.py:862
  (22 shorter events, 0.1 us)
Async XLA Ops:
  0.6 0.7 copy-start.3
  0.6 0.7 copy-start.4
  0.7 0.7 copy-start.6
  0.7 0.9 %copy-start.5 = (f32[8,8,1,256]{3,2,1,0:T(1,128)S(1)}, f32[8,8,1,256]{3,2,1,0:T(1,128)}, u32[]{:S(2)}) copy-start(f32[8,8,1,256]{3,2,1,0:T(1,128)} %param.11) | copy-start | bytes 196612
  0.7 6.4 %slice-start = ((s8[8388608]{0:T(1024)(128)(4,1)}), s8[4194304]{0:T(1024)(128)(4,1)S(1)}, s32[]{:S(2)}) async-start(s8[8388608]{0:T(1024)(128)(4,1)} %bitcast.26), calls=%async_computation.2 | async-start | bytes 8388608
  1.5 3.1 %copy-start = (f32[8,8,4,256]{3,2,1,0:T(4,128)S(1)}, f32[8,8,4,256]{3,2,1,0:T(4,128)}, u32[]{:S(2)}) copy-start(f32[8,8,4,256]{3,2,1,0:T(4,128)} %param.13) | copy-start | bytes 786436
  1.5 3.1 %copy-start.1 = (f32[8,8,1,256]{3,2,1,0:T(1,128)S(1)}, f32[8,8,1,256]{3,2,1,0:T(1,128)}, u32[]{:S(2)}) copy-start(f32[8,8,1,256]{3,2,1,0:T(1,128)} %param.12) | copy-start | bytes 196612
  1.5 3.1 %copy-start.2 = (f32[8,8]{1,0:T(8,128)S(1)}, f32[8,8]{1,0:T(8,128)}, u32[]{:S(2)}) copy-start(f32[8,8]{1,0:T(8,128)} %refs_4_.1) | copy-start | bytes 772
  1.5 5.5 %slice-start.1 = ((s8[8388608]{0:T(1024)(128)(4,1)}), s8[4194304]{0:T(1024)(128)(4,1)S(1)}, s32[]{:S(2)}) async-start(s8[8388608]{0:T(1024)(128)(4,1)} %bitcast.26), calls=%async_computation.3 | async-start | bytes 8388608
  1.6 5.5 %collective-permute-start = (f32[82,1,256]{2,1,0:T(1,128)S(1)}, f32[82,1,256]{2,1,0:T(1,128)S(1)}, u32[]{:S(2)}, u32[]{:S(2)}) collective-permute-start(f32[82,1,256]{2,1,0:T(1,128)S(1)} %field_rows.1.refs_5_), channel_id=1, source_target_pairs={{0,1},{1,0},{2,3},{3,2},{4,5},{5,4},{6,7},{7,6},{8,9},{9,8},{10,11... | collective-permute-start | bytes 251912 | tf_op jit(solution)/shard_map/ppermute | solution.py:877
  10.8 5.0 %collective-permute-start.1 = (f32[64,512]{1,0:T(8,128)S(1)}, f32[64,512]{1,0:T(8,128)S(1)}, u32[]{:S(2)}, u32[]{:S(2)}) collective-permute-start(f32[64,512]{1,0:T(8,128)S(1)} %get-tuple-element.53.refs_6_), channel_id=1, source_target_pairs={{0,1},{1,0},{2,3},{3,2},{4,5},{5,4},{6,7},{7,6},{8,9},{9,8},{10,11... | collective-permute-start | bytes 393224 | tf_op jit(solution)/shard_map/ppermute | solution.py:877
  17.4 13.0 %all-to-all-start = ((f32[32,1,128]{2,1,0:T(1,128)}), f32[32,1,128]{2,1,0:T(1,128)S(1)}, u32[]{:S(2)}, u32[]{:S(2)}) async-start(f32[32,1,128]{2,1,0:T(1,128)} %bitcast.8), calls=%async_computation | async-start | bytes 32768 | tf_op jit(solution)/shard_map/all_to_all | solution.py:940
  27.2 7.3 %collective-permute-start.2 = (f32[64,512]{1,0:T(8,128)S(1)}, f32[64,512]{1,0:T(8,128)S(1)}, u32[]{:S(2)}, u32[]{:S(2)}) collective-permute-start(f32[64,512]{1,0:T(8,128)S(1)} %data_part.4.refs_6_), channel_id=1, source_target_pairs={{0,1},{1,0},{2,3},{3,2},{4,5},{5,4},{6,7},{7,6},{8,9},{9,8},{10,11... | collective-permute-start | bytes 393224 | tf_op jit(solution)/shard_map/ppermute | solution.py:877
  36.1 10.4 %all-to-all-start.1 = ((f32[32,1,128]{2,1,0:T(1,128)}), f32[32,1,128]{2,1,0:T(1,128)S(1)}, u32[]{:S(2)}, u32[]{:S(2)}) async-start(f32[32,1,128]{2,1,0:T(1,128)} %bitcast.11), calls=%async_computation.1 | async-start | bytes 32768 | tf_op jit(solution)/shard_map/all_to_all | solution.py:940
  43.6 7.1 %collective-permute-start.3 = (f32[64,512]{1,0:T(8,128)S(1)}, f32[64,512]{1,0:T(8,128)S(1)}, u32[]{:S(2)}, u32[]{:S(2)}) collective-permute-start(f32[64,512]{1,0:T(8,128)S(1)} %data_part.5.refs_6_), channel_id=1, source_target_pairs={{0,1},{1,0},{2,3},{3,2},{4,5},{5,4},{6,7},{7,6},{8,9},{9,8},{10,11... | collective-permute-start | bytes 393224 | tf_op jit(solution)/shard_map/ppermute | solution.py:877
  52.3 1.3 %collective-permute-start.4 = (f32[136,128]{1,0:T(8,128)S(1)}, f32[136,128]{1,0:T(8,128)S(1)}, u32[]{:S(2)}, u32[]{:S(2)}) collective-permute-start(f32[136,128]{1,0:T(8,128)S(1)} %get-tuple-element.73), channel_id=1, source_target_pairs={{0,2},{2,0},{4,6},{6,4},{8,10},{10,8},{12,14},{14,12},{16,18},{18,... | collective-permute-start | bytes 208904 | tf_op jit(solution)/shard_map/ppermute | solution.py:873
  53.7 4.0 %collective-permute-start.5 = (f32[72,128]{1,0:T(8,128)S(1)}, f32[72,128]{1,0:T(8,128)S(1)}, u32[]{:S(2)}, u32[]{:S(2)}) collective-permute-start(f32[72,128]{1,0:T(8,128)S(1)} %get-tuple-element.75), channel_id=1, source_target_pairs={{0,4},{2,6},{4,0},{6,2},{8,12},{10,14},{12,8},{14,10},{16,20},{18,... | collective-permute-start | bytes 110600 | tf_op jit(solution)/shard_map/ppermute | solution.py:873
  54.3 4.3 %collective-permute-start.6 = (f32[72,128]{1,0:T(8,128)S(1)}, f32[72,128]{1,0:T(8,128)S(1)}, u32[]{:S(2)}, u32[]{:S(2)}) collective-permute-start(f32[72,128]{1,0:T(8,128)S(1)} %get-tuple-element.76), channel_id=1, source_target_pairs={{0,8},{2,10},{4,12},{6,14},{8,0},{10,2},{12,4},{14,6},{16,24},{18,... | collective-permute-start | bytes 110600 | tf_op jit(solution)/shard_map/ppermute | solution.py:873
  55.4 4.9 %collective-permute-start.7 = (f32[72,128]{1,0:T(8,128)S(1)}, f32[72,128]{1,0:T(8,128)S(1)}, u32[]{:S(2)}, u32[]{:S(2)}) collective-permute-start(f32[72,128]{1,0:T(8,128)S(1)} %get-tuple-element.77), channel_id=1, source_target_pairs={{0,12},{2,14},{4,8},{6,10},{8,4},{10,6},{12,0},{14,2},{16,28},{18,... | collective-permute-start | bytes 110600 | tf_op jit(solution)/shard_map/ppermute | solution.py:873
  60.4 6.0 %collective-permute-start.8 = (f32[136,128]{1,0:T(8,128)S(1)}, f32[136,128]{1,0:T(8,128)S(1)}, u32[]{:S(2)}, u32[]{:S(2)}) collective-permute-start(f32[136,128]{1,0:T(8,128)S(1)} %weigh.1.one), channel_id=1, source_target_pairs={{0,16},{2,18},{4,20},{6,22},{8,24},{10,26},{12,28},{14,30},{16,0},... | collective-permute-start | bytes 208904 | tf_op jit(solution)/shard_map/ppermute | solution.py:873
  66.6 5.5 %collective-permute-start.11 = (f32[64,128]{1,0:T(8,128)S(1)}, f32[64,128]{1,0:T(8,128)S(1)}, u32[]{:S(2)}, u32[]{:S(2)}) collective-permute-start(f32[64,128]{1,0:T(8,128)S(1)} %get-tuple-element.81), channel_id=1, source_target_pairs={{0,12},{2,14},{4,8},{6,10},{8,4},{10,6},{12,0},{14,2},{16,28},{18,... | collective-permute-start | bytes 98312 | tf_op jit(solution)/shard_map/ppermute | solution.py:873
  67.7 4.4 %collective-permute-start.10 = (f32[64,128]{1,0:T(8,128)S(1)}, f32[64,128]{1,0:T(8,128)S(1)}, u32[]{:S(2)}, u32[]{:S(2)}) collective-permute-start(f32[64,128]{1,0:T(8,128)S(1)} %get-tuple-element.81), channel_id=1, source_target_pairs={{0,8},{2,10},{4,12},{6,14},{8,0},{10,2},{12,4},{14,6},{16,24},{18,... | collective-permute-start | bytes 98312 | tf_op jit(solution)/shard_map/ppermute | solution.py:873
  68.2 3.9 %collective-permute-start.9 = (f32[64,128]{1,0:T(8,128)S(1)}, f32[64,128]{1,0:T(8,128)S(1)}, u32[]{:S(2)}, u32[]{:S(2)}) collective-permute-start(f32[64,128]{1,0:T(8,128)S(1)} %get-tuple-element.81), channel_id=1, source_target_pairs={{0,4},{2,6},{4,0},{6,2},{8,12},{10,14},{12,8},{14,10},{16,20},{18,... | collective-permute-start | bytes 98312 | tf_op jit(solution)/shard_map/ppermute | solution.py:873
  72.1 1.4 %collective-permute-start.12 = (f32[256,128]{1,0:T(8,128)S(1)}, f32[256,128]{1,0:T(8,128)S(1)}, u32[]{:S(2)}, u32[]{:S(2)}) collective-permute-start(f32[256,128]{1,0:T(8,128)S(1)} %constant_dynamic-update-slice_fusion.mine), channel_id=1, source_target_pairs={{0,2},{2,0},{4,6},{6,4},{8,10},{10,8},{12,14},{14,12},{16,18},{18,... | collective-permute-start | bytes 393224 | tf_op jit(solution)/shard_map/ppermute | solution.py:873

commit v7 on v6

--- a/solution.py
+++ b/solution.py
@@ -325,13 +325,6 @@
         slot, t = order[item // dumps], item % dumps
         return pltpu.make_async_copy(observed.at[slot, t], held.at[item], sems.at[item])
 
-    if not first_call:
-        for item in range(1, min(1 + AHEAD, slots * dumps)):
-
-            @pl.when(item < items)
-            def _():
-                copy_of(jnp.int32(item)).start()
-
     freq_value = frequency_of(chan_count)
     if first_call:
         if joined:
@@ -351,6 +344,13 @@
             xp[t, i] = pack(rows)
         for rj, rows in enumerate(right_rows(rot)):
             yp[t, rj] = pack(rows)
+    if not first_call:
+        for item in range(1, min(1 + AHEAD, slots * dumps)):
+
+            @pl.when(item < items)
+            def _():
+                copy_of(jnp.int32(item)).start()
+
     hl[...] = jnp.zeros_like(hl)
     ha[...] = jnp.zeros_like(ha)
 
@@ -480,8 +480,8 @@
 def apply_gram(gram, packed, rows):
     size = gram.shape[0]
     both = pack(gram)
-    wide = dot(both, packed[:rows], NN)
-    return wide[:size] + wide[size:] + dot(both[:size], packed[rows:], NN)
+    factors = jnp.concatenate([both[:size], both[size:], both[:size]], axis=1)
+    return dot(factors, jnp.concatenate([packed[:rows], packed], axis=0), NN)
 
 
 def lanes(parts, start, size):
@@ -503,9 +503,25 @@
         self.masks = {
             pair: (lane >= counts[:, k : k + 1]).astype(F32) for k, pair in enumerate(pairs)
         }
-        row = lax.broadcasted_iota(jnp.int32, (2 * self.size, 4 * self.size), 0) % self.size
-        col = lax.broadcasted_iota(jnp.int32, (2 * self.size, 4 * self.size), 1) % self.size
+        row = lax.broadcasted_iota(jnp.int32, (self.size, self.size), 0)
+        col = lax.broadcasted_iota(jnp.int32, (self.size, self.size), 1)
         self.upper = row < col
+
+    def kept(self, values):
+        n = self.size
+        return jnp.concatenate(
+            [
+                jnp.concatenate(
+                    [
+                        jnp.where(self.upper, values[i : i + n, j : j + n], 0.0)
+                        for j in range(0, 4 * n, n)
+                    ],
+                    axis=1,
+                )
+                for i in range(0, 2 * n, n)
+            ],
+            axis=0,
+        )
 
     def mask(self, pair, chunk):
         start = (chunk % self.per_block) * self.size
@@ -598,10 +614,12 @@
             xw = xc * chunks.mask(chunks.own_pair(c), c).astype(BF16)
             yn = jnp.concatenate([yc[:32], yc[:32], yc[32:], yc[32:]], axis=0)
             model = dot(jnp.concatenate([xw, xw], axis=0), yn, TN)
-            model = jnp.where(chunks.upper, model, 0.0)
+            model = chunks.kept(model)
             high, low = split(model)
             left = dot(yc, high, NT) + dot(yc, low, NT)
-            right = dot(xw, high, NN) + dot(xw, low, NN)
+            right = dot(
+                jnp.concatenate([xw, xw], axis=1), jnp.concatenate([high, low], axis=0), NN
+            )
             left = left[:32] + left[32:]
             right = right[:32] + right[32:]
             for pair, others in chunks.rect_terms(c):
@@ -703,7 +721,7 @@
                 jnp.concatenate([yc[:64], yc[:64], yc[64:], yc[64:]], axis=0),
                 TN,
             )
-            tangent = jnp.where(chunks.upper, tangent, 0.0)
+            tangent = chunks.kept(tangent)
             square = tangent * tangent
             squares = squares + jnp.sum(square.reshape(2 * size // 8, 8, 4 * size), axis=0)
             if c > 0:

time: 75.3 us -> 74.9 us (level)
  Pallas kernels: 31.4 us -> 30.5 us
    pallas_call x3, Pallas kernels: 12.3 us -> 11.4 us  [gradient_part(): pl.pallas_call(functools.partial(gradient_kernel, block, pairs, dumps, pe...]
  transfers between devices with their start and end apart: 15 -> 15, of which waited for: 11 -> 11; matrix products, arithmetic and copies ran while one was open for 0% -> 0% of each run, Pallas kernels for 29% -> 28%
where the time goes in v7:
time: 74.9 us; the launch traced here: 73.9 us
  Pallas kernels  30.5 us (41%)
  starting transfers between devices  23.6 us (32%)
  waiting for transfers between devices  18.1 us (24%)
  local copies, waits for them, and re-layouts  0.85 us (1%)
  between operations  0.85 us (1%)
    pallas_call x3, Pallas kernels, data_part(): pl.pallas_call(body, name='data_part', out_shape=tuple(shapes), in_specs=...  11.8 us
    pallas_call x3, Pallas kernels, gradient_part(): pl.pallas_call(functools.partial(gradient_kernel, block, pairs, dumps, pe...  11.4 us
    ppermute x9, waiting for transfers between devices, swap(): return lax.ppermute(value, 'chan', [(i, i ^ offset) for i in range(count)])  10.7 us
    ppermute x9, starting transfers between devices, swap(): return lax.ppermute(value, 'chan', [(i, i ^ offset) for i in range(count)])  9.76 us
    all_to_all x2, starting transfers between devices, shards(): sums = lax.all_to_all(sums, ('chan', 'stn'), 0, 0, tiled=True)  9.08 us
    all_to_all x2, waiting for transfers between devices, shards(): sums = lax.all_to_all(sums, ('chan', 'stn'), 0, 0, tiled=True)  5.08 us
    ppermute x4, starting transfers between devices, other_stations(): return lax.ppermute(value, 'stn', [(0, 1), (1, 0)])  4.81 us
    pallas_call x3, Pallas kernels, curvature_part(): pl.pallas_call(functools.partial(curvature_kernel, block, pairs, dumps, p...  4.67 us
  transfers between devices with their start and end apart: 15, of which 11 were waited for; matrix products, arithmetic and copies ran while one was open for 0% of the time, Pallas kernels for 28%

profile of v7, /device:TPU:0, one launch (start us, length us, event | category | flops | bytes accessed | tf_op | source)
XLA Modules:
  0.0 73.9 jit_solution(1363002439475161852)
XLA Ops:
  0.7 0.0 slice-start
  0.7 0.6 copy-done.3
  1.3 0.0 copy-done.4
  1.3 0.1 copy-done.6
  1.4 0.1 copy-done.5
  1.6 3.0 %collective-permute-start = (f32[82,1,256]{2,1,0:T(1,128)S(1)}, f32[82,1,256]{2,1,0:T(1,128)S(1)}, u32[]{:S(2)}, u32[]{:S(2)}) collective-permute-start(f32[82,1,256]{2,1,0:T(1,128)S(1)} %field_rows.1.refs_5_), channel_id=1, source_target_pairs={{0,1},{1,0},{2,3},{3,2},{4,5},{5,4},{6,7},{7,6},{8,9},{9,8},{10,11... | collective-permute-start | bytes 251912 | tf_op jit(solution)/shard_map/ppermute | solution.py:895
  4.6 0.7 prepare.1
  5.3 1.7 %collective-permute-done.refs_6_ = f32[82,1,256]{2,1,0:T(1,128)S(1)} collective-permute-done((f32[82,1,256]{2,1,0:T(1,128)S(1)}, f32[82,1,256]{2,1,0:T(1,128)S(1)}, u32[]{:S(2)}, u32[]{:S(2)}) %collective-permute-start) | collective-permute-done | bytes 84000 | tf_op jit(solution)/shard_map/ppermute | solution.py:895
  7.1 3.7 %data_part.3 = (f32[64,512]{1,0:T(8,128)S(1)}, f32[64,512]{1,0:T(8,128)S(1)}, f32[16,512]{1,0:T(8,128)S(1)}, f32[8,128]{1,0:T(8,128)S(1)}, bf16[8,256,256]{2,1,0:T(8,128)(2,1)S(1)}) custom-call(s32[4]{0:T(128)S(1)} %copy-done.3, s32[4]{0:T(128)S(1)} %copy-done.4, bf16[4,2,8,256,256]{4,3,2,1,0:T(8,128)(2,1)S(1)} %bitcast.28, ...), custom_call_target="tpu_custom_call" | custom-call | flops 6000000000 | bytes 8000000 | tf_op jit(solution)/shard_map/data_part/pallas_call | solution.py:454
  10.8 0.8 %collective-permute-start.1 = (f32[64,512]{1,0:T(8,128)S(1)}, f32[64,512]{1,0:T(8,128)S(1)}, u32[]{:S(2)}, u32[]{:S(2)}) collective-permute-start(f32[64,512]{1,0:T(8,128)S(1)} %get-tuple-element.53.refs_6_), channel_id=1, source_target_pairs={{0,1},{1,0},{2,3},{3,2},{4,5},{5,4},{6,7},{7,6},{8,9},{9,8},{10,11... | collective-permute-start | bytes 393224 | tf_op jit(solution)/shard_map/ppermute | solution.py:895
  11.5 3.7 %gradient_part.3 = (f32[64,512]{1,0:T(8,128)S(1)}, bf16[2,2,64,512]{3,2,1,0:T(8,128)(2,1)S(1)}, bf16[2,4,64,512]{3,2,1,0:T(8,128)(2,1)S(1)}) custom-call(f32[8,128]{1,0:T(8,128)S(1)} %get-tuple-element.47.refs_0_, f32[16,512]{1,0:T(8,128)S(1)} %get-tuple-element.48.refs_1_.refs_7_, f32[64,128]{1,0:T(8,128)S(1)} %get-tuple-element.44.refs_3_.refs_2_, ...), custom_call_target="tpu_custom_call" | custom-call | flops 4000000000 | bytes 2000000 | tf_op jit(solution)/shard_map/gradient_part/pallas_call | solution.py:654
  15.2 0.6 collective-permute-done.1.refs_7_
  15.8 1.6 %curvature_part.3 = (f32[64,512]{1,0:T(8,128)S(1)}, f32[64,512]{1,0:T(8,128)S(1)}, f32[32,128]{1,0:T(8,128)}) custom-call(f32[8,128]{1,0:T(8,128)S(1)} %get-tuple-element.47.refs_0_, f32[16,512]{1,0:T(8,128)S(1)} %get-tuple-element.48.refs_1_.refs_7_, f32[64,128]{1,0:T(8,128)S(1)} %get-tuple-element.44.refs_3_.refs_2_, ...), custom_call_target="tpu_custom_call" | custom-call | flops 2000000000 | bytes 2000000 | tf_op jit(solution)/shard_map/curvature_part/pallas_call | solution.py:761
  17.4 5.6 %all-to-all-start = ((f32[32,1,128]{2,1,0:T(1,128)}), f32[32,1,128]{2,1,0:T(1,128)S(1)}, u32[]{:S(2)}, u32[]{:S(2)}) async-start(f32[32,1,128]{2,1,0:T(1,128)} %bitcast.8), calls=%async_computation | async-start | bytes 32768 | tf_op jit(solution)/shard_map/all_to_all | solution.py:958
  23.0 4.0 %data_part.4.refs_6_ = f32[64,512]{1,0:T(8,128)S(1)} custom-call(s32[4]{0:T(128)S(1)} %copy-done.3, s32[4]{0:T(128)S(1)} %copy-done.4, bf16[4,2,8,256,256]{4,3,2,1,0:T(8,128)(2,1)} %bitcast.24, f32[64,128]{1,0:T(8,128)S(1)} %get-tuple-element.44.refs_3_.refs_2_, bf16[2,256,256]{2,1,0:T(8,128)(2,1)S(1)} %baseline_masks.1.masks.refs_4_, ...), custom_call_target="tpu_custom_call" | custom-call | flops 6000000000 | bytes 8000000 | tf_op jit(solution)/shard_map/data_part/pallas_call | solution.py:454
  26.9 0.5 collective-permute-start.2
  27.4 2.6 %all-to-all-done = f32[32,1,128]{2,1,0:T(1,128)S(1)} async-done(((f32[32,1,128]{2,1,0:T(1,128)}), f32[32,1,128]{2,1,0:T(1,128)S(1)}, u32[]{:S(2)}, u32[]{:S(2)}) %all-to-all-start) | async-done | bytes 16416 | tf_op jit(solution)/shard_map/all_to_all | solution.py:958
  30.1 3.9 %gradient_part.4 = (f32[64,512]{1,0:T(8,128)S(1)}, f32[64,512]{1,0:T(8,128)S(1)}, f32[8,128]{1,0:T(8,128)S(1)}, bf16[2,2,64,512]{3,2,1,0:T(8,128)(2,1)S(1)}, bf16[2,4,64,512]{3,2,1,0:T(8,128)(2,1)S(1)}) custom-call(f32[8,128]{1,0:T(8,128)S(1)} %get-tuple-element.47.refs_0_, f32[16,512]{1,0:T(8,128)S(1)} %get-tuple-element.48.refs_1_.refs_7_, ...), custom_call_target="tpu_custom_call" | custom-call | flops 4000000000 | bytes 2000000 | tf_op jit(solution)/shard_map/gradient_part/pallas_call | solution.py:654
  33.9 0.0 collective-permute-done.2.refs_7_
  34.0 1.6 %curvature_part.4 = (f32[64,512]{1,0:T(8,128)S(1)}, f32[64,512]{1,0:T(8,128)S(1)}, f32[32,128]{1,0:T(8,128)}) custom-call(f32[8,128]{1,0:T(8,128)S(1)} %get-tuple-element.47.refs_0_, f32[16,512]{1,0:T(8,128)S(1)} %get-tuple-element.48.refs_1_.refs_7_, f32[64,128]{1,0:T(8,128)S(1)} %get-tuple-element.44.refs_3_.refs_2_, ...), custom_call_target="tpu_custom_call" | custom-call | flops 2000000000 | bytes 2000000 | tf_op jit(solution)/shard_map/curvature_part/pallas_call | solution.py:761
  35.5 3.5 %all-to-all-start.1 = ((f32[32,1,128]{2,1,0:T(1,128)}), f32[32,1,128]{2,1,0:T(1,128)S(1)}, u32[]{:S(2)}, u32[]{:S(2)}) async-start(f32[32,1,128]{2,1,0:T(1,128)} %bitcast.11), calls=%async_computation.1 | async-start | bytes 32768 | tf_op jit(solution)/shard_map/all_to_all | solution.py:958
  39.0 4.1 %data_part.5.refs_6_ = f32[64,512]{1,0:T(8,128)S(1)} custom-call(s32[4]{0:T(128)S(1)} %copy-done.3, s32[4]{0:T(128)S(1)} %copy-done.4, bf16[4,2,8,256,256]{4,3,2,1,0:T(8,128)(2,1)} %bitcast.25, f32[64,128]{1,0:T(8,128)S(1)} %get-tuple-element.44.refs_3_.refs_2_, bf16[2,256,256]{2,1,0:T(8,128)(2,1)S(1)} %baseline_masks.1.masks.refs_4_, ...), custom_call_target="tpu_custom_call" | custom-call | flops 6000000000 | bytes 8000000 | tf_op jit(solution)/shard_map/data_part/pallas_call | solution.py:454
  43.2 0.5 collective-permute-start.3
  43.7 2.5 %all-to-all-done.1 = f32[32,1,128]{2,1,0:T(1,128)S(1)} async-done(((f32[32,1,128]{2,1,0:T(1,128)}), f32[32,1,128]{2,1,0:T(1,128)S(1)}, u32[]{:S(2)}, u32[]{:S(2)}) %all-to-all-start.1) | async-done | bytes 16416 | tf_op jit(solution)/shard_map/all_to_all | solution.py:958
  46.1 3.9 %gradient_part.5 = (f32[64,512]{1,0:T(8,128)S(1)}, f32[64,512]{1,0:T(8,128)S(1)}, f32[8,128]{1,0:T(8,128)S(1)}, bf16[2,2,64,512]{3,2,1,0:T(8,128)(2,1)S(1)}, bf16[2,4,64,512]{3,2,1,0:T(8,128)(2,1)S(1)}) custom-call(f32[8,128]{1,0:T(8,128)S(1)} %get-tuple-element.47.refs_0_, f32[16,512]{1,0:T(8,128)S(1)} %get-tuple-element.48.refs_1_.refs_7_, ...), custom_call_target="tpu_custom_call" | custom-call | flops 4000000000 | bytes 2000000 | tf_op jit(solution)/shard_map/gradient_part/pallas_call | solution.py:654
  50.0 0.0 collective-permute-done.3.refs_7_
  50.0 1.5 %curvature_part.5 = (f32[64,512]{1,0:T(8,128)S(1)}, f32[136,128]{1,0:T(8,128)S(1)}, f32[136,128]{1,0:T(8,128)S(1)}) custom-call(f32[8,128]{1,0:T(8,128)S(1)} %get-tuple-element.47.refs_0_, f32[16,512]{1,0:T(8,128)S(1)} %get-tuple-element.48.refs_1_.refs_7_, f32[64,128]{1,0:T(8,128)S(1)} %get-tuple-element.44.refs_3_.refs_2_, ...), custom_call_target="tpu_custom_call" | custom-call | flops 2000000000 | bytes 2000000 | tf_op jit(solution)/shard_map/curvature_part/pallas_call | solution.py:761
  51.6 0.1 collective-permute-start.4
  51.7 1.2 %collective-permute-done.4.theirs = f32[136,128]{1,0:T(8,128)S(1)} collective-permute-done((f32[136,128]{1,0:T(8,128)S(1)}, f32[136,128]{1,0:T(8,128)S(1)}, u32[]{:S(2)}, u32[]{:S(2)}) %collective-permute-start.4) | collective-permute-done | bytes 69664 | tf_op jit(solution)/shard_map/ppermute | solution.py:891
  52.9 0.6 collective-permute-start.5
  53.5 1.5 %collective-permute-start.6 = (f32[72,128]{1,0:T(8,128)S(1)}, f32[72,128]{1,0:T(8,128)S(1)}, u32[]{:S(2)}, u32[]{:S(2)}) collective-permute-start(f32[72,128]{1,0:T(8,128)S(1)} %get-tuple-element.76), channel_id=1, source_target_pairs={{0,8},{2,10},{4,12},{6,14},{8,0},{10,2},{12,4},{14,6},{16,24},{18,... | collective-permute-start | bytes 110600 | tf_op jit(solution)/shard_map/ppermute | solution.py:891
  55.0 1.5 %collective-permute-start.7 = (f32[72,128]{1,0:T(8,128)S(1)}, f32[72,128]{1,0:T(8,128)S(1)}, u32[]{:S(2)}, u32[]{:S(2)}) collective-permute-start(f32[72,128]{1,0:T(8,128)S(1)} %get-tuple-element.77), channel_id=1, source_target_pairs={{0,12},{2,14},{4,8},{6,10},{8,4},{10,6},{12,0},{14,2},{16,28},{18,... | collective-permute-start | bytes 110600 | tf_op jit(solution)/shard_map/ppermute | solution.py:891
  56.5 0.5 collective-permute-done.5.refs_1_
  56.9 0.8 %collective-permute-done.6.refs_2_ = f32[72,128]{1,0:T(8,128)S(1)} collective-permute-done((f32[72,128]{1,0:T(8,128)S(1)}, f32[72,128]{1,0:T(8,128)S(1)}, u32[]{:S(2)}, u32[]{:S(2)}) %collective-permute-start.6) | collective-permute-done | bytes 36896 | tf_op jit(solution)/shard_map/ppermute | solution.py:891
  57.8 2.1 %collective-permute-done.7.refs_3_ = f32[72,128]{1,0:T(8,128)S(1)} collective-permute-done((f32[72,128]{1,0:T(8,128)S(1)}, f32[72,128]{1,0:T(8,128)S(1)}, u32[]{:S(2)}, u32[]{:S(2)}) %collective-permute-start.7) | collective-permute-done | bytes 36896 | tf_op jit(solution)/shard_map/ppermute | solution.py:891
  59.8 0.1 weigh.1.one
  59.9 2.5 %collective-permute-start.8 = (f32[136,128]{1,0:T(8,128)S(1)}, f32[136,128]{1,0:T(8,128)S(1)}, u32[]{:S(2)}, u32[]{:S(2)}) collective-permute-start(f32[136,128]{1,0:T(8,128)S(1)} %weigh.1.one), channel_id=1, source_target_pairs={{0,16},{2,18},{4,20},{6,22},{8,24},{10,26},{12,28},{14,30},{16,0},... | collective-permute-start | bytes 208904 | tf_op jit(solution)/shard_map/ppermute | solution.py:891
  62.4 3.5 %collective-permute-done.8.two = f32[136,128]{1,0:T(8,128)S(1)} collective-permute-done((f32[136,128]{1,0:T(8,128)S(1)}, f32[136,128]{1,0:T(8,128)S(1)}, u32[]{:S(2)}, u32[]{:S(2)}) %collective-permute-start.8) | collective-permute-done | bytes 69664 | tf_op jit(solution)/shard_map/ppermute | solution.py:891
  66.0 0.2 combine.1
  66.2 0.8 %collective-permute-start.11 = (f32[64,128]{1,0:T(8,128)S(1)}, f32[64,128]{1,0:T(8,128)S(1)}, u32[]{:S(2)}, u32[]{:S(2)}) collective-permute-start(f32[64,128]{1,0:T(8,128)S(1)} %get-tuple-element.81), channel_id=1, source_target_pairs={{0,12},{2,14},{4,8},{6,10},{8,4},{10,6},{12,0},{14,2},{16,28},{18,... | collective-permute-start | bytes 98312 | tf_op jit(solution)/shard_map/ppermute | solution.py:891
  67.0 0.5 collective-permute-start.10
  67.5 2.2 %collective-permute-start.9 = (f32[64,128]{1,0:T(8,128)S(1)}, f32[64,128]{1,0:T(8,128)S(1)}, u32[]{:S(2)}, u32[]{:S(2)}) collective-permute-start(f32[64,128]{1,0:T(8,128)S(1)} %get-tuple-element.81), channel_id=1, source_target_pairs={{0,4},{2,6},{4,0},{6,2},{8,12},{10,14},{12,8},{14,10},{16,20},{18,... | collective-permute-start | bytes 98312 | tf_op jit(solution)/shard_map/ppermute | solution.py:891
  69.7 1.9 %collective-permute-done.9 = f32[64,128]{1,0:T(8,128)S(1)} collective-permute-done((f32[64,128]{1,0:T(8,128)S(1)}, f32[64,128]{1,0:T(8,128)S(1)}, u32[]{:S(2)}, u32[]{:S(2)}) %collective-permute-start.9) | collective-permute-done | bytes 32800 | tf_op jit(solution)/shard_map/ppermute | solution.py:891
  71.6 0.0 collective-permute-done.10
  71.6 0.1 collective-permute-start.12
  71.7 0.7 last_step.1
  72.4 0.6 collective-permute-done.12.theirs
  73.1 0.9 %consensus.1 = (f32[64,4,256]{2,1,0:T(4,128)}, f32[64,1,256]{2,1,0:T(1,128)}) custom-call(f32[256,128]{1,0:T(8,128)S(1)} %constant_dynamic-update-slice_fusion.mine, f32[256,128]{1,0:T(8,128)S(1)} %collective-permute-done.12.theirs, f32[64,1,256]{2,1,0:T(1,128)S(1)} %get-tuple-element.82.shifted), custom_call_target="tpu_custom_call" | custom-call | tf_op jit(solution)/shard_map/consensus/pallas_call | solution.py:880
  (22 shorter events, 0.1 us)
Async XLA Ops:
  0.6 0.7 copy-start.3
  0.6 0.7 copy-start.4
  0.7 0.7 copy-start.6
  0.7 0.9 %copy-start.5 = (f32[8,8,1,256]{3,2,1,0:T(1,128)S(1)}, f32[8,8,1,256]{3,2,1,0:T(1,128)}, u32[]{:S(2)}) copy-start(f32[8,8,1,256]{3,2,1,0:T(1,128)} %param.11) | copy-start | bytes 196612
  0.7 6.4 %slice-start = ((s8[8388608]{0:T(1024)(128)(4,1)}), s8[4194304]{0:T(1024)(128)(4,1)S(1)}, s32[]{:S(2)}) async-start(s8[8388608]{0:T(1024)(128)(4,1)} %bitcast.26), calls=%async_computation.2 | async-start | bytes 8388608
  1.5 3.1 %copy-start = (f32[8,8,4,256]{3,2,1,0:T(4,128)S(1)}, f32[8,8,4,256]{3,2,1,0:T(4,128)}, u32[]{:S(2)}) copy-start(f32[8,8,4,256]{3,2,1,0:T(4,128)} %param.13) | copy-start | bytes 786436
  1.5 3.1 %copy-start.1 = (f32[8,8,1,256]{3,2,1,0:T(1,128)S(1)}, f32[8,8,1,256]{3,2,1,0:T(1,128)}, u32[]{:S(2)}) copy-start(f32[8,8,1,256]{3,2,1,0:T(1,128)} %param.12) | copy-start | bytes 196612
  1.5 3.1 %copy-start.2 = (f32[8,8]{1,0:T(8,128)S(1)}, f32[8,8]{1,0:T(8,128)}, u32[]{:S(2)}) copy-start(f32[8,8]{1,0:T(8,128)} %refs_4_.1) | copy-start | bytes 772
  1.5 5.5 %slice-start.1 = ((s8[8388608]{0:T(1024)(128)(4,1)}), s8[4194304]{0:T(1024)(128)(4,1)S(1)}, s32[]{:S(2)}) async-start(s8[8388608]{0:T(1024)(128)(4,1)} %bitcast.26), calls=%async_computation.3 | async-start | bytes 8388608
  1.6 5.5 %collective-permute-start = (f32[82,1,256]{2,1,0:T(1,128)S(1)}, f32[82,1,256]{2,1,0:T(1,128)S(1)}, u32[]{:S(2)}, u32[]{:S(2)}) collective-permute-start(f32[82,1,256]{2,1,0:T(1,128)S(1)} %field_rows.1.refs_5_), channel_id=1, source_target_pairs={{0,1},{1,0},{2,3},{3,2},{4,5},{5,4},{6,7},{7,6},{8,9},{9,8},{10,11... | collective-permute-start | bytes 251912 | tf_op jit(solution)/shard_map/ppermute | solution.py:895
  10.8 5.0 %collective-permute-start.1 = (f32[64,512]{1,0:T(8,128)S(1)}, f32[64,512]{1,0:T(8,128)S(1)}, u32[]{:S(2)}, u32[]{:S(2)}) collective-permute-start(f32[64,512]{1,0:T(8,128)S(1)} %get-tuple-element.53.refs_6_), channel_id=1, source_target_pairs={{0,1},{1,0},{2,3},{3,2},{4,5},{5,4},{6,7},{7,6},{8,9},{9,8},{10,11... | collective-permute-start | bytes 393224 | tf_op jit(solution)/shard_map/ppermute | solution.py:895
  17.4 12.7 %all-to-all-start = ((f32[32,1,128]{2,1,0:T(1,128)}), f32[32,1,128]{2,1,0:T(1,128)S(1)}, u32[]{:S(2)}, u32[]{:S(2)}) async-start(f32[32,1,128]{2,1,0:T(1,128)} %bitcast.8), calls=%async_computation | async-start | bytes 32768 | tf_op jit(solution)/shard_map/all_to_all | solution.py:958
  26.9 7.0 %collective-permute-start.2 = (f32[64,512]{1,0:T(8,128)S(1)}, f32[64,512]{1,0:T(8,128)S(1)}, u32[]{:S(2)}, u32[]{:S(2)}) collective-permute-start(f32[64,512]{1,0:T(8,128)S(1)} %data_part.4.refs_6_), channel_id=1, source_target_pairs={{0,1},{1,0},{2,3},{3,2},{4,5},{5,4},{6,7},{7,6},{8,9},{9,8},{10,11... | collective-permute-start | bytes 393224 | tf_op jit(solution)/shard_map/ppermute | solution.py:895
  35.5 10.6 %all-to-all-start.1 = ((f32[32,1,128]{2,1,0:T(1,128)}), f32[32,1,128]{2,1,0:T(1,128)S(1)}, u32[]{:S(2)}, u32[]{:S(2)}) async-start(f32[32,1,128]{2,1,0:T(1,128)} %bitcast.11), calls=%async_computation.1 | async-start | bytes 32768 | tf_op jit(solution)/shard_map/all_to_all | solution.py:958
  43.2 6.8 %collective-permute-start.3 = (f32[64,512]{1,0:T(8,128)S(1)}, f32[64,512]{1,0:T(8,128)S(1)}, u32[]{:S(2)}, u32[]{:S(2)}) collective-permute-start(f32[64,512]{1,0:T(8,128)S(1)} %data_part.5.refs_6_), channel_id=1, source_target_pairs={{0,1},{1,0},{2,3},{3,2},{4,5},{5,4},{6,7},{7,6},{8,9},{9,8},{10,11... | collective-permute-start | bytes 393224 | tf_op jit(solution)/shard_map/ppermute | solution.py:895
  51.6 1.3 %collective-permute-start.4 = (f32[136,128]{1,0:T(8,128)S(1)}, f32[136,128]{1,0:T(8,128)S(1)}, u32[]{:S(2)}, u32[]{:S(2)}) collective-permute-start(f32[136,128]{1,0:T(8,128)S(1)} %get-tuple-element.73), channel_id=1, source_target_pairs={{0,2},{2,0},{4,6},{6,4},{8,10},{10,8},{12,14},{14,12},{16,18},{18,... | collective-permute-start | bytes 208904 | tf_op jit(solution)/shard_map/ppermute | solution.py:891
  52.9 4.0 %collective-permute-start.5 = (f32[72,128]{1,0:T(8,128)S(1)}, f32[72,128]{1,0:T(8,128)S(1)}, u32[]{:S(2)}, u32[]{:S(2)}) collective-permute-start(f32[72,128]{1,0:T(8,128)S(1)} %get-tuple-element.75), channel_id=1, source_target_pairs={{0,4},{2,6},{4,0},{6,2},{8,12},{10,14},{12,8},{14,10},{16,20},{18,... | collective-permute-start | bytes 110600 | tf_op jit(solution)/shard_map/ppermute | solution.py:891
  53.5 4.3 %collective-permute-start.6 = (f32[72,128]{1,0:T(8,128)S(1)}, f32[72,128]{1,0:T(8,128)S(1)}, u32[]{:S(2)}, u32[]{:S(2)}) collective-permute-start(f32[72,128]{1,0:T(8,128)S(1)} %get-tuple-element.76), channel_id=1, source_target_pairs={{0,8},{2,10},{4,12},{6,14},{8,0},{10,2},{12,4},{14,6},{16,24},{18,... | collective-permute-start | bytes 110600 | tf_op jit(solution)/shard_map/ppermute | solution.py:891
  55.0 4.9 %collective-permute-start.7 = (f32[72,128]{1,0:T(8,128)S(1)}, f32[72,128]{1,0:T(8,128)S(1)}, u32[]{:S(2)}, u32[]{:S(2)}) collective-permute-start(f32[72,128]{1,0:T(8,128)S(1)} %get-tuple-element.77), channel_id=1, source_target_pairs={{0,12},{2,14},{4,8},{6,10},{8,4},{10,6},{12,0},{14,2},{16,28},{18,... | collective-permute-start | bytes 110600 | tf_op jit(solution)/shard_map/ppermute | solution.py:891
  59.9 6.0 %collective-permute-start.8 = (f32[136,128]{1,0:T(8,128)S(1)}, f32[136,128]{1,0:T(8,128)S(1)}, u32[]{:S(2)}, u32[]{:S(2)}) collective-permute-start(f32[136,128]{1,0:T(8,128)S(1)} %weigh.1.one), channel_id=1, source_target_pairs={{0,16},{2,18},{4,20},{6,22},{8,24},{10,26},{12,28},{14,30},{16,0},... | collective-permute-start | bytes 208904 | tf_op jit(solution)/shard_map/ppermute | solution.py:891
  66.2 5.5 %collective-permute-start.11 = (f32[64,128]{1,0:T(8,128)S(1)}, f32[64,128]{1,0:T(8,128)S(1)}, u32[]{:S(2)}, u32[]{:S(2)}) collective-permute-start(f32[64,128]{1,0:T(8,128)S(1)} %get-tuple-element.81), channel_id=1, source_target_pairs={{0,12},{2,14},{4,8},{6,10},{8,4},{10,6},{12,0},{14,2},{16,28},{18,... | collective-permute-start | bytes 98312 | tf_op jit(solution)/shard_map/ppermute | solution.py:891
  67.0 4.7 %collective-permute-start.10 = (f32[64,128]{1,0:T(8,128)S(1)}, f32[64,128]{1,0:T(8,128)S(1)}, u32[]{:S(2)}, u32[]{:S(2)}) collective-permute-start(f32[64,128]{1,0:T(8,128)S(1)} %get-tuple-element.81), channel_id=1, source_target_pairs={{0,8},{2,10},{4,12},{6,14},{8,0},{10,2},{12,4},{14,6},{16,24},{18,... | collective-permute-start | bytes 98312 | tf_op jit(solution)/shard_map/ppermute | solution.py:891
  67.5 4.1 %collective-permute-start.9 = (f32[64,128]{1,0:T(8,128)S(1)}, f32[64,128]{1,0:T(8,128)S(1)}, u32[]{:S(2)}, u32[]{:S(2)}) collective-permute-start(f32[64,128]{1,0:T(8,128)S(1)} %get-tuple-element.81), channel_id=1, source_target_pairs={{0,4},{2,6},{4,0},{6,2},{8,12},{10,14},{12,8},{14,10},{16,20},{18,... | collective-permute-start | bytes 98312 | tf_op jit(solution)/shard_map/ppermute | solution.py:891
  71.6 1.4 %collective-permute-start.12 = (f32[256,128]{1,0:T(8,128)S(1)}, f32[256,128]{1,0:T(8,128)S(1)}, u32[]{:S(2)}, u32[]{:S(2)}) collective-permute-start(f32[256,128]{1,0:T(8,128)S(1)} %constant_dynamic-update-slice_fusion.mine), channel_id=1, source_target_pairs={{0,2},{2,0},{4,6},{6,4},{8,10},{10,8},{12,14},{14,12},{16,18},{18,... | collective-permute-start | bytes 393224 | tf_op jit(solution)/shard_map/ppermute | solution.py:891

commit v8 on v7

--- a/solution.py
+++ b/solution.py
@@ -93,6 +93,15 @@
     return 1.0 - 2.0 * sin_half * sin_half, 2.0 * sin_half * cos_half
 
 
+def turned(turns_ref, t):
+    dumps = turns_ref.shape[0] // 16
+
+    def rows(n):
+        return turns_ref[pl.ds(n if isinstance(n, int) else pl.multiple_of(n, 8), 8), :]
+
+    return rows(8 * t), rows(8 * (t + dumps))
+
+
 def rotate(field, cosine, sine):
     re = [field[8 * m : 8 * m + 8] for m in range(4)]
     im = [field[32 + 8 * m : 40 + 8 * m] for m in range(4)]
@@ -325,20 +334,23 @@
         slot, t = order[item // dumps], item % dumps
         return pltpu.make_async_copy(observed.at[slot, t], held.at[item], sems.at[item])
 
-    freq_value = frequency_of(chan_count)
     if first_call:
         if joined:
             rows_other = rows_all
             field_ref[...] = rows_all[:64, 0, :]
-            delay_ref[...] = rows_all[64 : 64 + 8 * dumps, 0, :]
+            delay_ref[: 8 * dumps, :] = rows_all[64 : 64 + 8 * dumps, 0, :]
         else:
             at_other = pl.ds(pl.multiple_of((1 - lax.axis_index("stn")) * block, CHUNK), block)
             for at, rows in ((at_own, rows_mine), (at_other, rows_other)):
                 field_ref[:, at] = rows[:64, 0, :]
-                delay_ref[:, at] = rows[64 : 64 + 8 * dumps, 0, :]
+                delay_ref[: 8 * dumps, at] = rows[64 : 64 + 8 * dumps, 0, :]
+    if first_call:
+        cosine, sine = trig(delay_ref[: 8 * dumps, :], frequency_of(chan_count))
+        delay_ref[: 8 * dumps, :] = cosine
+        delay_ref[8 * dumps :, :] = sine
     bright = coherency_rows(coh_ref[...], stations)
     for t in range(dumps):
-        cosine, sine = trig(delay_ref[8 * t : 8 * t + 8, :], freq_value)
+        cosine, sine = turned(delay_ref, t)
         rot = rotate(field_ref[...], cosine, sine)
         for i, rows in enumerate(left_rows(rot, bright)):
             xp[t, i] = pack(rows)
@@ -412,7 +424,7 @@
 
     total = None
     for t in range(dumps):
-        cosine, sine = trig(delay_ref[8 * t : 8 * t + 8, :], freq_value)
+        cosine, sine = turned(delay_ref, t)
         piece = field_gradient(
             [hl[t, i] for i in range(2)], [ha[t, rj] for rj in range(4)], bright, cosine, sine
         )
@@ -442,7 +454,7 @@
     )
     shapes = [shape(64, stations)]
     if first_call:
-        shapes += [shape(64, stations), shape(8 * dumps, stations), shape(8, 128)]
+        shapes += [shape(64, stations), shape(16 * dumps, stations), shape(8, 128)]
         shapes.append(shape(*observed.shape[2:], dtype=BF16))
         place, copies = vmem_specs(1), []
     else:
@@ -591,11 +603,10 @@
         alpha_out[...] = jnp.broadcast_to(alpha, (8, 128))
         current = current - alpha * direction_ref[...]
         current_out[...] = current
-    freq_value = frequency_of(chan_count)
     bright = coherency_rows(coh_ref[...], stations)
     gradient = None
     for t in range(dumps):
-        cosine, sine = trig(delay_ref[8 * t : 8 * t + 8, :], freq_value)
+        cosine, sine = turned(delay_ref, t)
         rot = rotate(current, cosine, sine)
         xs = [pack(v) for v in left_rows(rot, bright)]
         ys = [pack(v) for v in right_rows(rot)]
@@ -686,7 +697,6 @@
     if not last:
         linear_out[...] = linear
 
-    freq_value = frequency_of(chan_count)
     bright = coherency_rows(coh_ref[...], stations)
     squares = jnp.zeros((8, 4 * size), F32)
     grams = jnp.zeros((64, 64), F32)
@@ -698,8 +708,7 @@
         visited = [lax.axis_index("stn") % dumps] if shared else range(dumps)
         repeats, copies = (stn_count // dumps if shared else stn_count), stn_count
     for t in visited:
-        delay = delay_ref[pl.ds(pl.multiple_of(8 * t, 8), 8), :]
-        cosine, sine = trig(delay, freq_value)
+        cosine, sine = turned(delay_ref, t)
         step = rotate(direction, cosine, sine)
         xs = [xp[t, i] for i in range(2)]
         ys = [yp[t, rj] for rj in range(4)]

time: 74.9 us -> 74.8 us (level)
  no operation moved by 1% of the time
where the time goes in v8:
time: 74.8 us; the launch traced here: 73.8 us
  Pallas kernels  30.4 us (41%)
  starting transfers between devices  23.7 us (32%)
  waiting for transfers between devices  18.1 us (24%)
  local copies, waits for them, and re-layouts  0.85 us (1%)
  between operations  0.85 us (1%)
    pallas_call x3, Pallas kernels, data_part(): pl.pallas_call(body, name='data_part', out_shape=tuple(shapes), in_specs=...  11.7 us
    pallas_call x3, Pallas kernels, gradient_part(): pl.pallas_call(functools.partial(gradient_kernel, block, pairs, dumps, pe...  11.4 us
    ppermute x9, waiting for transfers between devices, swap(): return lax.ppermute(value, 'chan', [(i, i ^ offset) for i in range(count)])  10.7 us
    ppermute x9, starting transfers between devices, swap(): return lax.ppermute(value, 'chan', [(i, i ^ offset) for i in range(count)])  9.75 us
    all_to_all x2, starting transfers between devices, shards(): sums = lax.all_to_all(sums, ('chan', 'stn'), 0, 0, tiled=True)  9.07 us
    all_to_all x2, waiting for transfers between devices, shards(): sums = lax.all_to_all(sums, ('chan', 'stn'), 0, 0, tiled=True)  5.14 us
    ppermute x4, starting transfers between devices, other_stations(): return lax.ppermute(value, 'stn', [(0, 1), (1, 0)])  4.83 us
    pallas_call x3, Pallas kernels, curvature_part(): pl.pallas_call(functools.partial(curvature_kernel, block, pairs, dumps, p...  4.65 us
  transfers between devices with their start and end apart: 15, of which 11 were waited for; matrix products, arithmetic and copies ran while one was open for 0% of the time, Pallas kernels for 28%

profile of v8, /device:TPU:0, one launch (start us, length us, event | category | flops | bytes accessed | tf_op | source)
XLA Modules:
  0.0 73.8 jit_solution(2783961179844318791)
XLA Ops:
  0.7 0.0 slice-start
  0.7 0.6 copy-done.3
  1.3 0.0 copy-done.4
  1.3 0.1 copy-done.6
  1.4 0.1 copy-done.5
  1.6 3.0 %collective-permute-start = (f32[82,1,256]{2,1,0:T(1,128)S(1)}, f32[82,1,256]{2,1,0:T(1,128)S(1)}, u32[]{:S(2)}, u32[]{:S(2)}) collective-permute-start(f32[82,1,256]{2,1,0:T(1,128)S(1)} %field_rows.1.refs_5_), channel_id=1, source_target_pairs={{0,1},{1,0},{2,3},{3,2},{4,5},{5,4},{6,7},{7,6},{8,9},{9,8},{10,11... | collective-permute-start | bytes 251912 | tf_op jit(solution)/shard_map/ppermute | solution.py:904
  4.6 0.7 prepare.1
  5.3 1.7 %collective-permute-done.refs_6_ = f32[82,1,256]{2,1,0:T(1,128)S(1)} collective-permute-done((f32[82,1,256]{2,1,0:T(1,128)S(1)}, f32[82,1,256]{2,1,0:T(1,128)S(1)}, u32[]{:S(2)}, u32[]{:S(2)}) %collective-permute-start) | collective-permute-done | bytes 84000 | tf_op jit(solution)/shard_map/ppermute | solution.py:904
  7.1 3.6 %data_part.3 = (f32[64,512]{1,0:T(8,128)S(1)}, f32[64,512]{1,0:T(8,128)S(1)}, f32[32,512]{1,0:T(8,128)S(1)}, f32[8,128]{1,0:T(8,128)S(1)}, bf16[8,256,256]{2,1,0:T(8,128)(2,1)S(1)}) custom-call(s32[4]{0:T(128)S(1)} %copy-done.3, s32[4]{0:T(128)S(1)} %copy-done.4, bf16[4,2,8,256,256]{4,3,2,1,0:T(8,128)(2,1)S(1)} %bitcast.28, ...), custom_call_target="tpu_custom_call" | custom-call | flops 6000000000 | bytes 8000000 | tf_op jit(solution)/shard_map/data_part/pallas_call | solution.py:466
  10.7 0.8 %collective-permute-start.1 = (f32[64,512]{1,0:T(8,128)S(1)}, f32[64,512]{1,0:T(8,128)S(1)}, u32[]{:S(2)}, u32[]{:S(2)}) collective-permute-start(f32[64,512]{1,0:T(8,128)S(1)} %get-tuple-element.53.refs_6_), channel_id=1, source_target_pairs={{0,1},{1,0},{2,3},{3,2},{4,5},{5,4},{6,7},{7,6},{8,9},{9,8},{10,11... | collective-permute-start | bytes 393224 | tf_op jit(solution)/shard_map/ppermute | solution.py:904
  11.5 3.7 %gradient_part.3 = (f32[64,512]{1,0:T(8,128)S(1)}, bf16[2,2,64,512]{3,2,1,0:T(8,128)(2,1)S(1)}, bf16[2,4,64,512]{3,2,1,0:T(8,128)(2,1)S(1)}) custom-call(f32[8,128]{1,0:T(8,128)S(1)} %get-tuple-element.47.refs_0_, f32[32,512]{1,0:T(8,128)S(1)} %get-tuple-element.48.refs_1_.refs_7_, f32[64,128]{1,0:T(8,128)S(1)} %get-tuple-element.44.refs_3_.refs_2_, ...), custom_call_target="tpu_custom_call" | custom-call | flops 4000000000 | bytes 2000000 | tf_op jit(solution)/shard_map/gradient_part/pallas_call | solution.py:665
  15.2 0.6 collective-permute-done.1.refs_7_
  15.8 1.6 %curvature_part.3 = (f32[64,512]{1,0:T(8,128)S(1)}, f32[64,512]{1,0:T(8,128)S(1)}, f32[32,128]{1,0:T(8,128)}) custom-call(f32[8,128]{1,0:T(8,128)S(1)} %get-tuple-element.47.refs_0_, f32[32,512]{1,0:T(8,128)S(1)} %get-tuple-element.48.refs_1_.refs_7_, f32[64,128]{1,0:T(8,128)S(1)} %get-tuple-element.44.refs_3_.refs_2_, ...), custom_call_target="tpu_custom_call" | custom-call | flops 2000000000 | bytes 2000000 | tf_op jit(solution)/shard_map/curvature_part/pallas_call | solution.py:770
  17.3 5.6 %all-to-all-start = ((f32[32,1,128]{2,1,0:T(1,128)}), f32[32,1,128]{2,1,0:T(1,128)S(1)}, u32[]{:S(2)}, u32[]{:S(2)}) async-start(f32[32,1,128]{2,1,0:T(1,128)} %bitcast.8), calls=%async_computation | async-start | bytes 32768 | tf_op jit(solution)/shard_map/all_to_all | solution.py:967
  22.9 3.9 %data_part.4.refs_6_ = f32[64,512]{1,0:T(8,128)S(1)} custom-call(s32[4]{0:T(128)S(1)} %copy-done.3, s32[4]{0:T(128)S(1)} %copy-done.4, bf16[4,2,8,256,256]{4,3,2,1,0:T(8,128)(2,1)} %bitcast.24, f32[64,128]{1,0:T(8,128)S(1)} %get-tuple-element.44.refs_3_.refs_2_, bf16[2,256,256]{2,1,0:T(8,128)(2,1)S(1)} %baseline_masks.1.masks.refs_4_, ...), custom_call_target="tpu_custom_call" | custom-call | flops 6000000000 | bytes 8000000 | tf_op jit(solution)/shard_map/data_part/pallas_call | solution.py:466
  26.9 0.5 collective-permute-start.2
  27.4 2.7 %all-to-all-done = f32[32,1,128]{2,1,0:T(1,128)S(1)} async-done(((f32[32,1,128]{2,1,0:T(1,128)}), f32[32,1,128]{2,1,0:T(1,128)S(1)}, u32[]{:S(2)}, u32[]{:S(2)}) %all-to-all-start) | async-done | bytes 16416 | tf_op jit(solution)/shard_map/all_to_all | solution.py:967
  30.0 3.9 %gradient_part.4 = (f32[64,512]{1,0:T(8,128)S(1)}, f32[64,512]{1,0:T(8,128)S(1)}, f32[8,128]{1,0:T(8,128)S(1)}, bf16[2,2,64,512]{3,2,1,0:T(8,128)(2,1)S(1)}, bf16[2,4,64,512]{3,2,1,0:T(8,128)(2,1)S(1)}) custom-call(f32[8,128]{1,0:T(8,128)S(1)} %get-tuple-element.47.refs_0_, f32[32,512]{1,0:T(8,128)S(1)} %get-tuple-element.48.refs_1_.refs_7_, ...), custom_call_target="tpu_custom_call" | custom-call | flops 4000000000 | bytes 2000000 | tf_op jit(solution)/shard_map/gradient_part/pallas_call | solution.py:665
  33.9 0.0 collective-permute-done.2.refs_7_
  33.9 1.6 %curvature_part.4 = (f32[64,512]{1,0:T(8,128)S(1)}, f32[64,512]{1,0:T(8,128)S(1)}, f32[32,128]{1,0:T(8,128)}) custom-call(f32[8,128]{1,0:T(8,128)S(1)} %get-tuple-element.47.refs_0_, f32[32,512]{1,0:T(8,128)S(1)} %get-tuple-element.48.refs_1_.refs_7_, f32[64,128]{1,0:T(8,128)S(1)} %get-tuple-element.44.refs_3_.refs_2_, ...), custom_call_target="tpu_custom_call" | custom-call | flops 2000000000 | bytes 2000000 | tf_op jit(solution)/shard_map/curvature_part/pallas_call | solution.py:770
  35.5 3.5 %all-to-all-start.1 = ((f32[32,1,128]{2,1,0:T(1,128)}), f32[32,1,128]{2,1,0:T(1,128)S(1)}, u32[]{:S(2)}, u32[]{:S(2)}) async-start(f32[32,1,128]{2,1,0:T(1,128)} %bitcast.11), calls=%async_computation.1 | async-start | bytes 32768 | tf_op jit(solution)/shard_map/all_to_all | solution.py:967
  39.0 4.1 %data_part.5.refs_6_ = f32[64,512]{1,0:T(8,128)S(1)} custom-call(s32[4]{0:T(128)S(1)} %copy-done.3, s32[4]{0:T(128)S(1)} %copy-done.4, bf16[4,2,8,256,256]{4,3,2,1,0:T(8,128)(2,1)} %bitcast.25, f32[64,128]{1,0:T(8,128)S(1)} %get-tuple-element.44.refs_3_.refs_2_, bf16[2,256,256]{2,1,0:T(8,128)(2,1)S(1)} %baseline_masks.1.masks.refs_4_, ...), custom_call_target="tpu_custom_call" | custom-call | flops 6000000000 | bytes 8000000 | tf_op jit(solution)/shard_map/data_part/pallas_call | solution.py:466
  43.1 0.5 collective-permute-start.3
  43.6 2.5 %all-to-all-done.1 = f32[32,1,128]{2,1,0:T(1,128)S(1)} async-done(((f32[32,1,128]{2,1,0:T(1,128)}), f32[32,1,128]{2,1,0:T(1,128)S(1)}, u32[]{:S(2)}, u32[]{:S(2)}) %all-to-all-start.1) | async-done | bytes 16416 | tf_op jit(solution)/shard_map/all_to_all | solution.py:967
  46.1 3.9 %gradient_part.5 = (f32[64,512]{1,0:T(8,128)S(1)}, f32[64,512]{1,0:T(8,128)S(1)}, f32[8,128]{1,0:T(8,128)S(1)}, bf16[2,2,64,512]{3,2,1,0:T(8,128)(2,1)S(1)}, bf16[2,4,64,512]{3,2,1,0:T(8,128)(2,1)S(1)}) custom-call(f32[8,128]{1,0:T(8,128)S(1)} %get-tuple-element.47.refs_0_, f32[32,512]{1,0:T(8,128)S(1)} %get-tuple-element.48.refs_1_.refs_7_, ...), custom_call_target="tpu_custom_call" | custom-call | flops 4000000000 | bytes 2000000 | tf_op jit(solution)/shard_map/gradient_part/pallas_call | solution.py:665
  50.0 0.0 collective-permute-done.3.refs_7_
  50.0 1.5 %curvature_part.5 = (f32[64,512]{1,0:T(8,128)S(1)}, f32[136,128]{1,0:T(8,128)S(1)}, f32[136,128]{1,0:T(8,128)S(1)}) custom-call(f32[8,128]{1,0:T(8,128)S(1)} %get-tuple-element.47.refs_0_, f32[32,512]{1,0:T(8,128)S(1)} %get-tuple-element.48.refs_1_.refs_7_, f32[64,128]{1,0:T(8,128)S(1)} %get-tuple-element.44.refs_3_.refs_2_, ...), custom_call_target="tpu_custom_call" | custom-call | flops 2000000000 | bytes 2000000 | tf_op jit(solution)/shard_map/curvature_part/pallas_call | solution.py:770
  51.5 0.1 collective-permute-start.4
  51.6 1.2 %collective-permute-done.4.theirs = f32[136,128]{1,0:T(8,128)S(1)} collective-permute-done((f32[136,128]{1,0:T(8,128)S(1)}, f32[136,128]{1,0:T(8,128)S(1)}, u32[]{:S(2)}, u32[]{:S(2)}) %collective-permute-start.4) | collective-permute-done | bytes 69664 | tf_op jit(solution)/shard_map/ppermute | solution.py:900
  52.9 0.6 collective-permute-start.5
  53.4 1.5 %collective-permute-start.6 = (f32[72,128]{1,0:T(8,128)S(1)}, f32[72,128]{1,0:T(8,128)S(1)}, u32[]{:S(2)}, u32[]{:S(2)}) collective-permute-start(f32[72,128]{1,0:T(8,128)S(1)} %get-tuple-element.76), channel_id=1, source_target_pairs={{0,8},{2,10},{4,12},{6,14},{8,0},{10,2},{12,4},{14,6},{16,24},{18,... | collective-permute-start | bytes 110600 | tf_op jit(solution)/shard_map/ppermute | solution.py:900
  54.9 1.5 %collective-permute-start.7 = (f32[72,128]{1,0:T(8,128)S(1)}, f32[72,128]{1,0:T(8,128)S(1)}, u32[]{:S(2)}, u32[]{:S(2)}) collective-permute-start(f32[72,128]{1,0:T(8,128)S(1)} %get-tuple-element.77), channel_id=1, source_target_pairs={{0,12},{2,14},{4,8},{6,10},{8,4},{10,6},{12,0},{14,2},{16,28},{18,... | collective-permute-start | bytes 110600 | tf_op jit(solution)/shard_map/ppermute | solution.py:900
  56.4 0.5 collective-permute-done.5.refs_1_
  56.9 0.8 %collective-permute-done.6.refs_2_ = f32[72,128]{1,0:T(8,128)S(1)} collective-permute-done((f32[72,128]{1,0:T(8,128)S(1)}, f32[72,128]{1,0:T(8,128)S(1)}, u32[]{:S(2)}, u32[]{:S(2)}) %collective-permute-start.6) | collective-permute-done | bytes 36896 | tf_op jit(solution)/shard_map/ppermute | solution.py:900
  57.7 2.0 %collective-permute-done.7.refs_3_ = f32[72,128]{1,0:T(8,128)S(1)} collective-permute-done((f32[72,128]{1,0:T(8,128)S(1)}, f32[72,128]{1,0:T(8,128)S(1)}, u32[]{:S(2)}, u32[]{:S(2)}) %collective-permute-start.7) | collective-permute-done | bytes 36896 | tf_op jit(solution)/shard_map/ppermute | solution.py:900
  59.7 0.1 weigh.1.one
  59.8 2.5 %collective-permute-start.8 = (f32[136,128]{1,0:T(8,128)S(1)}, f32[136,128]{1,0:T(8,128)S(1)}, u32[]{:S(2)}, u32[]{:S(2)}) collective-permute-start(f32[136,128]{1,0:T(8,128)S(1)} %weigh.1.one), channel_id=1, source_target_pairs={{0,16},{2,18},{4,20},{6,22},{8,24},{10,26},{12,28},{14,30},{16,0},... | collective-permute-start | bytes 208904 | tf_op jit(solution)/shard_map/ppermute | solution.py:900
  62.3 3.5 %collective-permute-done.8.two = f32[136,128]{1,0:T(8,128)S(1)} collective-permute-done((f32[136,128]{1,0:T(8,128)S(1)}, f32[136,128]{1,0:T(8,128)S(1)}, u32[]{:S(2)}, u32[]{:S(2)}) %collective-permute-start.8) | collective-permute-done | bytes 69664 | tf_op jit(solution)/shard_map/ppermute | solution.py:900
  65.9 0.2 combine.1
  66.1 0.8 %collective-permute-start.11 = (f32[64,128]{1,0:T(8,128)S(1)}, f32[64,128]{1,0:T(8,128)S(1)}, u32[]{:S(2)}, u32[]{:S(2)}) collective-permute-start(f32[64,128]{1,0:T(8,128)S(1)} %get-tuple-element.81), channel_id=1, source_target_pairs={{0,12},{2,14},{4,8},{6,10},{8,4},{10,6},{12,0},{14,2},{16,28},{18,... | collective-permute-start | bytes 98312 | tf_op jit(solution)/shard_map/ppermute | solution.py:900
  66.9 0.5 collective-permute-start.10
  67.4 2.2 %collective-permute-start.9 = (f32[64,128]{1,0:T(8,128)S(1)}, f32[64,128]{1,0:T(8,128)S(1)}, u32[]{:S(2)}, u32[]{:S(2)}) collective-permute-start(f32[64,128]{1,0:T(8,128)S(1)} %get-tuple-element.81), channel_id=1, source_target_pairs={{0,4},{2,6},{4,0},{6,2},{8,12},{10,14},{12,8},{14,10},{16,20},{18,... | collective-permute-start | bytes 98312 | tf_op jit(solution)/shard_map/ppermute | solution.py:900
  69.6 1.9 %collective-permute-done.9 = f32[64,128]{1,0:T(8,128)S(1)} collective-permute-done((f32[64,128]{1,0:T(8,128)S(1)}, f32[64,128]{1,0:T(8,128)S(1)}, u32[]{:S(2)}, u32[]{:S(2)}) %collective-permute-start.9) | collective-permute-done | bytes 32800 | tf_op jit(solution)/shard_map/ppermute | solution.py:900
  71.5 0.0 collective-permute-done.10
  71.6 0.1 collective-permute-start.12
  71.6 0.7 last_step.1
  72.3 0.6 collective-permute-done.12.theirs
  73.0 0.9 %consensus.1 = (f32[64,4,256]{2,1,0:T(4,128)}, f32[64,1,256]{2,1,0:T(1,128)}) custom-call(f32[256,128]{1,0:T(8,128)S(1)} %constant_dynamic-update-slice_fusion.mine, f32[256,128]{1,0:T(8,128)S(1)} %collective-permute-done.12.theirs, f32[64,1,256]{2,1,0:T(1,128)S(1)} %get-tuple-element.82.shifted), custom_call_target="tpu_custom_call" | custom-call | tf_op jit(solution)/shard_map/consensus/pallas_call | solution.py:889
  (22 shorter events, 0.1 us)
Async XLA Ops:
  0.6 0.7 copy-start.3
  0.6 0.7 copy-start.4
  0.7 0.7 copy-start.6
  0.7 0.9 %copy-start.5 = (f32[8,8,1,256]{3,2,1,0:T(1,128)S(1)}, f32[8,8,1,256]{3,2,1,0:T(1,128)}, u32[]{:S(2)}) copy-start(f32[8,8,1,256]{3,2,1,0:T(1,128)} %param.11) | copy-start | bytes 196612
  0.7 6.4 %slice-start = ((s8[8388608]{0:T(1024)(128)(4,1)}), s8[4194304]{0:T(1024)(128)(4,1)S(1)}, s32[]{:S(2)}) async-start(s8[8388608]{0:T(1024)(128)(4,1)} %bitcast.26), calls=%async_computation.2 | async-start | bytes 8388608
  1.5 3.1 %copy-start = (f32[8,8,4,256]{3,2,1,0:T(4,128)S(1)}, f32[8,8,4,256]{3,2,1,0:T(4,128)}, u32[]{:S(2)}) copy-start(f32[8,8,4,256]{3,2,1,0:T(4,128)} %param.13) | copy-start | bytes 786436
  1.5 3.1 %copy-start.1 = (f32[8,8,1,256]{3,2,1,0:T(1,128)S(1)}, f32[8,8,1,256]{3,2,1,0:T(1,128)}, u32[]{:S(2)}) copy-start(f32[8,8,1,256]{3,2,1,0:T(1,128)} %param.12) | copy-start | bytes 196612
  1.5 3.1 %copy-start.2 = (f32[8,8]{1,0:T(8,128)S(1)}, f32[8,8]{1,0:T(8,128)}, u32[]{:S(2)}) copy-start(f32[8,8]{1,0:T(8,128)} %refs_4_.1) | copy-start | bytes 772
  1.5 5.5 %slice-start.1 = ((s8[8388608]{0:T(1024)(128)(4,1)}), s8[4194304]{0:T(1024)(128)(4,1)S(1)}, s32[]{:S(2)}) async-start(s8[8388608]{0:T(1024)(128)(4,1)} %bitcast.26), calls=%async_computation.3 | async-start | bytes 8388608
  1.6 5.5 %collective-permute-start = (f32[82,1,256]{2,1,0:T(1,128)S(1)}, f32[82,1,256]{2,1,0:T(1,128)S(1)}, u32[]{:S(2)}, u32[]{:S(2)}) collective-permute-start(f32[82,1,256]{2,1,0:T(1,128)S(1)} %field_rows.1.refs_5_), channel_id=1, source_target_pairs={{0,1},{1,0},{2,3},{3,2},{4,5},{5,4},{6,7},{7,6},{8,9},{9,8},{10,11... | collective-permute-start | bytes 251912 | tf_op jit(solution)/shard_map/ppermute | solution.py:904
  10.7 5.0 %collective-permute-start.1 = (f32[64,512]{1,0:T(8,128)S(1)}, f32[64,512]{1,0:T(8,128)S(1)}, u32[]{:S(2)}, u32[]{:S(2)}) collective-permute-start(f32[64,512]{1,0:T(8,128)S(1)} %get-tuple-element.53.refs_6_), channel_id=1, source_target_pairs={{0,1},{1,0},{2,3},{3,2},{4,5},{5,4},{6,7},{7,6},{8,9},{9,8},{10,11... | collective-permute-start | bytes 393224 | tf_op jit(solution)/shard_map/ppermute | solution.py:904
  17.3 12.7 %all-to-all-start = ((f32[32,1,128]{2,1,0:T(1,128)}), f32[32,1,128]{2,1,0:T(1,128)S(1)}, u32[]{:S(2)}, u32[]{:S(2)}) async-start(f32[32,1,128]{2,1,0:T(1,128)} %bitcast.8), calls=%async_computation | async-start | bytes 32768 | tf_op jit(solution)/shard_map/all_to_all | solution.py:967
  26.9 7.1 %collective-permute-start.2 = (f32[64,512]{1,0:T(8,128)S(1)}, f32[64,512]{1,0:T(8,128)S(1)}, u32[]{:S(2)}, u32[]{:S(2)}) collective-permute-start(f32[64,512]{1,0:T(8,128)S(1)} %data_part.4.refs_6_), channel_id=1, source_target_pairs={{0,1},{1,0},{2,3},{3,2},{4,5},{5,4},{6,7},{7,6},{8,9},{9,8},{10,11... | collective-permute-start | bytes 393224 | tf_op jit(solution)/shard_map/ppermute | solution.py:904
  35.5 10.6 %all-to-all-start.1 = ((f32[32,1,128]{2,1,0:T(1,128)}), f32[32,1,128]{2,1,0:T(1,128)S(1)}, u32[]{:S(2)}, u32[]{:S(2)}) async-start(f32[32,1,128]{2,1,0:T(1,128)} %bitcast.11), calls=%async_computation.1 | async-start | bytes 32768 | tf_op jit(solution)/shard_map/all_to_all | solution.py:967
  43.1 6.9 %collective-permute-start.3 = (f32[64,512]{1,0:T(8,128)S(1)}, f32[64,512]{1,0:T(8,128)S(1)}, u32[]{:S(2)}, u32[]{:S(2)}) collective-permute-start(f32[64,512]{1,0:T(8,128)S(1)} %data_part.5.refs_6_), channel_id=1, source_target_pairs={{0,1},{1,0},{2,3},{3,2},{4,5},{5,4},{6,7},{7,6},{8,9},{9,8},{10,11... | collective-permute-start | bytes 393224 | tf_op jit(solution)/shard_map/ppermute | solution.py:904
  51.5 1.3 %collective-permute-start.4 = (f32[136,128]{1,0:T(8,128)S(1)}, f32[136,128]{1,0:T(8,128)S(1)}, u32[]{:S(2)}, u32[]{:S(2)}) collective-permute-start(f32[136,128]{1,0:T(8,128)S(1)} %get-tuple-element.73), channel_id=1, source_target_pairs={{0,2},{2,0},{4,6},{6,4},{8,10},{10,8},{12,14},{14,12},{16,18},{18,... | collective-permute-start | bytes 208904 | tf_op jit(solution)/shard_map/ppermute | solution.py:900
  52.9 4.0 %collective-permute-start.5 = (f32[72,128]{1,0:T(8,128)S(1)}, f32[72,128]{1,0:T(8,128)S(1)}, u32[]{:S(2)}, u32[]{:S(2)}) collective-permute-start(f32[72,128]{1,0:T(8,128)S(1)} %get-tuple-element.75), channel_id=1, source_target_pairs={{0,4},{2,6},{4,0},{6,2},{8,12},{10,14},{12,8},{14,10},{16,20},{18,... | collective-permute-start | bytes 110600 | tf_op jit(solution)/shard_map/ppermute | solution.py:900
  53.4 4.3 %collective-permute-start.6 = (f32[72,128]{1,0:T(8,128)S(1)}, f32[72,128]{1,0:T(8,128)S(1)}, u32[]{:S(2)}, u32[]{:S(2)}) collective-permute-start(f32[72,128]{1,0:T(8,128)S(1)} %get-tuple-element.76), channel_id=1, source_target_pairs={{0,8},{2,10},{4,12},{6,14},{8,0},{10,2},{12,4},{14,6},{16,24},{18,... | collective-permute-start | bytes 110600 | tf_op jit(solution)/shard_map/ppermute | solution.py:900
  54.9 4.9 %collective-permute-start.7 = (f32[72,128]{1,0:T(8,128)S(1)}, f32[72,128]{1,0:T(8,128)S(1)}, u32[]{:S(2)}, u32[]{:S(2)}) collective-permute-start(f32[72,128]{1,0:T(8,128)S(1)} %get-tuple-element.77), channel_id=1, source_target_pairs={{0,12},{2,14},{4,8},{6,10},{8,4},{10,6},{12,0},{14,2},{16,28},{18,... | collective-permute-start | bytes 110600 | tf_op jit(solution)/shard_map/ppermute | solution.py:900
  59.8 6.0 %collective-permute-start.8 = (f32[136,128]{1,0:T(8,128)S(1)}, f32[136,128]{1,0:T(8,128)S(1)}, u32[]{:S(2)}, u32[]{:S(2)}) collective-permute-start(f32[136,128]{1,0:T(8,128)S(1)} %weigh.1.one), channel_id=1, source_target_pairs={{0,16},{2,18},{4,20},{6,22},{8,24},{10,26},{12,28},{14,30},{16,0},... | collective-permute-start | bytes 208904 | tf_op jit(solution)/shard_map/ppermute | solution.py:900
  66.1 5.5 %collective-permute-start.11 = (f32[64,128]{1,0:T(8,128)S(1)}, f32[64,128]{1,0:T(8,128)S(1)}, u32[]{:S(2)}, u32[]{:S(2)}) collective-permute-start(f32[64,128]{1,0:T(8,128)S(1)} %get-tuple-element.81), channel_id=1, source_target_pairs={{0,12},{2,14},{4,8},{6,10},{8,4},{10,6},{12,0},{14,2},{16,28},{18,... | collective-permute-start | bytes 98312 | tf_op jit(solution)/shard_map/ppermute | solution.py:900
  66.9 4.6 %collective-permute-start.10 = (f32[64,128]{1,0:T(8,128)S(1)}, f32[64,128]{1,0:T(8,128)S(1)}, u32[]{:S(2)}, u32[]{:S(2)}) collective-permute-start(f32[64,128]{1,0:T(8,128)S(1)} %get-tuple-element.81), channel_id=1, source_target_pairs={{0,8},{2,10},{4,12},{6,14},{8,0},{10,2},{12,4},{14,6},{16,24},{18,... | collective-permute-start | bytes 98312 | tf_op jit(solution)/shard_map/ppermute | solution.py:900
  67.4 4.1 %collective-permute-start.9 = (f32[64,128]{1,0:T(8,128)S(1)}, f32[64,128]{1,0:T(8,128)S(1)}, u32[]{:S(2)}, u32[]{:S(2)}) collective-permute-start(f32[64,128]{1,0:T(8,128)S(1)} %get-tuple-element.81), channel_id=1, source_target_pairs={{0,4},{2,6},{4,0},{6,2},{8,12},{10,14},{12,8},{14,10},{16,20},{18,... | collective-permute-start | bytes 98312 | tf_op jit(solution)/shard_map/ppermute | solution.py:900
  71.6 1.4 %collective-permute-start.12 = (f32[256,128]{1,0:T(8,128)S(1)}, f32[256,128]{1,0:T(8,128)S(1)}, u32[]{:S(2)}, u32[]{:S(2)}) collective-permute-start(f32[256,128]{1,0:T(8,128)S(1)} %constant_dynamic-update-slice_fusion.mine), channel_id=1, source_target_pairs={{0,2},{2,0},{4,6},{6,4},{8,10},{10,8},{12,14},{14,12},{16,18},{18,... | collective-permute-start | bytes 393224 | tf_op jit(solution)/shard_map/ppermute | solution.py:900
